TPU v7x, 32 devices: a whole 2x2x4 slice. The times are simulated.
32 devices in a mesh: tensor: 4 (over z), dp: 4 (over x, core), pipe: 2 (over y).
Axes of the slice: x: 2, y: 2, z: 4, core: 2. Of those that a mesh axis runs over, the one named last changes fastest.
Arguments:
- mix: bfloat16 [2, 2, 4, 64, 4096], P('pipe', None, 'dp', None, 'tensor'), may hold values from -6 to 6
- hidden_in: bfloat16 [2, 4, 64, 8192], P(None, 'dp', 'tensor'), may hold values from -40 to 40
- cotangent: bfloat16 [2, 4, 64, 8192], P(None, 'dp', 'tensor'), may hold values from -6 to 6
- frozen_weight: bfloat16 [2, 4096, 8192], P('pipe', 'tensor', 'dp'), may hold values from -0.09375 to 0.09375
- right_factor: bfloat16 [2, 4, 1024, 128], P('pipe', 'tensor'), may hold values from -0.1875 to 0.1875
- left_factor: bfloat16 [2, 4, 128, 2048], P('pipe', 'tensor'), may hold values from -0.5 to 0.5
- norm_gain: bfloat16 [8192], replicated, may hold values from 0.25 to 1.75
Outputs:
- section_out: bfloat16 [2, 2, 4, 64, 8192], P('pipe', None, 'dp', 'tensor')
- grad_mix: bfloat16 [2, 2, 4, 64, 4096], P('pipe', None, 'dp', None, 'tensor')
- grad_right: float32 [2, 4, 1024, 128], P('pipe', 'tensor')
- grad_left: float32 [2, 4, 128, 2048], P('pipe', 'tensor')
All inputs are finite; a program needn't handle non-finite values.
Results may differ from a plain program's by a relative error of at most 0.0054.
Values may be sent and summed in bfloat16 or wider, within the bound.
No kernel may reach another device: no remote copies, remote signals or barrier semaphores. Data moves between devices by JAX's collectives and lax.ppermute only.
A program may use at most 128 MiB of HBM per device.

v0:
```python
import jax
import jax.numpy as jnp
from jax import lax
from jax.sharding import PartitionSpec as P


def passed_along(value, axis, steps):
    count = lax.axis_size(axis)
    first, last = (max(0, -steps), min(count, count - steps))
    return lax.ppermute(value, axis, [(source, source + steps) for source in range(first, last)])


def contract(left_side, right_side, left_dim, right_dim):
    return lax.dot_general(
        left_side,
        right_side,
        (((left_dim,), (right_dim,)), ((), ())),
        preferred_element_type=jnp.float32,
    )


def on_device(mix, hidden_in, cotangent, frozen_weight, right_factor, left_factor, norm_gain):
    section = lax.axis_index("pipe")
    sections = lax.axis_size("pipe")
    blocks = lax.axis_size("tensor")
    last = sections - 1
    weight = lax.all_gather(frozen_weight[0], "dp", axis=1, tiled=True)
    right = right_factor[0, 0]
    left = left_factor[0, 0]
    mixes = mix[0, :, 0]
    starts = hidden_in[:, 0]
    upstream_all = cotangent[:, 0]
    micro = mixes.shape[0]
    tokens = mixes.shape[1]
    head_cols = mixes.shape[2]
    rank = right.shape[1]
    group_width = rank // blocks
    width = weight.shape[1]
    block_cols = width // blocks
    own_rows = tokens // blocks
    ticks = micro + sections - 1
    received = jnp.zeros((own_rows, width), jnp.bfloat16)
    kept_out = [jnp.zeros((own_rows, width), jnp.bfloat16) for slot in range(micro)]
    kept_inner = [jnp.zeros((tokens, rank), jnp.bfloat16) for slot in range(micro)]
    for tick in range(ticks):
        index = tick - section
        valid = (index >= 0) & (index < micro)
        safe = jnp.clip(index, 0, micro - 1)
        own_mix = lax.dynamic_index_in_dim(mixes, safe, 0, keepdims=False)
        first = lax.dynamic_index_in_dim(starts, safe, 0, keepdims=False)
        entering = jnp.where(section == 0, first, received)
        inner = jnp.dot(own_mix, right, preferred_element_type=jnp.float32).astype(jnp.bfloat16)
        kept_now = lax.all_to_all(
            inner.reshape(tokens, blocks, group_width),
            "tensor",
            split_axis=1,
            concat_axis=1,
            tiled=True,
        ).reshape(tokens, rank)
        update = lax.psum_scatter(
            jnp.dot(own_mix, weight, preferred_element_type=jnp.float32),
            "tensor",
            scatter_dimension=0,
            tiled=True,
        )
        extra = jnp.dot(kept_now, left, preferred_element_type=jnp.float32)
        update = update + lax.all_to_all(extra, "tensor", split_axis=0, concat_axis=1, tiled=True)
        leaving = (entering.astype(jnp.float32) + update).astype(jnp.bfloat16)
        for slot in range(micro):
            chosen = valid & (index == slot)
            kept_out[slot] = jnp.where(chosen, leaving, kept_out[slot])
            kept_inner[slot] = jnp.where(chosen, kept_now, kept_inner[slot])
        if tick + 1 < ticks:
            received = passed_along(leaving, "pipe", 1)
    out_stack = jnp.stack(kept_out)
    inner_stack = jnp.stack(kept_inner)
    grad_right = jnp.zeros((head_cols, rank), jnp.float32)
    grad_left = jnp.zeros((rank, block_cols), jnp.float32)
    mix_grads = [jnp.zeros((tokens, head_cols), jnp.bfloat16) for slot in range(micro)]
    arriving = jnp.zeros((own_rows, width), jnp.bfloat16)
    gain = norm_gain.astype(jnp.float32)
    for tick in range(ticks):
        index = tick - (last - section)
        valid = (index >= 0) & (index < micro)
        safe = jnp.clip(index, 0, micro - 1)
        weight_now = valid.astype(jnp.float32)
        final = lax.dynamic_index_in_dim(out_stack, safe, 0, keepdims=False).astype(jnp.float32)
        upstream = (
            lax.dynamic_index_in_dim(upstream_all, safe, 0, keepdims=False).astype(jnp.float32)
            * gain
        )
        scale = lax.rsqrt(jnp.mean(final * final, axis=-1, keepdims=True) + 1e-05)
        normed = final * scale
        grad_top = (
            scale * (upstream - normed * jnp.mean(upstream * normed, axis=-1, keepdims=True))
        ).astype(jnp.bfloat16)
        grad_here = jnp.where(section == last, grad_top, arriving)
        grad_full = lax.all_gather(grad_here, "tensor", axis=0, tiled=True)
        own_mix = lax.dynamic_index_in_dim(mixes, safe, 0, keepdims=False)
        kept_now = lax.dynamic_index_in_dim(inner_stack, safe, 0, keepdims=False)
        back = contract(grad_full, weight, 1, 1)
        grad_cols = lax.dynamic_slice_in_dim(
            grad_full, lax.axis_index("tensor") * block_cols, block_cols, 1
        )
        grad_permuted = contract(grad_cols, left, 1, 1).astype(jnp.bfloat16)
        grad_inner = lax.all_to_all(
            grad_permuted.reshape(tokens, blocks, group_width),
            "tensor",
            split_axis=1,
            concat_axis=1,
            tiled=True,
        ).reshape(tokens, rank)
        grad_left = grad_left + weight_now * contract(kept_now, grad_cols, 0, 0)
        mix_grad = (back + contract(grad_inner, right, 1, 1)).astype(jnp.bfloat16)
        grad_right = grad_right + weight_now * contract(own_mix, grad_inner, 0, 0)
        for slot in range(micro):
            mix_grads[slot] = jnp.where(valid & (index == slot), mix_grad, mix_grads[slot])
        if tick + 1 < ticks:
            arriving = passed_along(grad_here, "pipe", -1)
    grad_right, grad_left = lax.psum((grad_right, grad_left), "dp")
    section_out = out_stack.reshape(1, micro, 1, own_rows, width)
    grad_mix = jnp.stack(mix_grads).reshape(1, micro, 1, tokens, head_cols)
    return (
        section_out,
        grad_mix,
        grad_right.reshape(1, 1, head_cols, rank),
        grad_left.reshape(1, 1, rank, block_cols),
    )


def solution(mesh):
    return jax.shard_map(
        on_device,
        mesh=mesh,
        in_specs=(
            P("pipe", None, "dp", None, "tensor"),
            P(None, "dp", "tensor", None),
            P(None, "dp", "tensor", None),
            P("pipe", "tensor", "dp"),
            P("pipe", "tensor", None, None),
            P("pipe", "tensor", None, None),
            P(),
        ),
        out_specs=(
            P("pipe", None, "dp", "tensor", None),
            P("pipe", None, "dp", None, "tensor"),
            P("pipe", "tensor", None, None),
            P("pipe", "tensor", None, None),
        ),
        check_vma=False,
    )
```

profile of v0, /device:TPU:0, one launch (start us, length us, event | category | flops | bytes accessed | tf_op | source)
XLA Modules:
  0.0 446.3 jit_solution(8033087416310197073)
XLA Ops:
  7.2 0.7 all-gather.12.cloned.1.call-update
  8.0 110.3 %all-gather.12.cloned.1.call-done = bf16[1,1024,8192]{2,1,0:T(8,128)(2,1)} async-done(((bf16[1,1024,2048]{2,1,0:T(8,128)(2,1)}), bf16[1,1024,8192]{2,1,0:T(8,128)(2,1)}) %all-gather.12.cloned.1.call-update) | async-done | bytes 16777232 | tf_op jit(solution)/shard_map/all_gather | solution.py:27
  118.2 10.2 %fusion.10 = f32[64,8192]{1,0:T(8,128)} fusion(bf16[1,1024,8192]{2,1,0:T(8,128)(2,1)} %all-gather.12.cloned.1.call-done, bf16[1,2,1,64,1024]{4,3,2,1,0:T(8,128)(2,1)} %param.7, s32[]{:T(128)S(6)} %min.21), kind=kOutput, calls=%fused_computation.10 | convolution fusion | flops 1073741824 | bytes 19005444 | tf_op jit(solution)/shard_map/dot_general | solution.py:61
  128.5 10.1 %fusion.8 = f32[64,8192]{1,0:T(8,128)} fusion(bf16[1,1024,8192]{2,1,0:T(8,128)(2,1)} %all-gather.12.cloned.1.call-done, bf16[1,2,1,64,1024]{4,3,2,1,0:T(8,128)(2,1)S(1)} %copy-done.2, s32[]{:T(128)S(6)} %min.20), kind=kOutput, calls=%fused_computation.8 | convolution fusion | flops 1073741824 | bytes 19005444 | tf_op jit(solution)/shard_map/dot_general | solution.py:61
  139.0 0.7 reshape.241
  139.7 4.6 %all-to-all-start.2 = ((bf16[4,2,1024]{2,1,0:T(2,128)(2,1)}), bf16[4,2,1024]{2,1,0:T(2,128)(2,1)S(1)}, u32[]{:S(2)}, u32[]{:S(2)}) async-start(bf16[4,2,1024]{2,1,0:T(2,128)(2,1)} %reshape.241), calls=%async_computation.4 | async-start | bytes 32768 | tf_op jit(solution)/shard_map/all_to_all | solution.py:53
  144.6 0.7 reshape.243
  145.3 4.7 %all-to-all-done.2 = bf16[4,2,1024]{2,1,0:T(2,128)(2,1)S(1)} async-done(((bf16[4,2,1024]{2,1,0:T(2,128)(2,1)}), bf16[4,2,1024]{2,1,0:T(2,128)(2,1)S(1)}, u32[]{:S(2)}, u32[]{:S(2)}) %all-to-all-start.2) | async-done | bytes 16416 | tf_op jit(solution)/shard_map/all_to_all | solution.py:53
  150.1 3.3 all-to-all-start
  153.6 0.7 reshape.239
  154.7 4.6 %all-to-all-done = bf16[4,2,1024]{2,1,0:T(2,128)(2,1)S(1)} async-done(((bf16[4,2,1024]{2,1,0:T(2,128)(2,1)}), bf16[4,2,1024]{2,1,0:T(2,128)(2,1)S(1)}, u32[]{:S(2)}, u32[]{:S(2)}) %all-to-all-start) | async-done | bytes 16416 | tf_op jit(solution)/shard_map/all_to_all | solution.py:53
  159.6 1.0 fusion.58
  160.6 3.5 all-to-all-start.1
  164.2 10.3 %fusion.6 = f32[64,8192]{1,0:T(8,128)} fusion(bf16[1,1024,8192]{2,1,0:T(8,128)(2,1)} %all-gather.12.cloned.1.call-done, bf16[1,2,1,64,1024]{4,3,2,1,0:T(8,128)(2,1)S(1)} %copy-done.2, s32[]{:T(128)S(6)} %min.19), kind=kOutput, calls=%fused_computation.6 | convolution fusion | flops 1073741824 | bytes 19005444 | tf_op jit(solution)/shard_map/dot_general | solution.py:61
  174.5 8.7 %all-to-all-done.1 = f32[4,16,2048]{2,1,0:T(8,128)S(1)} async-done(((f32[4,16,2048]{2,1,0:T(8,128)}), f32[4,16,2048]{2,1,0:T(8,128)S(1)}, u32[]{:S(2)}, u32[]{:S(2)}) %all-to-all-start.1) | async-done | bytes 524320 | tf_op jit(solution)/shard_map/all_to_all | solution.py:67
  183.2 3.3 all-to-all-start.4
  186.4 1.0 fusion.56
  187.5 4.5 %all-to-all-done.4 = bf16[4,2,1024]{2,1,0:T(2,128)(2,1)S(1)} async-done(((bf16[4,2,1024]{2,1,0:T(2,128)(2,1)}), bf16[4,2,1024]{2,1,0:T(2,128)(2,1)S(1)}, u32[]{:S(2)}, u32[]{:S(2)}) %all-to-all-start.4) | async-done | bytes 16416 | tf_op jit(solution)/shard_map/all_to_all | solution.py:53
  192.0 3.5 all-to-all-start.3
  195.5 1.2 fusion.53
  196.7 3.4 collective-permute-start
  200.5 1.0 fusion.54
  201.5 22.5 %all-to-all-done.3 = f32[4,16,2048]{2,1,0:T(8,128)S(1)} async-done(((f32[4,16,2048]{2,1,0:T(8,128)}), f32[4,16,2048]{2,1,0:T(8,128)S(1)}, u32[]{:S(2)}, u32[]{:S(2)}) %all-to-all-start.3) | async-done | bytes 524320 | tf_op jit(solution)/shard_map/all_to_all | solution.py:67
  223.9 4.8 %all-to-all-start.5 = ((f32[4,16,2048]{2,1,0:T(8,128)}), f32[4,16,2048]{2,1,0:T(8,128)S(1)}, u32[]{:S(2)}, u32[]{:S(2)}) async-start(f32[4,16,2048]{2,1,0:T(8,128)} %fusion.54), calls=%async_computation.8 | async-start | bytes 1048576 | tf_op jit(solution)/shard_map/all_to_all | solution.py:67
  228.7 1.1 copy.31
  229.8 3.1 reduce-scatter.6.cloned.1.call-done
  232.9 1.2 add_convert_fusion.1
  234.1 3.5 collective-permute-start.1
  237.8 7.9 %all-to-all-done.5 = f32[4,16,2048]{2,1,0:T(8,128)S(1)} async-done(((f32[4,16,2048]{2,1,0:T(8,128)}), f32[4,16,2048]{2,1,0:T(8,128)S(1)}, u32[]{:S(2)}, u32[]{:S(2)}) %all-to-all-start.5) | async-done | bytes 524320 | tf_op jit(solution)/shard_map/all_to_all | solution.py:67
  245.7 42.6 %reduce-scatter.8.cloned.1.call-done = f32[16,8192]{1,0:T(8,128)} async-done(((f32[64,8192]{1,0:T(8,128)}), f32[16,8192]{1,0:T(8,128)}) %reduce-scatter.8.cloned.1.call-update) | async-done | bytes 524304 | tf_op jit(solution)/shard_map/reduce_scatter | solution.py:60
  288.3 0.7 copy-done.7
  289.0 1.2 select_bitcast_fusion.1
  291.5 1.3 collective-permute-start.2
  292.9 8.5 %collective-permute-done.2 = bf16[16,8192]{1,0:T(8,128)(2,1)} collective-permute-done((bf16[16,8192]{1,0:T(8,128)(2,1)S(1)}, bf16[16,8192]{1,0:T(8,128)(2,1)}, u32[]{:S(2)}, u32[]{:S(2)}) %collective-permute-start.2) | collective-permute-done | bytes 262176 | tf_op jit(solution)/shard_map/ppermute | solution.py:10
  301.4 1.2 fusion.64
  302.5 1.3 collective-permute-start.3
  303.8 0.8 fusion.52
  304.9 6.5 %collective-permute-done.3 = bf16[16,8192]{1,0:T(8,128)(2,1)S(1)} collective-permute-done((bf16[16,8192]{1,0:T(8,128)(2,1)S(1)}, bf16[16,8192]{1,0:T(8,128)(2,1)S(1)}, u32[]{:S(2)}, u32[]{:S(2)}) %collective-permute-start.3) | collective-permute-done | bytes 262176 | tf_op jit(solution)/shard_map/ppermute | solution.py:10
  311.4 0.9 fusion.63
  312.4 9.7 %all-gather.10.cloned.1.call-done = bf16[64,8192]{1,0:T(8,128)(2,1)} async-done(((bf16[16,8192]{1,0:T(8,128)(2,1)}), bf16[64,8192]{1,0:T(8,128)(2,1)}) %all-gather.10.cloned.1.call-update) | async-done | bytes 1048592 | tf_op jit(solution)/shard_map/all_gather | solution.py:98
  322.1 1.2 convolution_convert_fusion
  323.4 0.7 reshape.249
  324.2 3.3 all-to-all-start.8
  327.4 11.6 %fusion = f32[64,1024]{1,0:T(8,128)S(1)} fusion(bf16[64,8192]{1,0:T(8,128)(2,1)} %all-gather.10.cloned.1.call-done, bf16[1,1024,8192]{2,1,0:T(8,128)(2,1)} %all-gather.12.cloned.1.call-done), kind=kOutput, calls=%fused_computation | convolution fusion | flops 1073741824 | bytes 18087936 | tf_op jit(solution)/shard_map/dot_general | solution.py:14
  339.0 1.2 convolution_multiply_fusion.2
  340.6 11.0 %all-gather.8.cloned.1.call-done = bf16[64,8192]{1,0:T(8,128)(2,1)} async-done(((bf16[16,8192]{1,0:T(8,128)(2,1)}), bf16[64,8192]{1,0:T(8,128)(2,1)}) %all-gather.8.cloned.1.call-update) | async-done | bytes 1048592 | tf_op jit(solution)/shard_map/all_gather | solution.py:98
  351.6 1.2 convolution_convert_fusion.1
  353.0 0.7 reshape.247
  353.7 3.3 all-to-all-start.7
  357.0 1.3 fusion.14
  358.2 4.3 all-to-all-done.7
  363.1 11.4 %fusion.25 = bf16[64,1024]{1,0:T(8,128)(2,1)S(1)} fusion(f32[64,1024]{1,0:T(8,128)S(1)} %fusion.73, bf16[64,8192]{1,0:T(8,128)(2,1)} %all-gather.8.cloned.1.call-done, bf16[1,1024,8192]{2,1,0:T(8,128)(2,1)} %all-gather.12.cloned.1.call-done), kind=kOutput, calls=%fused_computation.28 | convolution fusion | flops 1073872896 | bytes 18219008 | tf_op jit(solution)/shard_map/dot_general | solution.py:14
  374.5 6.8 %all-gather.6.cloned.1.call-done = bf16[64,8192]{1,0:T(8,128)(2,1)} async-done(((bf16[16,8192]{1,0:T(8,128)(2,1)}), bf16[64,8192]{1,0:T(8,128)(2,1)}) %all-gather.6.cloned.1.call-update) | async-done | bytes 1048592 | tf_op jit(solution)/shard_map/all_gather | solution.py:98
  381.3 1.2 convolution_convert_fusion.2
  382.7 0.7 reshape.245
  383.4 3.3 all-to-all-start.6
  386.9 2.2 fusion.13
  389.1 3.1 all-to-all-done.6
  392.8 1.1 fusion.17
  393.9 11.6 %select_bitcast_fusion.3 = (bf16[1,64,1024]{2,1,0:T(8,128)(2,1)S(1)}, bf16[1,64,1024]{2,1,0:T(8,128)(2,1)S(1)}) fusion(bf16[64,1024]{1,0:T(8,128)(2,1)S(1)} %fusion.25, bf16[64,1024]{1,0:T(8,128)(2,1)S(1)} %fusion.24, pred[]{:T(512)S(6)} %and.70, pred[]{:T(512)S(6)} %and.68, pred[]{:T(512)S(6)} %and.66, pred[]{:T(512)S(6)} %and.73, pred[]{:T(512)S(6)} %and.72, ...), kind=kOutput, calls=%fused_computation.128 | convolution fusion | flops 1074266112 | bytes 18612230 | tf_op jit(solution)/shard_map/dot_general | solution.py:14
  405.5 0.7 maximum_bitcast_fusion
  406.3 29.1 %all-reduce.3.cloned.1.call-done = (f32[1,1,1024,128]{3,2,1,0:T(8,128)}, f32[1,1,128,2048]{3,2,1,0:T(8,128)}) async-done(((f32[1,1,1024,128]{3,2,1,0:T(8,128)}, f32[1,1,128,2048]{3,2,1,0:T(8,128)}), (f32[1,1,1024,128]{3,2,1,0:T(8,128)}, f32[1,1,128,2048]{3,2,1,0:T(8,128)})) %all-reduce.3.cloned.1.call-update) | async-done | bytes 1572880 | tf_op jit(solution)/shard_map/psum | solution.py:120
  435.3 1.9 copy.35
  437.2 2.3 copy.36
  (75 shorter events, 5.9 us)
Async XLA Ops:
  7.2 152.4 %copy-start = (bf16[1,1,128,2048]{3,2,1,0:T(8,128)(2,1)S(1)}, bf16[1,1,128,2048]{3,2,1,0:T(8,128)(2,1)}, u32[]{:S(2)}) copy-start(bf16[1,1,128,2048]{3,2,1,0:T(8,128)(2,1)} %param.12) | copy-start | bytes 1572868
  7.2 121.3 %copy-start.2 = (bf16[1,2,1,64,1024]{4,3,2,1,0:T(8,128)(2,1)S(1)}, bf16[1,2,1,64,1024]{4,3,2,1,0:T(8,128)(2,1)}, u32[]{:S(2)}) copy-start(bf16[1,2,1,64,1024]{4,3,2,1,0:T(8,128)(2,1)} %param.7) | copy-start | bytes 786436
  7.2 111.0 %all-gather.12.cloned.1.call-start = ((), (), s32[]{:S(2)}) async-start(), calls=%async_computation.18 | async-start | bytes 20971520 | tf_op jit(solution)/shard_map/all_gather | solution.py:27
  7.9 187.6 %reduce-scatter.4.cloned.1.call-start = ((), (), s32[]{:S(2)}) async-start(), calls=%async_computation.12 | async-start | bytes 2621440 | tf_op jit(solution)/shard_map/reduce_scatter | solution.py:60
  128.4 10.3 %copy-start.1 = (bf16[1,1,1024,128]{3,2,1,0:T(8,128)(2,1)S(1)}, bf16[1,1,1024,128]{3,2,1,0:T(8,128)(2,1)}, u32[]{:S(2)}) copy-start(bf16[1,1,1024,128]{3,2,1,0:T(8,128)(2,1)} %param.11) | copy-start | bytes 786436
  128.5 104.5 %reduce-scatter.6.cloned.1.call-start = ((), (), s32[]{:S(2)}) async-start(), calls=%async_computation.13 | async-start | bytes 2621440 | tf_op jit(solution)/shard_map/reduce_scatter | solution.py:60
  139.7 10.3 %all-to-all-start.2 = ((bf16[4,2,1024]{2,1,0:T(2,128)(2,1)}), bf16[4,2,1024]{2,1,0:T(2,128)(2,1)S(1)}, u32[]{:S(2)}, u32[]{:S(2)}) async-start(bf16[4,2,1024]{2,1,0:T(2,128)(2,1)} %reshape.241), calls=%async_computation.4 | async-start | bytes 32768 | tf_op jit(solution)/shard_map/all_to_all | solution.py:53
  150.1 9.2 %all-to-all-start = ((bf16[4,2,1024]{2,1,0:T(2,128)(2,1)}), bf16[4,2,1024]{2,1,0:T(2,128)(2,1)S(1)}, u32[]{:S(2)}, u32[]{:S(2)}) async-start(bf16[4,2,1024]{2,1,0:T(2,128)(2,1)} %reshape.243), calls=%async_computation.1 | async-start | bytes 32768 | tf_op jit(solution)/shard_map/all_to_all | solution.py:53
  160.6 22.5 %all-to-all-start.1 = ((f32[4,16,2048]{2,1,0:T(8,128)}), f32[4,16,2048]{2,1,0:T(8,128)S(1)}, u32[]{:S(2)}, u32[]{:S(2)}) async-start(f32[4,16,2048]{2,1,0:T(8,128)} %fusion.58), calls=%async_computation.2 | async-start | bytes 1048576 | tf_op jit(solution)/shard_map/all_to_all | solution.py:67
  164.1 73.6 %copy-start.8 = (bf16[8192]{0:T(1024)(128)(2,1)S(1)}, bf16[8192]{0:T(1024)(128)(2,1)}, u32[]{:S(2)}) copy-start(bf16[8192]{0:T(1024)(128)(2,1)} %param.13) | copy-start | bytes 49156
  164.1 126.7 %copy-start.3 = (bf16[2,1,16,8192]{3,2,1,0:T(8,128)(2,1)S(1)}, bf16[2,1,16,8192]{3,2,1,0:T(8,128)(2,1)}, u32[]{:S(2)}) copy-start(bf16[2,1,16,8192]{3,2,1,0:T(8,128)(2,1)} %param.9) | copy-start | bytes 1572868
  164.1 124.2 %reduce-scatter.8.cloned.1.call-start = ((), (), s32[]{:S(2)}) async-start(), calls=%async_computation.14 | async-start | bytes 2621440 | tf_op jit(solution)/shard_map/reduce_scatter | solution.py:60
  183.2 8.9 %all-to-all-start.4 = ((bf16[4,2,1024]{2,1,0:T(2,128)(2,1)}), bf16[4,2,1024]{2,1,0:T(2,128)(2,1)S(1)}, u32[]{:S(2)}, u32[]{:S(2)}) async-start(bf16[4,2,1024]{2,1,0:T(2,128)(2,1)} %reshape.239), calls=%async_computation.7 | async-start | bytes 32768 | tf_op jit(solution)/shard_map/all_to_all | solution.py:53
  192.0 31.9 %all-to-all-start.3 = ((f32[4,16,2048]{2,1,0:T(8,128)}), f32[4,16,2048]{2,1,0:T(8,128)S(1)}, u32[]{:S(2)}, u32[]{:S(2)}) async-start(f32[4,16,2048]{2,1,0:T(8,128)} %fusion.56), calls=%async_computation.5 | async-start | bytes 1048576 | tf_op jit(solution)/shard_map/all_to_all | solution.py:67
  196.7 36.2 %collective-permute-start = (bf16[16,8192]{1,0:T(8,128)(2,1)S(1)}, bf16[16,8192]{1,0:T(8,128)(2,1)S(1)}, u32[]{:S(2)}, u32[]{:S(2)}) collective-permute-start(bf16[16,8192]{1,0:T(8,128)(2,1)S(1)} %fusion.53), channel_id=1, source_target_pairs={{0,1},{2,3},{4,5},{6,7},{8,9},{10,11},{12,13},{14,15},{16,17},{18,... | collective-permute-start | bytes 786440 | tf_op jit(solution)/shard_map/ppermute | solution.py:10
  223.9 4.8 %copy-start.4 = (f32[4,16,2048]{2,1,0:T(8,128)}, f32[4,16,2048]{2,1,0:T(8,128)S(1)}, u32[]{:S(2)}) copy-start(f32[4,16,2048]{2,1,0:T(8,128)S(1)} %all-to-all-done.3) | copy-start | bytes 1572868
  223.9 21.8 %all-to-all-start.5 = ((f32[4,16,2048]{2,1,0:T(8,128)}), f32[4,16,2048]{2,1,0:T(8,128)S(1)}, u32[]{:S(2)}, u32[]{:S(2)}) async-start(f32[4,16,2048]{2,1,0:T(8,128)} %fusion.54), calls=%async_computation.8 | async-start | bytes 1048576 | tf_op jit(solution)/shard_map/all_to_all | solution.py:67
  228.7 93.3 %all-gather.10.cloned.1.call-start = ((), (), s32[]{:S(2)}) async-start(), calls=%async_computation.17 | async-start | bytes 1310720 | tf_op jit(solution)/shard_map/all_gather | solution.py:98
  234.1 54.2 %collective-permute-start.1 = (bf16[16,8192]{1,0:T(8,128)(2,1)S(1)}, bf16[16,8192]{1,0:T(8,128)(2,1)S(1)}, u32[]{:S(2)}, u32[]{:S(2)}) collective-permute-start(bf16[16,8192]{1,0:T(8,128)(2,1)S(1)} %add_convert_fusion.1), channel_id=1, source_target_pairs={{0,1},{2,3},{4,5},{6,7},{8,9},{10,11},{12,13},{14,15},{16,17},{18,... | collective-permute-start | bytes 786440 | tf_op jit(solution)/shard_map/ppermute | solution.py:10
  288.3 0.7 copy-start.7
  291.5 1.3 copy-start.5
  291.5 9.9 %collective-permute-start.2 = (bf16[16,8192]{1,0:T(8,128)(2,1)S(1)}, bf16[16,8192]{1,0:T(8,128)(2,1)}, u32[]{:S(2)}, u32[]{:S(2)}) collective-permute-start(bf16[16,8192]{1,0:T(8,128)(2,1)S(1)} %fusion.65), channel_id=1, source_target_pairs={{1,0},{3,2},{5,4},{7,6},{9,8},{11,10},{13,12},{15,14},{17,16},{19,... | collective-permute-start | bytes 786440 | tf_op jit(solution)/shard_map/ppermute | solution.py:10
  292.8 58.8 %all-gather.8.cloned.1.call-start = ((), (), s32[]{:S(2)}) async-start(), calls=%async_computation.16 | async-start | bytes 1310720 | tf_op jit(solution)/shard_map/all_gather | solution.py:98
  302.5 2.2 copy-start.6
  302.5 8.9 %collective-permute-start.3 = (bf16[16,8192]{1,0:T(8,128)(2,1)S(1)}, bf16[16,8192]{1,0:T(8,128)(2,1)S(1)}, u32[]{:S(2)}, u32[]{:S(2)}) collective-permute-start(bf16[16,8192]{1,0:T(8,128)(2,1)S(1)} %fusion.64), channel_id=1, source_target_pairs={{1,0},{3,2},{5,4},{7,6},{9,8},{11,10},{13,12},{15,14},{17,16},{19,... | collective-permute-start | bytes 786440 | tf_op jit(solution)/shard_map/ppermute | solution.py:10
  304.7 76.6 %all-gather.6.cloned.1.call-start = ((), (), s32[]{:S(2)}) async-start(), calls=%async_computation.15 | async-start | bytes 1310720 | tf_op jit(solution)/shard_map/all_gather | solution.py:98
  324.2 16.1 %all-to-all-start.8 = ((bf16[4,2,1024]{2,1,0:T(2,128)(2,1)}), bf16[4,2,1024]{2,1,0:T(2,128)(2,1)S(1)}, u32[]{:S(2)}, u32[]{:S(2)}) async-start(bf16[4,2,1024]{2,1,0:T(2,128)(2,1)} %reshape.249), calls=%async_computation.11 | async-start | bytes 32768 | tf_op jit(solution)/shard_map/all_to_all | solution.py:106
  353.7 8.8 %all-to-all-start.7 = ((bf16[4,2,1024]{2,1,0:T(2,128)(2,1)}), bf16[4,2,1024]{2,1,0:T(2,128)(2,1)S(1)}, u32[]{:S(2)}, u32[]{:S(2)}) async-start(bf16[4,2,1024]{2,1,0:T(2,128)(2,1)} %reshape.247), calls=%async_computation.10 | async-start | bytes 32768 | tf_op jit(solution)/shard_map/all_to_all | solution.py:106
  383.4 8.8 %all-to-all-start.6 = ((bf16[4,2,1024]{2,1,0:T(2,128)(2,1)}), bf16[4,2,1024]{2,1,0:T(2,128)(2,1)S(1)}, u32[]{:S(2)}, u32[]{:S(2)}) async-start(bf16[4,2,1024]{2,1,0:T(2,128)(2,1)} %reshape.245), calls=%async_computation.9 | async-start | bytes 32768 | tf_op jit(solution)/shard_map/all_to_all | solution.py:106
  386.6 48.7 %all-reduce.3.cloned.1.call-start = ((), (), s32[]{:S(2)}) async-start(), calls=%async_computation.19 | async-start | bytes 3145728 | tf_op jit(solution)/shard_map/psum | solution.py:120
Sparse Core Ops, SparseCore 0:
  9.6 108.6 all-gather.11
  128.6 47.9 reduce-scatter.3
  178.9 53.9 reduce-scatter.5
  235.1 53.1 reduce-scatter.7
  293.0 29.0 all-gather.9
  324.2 27.4 all-gather.7
  353.8 27.4 all-gather.5
  394.0 41.2 all-reduce.2
where the time goes:
time: 448 us; the launch traced here: 446 us
  waiting for transfers between devices  289 us (65%)
  matrix products  79.5 us (18%)
  starting transfers between devices  42.8 us (10%)
  between operations  14.7 us (3%)
  local copies, waits for them, and re-layouts  12.3 us (3%)
  other arithmetic  8.52 us (2%)
    all_gather x1, waiting for transfers between devices, on_device(): weight = lax.all_gather(frozen_weight[0], 'dp', axis=1, tiled=True)  110 us
    reduce_scatter x3, waiting for transfers between devices, on_device(): lax.psum_scatter(jnp.dot(own_mix, weight, preferred_element_type=jnp.floa...  45.7 us
    dot_general x15, matrix products, contract(): lax.dot_general(left_side, right_side, (((left_dim,), (right_dim,)), ((),...  45.3 us
    all_to_all x3, waiting for transfers between devices, on_device(): lax.all_to_all(extra, 'tensor', split_axis=0, concat_axis=1, tiled=True)  39.1 us
    dot_general x3, matrix products, on_device(): jnp.dot(own_mix, weight, preferred_element_type=jnp.float32)  30.6 us
    psum x1, waiting for transfers between devices, on_device(): grad_right, grad_left = lax.psum((grad_right, grad_left), 'dp')  29.1 us
    all_gather x3, waiting for transfers between devices, on_device(): grad_full = lax.all_gather(grad_here, 'tensor', axis=0, tiled=True)  27.5 us
    ppermute x4, waiting for transfers between devices, passed_along(): lax.ppermute(value, axis, [(source, source + steps) for source in range(f...  15 us
  transfers between devices with their start and end apart: 21, of which 17 were waited for; matrix products, arithmetic and copies ran while one was open for 18% of the time, Pallas kernels for 0%

commit v1 on v0

v1 whole, which is shorter than its diff:
```python
import jax
import jax.numpy as jnp
from jax import lax
from jax.sharding import PartitionSpec as P

F32 = jnp.float32
BF16 = jnp.bfloat16


def dot(left_side, right_side, left_dim, right_dim):
    return lax.dot_general(
        left_side,
        right_side,
        (((left_dim,), (right_dim,)), ((), ())),
        preferred_element_type=F32,
    )


def pick(value, index):
    return lax.dynamic_index_in_dim(value, index, 0, keepdims=False)


def columns(value, start, size):
    return lax.dynamic_slice_in_dim(value, start, size, value.ndim - 1)


def on_device(mix, hidden_in, cotangent, frozen_weight, right_factor, left_factor, norm_gain):
    blocks = lax.axis_size("tensor")
    parts = lax.axis_size("dp")
    sections = lax.axis_size("pipe")
    t = lax.axis_index("tensor")
    d = lax.axis_index("dp")
    section = lax.axis_index("pipe")
    outers = parts // 2
    outer = d // 2
    core = d % 2

    def to_core(value):
        return lax.ppermute(value, "dp", [(i, i ^ 1) for i in range(parts)])

    def to_outer(value, step):
        pairs = [(i, (i + 2 * step) % parts) for i in range(parts)]
        return lax.ppermute(value, "dp", pairs)

    mixes = mix[0, :, 0]
    micro, tokens, head_cols = mixes.shape
    own_rows = tokens // blocks
    weight = frozen_weight[0]
    right = right_factor[0, 0]
    left = left_factor[0, 0]
    rank, block_cols = left.shape
    sub = rank // blocks
    width = weight.shape[1]
    features = width * parts
    rows = outers * own_rows
    all_rows = blocks * rows
    per_block = parts // blocks
    slots = (d, d ^ 1)

    def block_of(part):
        return part // per_block

    own = mixes.reshape(micro, blocks, 1, own_rows, head_cols)
    taken = [
        jnp.concatenate(
            [own[m]] + [to_outer(own[m], step) for step in range(1, outers)], axis=1
        ).reshape(all_rows, head_cols)
        for m in range(micro)
    ]
    weights = (weight, to_core(weight))
    pieces = lax.all_to_all(
        left.reshape(blocks, sub, block_cols), "tensor", split_axis=0, concat_axis=0, tiled=True
    )
    left_slots = [
        columns(pick(pieces, block_of(part)), (part % per_block) * width, width) for part in slots
    ]

    def by_column(step):
        target = (outer + step) % outers
        cuts = [2 * target + core, 2 * target + (1 - core)]
        return jnp.stack(
            [
                jnp.stack([columns(value[:, 0], part * width, width) for part in cuts])
                for value in (hidden_in, cotangent)
            ]
        )

    entering = jnp.concatenate(
        [by_column(0)] + [to_outer(by_column(step), step) for step in range(1, outers)], axis=3
    )
    gains = jnp.stack([columns(norm_gain, part * width, width) for part in slots]).astype(F32)

    inners = [dot(taken[m], right, 1, 0).astype(BF16) for m in range(micro)]
    inner_cols = [
        [columns(inners[m], block_of(part) * sub, sub) for part in slots] for m in range(micro)
    ]
    partial = [
        jnp.stack(
            [
                (
                    dot(taken[m], weights[slot], 1, 0)
                    + dot(inner_cols[m][slot], left_slots[slot], 1, 0)
                ).astype(BF16)
                for slot in range(2)
            ]
        ).reshape(2, blocks, rows, width)
        for m in range(micro)
    ]

    def shard(m, index):
        return lax.dynamic_index_in_dim(
            partial[m], jnp.clip(index, 0, blocks - 1), 1, keepdims=False
        ).astype(F32)

    zero = jnp.zeros((2, rows, width), BF16)
    going_up = [zero] * micro
    going_down = [zero] * micro
    for step in range(1, blocks):
        up = [(i, i + 1) for i in range(min(step, blocks - 1))]
        down = [(blocks - 1 - i, blocks - 2 - i) for i in range(min(step, blocks - 1))]
        for m in range(micro):
            send_up = (shard(m, blocks - step + t) + going_up[m].astype(F32)).astype(BF16)
            send_down = (shard(m, t + step - blocks) + going_down[m].astype(F32)).astype(BF16)
            going_up[m] = lax.ppermute(send_up, "tensor", up)
            going_down[m] = lax.ppermute(send_down, "tensor", down)

    grads = []
    leaving = []
    for m in range(micro):
        update = shard(m, t) + going_up[m].astype(F32) + going_down[m].astype(F32)
        sent = update.astype(BF16)
        updates = [update] + [
            lax.ppermute(
                sent, "pipe", [(i, (i + step) % sections) for i in range(sections)]
            ).astype(F32)
            for step in range(1, sections)
        ]
        state = entering[0, :, m]
        kept = state
        for s in range(sections):
            add = updates[0]
            for step in range(1, sections):
                add = jnp.where((section - step) % sections == s, updates[step], add)
            state = (state.astype(F32) + add).astype(BF16)
            kept = jnp.where(section == s, state, kept)
        leaving.append(kept)
        final = state.astype(F32)
        upstream = entering[1, :, m].astype(F32) * gains[:, None, :]
        sums = jnp.stack(
            [jnp.sum(final * final, axis=(0, 2)), jnp.sum(upstream * final, axis=(0, 2))]
        ).reshape(2, outers, own_rows)
        total = sums
        for step in range(1, outers):
            total = total + jnp.roll(to_outer(sums, step), step, axis=1)
        total = total.reshape(2, rows) / features
        scale = lax.rsqrt(total[0] + 1e-05)
        shrink = scale * scale * total[1]
        grads.append(
            (scale[None, :, None] * (upstream - final * shrink[None, :, None])).astype(BF16)
        )

    outs = []
    for m in range(micro):
        pieces_out = [leaving[m].reshape(2, outers, own_rows, width)[:, 0]]
        source = [outer]
        for step in range(1, outers):
            pieces_out.append(
                to_outer(leaving[m].reshape(2, outers, own_rows, width)[:, step], outers - step)
            )
            source.append((outer + step) % outers)
        row = jnp.zeros((own_rows, features), BF16)
        for piece, at in zip(pieces_out, source):
            row = lax.dynamic_update_slice_in_dim(row, piece[0], (2 * at + core) * width, 1)
            row = lax.dynamic_update_slice_in_dim(row, piece[1], (2 * at + 1 - core) * width, 1)
        outs.append(row)
    section_out = jnp.stack(outs).reshape(1, micro, 1, own_rows, features)

    full = []
    for m in range(micro):
        buffer = jnp.zeros((2, blocks, rows, width), BF16)
        buffer = lax.dynamic_update_slice_in_dim(buffer, grads[m][:, None], t, 1)
        ups, downs = [grads[m]], [grads[m]]
        for step in range(1, blocks):
            ups.append(
                lax.ppermute(ups[-1], "tensor", [(i, i + 1) for i in range(step - 1, blocks - 1)])
            )
            downs.append(
                lax.ppermute(
                    downs[-1], "tensor", [(i + 1, i) for i in range(0, blocks - step)]
                )
            )
        for step in range(1, blocks):
            value = jnp.where(t >= step, ups[step], downs[blocks - step])
            buffer = lax.dynamic_update_slice_in_dim(
                buffer, value[:, None], (t - step) % blocks, 1
            )
        full.append(buffer.reshape(2, all_rows, width))

    inner_stack = jnp.concatenate(inners, axis=0)
    permuted = lax.all_to_all(
        inner_stack.T.reshape(blocks, sub, micro * all_rows),
        "tensor",
        split_axis=0,
        concat_axis=0,
        tiled=True,
    ).reshape(rank, micro * all_rows)

    holder = (t * per_block) // 2
    mix_grads = []
    grad_right = jnp.zeros((head_cols, rank), F32)
    left_sum = jnp.zeros((rank, block_cols), F32)
    for m in range(micro):
        inner_grads = [dot(full[m][slot], left_slots[slot], 1, 1) for slot in range(2)]
        if per_block == 1:
            mine = jnp.where(
                core == 0,
                jnp.concatenate(inner_grads, axis=1),
                jnp.concatenate(inner_grads[::-1], axis=1),
            ).astype(BF16)
        else:
            mine = (inner_grads[0] + inner_grads[1]).astype(BF16)
        per_outer = mine.shape[1]
        partial_mix = (
            dot(full[m][0], weights[0], 1, 1)
            + dot(full[m][1], weights[1], 1, 1)
            + dot(mine, columns(right, outer * per_outer, per_outer), 1, 1)
        ).reshape(blocks, outers, own_rows, head_cols)
        summed = partial_mix[:, 0]
        for step in range(1, outers):
            summed = summed + to_outer(
                partial_mix[:, step].astype(BF16), outers - step
            ).astype(F32)
        mix_grads.append(summed.astype(BF16).reshape(tokens, head_cols))

        inner_full = jnp.zeros((blocks, outers, own_rows, rank), BF16)
        mine_rows = mine.reshape(blocks, outers, own_rows, per_outer)
        for step in range(outers):
            arrived = to_outer(mine_rows, step) if step else mine_rows
            ordered = jnp.zeros_like(arrived)
            for s in range(outers):
                ordered = lax.dynamic_update_slice_in_dim(
                    ordered, arrived[:, s : s + 1], (outer - step - s) % outers, 1
                )
            inner_full = lax.dynamic_update_slice_in_dim(
                inner_full, ordered, ((outer - step) % outers) * per_outer, 3
            )
        mix_rows = taken[m].reshape(blocks, outers, own_rows, head_cols)
        ordered_mix = jnp.zeros_like(mix_rows)
        for s in range(outers):
            ordered_mix = lax.dynamic_update_slice_in_dim(
                ordered_mix, mix_rows[:, s : s + 1], (outer - s) % outers, 1
            )
        grad_right = grad_right + dot(
            ordered_mix.reshape(all_rows, head_cols), inner_full.reshape(all_rows, rank), 0, 0
        )

        if per_block == 1:
            cols = pick(full[m], jnp.where(t % 2 == core, 0, 1))
        else:
            cols = jnp.where(
                core == 0,
                jnp.concatenate([full[m][0], full[m][1]], axis=1),
                jnp.concatenate([full[m][1], full[m][0]], axis=1),
            )
        left_sum = left_sum + dot(
            permuted[:, m * all_rows : (m + 1) * all_rows], cols, 1, 0
        )

    grad_right = grad_right + to_core(grad_right)

    half = block_cols // 2
    mine = columns(left_sum, core * half, half)
    other = to_core(columns(left_sum, (1 - core) * half, half))
    half_sum = (mine + other).astype(BF16)
    best = half_sum
    for step in range(1, outers):
        pairs = []
        for i in range(blocks):
            for c in range(2):
                at = (i * per_block) // 2
                pairs.append(
                    (i * parts + 2 * at + c, i * parts + 2 * ((at + step) % outers) + c)
                )
        arrived = lax.ppermute(half_sum, ("tensor", "dp"), pairs)
        best = jnp.where((outer - holder) % outers == step, arrived, best)
    there = to_core(best)
    grad_left = jnp.where(
        core == 0,
        jnp.concatenate([best, there], axis=1),
        jnp.concatenate([there, best], axis=1),
    ).astype(F32)

    grad_mix = jnp.stack(mix_grads).reshape(1, micro, 1, tokens, head_cols)
    return (
        section_out,
        grad_mix,
        grad_right.reshape(1, 1, head_cols, rank),
        grad_left.reshape(1, 1, rank, block_cols),
    )


def solution(mesh):
    return jax.shard_map(
        on_device,
        mesh=mesh,
        in_specs=(
            P("pipe", None, "dp", None, "tensor"),
            P(None, "dp", "tensor", None),
            P(None, "dp", "tensor", None),
            P("pipe", "tensor", "dp"),
            P("pipe", "tensor", None, None),
            P("pipe", "tensor", None, None),
            P(),
        ),
        out_specs=(
            P("pipe", None, "dp", "tensor", None),
            P("pipe", None, "dp", None, "tensor"),
            P("pipe", "tensor", None, None),
            P("pipe", "tensor", None, None),
        ),
        check_vma=False,
    )
```

time: 448 us -> 198 us (0.44)
  waiting for transfers between devices: 289 us -> 38.9 us
  matrix products: 79.5 us -> 33.7 us
  starting transfers between devices: 42.8 us -> 82 us
  between operations: 14.7 us -> 1.98 us
  local copies, waits for them, and re-layouts: 12.3 us -> 24.5 us
  other arithmetic: 8.52 us -> 14.8 us
    all_gather x4 -> x0, waiting for transfers between devices: 138 us -> none  [the longest x1 110 us: on_device(): weight = lax.all_gather(frozen_weight[0], 'dp', axis=1, tiled=True)]
    ppermute x4 -> x42, starting transfers between devices: 9.52 us -> 72.3 us  [the longest x6 26.8 us: on_device(): going_up[m] = lax.ppermute(send_up, 'tensor', up)]
    all_to_all x9 -> x2, waiting for transfers between devices: 60.3 us -> 0.29 us  [the longest x1 0.29 us: on_device(): lax.all_to_all(left.reshape(blocks, sub, block_cols), 'tensor', split_axi...]
    dot_general x24, matrix products: 79.5 us -> 33.7 us  [dot(): lax.dot_general(left_side, right_side, (((left_dim,), (right_dim,)), ((),...]
    reduce_scatter x3 -> x0, waiting for transfers between devices: 45.7 us -> none  [on_device(): lax.psum_scatter(jnp.dot(own_mix, weight, preferred_element_type=jnp.floa...]
    psum x1 -> x0, waiting for transfers between devices: 29.1 us -> none  [on_device(): grad_right, grad_left = lax.psum((grad_right, grad_left), 'dp')]
    ppermute x4 -> x42, waiting for transfers between devices: 15 us -> 38.6 us  [the longest x6 14.1 us: on_device(): lax.ppermute(downs[-1], 'tensor', [(i + 1, i) for i in range(0, blocks -...]
    all_to_all x9 -> x2, starting transfers between devices: 32.6 us -> 9.76 us  [the longest x1 4.89 us: on_device(): lax.all_to_all(inner_stack.T.reshape(blocks, sub, micro * all_rows), 'ten...]
  transfers between devices with their start and end apart: 21 -> 44, of which waited for: 17 -> 16; matrix products, arithmetic and copies ran while one was open for 18% -> 36% of each run, Pallas kernels for 0% -> 0%
where the time goes in v1:
time: 198 us; the launch traced here: 196 us
  starting transfers between devices  82 us (41%)
  waiting for transfers between devices  38.9 us (20%)
  matrix products  33.7 us (17%)
  local copies, waits for them, and re-layouts  24.5 us (12%)
  other arithmetic  14.8 us (7%)
  between operations  1.98 us (1%)
    dot_general x24, matrix products, dot(): lax.dot_general(left_side, right_side, (((left_dim,), (right_dim,)), ((),...  33.7 us
    ppermute x6, starting transfers between devices, on_device(): going_up[m] = lax.ppermute(send_up, 'tensor', up)  26.8 us
    ppermute x6, waiting for transfers between devices, on_device(): lax.ppermute(downs[-1], 'tensor', [(i + 1, i) for i in range(0, blocks -...  14.1 us
    ppermute x11, starting transfers between devices, to_outer(): return lax.ppermute(value, 'dp', pairs)  13 us
    ppermute x6, starting transfers between devices, on_device(): lax.ppermute(ups[-1], 'tensor', [(i, i + 1) for i in range(step - 1, bloc...  12.7 us
    ppermute x11, waiting for transfers between devices, to_outer(): return lax.ppermute(value, 'dp', pairs)  12.5 us
    ppermute x6, starting transfers between devices, on_device(): lax.ppermute(downs[-1], 'tensor', [(i + 1, i) for i in range(0, blocks -...  7.69 us
    ppermute x6, starting transfers between devices, on_device(): going_down[m] = lax.ppermute(send_down, 'tensor', down)  5.43 us
  transfers between devices with their start and end apart: 44, of which 16 were waited for; matrix products, arithmetic and copies ran while one was open for 36% of the time, Pallas kernels for 0%

profile of v1, /device:TPU:0, one launch (start us, length us, event | category | flops | bytes accessed | tf_op | source)
XLA Modules:
  0.0 195.9 jit_solution(2304859286617342223)
XLA Ops:
  1.2 1.4 dynamic-slice_bitcast_fusion.5
  2.7 2.7 %collective-permute-start = (bf16[2,2,2,16,2048]{4,3,1,2,0:T(8,128)(2,1)S(1)}, bf16[2,2,2,16,2048]{4,3,1,2,0:T(8,128)(2,1)}, u32[]{:S(2)}, u32[]{:S(2)}) collective-permute-start(bf16[2,2,2,16,2048]{4,3,1,2,0:T(8,128)(2,1)S(1)} %pad_maximum_fusion.1), channel_id=1, source_target_pairs={{0,4},{2,6},{4,0},{6,2},{1,5},{3,7},{5,1},{7,3},{8,12},{10,14},{12... | collective-permute-start | bytes 1572872 | tf_op jit(solution)/shard_map/ppermute | solution.py:43
  5.3 4.9 %all-to-all-start = ((bf16[4,32,2048]{2,1,0:T(8,128)(2,1)}), bf16[4,32,2048]{2,1,0:T(8,128)(2,1)S(1)}, u32[]{:S(2)}, u32[]{:S(2)}) async-start(bf16[4,32,2048]{2,1,0:T(8,128)(2,1)} %bitcast.19), calls=%async_computation | async-start | bytes 1048576 | tf_op jit(solution)/shard_map/all_to_all | solution.py:71
  10.8 1.5 collective-permute-start.11
  13.3 7.6 %collective-permute-done.1 = bf16[4,1,16,1024]{3,2,1,0:T(8,128)(2,1)S(1)} collective-permute-done((bf16[4,1,16,1024]{3,2,1,0:T(8,128)(2,1)S(1)}, bf16[4,1,16,1024]{3,2,1,0:T(8,128)(2,1)S(1)}, u32[]{:S(2)}, u32[]{:S(2)}) %collective-permute-start.1) | collective-permute-done | bytes 131104 | tf_op jit(solution)/shard_map/ppermute | solution.py:43
  21.0 2.5 %collective-permute-done.11 = bf16[4,1,16,1024]{3,2,1,0:T(8,128)(2,1)S(1)} collective-permute-done((bf16[4,1,16,1024]{3,2,1,0:T(8,128)(2,1)S(1)}, bf16[4,1,16,1024]{3,2,1,0:T(8,128)(2,1)S(1)}, u32[]{:S(2)}, u32[]{:S(2)}) %collective-permute-start.11) | collective-permute-done | bytes 131104 | tf_op jit(solution)/shard_map/ppermute | solution.py:43
  25.0 4.9 %all-to-all-start.1 = ((bf16[4,32,256]{2,1,0:T(8,128)(2,1)}), bf16[4,32,256]{2,1,0:T(8,128)(2,1)S(1)}, u32[]{:S(2)}, u32[]{:S(2)}) async-start(bf16[4,32,256]{2,1,0:T(8,128)(2,1)} %bitcast.110), calls=%async_computation.1 | async-start | bytes 131072 | tf_op jit(solution)/shard_map/all_to_all | solution.py:200
  33.6 3.0 %fusion.1 = bf16[128,2048]{1,0:T(8,128)(2,1)S(1)} fusion(f32[128,2048]{1,0:T(8,128)S(1)} %fusion.93, bf16[128,1024]{1,0:T(8,128)(2,1)S(1)} %bitcast.362, bf16[1024,2048]{1,0:T(8,128)(2,1)} %collective-permute-done.2), kind=kOutput, calls=%fused_computation.6 | convolution fusion | flops 537395200 | bytes 6029312 | tf_op jit(solution)/shard_map/dot_general | solution.py:11
  36.7 3.9 %collective-permute-start.3 = (bf16[2,32,2048]{2,1,0:T(8,128)(2,1)S(1)}, bf16[2,32,2048]{2,1,0:T(8,128)(2,1)S(1)}, u32[]{:S(2)}, u32[]{:S(2)}) collective-permute-start(bf16[2,32,2048]{2,1,0:T(8,128)(2,1)S(1)} %get-tuple-element.34), channel_id=1, source_target_pairs={{0,8},{1,9},{2,10},{3,11},{4,12},{5,13},{6,14},{7,15}} | collective-permute-start | bytes 786440 | tf_op jit(solution)/shard_map/ppermute | solution.py:124
  41.3 2.9 %fusion.3 = bf16[128,2048]{1,0:T(8,128)(2,1)S(1)} fusion(f32[128,2048]{1,0:T(8,128)S(1)} %fusion.91, bf16[128,1024]{1,0:T(8,128)(2,1)S(1)} %bitcast.359, bf16[1024,2048]{1,0:T(8,128)(2,1)} %collective-permute-done.2), kind=kOutput, calls=%fused_computation.8 | convolution fusion | flops 537395200 | bytes 6029312 | tf_op jit(solution)/shard_map/dot_general | solution.py:11
  44.3 1.3 collective-permute-start.12
  46.5 4.0 %collective-permute-start.4 = (bf16[2,32,2048]{2,1,0:T(8,128)(2,1)S(1)}, bf16[2,32,2048]{2,1,0:T(8,128)(2,1)S(1)}, u32[]{:S(2)}, u32[]{:S(2)}) collective-permute-start(bf16[2,32,2048]{2,1,0:T(8,128)(2,1)S(1)} %get-tuple-element.32), channel_id=1, source_target_pairs={{0,8},{8,16},{1,9},{9,17},{2,10},{10,18},{3,11},{11,19},{4,12},{12... | collective-permute-start | bytes 786440 | tf_op jit(solution)/shard_map/ppermute | solution.py:124
  51.1 1.2 collective-permute-done.12
  52.5 4.4 %collective-permute-start.13 = (bf16[2,32,2048]{2,1,0:T(8,128)(2,1)S(1)}, bf16[2,32,2048]{2,1,0:T(8,128)(2,1)S(1)}, u32[]{:S(2)}, u32[]{:S(2)}) collective-permute-start(bf16[2,32,2048]{2,1,0:T(8,128)(2,1)S(1)} %get-tuple-element.26), channel_id=1, source_target_pairs={{0,8},{8,16},{1,9},{9,17},{2,10},{10,18},{3,11},{11,19},{4,12},{12... | collective-permute-start | bytes 786440 | tf_op jit(solution)/shard_map/ppermute | solution.py:124
  58.1 1.3 collective-permute-start.8
  59.4 5.4 %collective-permute-start.5 = (bf16[2,32,2048]{2,1,0:T(8,128)(2,1)S(1)}, bf16[2,32,2048]{2,1,0:T(8,128)(2,1)S(1)}, u32[]{:S(2)}, u32[]{:S(2)}) collective-permute-start(bf16[2,32,2048]{2,1,0:T(8,128)(2,1)S(1)} %get-tuple-element.30), channel_id=1, source_target_pairs={{0,8},{8,16},{16,24},{1,9},{9,17},{17,25},{2,10},{10,18},{18,26},{... | collective-permute-start | bytes 786440 | tf_op jit(solution)/shard_map/ppermute | solution.py:124
  65.0 1.3 collective-permute-start.17
  66.3 7.8 %collective-permute-start.14 = (bf16[2,32,2048]{2,1,0:T(8,128)(2,1)S(1)}, bf16[2,32,2048]{2,1,0:T(8,128)(2,1)S(1)}, u32[]{:S(2)}, u32[]{:S(2)}) collective-permute-start(bf16[2,32,2048]{2,1,0:T(8,128)(2,1)S(1)} %get-tuple-element.24), channel_id=1, source_target_pairs={{0,8},{8,16},{16,24},{1,9},{9,17},{17,25},{2,10},{10,18},{18,26},{... | collective-permute-start | bytes 786440 | tf_op jit(solution)/shard_map/ppermute | solution.py:124
  74.2 1.6 collective-permute-start.9
  76.5 1.5 collective-permute-done.14
  78.1 1.6 collective-permute-start.18
  79.7 1.2 pad_maximum_fusion
  80.9 3.6 %collective-permute-done.18 = bf16[2,32,2048]{2,1,0:T(8,128)(2,1)S(1)} collective-permute-done((bf16[2,32,2048]{2,1,0:T(8,128)(2,1)S(1)}, bf16[2,32,2048]{2,1,0:T(8,128)(2,1)S(1)}, u32[]{:S(2)}, u32[]{:S(2)}) %collective-permute-start.18) | collective-permute-done | bytes 262176 | tf_op jit(solution)/shard_map/ppermute | solution.py:133
  86.4 1.5 collective-permute-start.19
  89.5 1.5 collective-permute-start.28
  91.7 2.4 %collective-permute-done.28 = f32[2,2,16]{2,1,0:T(2,128)S(1)} collective-permute-done((f32[2,2,16]{2,1,0:T(2,128)S(1)}, f32[2,2,16]{2,1,0:T(2,128)S(1)}, u32[]{:S(2)}, u32[]{:S(2)}) %collective-permute-start.28) | collective-permute-done | bytes 288 | tf_op jit(solution)/shard_map/ppermute | solution.py:43
  95.2 5.1 %collective-permute-start.29 = (bf16[2,32,2048]{2,1,0:T(8,128)(2,1)}, bf16[2,32,2048]{2,1,0:T(8,128)(2,1)}, u32[]{:S(2)}, u32[]{:S(2)}) collective-permute-start(bf16[2,32,2048]{2,1,0:T(8,128)(2,1)} %get-tuple-element.11), channel_id=1, source_target_pairs={{0,8},{8,16},{16,24},{1,9},{9,17},{17,25},{2,10},{10,18},{18,26},{... | collective-permute-start | bytes 786440 | tf_op jit(solution)/shard_map/ppermute | solution.py:185
  100.3 1.3 collective-permute-start.30
  101.9 1.3 bitcast_dynamic-update-slice_fusion.7
  103.2 4.7 %collective-permute-start.21 = (bf16[2,32,2048]{2,1,0:T(8,128)(2,1)S(1)}, bf16[2,32,2048]{2,1,0:T(8,128)(2,1)S(1)}, u32[]{:S(2)}, u32[]{:S(2)}) collective-permute-start(bf16[2,32,2048]{2,1,0:T(8,128)(2,1)S(1)} %get-tuple-element.9), channel_id=1, source_target_pairs={{0,8},{8,16},{16,24},{1,9},{9,17},{17,25},{2,10},{10,18},{18,26},{... | collective-permute-start | bytes 786440 | tf_op jit(solution)/shard_map/ppermute | solution.py:185
  107.9 1.3 collective-permute-start.22
  109.2 1.5 slice_dynamic-update-slice_fusion.1
  110.7 1.5 slice_dynamic-update-slice_fusion
  112.2 1.5 slice_dynamic-update-slice_fusion.3
  113.6 1.3 collective-permute-start.31
  114.9 1.5 slice_dynamic-update-slice_fusion.2
  117.7 1.3 collective-permute-start.23
  119.7 5.5 %collective-permute-done.31 = bf16[2,32,2048]{2,1,0:T(8,128)(2,1)S(1)} collective-permute-done((bf16[2,32,2048]{2,1,0:T(8,128)(2,1)}, bf16[2,32,2048]{2,1,0:T(8,128)(2,1)S(1)}, u32[]{:S(2)}, u32[]{:S(2)}) %collective-permute-start.31) | collective-permute-done | bytes 262176 | tf_op jit(solution)/shard_map/ppermute | solution.py:188
  125.2 1.3 collective-permute-start.32
  126.5 1.9 maximum_bitcast_fusion
  129.0 3.2 %collective-permute-done.23 = bf16[2,32,2048]{2,1,0:T(8,128)(2,1)S(1)} collective-permute-done((bf16[2,32,2048]{2,1,0:T(8,128)(2,1)S(1)}, bf16[2,32,2048]{2,1,0:T(8,128)(2,1)S(1)}, u32[]{:S(2)}, u32[]{:S(2)}) %collective-permute-start.23) | collective-permute-done | bytes 262176 | tf_op jit(solution)/shard_map/ppermute | solution.py:188
  132.2 1.3 collective-permute-start.24
  134.4 1.2 collective-permute-done.32
  135.8 1.0 bitcast_dynamic-update-slice_fusion
  136.9 3.6 %collective-permute-done.24 = bf16[2,32,2048]{2,1,0:T(8,128)(2,1)S(1)} collective-permute-done((bf16[2,32,2048]{2,1,0:T(8,128)(2,1)S(1)}, bf16[2,32,2048]{2,1,0:T(8,128)(2,1)S(1)}, u32[]{:S(2)}, u32[]{:S(2)}) %collective-permute-start.24) | collective-permute-done | bytes 262176 | tf_op jit(solution)/shard_map/ppermute | solution.py:188
  140.6 2.3 %fusion.141 = f32[128,1024]{1,0:T(8,128)} fusion(bf16[128,2048]{1,0:T(8,128)(2,1)S(1)} %bitcast.351, bf16[1,1024,2048]{2,1,0:T(8,128)(2,1)S(1)} %copy-done.2), kind=kOutput, calls=%fused_computation.281 | convolution fusion | flops 536870912 | bytes 5242880 | tf_op jit(solution)/shard_map/dot_general | solution.py:11
  144.0 2.3 %fusion.143 = f32[128,1024]{1,0:T(8,128)} fusion(bf16[128,2048]{1,0:T(8,128)(2,1)S(1)} %bitcast.355, bf16[1,1024,2048]{2,1,0:T(8,128)(2,1)S(1)} %copy-done.2), kind=kOutput, calls=%fused_computation.283 | convolution fusion | flops 536870912 | bytes 5242880 | tf_op jit(solution)/shard_map/dot_general | solution.py:11
  146.3 1.2 fusion.87
  147.6 1.2 fusion.95
  149.5 1.3 fusion.89
  151.0 1.9 fusion.77
  152.9 1.4 fusion.97
  154.3 1.1 fusion.79
  156.2 4.1 %fusion.5 = f32[128,1024]{1,0:T(8,128)S(1)} fusion(f32[128,1024]{1,0:T(8,128)} %fusion.77, f32[128,1024]{1,0:T(8,128)} %fusion.141, bf16[128,2048]{1,0:T(8,128)(2,1)S(1)} %bitcast.350, bf16[1024,2048]{1,0:T(8,128)(2,1)} %collective-permute-done.2), kind=kOutput, calls=%fused_computation.42 | convolution fusion | flops 537133056 | bytes 6291456 | tf_op jit(solution)/shard_map/dot_general | solution.py:11
  161.4 3.7 %fusion.4 = f32[128,1024]{1,0:T(8,128)S(1)} fusion(f32[128,1024]{1,0:T(8,128)S(1)} %copy-done.8, f32[128,1024]{1,0:T(8,128)S(1)} %copy-done.7, bf16[128,2048]{1,0:T(8,128)(2,1)S(1)} %bitcast.354, bf16[1024,2048]{1,0:T(8,128)(2,1)} %collective-permute-done.2), kind=kOutput, calls=%fused_computation.41 | convolution fusion | flops 537133056 | bytes 6291456 | tf_op jit(solution)/shard_map/dot_general | solution.py:11
  165.8 1.6 collective-permute-start.27
  170.1 1.7 collective-permute-start.36
  176.0 1.3 dynamic_update_slice.135
  178.8 2.0 %convolution_bitcast_fusion = f32[1024,128]{1,0:T(8,128)} fusion(bf16[4,2,16,1024]{3,2,1,0:T(8,128)(2,1)} %copy-done.14, bf16[4,2,16,128]{3,2,1,0:T(8,128)(2,1)S(1)} %dynamic_update_slice.135), kind=kOutput, calls=%fused_computation.39 | convolution fusion | flops 33554432 | bytes 819200 | tf_op jit(solution)/shard_map/dot_general | solution.py:11
  180.8 1.3 dynamic_update_slice.127
  182.1 1.4 fusion.6
  185.1 2.3 %collective-permute-start.40 = (bf16[128,1024]{1,0:T(8,128)(2,1)S(1)}, bf16[128,1024]{1,0:T(8,128)(2,1)S(1)}, u32[]{:S(2)}, u32[]{:S(2)}) collective-permute-start(bf16[128,1024]{1,0:T(8,128)(2,1)S(1)} %add_convert_fusion), channel_id=1, source_target_pairs={{0,4},{2,6},{8,12},{10,14},{20,16},{22,18},{28,24},{30,26},{1,5},{... | collective-permute-start | bytes 786440 | tf_op jit(solution)/shard_map/ppermute | solution.py:284
  189.1 4.0 %collective-permute-done.40 = bf16[128,1024]{1,0:T(8,128)(2,1)S(1)} collective-permute-done((bf16[128,1024]{1,0:T(8,128)(2,1)S(1)}, bf16[128,1024]{1,0:T(8,128)(2,1)S(1)}, u32[]{:S(2)}, u32[]{:S(2)}) %collective-permute-start.40) | collective-permute-done | bytes 262176 | tf_op jit(solution)/shard_map/ppermute | solution.py:284
  194.8 1.1 fusion.25
  (202 shorter events, 38.8 us)
Async XLA Ops:
  0.6 22.8 %copy-start = (bf16[1,1,1024,128]{3,2,1,0:T(8,128)(2,1)S(1)}, bf16[1,1,1024,128]{3,2,1,0:T(8,128)(2,1)}, u32[]{:S(2)}) copy-start(bf16[1,1,1024,128]{3,2,1,0:T(8,128)(2,1)} %param.11) | copy-start | bytes 786436
  0.6 9.6 %copy-start.13 = (bf16[1,2,1,64,1024]{4,3,2,1,0:T(8,128)(2,1)S(1)}, bf16[1,2,1,64,1024]{4,3,2,1,0:T(8,128)(2,1)}, u32[]{:S(2)}) copy-start(bf16[1,2,1,64,1024]{4,3,2,1,0:T(8,128)(2,1)} %param.7) | copy-start | bytes 786436
  0.7 11.7 %copy-start.22 = (bf16[8192]{0:T(1024)(128)(2,1)S(1)}, bf16[8192]{0:T(1024)(128)(2,1)}, u32[]{:S(2)}) copy-start(bf16[8192]{0:T(1024)(128)(2,1)} %param.13) | copy-start | bytes 49156
  0.7 33.0 %collective-permute-start.2 = (bf16[1024,2048]{1,0:T(8,128)(2,1)}, bf16[1024,2048]{1,0:T(8,128)(2,1)}, u32[]{:S(2)}, u32[]{:S(2)}) collective-permute-start(bf16[1024,2048]{1,0:T(8,128)(2,1)} %bitcast.330), channel_id=1, source_target_pairs={{0,2},{2,0},{4,6},{6,4},{1,3},{3,1},{5,7},{7,5},{8,10},{10,8},{12,... | collective-permute-start | bytes 12582920 | tf_op jit(solution)/shard_map/ppermute | solution.py:39
  2.7 77.0 %collective-permute-start = (bf16[2,2,2,16,2048]{4,3,1,2,0:T(8,128)(2,1)S(1)}, bf16[2,2,2,16,2048]{4,3,1,2,0:T(8,128)(2,1)}, u32[]{:S(2)}, u32[]{:S(2)}) collective-permute-start(bf16[2,2,2,16,2048]{4,3,1,2,0:T(8,128)(2,1)S(1)} %pad_maximum_fusion.1), channel_id=1, source_target_pairs={{0,4},{2,6},{4,0},{6,2},{1,5},{3,7},{5,1},{7,3},{8,12},{10,14},{12... | collective-permute-start | bytes 1572872 | tf_op jit(solution)/shard_map/ppermute | solution.py:43
  5.3 19.7 %all-to-all-start = ((bf16[4,32,2048]{2,1,0:T(8,128)(2,1)}), bf16[4,32,2048]{2,1,0:T(8,128)(2,1)S(1)}, u32[]{:S(2)}, u32[]{:S(2)}) async-start(bf16[4,32,2048]{2,1,0:T(8,128)(2,1)} %bitcast.19), calls=%async_computation | async-start | bytes 1048576 | tf_op jit(solution)/shard_map/all_to_all | solution.py:71
  10.2 10.7 %collective-permute-start.1 = (bf16[4,1,16,1024]{3,2,1,0:T(8,128)(2,1)S(1)}, bf16[4,1,16,1024]{3,2,1,0:T(8,128)(2,1)S(1)}, u32[]{:S(2)}, u32[]{:S(2)}) collective-permute-start(bf16[4,1,16,1024]{3,2,1,0:T(8,128)(2,1)S(1)} %bitcast.370), channel_id=1, source_target_pairs={{0,4},{2,6},{4,0},{6,2},{1,5},{3,7},{5,1},{7,3},{8,12},{10,14},{12... | collective-permute-start | bytes 393224 | tf_op jit(solution)/shard_map/ppermute | solution.py:43
  10.8 12.6 %collective-permute-start.11 = (bf16[4,1,16,1024]{3,2,1,0:T(8,128)(2,1)S(1)}, bf16[4,1,16,1024]{3,2,1,0:T(8,128)(2,1)S(1)}, u32[]{:S(2)}, u32[]{:S(2)}) collective-permute-start(bf16[4,1,16,1024]{3,2,1,0:T(8,128)(2,1)S(1)} %bitcast.367), channel_id=1, source_target_pairs={{0,4},{2,6},{4,0},{6,2},{1,5},{3,7},{5,1},{7,3},{8,12},{10,14},{12... | collective-permute-start | bytes 393224 | tf_op jit(solution)/shard_map/ppermute | solution.py:43
  24.7 8.1 %copy-start.14 = (bf16[4,2,16,1024]{3,2,1,0:T(8,128)(2,1)}, bf16[4,2,16,1024]{3,2,1,0:T(8,128)(2,1)S(1)}, u32[]{:S(2)}) copy-start(bf16[4,2,16,1024]{3,2,1,0:T(8,128)(2,1)S(1)} %constant_dynamic-update-slice_fusion.4) | copy-start | bytes 786436
  25.0 7.8 %copy-start.5 = (bf16[4,32,2048]{2,1,0:T(8,128)(2,1)}, bf16[4,32,2048]{2,1,0:T(8,128)(2,1)S(1)}, u32[]{:S(2)}) copy-start(bf16[4,32,2048]{2,1,0:T(8,128)(2,1)S(1)} %all-to-all-done) | copy-start | bytes 1572868
  25.0 146.8 %all-to-all-start.1 = ((bf16[4,32,256]{2,1,0:T(8,128)(2,1)}), bf16[4,32,256]{2,1,0:T(8,128)(2,1)S(1)}, u32[]{:S(2)}, u32[]{:S(2)}) async-start(bf16[4,32,256]{2,1,0:T(8,128)(2,1)} %bitcast.110), calls=%async_computation.1 | async-start | bytes 131072 | tf_op jit(solution)/shard_map/all_to_all | solution.py:200
  29.9 2.2 %copy-start.1 = (bf16[1,1024,2048]{2,1,0:T(8,128)(2,1)S(1)}, bf16[1,1024,2048]{2,1,0:T(8,128)(2,1)}, u32[]{:S(2)}) copy-start(bf16[1,1024,2048]{2,1,0:T(8,128)(2,1)} %param.10) | copy-start | bytes 12582916
  36.7 9.7 %collective-permute-start.3 = (bf16[2,32,2048]{2,1,0:T(8,128)(2,1)S(1)}, bf16[2,32,2048]{2,1,0:T(8,128)(2,1)S(1)}, u32[]{:S(2)}, u32[]{:S(2)}) collective-permute-start(bf16[2,32,2048]{2,1,0:T(8,128)(2,1)S(1)} %get-tuple-element.34), channel_id=1, source_target_pairs={{0,8},{1,9},{2,10},{3,11},{4,12},{5,13},{6,14},{7,15}} | collective-permute-start | bytes 786440 | tf_op jit(solution)/shard_map/ppermute | solution.py:124
  40.6 5.7 %collective-permute-start.6 = (bf16[2,32,2048]{2,1,0:T(8,128)(2,1)S(1)}, bf16[2,32,2048]{2,1,0:T(8,128)(2,1)S(1)}, u32[]{:S(2)}, u32[]{:S(2)}) collective-permute-start(bf16[2,32,2048]{2,1,0:T(8,128)(2,1)S(1)} %get-tuple-element.35), channel_id=1, source_target_pairs={{24,16},{25,17},{26,18},{27,19},{28,20},{29,21},{30,22},{31,23}} | collective-permute-start | bytes 786440 | tf_op jit(solution)/shard_map/ppermute | solution.py:125
  44.3 8.0 %collective-permute-start.12 = (bf16[2,32,2048]{2,1,0:T(8,128)(2,1)S(1)}, bf16[2,32,2048]{2,1,0:T(8,128)(2,1)S(1)}, u32[]{:S(2)}, u32[]{:S(2)}) collective-permute-start(bf16[2,32,2048]{2,1,0:T(8,128)(2,1)S(1)} %get-tuple-element.28), channel_id=1, source_target_pairs={{0,8},{1,9},{2,10},{3,11},{4,12},{5,13},{6,14},{7,15}} | collective-permute-start | bytes 786440 | tf_op jit(solution)/shard_map/ppermute | solution.py:124
  45.6 6.7 %collective-permute-start.15 = (bf16[2,32,2048]{2,1,0:T(8,128)(2,1)S(1)}, bf16[2,32,2048]{2,1,0:T(8,128)(2,1)S(1)}, u32[]{:S(2)}, u32[]{:S(2)}) collective-permute-start(bf16[2,32,2048]{2,1,0:T(8,128)(2,1)S(1)} %get-tuple-element.29), channel_id=1, source_target_pairs={{24,16},{25,17},{26,18},{27,19},{28,20},{29,21},{30,22},{31,23}} | collective-permute-start | bytes 786440 | tf_op jit(solution)/shard_map/ppermute | solution.py:125
  46.5 11.5 %collective-permute-start.4 = (bf16[2,32,2048]{2,1,0:T(8,128)(2,1)S(1)}, bf16[2,32,2048]{2,1,0:T(8,128)(2,1)S(1)}, u32[]{:S(2)}, u32[]{:S(2)}) collective-permute-start(bf16[2,32,2048]{2,1,0:T(8,128)(2,1)S(1)} %get-tuple-element.32), channel_id=1, source_target_pairs={{0,8},{8,16},{1,9},{9,17},{2,10},{10,18},{3,11},{11,19},{4,12},{12... | collective-permute-start | bytes 786440 | tf_op jit(solution)/shard_map/ppermute | solution.py:124
  50.5 7.5 %collective-permute-start.7 = (bf16[2,32,2048]{2,1,0:T(8,128)(2,1)S(1)}, bf16[2,32,2048]{2,1,0:T(8,128)(2,1)S(1)}, u32[]{:S(2)}, u32[]{:S(2)}) collective-permute-start(bf16[2,32,2048]{2,1,0:T(8,128)(2,1)S(1)} %get-tuple-element.33), channel_id=1, source_target_pairs={{24,16},{16,8},{25,17},{17,9},{26,18},{18,10},{27,19},{19,11},{28,... | collective-permute-start | bytes 786440 | tf_op jit(solution)/shard_map/ppermute | solution.py:125
  52.5 12.4 %collective-permute-start.13 = (bf16[2,32,2048]{2,1,0:T(8,128)(2,1)S(1)}, bf16[2,32,2048]{2,1,0:T(8,128)(2,1)S(1)}, u32[]{:S(2)}, u32[]{:S(2)}) collective-permute-start(bf16[2,32,2048]{2,1,0:T(8,128)(2,1)S(1)} %get-tuple-element.26), channel_id=1, source_target_pairs={{0,8},{8,16},{1,9},{9,17},{2,10},{10,18},{3,11},{11,19},{4,12},{12... | collective-permute-start | bytes 786440 | tf_op jit(solution)/shard_map/ppermute | solution.py:124
  56.9 22.7 %copy-start.16 = (bf16[4,2,16,1024]{3,2,1,0:T(8,128)(2,1)S(1)}, bf16[4,2,16,1024]{3,2,1,0:T(8,128)(2,1)}, u32[]{:S(2)}) copy-start(bf16[4,2,16,1024]{3,2,1,0:T(8,128)(2,1)} %copy-done.15) | copy-start | bytes 786436
  56.9 7.9 %collective-permute-start.16 = (bf16[2,32,2048]{2,1,0:T(8,128)(2,1)S(1)}, bf16[2,32,2048]{2,1,0:T(8,128)(2,1)S(1)}, u32[]{:S(2)}, u32[]{:S(2)}) collective-permute-start(bf16[2,32,2048]{2,1,0:T(8,128)(2,1)S(1)} %get-tuple-element.27), channel_id=1, source_target_pairs={{24,16},{16,8},{25,17},{17,9},{26,18},{18,10},{27,19},{19,11},{28,... | collective-permute-start | bytes 786440 | tf_op jit(solution)/shard_map/ppermute | solution.py:125
  58.1 16.0 %collective-permute-start.8 = (bf16[2,32,2048]{2,1,0:T(8,128)(2,1)S(1)}, bf16[2,32,2048]{2,1,0:T(8,128)(2,1)S(1)}, u32[]{:S(2)}, u32[]{:S(2)}) collective-permute-start(bf16[2,32,2048]{2,1,0:T(8,128)(2,1)S(1)} %get-tuple-element.31), channel_id=1, source_target_pairs={{24,16},{16,8},{8,0},{25,17},{17,9},{9,1},{26,18},{18,10},{10,2},{... | collective-permute-start | bytes 786440 | tf_op jit(solution)/shard_map/ppermute | solution.py:125
  59.4 14.7 %collective-permute-start.5 = (bf16[2,32,2048]{2,1,0:T(8,128)(2,1)S(1)}, bf16[2,32,2048]{2,1,0:T(8,128)(2,1)S(1)}, u32[]{:S(2)}, u32[]{:S(2)}) collective-permute-start(bf16[2,32,2048]{2,1,0:T(8,128)(2,1)S(1)} %get-tuple-element.30), channel_id=1, source_target_pairs={{0,8},{8,16},{16,24},{1,9},{9,17},{17,25},{2,10},{10,18},{18,26},{... | collective-permute-start | bytes 786440 | tf_op jit(solution)/shard_map/ppermute | solution.py:124
  65.0 11.5 %collective-permute-start.17 = (bf16[2,32,2048]{2,1,0:T(8,128)(2,1)S(1)}, bf16[2,32,2048]{2,1,0:T(8,128)(2,1)S(1)}, u32[]{:S(2)}, u32[]{:S(2)}) collective-permute-start(bf16[2,32,2048]{2,1,0:T(8,128)(2,1)S(1)} %get-tuple-element.25), channel_id=1, source_target_pairs={{24,16},{16,8},{8,0},{25,17},{17,9},{9,1},{26,18},{18,10},{10,2},{... | collective-permute-start | bytes 786440 | tf_op jit(solution)/shard_map/ppermute | solution.py:125
  66.3 11.6 %collective-permute-start.14 = (bf16[2,32,2048]{2,1,0:T(8,128)(2,1)S(1)}, bf16[2,32,2048]{2,1,0:T(8,128)(2,1)S(1)}, u32[]{:S(2)}, u32[]{:S(2)}) collective-permute-start(bf16[2,32,2048]{2,1,0:T(8,128)(2,1)S(1)} %get-tuple-element.24), channel_id=1, source_target_pairs={{0,8},{8,16},{16,24},{1,9},{9,17},{17,25},{2,10},{10,18},{18,26},{... | collective-permute-start | bytes 786440 | tf_op jit(solution)/shard_map/ppermute | solution.py:124
  74.2 6.7 %collective-permute-start.9 = (bf16[2,32,2048]{2,1,0:T(8,128)(2,1)S(1)}, bf16[2,32,2048]{2,1,0:T(8,128)(2,1)S(1)}, u32[]{:S(2)}, u32[]{:S(2)}) collective-permute-start(bf16[2,32,2048]{2,1,0:T(8,128)(2,1)S(1)} %get-tuple-element.14), channel_id=1, source_target_pairs={{0,1},{1,0},{2,3},{3,2},{4,5},{5,4},{6,7},{7,6},{8,9},{9,8},{10,11... | collective-permute-start | bytes 786440 | tf_op jit(solution)/shard_map/ppermute | solution.py:133
  78.1 6.4 %collective-permute-start.18 = (bf16[2,32,2048]{2,1,0:T(8,128)(2,1)S(1)}, bf16[2,32,2048]{2,1,0:T(8,128)(2,1)S(1)}, u32[]{:S(2)}, u32[]{:S(2)}) collective-permute-start(bf16[2,32,2048]{2,1,0:T(8,128)(2,1)S(1)} %get-tuple-element.16), channel_id=1, source_target_pairs={{0,1},{1,0},{2,3},{3,2},{4,5},{5,4},{6,7},{7,6},{8,9},{9,8},{10,11... | collective-permute-start | bytes 786440 | tf_op jit(solution)/shard_map/ppermute | solution.py:133
  79.7 4.8 %copy-start.17 = (bf16[4,2,16,1024]{3,2,1,0:T(8,128)(2,1)}, bf16[4,2,16,1024]{3,2,1,0:T(8,128)(2,1)S(1)}, u32[]{:S(2)}) copy-start(bf16[4,2,16,1024]{3,2,1,0:T(8,128)(2,1)S(1)} %constant_dynamic-update-slice_fusion.10) | copy-start | bytes 786436
  86.4 21.4 %collective-permute-start.19 = (bf16[2,16,2048]{2,1,0:T(8,128)(2,1)}, bf16[2,16,2048]{2,1,0:T(8,128)(2,1)}, u32[]{:S(2)}, u32[]{:S(2)}) collective-permute-start(bf16[2,16,2048]{2,1,0:T(8,128)(2,1)} %slice_bitcast_fusion.6), channel_id=1, source_target_pairs={{0,4},{2,6},{4,0},{6,2},{1,5},{3,7},{5,1},{7,3},{8,12},{10,14},{12... | collective-permute-start | bytes 393224 | tf_op jit(solution)/shard_map/ppermute | solution.py:43
  88.7 13.1 %copy-start.12 = (bf16[1,16,8192]{2,1,0:T(8,128)(2,1)}, bf16[1,16,8192]{2,1,0:T(8,128)(2,1)S(1)}, u32[]{:S(2)}) copy-start(bf16[1,16,8192]{2,1,0:T(8,128)(2,1)S(1)} %fusion.111) | copy-start | bytes 786436
  88.7 13.0 %copy-start.11 = (bf16[1,16,8192]{2,1,0:T(8,128)(2,1)}, bf16[1,16,8192]{2,1,0:T(8,128)(2,1)S(1)}, u32[]{:S(2)}) copy-start(bf16[1,16,8192]{2,1,0:T(8,128)(2,1)S(1)} %fusion.113) | copy-start | bytes 786436
  88.8 23.4 %collective-permute-start.10 = (bf16[2,16,2048]{2,1,0:T(8,128)(2,1)}, bf16[2,16,2048]{2,1,0:T(8,128)(2,1)}, u32[]{:S(2)}, u32[]{:S(2)}) collective-permute-start(bf16[2,16,2048]{2,1,0:T(8,128)(2,1)} %slice_bitcast_fusion.7), channel_id=1, source_target_pairs={{0,4},{2,6},{4,0},{6,2},{1,5},{3,7},{5,1},{7,3},{8,12},{10,14},{12... | collective-permute-start | bytes 393224 | tf_op jit(solution)/shard_map/ppermute | solution.py:43
  89.5 4.6 %collective-permute-start.28 = (f32[2,2,16]{2,1,0:T(2,128)S(1)}, f32[2,2,16]{2,1,0:T(2,128)S(1)}, u32[]{:S(2)}, u32[]{:S(2)}) collective-permute-start(f32[2,2,16]{2,1,0:T(2,128)S(1)} %pad_maximum_fusion.7), channel_id=1, source_target_pairs={{0,4},{2,6},{4,0},{6,2},{1,5},{3,7},{5,1},{7,3},{8,12},{10,14},{12... | collective-permute-start | bytes 776 | tf_op jit(solution)/shard_map/ppermute | solution.py:43
  91.2 10.4 %collective-permute-start.20 = (f32[2,2,16]{2,1,0:T(2,128)S(1)}, f32[2,2,16]{2,1,0:T(2,128)S(1)}, u32[]{:S(2)}, u32[]{:S(2)}) collective-permute-start(f32[2,2,16]{2,1,0:T(2,128)S(1)} %pad_maximum_fusion.5), channel_id=1, source_target_pairs={{0,4},{2,6},{4,0},{6,2},{1,5},{3,7},{5,1},{7,3},{8,12},{10,14},{12... | collective-permute-start | bytes 776 | tf_op jit(solution)/shard_map/ppermute | solution.py:43
  95.2 21.2 %collective-permute-start.29 = (bf16[2,32,2048]{2,1,0:T(8,128)(2,1)}, bf16[2,32,2048]{2,1,0:T(8,128)(2,1)}, u32[]{:S(2)}, u32[]{:S(2)}) collective-permute-start(bf16[2,32,2048]{2,1,0:T(8,128)(2,1)} %get-tuple-element.11), channel_id=1, source_target_pairs={{0,8},{8,16},{16,24},{1,9},{9,17},{17,25},{2,10},{10,18},{18,26},{... | collective-permute-start | bytes 786440 | tf_op jit(solution)/shard_map/ppermute | solution.py:185
  100.3 13.3 %collective-permute-start.30 = (bf16[2,32,2048]{2,1,0:T(8,128)(2,1)}, bf16[2,32,2048]{2,1,0:T(8,128)(2,1)}, u32[]{:S(2)}, u32[]{:S(2)}) collective-permute-start(bf16[2,32,2048]{2,1,0:T(8,128)(2,1)} %get-tuple-element.11), channel_id=1, source_target_pairs={{8,0},{16,8},{24,16},{9,1},{17,9},{25,17},{10,2},{18,10},{26,18},{... | collective-permute-start | bytes 786440 | tf_op jit(solution)/shard_map/ppermute | solution.py:188
  101.9 38.7 %copy-start.2 = (bf16[1,1024,2048]{2,1,0:T(8,128)(2,1)S(1)}, bf16[1,1024,2048]{2,1,0:T(8,128)(2,1)}, u32[]{:S(2)}) copy-start(bf16[1,1024,2048]{2,1,0:T(8,128)(2,1)} %param.10) | copy-start | bytes 12582916
  103.2 15.8 %collective-permute-start.21 = (bf16[2,32,2048]{2,1,0:T(8,128)(2,1)S(1)}, bf16[2,32,2048]{2,1,0:T(8,128)(2,1)S(1)}, u32[]{:S(2)}, u32[]{:S(2)}) collective-permute-start(bf16[2,32,2048]{2,1,0:T(8,128)(2,1)S(1)} %get-tuple-element.9), channel_id=1, source_target_pairs={{0,8},{8,16},{16,24},{1,9},{9,17},{17,25},{2,10},{10,18},{18,26},{... | collective-permute-start | bytes 786440 | tf_op jit(solution)/shard_map/ppermute | solution.py:185
  107.9 9.8 %collective-permute-start.22 = (bf16[2,32,2048]{2,1,0:T(8,128)(2,1)S(1)}, bf16[2,32,2048]{2,1,0:T(8,128)(2,1)S(1)}, u32[]{:S(2)}, u32[]{:S(2)}) collective-permute-start(bf16[2,32,2048]{2,1,0:T(8,128)(2,1)S(1)} %get-tuple-element.9), channel_id=1, source_target_pairs={{8,0},{16,8},{24,16},{9,1},{17,9},{25,17},{10,2},{18,10},{26,18},{... | collective-permute-start | bytes 786440 | tf_op jit(solution)/shard_map/ppermute | solution.py:188
  113.6 11.6 %collective-permute-start.31 = (bf16[2,32,2048]{2,1,0:T(8,128)(2,1)}, bf16[2,32,2048]{2,1,0:T(8,128)(2,1)S(1)}, u32[]{:S(2)}, u32[]{:S(2)}) collective-permute-start(bf16[2,32,2048]{2,1,0:T(8,128)(2,1)} %collective-permute-done.30), channel_id=1, source_target_pairs={{8,0},{16,8},{9,1},{17,9},{10,2},{18,10},{11,3},{19,11},{12,4},{20... | collective-permute-start | bytes 786440 | tf_op jit(solution)/shard_map/ppermute | solution.py:188
  116.4 12.0 %collective-permute-start.33 = (bf16[2,32,2048]{2,1,0:T(8,128)(2,1)}, bf16[2,32,2048]{2,1,0:T(8,128)(2,1)S(1)}, u32[]{:S(2)}, u32[]{:S(2)}) collective-permute-start(bf16[2,32,2048]{2,1,0:T(8,128)(2,1)} %collective-permute-done.29), channel_id=1, source_target_pairs={{8,16},{16,24},{9,17},{17,25},{10,18},{18,26},{11,19},{19,27},{12,... | collective-permute-start | bytes 786440 | tf_op jit(solution)/shard_map/ppermute | solution.py:185
  117.7 14.5 %collective-permute-start.23 = (bf16[2,32,2048]{2,1,0:T(8,128)(2,1)S(1)}, bf16[2,32,2048]{2,1,0:T(8,128)(2,1)S(1)}, u32[]{:S(2)}, u32[]{:S(2)}) collective-permute-start(bf16[2,32,2048]{2,1,0:T(8,128)(2,1)S(1)} %collective-permute-done.22), channel_id=1, source_target_pairs={{8,0},{16,8},{9,1},{17,9},{10,2},{18,10},{11,3},{19,11},{12,4},{20... | collective-permute-start | bytes 786440 | tf_op jit(solution)/shard_map/ppermute | solution.py:188
  119.0 14.5 %collective-permute-start.25 = (bf16[2,32,2048]{2,1,0:T(8,128)(2,1)S(1)}, bf16[2,32,2048]{2,1,0:T(8,128)(2,1)S(1)}, u32[]{:S(2)}, u32[]{:S(2)}) collective-permute-start(bf16[2,32,2048]{2,1,0:T(8,128)(2,1)S(1)} %collective-permute-done.21), channel_id=1, source_target_pairs={{8,16},{16,24},{9,17},{17,25},{10,18},{18,26},{11,19},{19,27},{12,... | collective-permute-start | bytes 786440 | tf_op jit(solution)/shard_map/ppermute | solution.py:185
  125.2 10.4 %collective-permute-start.32 = (bf16[2,32,2048]{2,1,0:T(8,128)(2,1)S(1)}, bf16[2,32,2048]{2,1,0:T(8,128)(2,1)S(1)}, u32[]{:S(2)}, u32[]{:S(2)}) collective-permute-start(bf16[2,32,2048]{2,1,0:T(8,128)(2,1)S(1)} %collective-permute-done.31), channel_id=1, source_target_pairs={{8,0},{9,1},{10,2},{11,3},{12,4},{13,5},{14,6},{15,7}} | collective-permute-start | bytes 786440 | tf_op jit(solution)/shard_map/ppermute | solution.py:188
  128.4 7.4 %collective-permute-start.34 = (bf16[2,32,2048]{2,1,0:T(8,128)(2,1)S(1)}, bf16[2,32,2048]{2,1,0:T(8,128)(2,1)S(1)}, u32[]{:S(2)}, u32[]{:S(2)}) collective-permute-start(bf16[2,32,2048]{2,1,0:T(8,128)(2,1)S(1)} %collective-permute-done.33), channel_id=1, source_target_pairs={{16,24},{17,25},{18,26},{19,27},{20,28},{21,29},{22,30},{23,31}} | collective-permute-start | bytes 786440 | tf_op jit(solution)/shard_map/ppermute | solution.py:185
  132.2 8.3 %collective-permute-start.24 = (bf16[2,32,2048]{2,1,0:T(8,128)(2,1)S(1)}, bf16[2,32,2048]{2,1,0:T(8,128)(2,1)S(1)}, u32[]{:S(2)}, u32[]{:S(2)}) collective-permute-start(bf16[2,32,2048]{2,1,0:T(8,128)(2,1)S(1)} %collective-permute-done.23), channel_id=1, source_target_pairs={{8,0},{9,1},{10,2},{11,3},{12,4},{13,5},{14,6},{15,7}} | collective-permute-start | bytes 786440 | tf_op jit(solution)/shard_map/ppermute | solution.py:188
  133.5 9.4 %collective-permute-start.26 = (bf16[2,32,2048]{2,1,0:T(8,128)(2,1)S(1)}, bf16[2,32,2048]{2,1,0:T(8,128)(2,1)S(1)}, u32[]{:S(2)}, u32[]{:S(2)}) collective-permute-start(bf16[2,32,2048]{2,1,0:T(8,128)(2,1)S(1)} %collective-permute-done.25), channel_id=1, source_target_pairs={{16,24},{17,25},{18,26},{19,27},{20,28},{21,29},{22,30},{23,31}} | collective-permute-start | bytes 786440 | tf_op jit(solution)/shard_map/ppermute | solution.py:185
  144.0 2.3 %copy-start.4 = (bf16[1,4,32,2048]{3,2,1,0:T(8,128)(2,1)}, bf16[1,4,32,2048]{3,2,1,0:T(8,128)(2,1)S(1)}, u32[]{:S(2)}) copy-start(bf16[1,4,32,2048]{3,2,1,0:T(8,128)(2,1)S(1)} %get-tuple-element.18) | copy-start | bytes 1572868
  152.9 8.4 %copy-start.3 = (bf16[1,4,32,2048]{3,2,1,0:T(8,128)(2,1)S(1)}, bf16[1,4,32,2048]{3,2,1,0:T(8,128)(2,1)}, u32[]{:S(2)}) copy-start(bf16[1,4,32,2048]{3,2,1,0:T(8,128)(2,1)} %get-tuple-element.19) | copy-start | bytes 1572868
  156.2 5.2 %copy-start.7 = (f32[128,1024]{1,0:T(8,128)S(1)}, f32[128,1024]{1,0:T(8,128)}, u32[]{:S(2)}) copy-start(f32[128,1024]{1,0:T(8,128)} %fusion.143) | copy-start | bytes 1572868
  156.2 5.2 %copy-start.8 = (f32[128,1024]{1,0:T(8,128)S(1)}, f32[128,1024]{1,0:T(8,128)}, u32[]{:S(2)}) copy-start(f32[128,1024]{1,0:T(8,128)} %fusion.79) | copy-start | bytes 1572868
  160.2 4.8 %copy-start.9 = (f32[128,1024]{1,0:T(8,128)}, f32[128,1024]{1,0:T(8,128)S(1)}, u32[]{:S(2)}) copy-start(f32[128,1024]{1,0:T(8,128)S(1)} %fusion.5) | copy-start | bytes 1572868
  160.2 7.1 %copy-start.18 = (bf16[128,32]{1,0:T(8,128)(2,1)S(1)}, bf16[128,32]{1,0:T(8,128)(2,1)}, u32[]{:S(2)}) copy-start(bf16[128,32]{1,0:T(8,128)(2,1)} %copy.55) | copy-start | bytes 24580
  160.3 9.7 %copy-start.19 = (bf16[128,32]{1,0:T(8,128)(2,1)S(1)}, bf16[128,32]{1,0:T(8,128)(2,1)}, u32[]{:S(2)}) copy-start(bf16[128,32]{1,0:T(8,128)(2,1)} %copy.52) | copy-start | bytes 24580
  160.9 23.1 %collective-permute-start.35 = (bf16[4,16,1024]{2,1,0:T(8,128)(2,1)}, bf16[4,16,1024]{2,1,0:T(8,128)(2,1)}, u32[]{:S(2)}, u32[]{:S(2)}) collective-permute-start(bf16[4,16,1024]{2,1,0:T(8,128)(2,1)} %fusion.86), channel_id=1, source_target_pairs={{0,4},{2,6},{4,0},{6,2},{1,5},{3,7},{5,1},{7,3},{8,12},{10,14},{12... | collective-permute-start | bytes 393224 | tf_op jit(solution)/shard_map/ppermute | solution.py:43
  165.8 21.7 %collective-permute-start.27 = (bf16[4,16,1024]{2,1,0:T(8,128)(2,1)}, bf16[4,16,1024]{2,1,0:T(8,128)(2,1)}, u32[]{:S(2)}, u32[]{:S(2)}) collective-permute-start(bf16[4,16,1024]{2,1,0:T(8,128)(2,1)} %fusion.85), channel_id=1, source_target_pairs={{0,4},{2,6},{4,0},{6,2},{1,5},{3,7},{5,1},{7,3},{8,12},{10,14},{12... | collective-permute-start | bytes 393224 | tf_op jit(solution)/shard_map/ppermute | solution.py:43
  168.1 6.4 %collective-permute-start.37 = (bf16[4,2,16,64]{3,2,1,0:T(8,128)(2,1)}, bf16[4,2,16,64]{3,2,1,0:T(8,128)(2,1)}, u32[]{:S(2)}, u32[]{:S(2)}) collective-permute-start(bf16[4,2,16,64]{3,2,1,0:T(8,128)(2,1)} %fusion.116), channel_id=1, source_target_pairs={{0,4},{2,6},{4,0},{6,2},{1,5},{3,7},{5,1},{7,3},{8,12},{10,14},{12... | collective-permute-start | bytes 49160 | tf_op jit(solution)/shard_map/ppermute | solution.py:43
  170.0 1.8 copy-start.20
  170.1 7.2 %collective-permute-start.36 = (bf16[4,2,16,64]{3,2,1,0:T(8,128)(2,1)S(1)}, bf16[4,2,16,64]{3,2,1,0:T(8,128)(2,1)}, u32[]{:S(2)}, u32[]{:S(2)}) collective-permute-start(bf16[4,2,16,64]{3,2,1,0:T(8,128)(2,1)S(1)} %fusion.115), channel_id=1, source_target_pairs={{0,4},{2,6},{4,0},{6,2},{1,5},{3,7},{5,1},{7,3},{8,12},{10,14},{12... | collective-permute-start | bytes 49160 | tf_op jit(solution)/shard_map/ppermute | solution.py:43
  172.1 12.0 %copy-start.10 = (f32[128,1024]{1,0:T(8,128)S(1)}, f32[128,1024]{1,0:T(8,128)}, u32[]{:S(2)}) copy-start(f32[128,1024]{1,0:T(8,128)} %copy-done.9) | copy-start | bytes 1572868
  173.3 11.7 %collective-permute-start.39 = (f32[128,1024]{1,0:T(8,128)}, f32[128,1024]{1,0:T(8,128)S(1)}, u32[]{:S(2)}, u32[]{:S(2)}) collective-permute-start(f32[128,1024]{1,0:T(8,128)} %constant_dynamic-slice_fusion), channel_id=1, source_target_pairs={{0,2},{2,0},{4,6},{6,4},{1,3},{3,1},{5,7},{7,5},{8,10},{10,8},{12,... | collective-permute-start | bytes 1572872 | tf_op jit(solution)/shard_map/ppermute | solution.py:39
  183.5 9.8 %collective-permute-start.38 = (f32[1024,128]{1,0:T(8,128)S(1)}, f32[1024,128]{1,0:T(8,128)S(1)}, u32[]{:S(2)}, u32[]{:S(2)}) collective-permute-start(f32[1024,128]{1,0:T(8,128)S(1)} %fusion.6), channel_id=1, source_target_pairs={{0,2},{2,0},{4,6},{6,4},{1,3},{3,1},{5,7},{7,5},{8,10},{10,8},{12,... | collective-permute-start | bytes 1572872 | tf_op jit(solution)/shard_map/ppermute | solution.py:39
  185.1 8.1 %collective-permute-start.40 = (bf16[128,1024]{1,0:T(8,128)(2,1)S(1)}, bf16[128,1024]{1,0:T(8,128)(2,1)S(1)}, u32[]{:S(2)}, u32[]{:S(2)}) collective-permute-start(bf16[128,1024]{1,0:T(8,128)(2,1)S(1)} %add_convert_fusion), channel_id=1, source_target_pairs={{0,4},{2,6},{8,12},{10,14},{20,16},{22,18},{28,24},{30,26},{1,5},{... | collective-permute-start | bytes 786440 | tf_op jit(solution)/shard_map/ppermute | solution.py:284
  193.2 1.6 collective-permute-start.41
  (3 other events, 2.2 us)

commit v2 on v1

v2 whole, which is shorter than its diff:
```python
import jax
import jax.numpy as jnp
from jax import lax
from jax.sharding import PartitionSpec as P

F32 = jnp.float32
BF16 = jnp.bfloat16


def dot(left_side, right_side, left_dim, right_dim):
    return lax.dot_general(
        left_side,
        right_side,
        (((left_dim,), (right_dim,)), ((), ())),
        preferred_element_type=F32,
    )


def pick(value, index, dim=0):
    return lax.dynamic_index_in_dim(value, index, dim, keepdims=False)


def columns(value, start, size):
    return lax.dynamic_slice_in_dim(value, start, size, value.ndim - 1)


def after(value, *others):
    return lax.optimization_barrier((value, *others))[0]


def on_device(mix, hidden_in, cotangent, frozen_weight, right_factor, left_factor, norm_gain):
    blocks = lax.axis_size("tensor")
    parts = lax.axis_size("dp")
    sections = lax.axis_size("pipe")
    t = lax.axis_index("tensor")
    d = lax.axis_index("dp")
    section = lax.axis_index("pipe")
    outers = parts // 2
    outer = d // 2
    core = d % 2

    def to_core(value):
        return lax.ppermute(value, "dp", [(i, i ^ 1) for i in range(parts)])

    def to_outer(value, step):
        return lax.ppermute(value, "dp", [(i, (i + 2 * step) % parts) for i in range(parts)])

    def to_block(value, step):
        return lax.ppermute(value, "tensor", [(i, (i + step) % blocks) for i in range(blocks)])

    def of_cores(value):
        return jnp.where(core == 0, value, value[::-1])

    mixes = mix[0, :, 0]
    micro, tokens, head_cols = mixes.shape
    own_rows = tokens // blocks
    weight = frozen_weight[0]
    right = right_factor[0, 0]
    left = left_factor[0, 0]
    rank, block_cols = left.shape
    sub = rank // blocks
    width = weight.shape[1]
    features = width * parts
    rows = outers * own_rows
    all_rows = blocks * rows
    per_block = parts // blocks
    slots = (d, d ^ 1)

    def block_of(part):
        return part // per_block

    weights = (weight, to_core(weight))
    own = mixes.reshape(micro, blocks, 1, own_rows, head_cols)
    taken = [
        jnp.concatenate(
            [own[m]] + [to_outer(own[m], step) for step in range(1, outers)], axis=1
        ).reshape(all_rows, head_cols)
        for m in range(micro)
    ]
    own_inner = dot(right, mixes.reshape(micro * tokens, head_cols), 0, 1).astype(BF16)
    pieces = lax.all_to_all(
        jnp.concatenate(
            [
                left.reshape(blocks, sub, block_cols),
                own_inner.reshape(blocks, sub, micro * tokens),
            ],
            axis=2,
        ),
        "tensor",
        split_axis=0,
        concat_axis=0,
        tiled=True,
    )
    left_slots = [
        columns(pick(pieces, block_of(part)), (part % per_block) * width, width) for part in slots
    ]
    right_slots = [columns(right, block_of(part) * sub, sub) for part in slots]
    own_permuted = pieces[:, :, block_cols:].reshape(rank, micro * tokens)
    own_permuted = after(own_permuted, *taken)
    permuted = [own_permuted] + [to_outer(own_permuted, step) for step in range(1, outers)]

    inners = [dot(taken[m], right, 1, 0).astype(BF16) for m in range(micro)]
    partial = [
        jnp.stack(
            [
                (
                    dot(taken[m], weights[slot], 1, 0)
                    + dot(
                        columns(inners[m], block_of(part) * sub, sub), left_slots[slot], 1, 0
                    )
                ).astype(BF16)
                for slot, part in enumerate(slots)
            ]
        ).reshape(2, blocks, rows, width)
        for m in range(micro)
    ]

    def shard(m, index):
        return pick(partial[m], index, 1)

    updates_here = []
    arrived_last = None
    for m in range(micro):
        total = shard(m, t).astype(F32)
        if blocks != 4:
            for step in range(1, blocks):
                total = total + to_block(shard(m, (t + step) % blocks), step).astype(F32)
            updates_here.append(total)
            continue
        far = shard(m, jnp.where(t < 2, 3, 0))
        if arrived_last is not None:
            far = after(far, arrived_last)
        passed = lax.ppermute(far, "tensor", [(0, 1), (3, 2)])
        mid = lax.ppermute(
            after(shard(m, jnp.where(t < 2, 2, 1)), far), "tensor", [(1, 2), (2, 1)]
        )
        beside = lax.ppermute(after(shard(m, t ^ 1), far), "tensor", [(i, i ^ 1) for i in range(4)])
        middle = (t == 1) | (t == 2)
        two_away = jnp.where(
            middle, (far.astype(F32) + passed.astype(F32)).astype(BF16), shard(m, t ^ 2)
        )
        arrived_last = two_away
        crossed = to_block(two_away, 2)
        updates_here.append(
            total + beside.astype(F32) + mid.astype(F32) + crossed.astype(F32)
        )

    hidden_late = after(hidden_in, *taken)

    def by_column(step):
        target = (outer + step) % outers
        cuts = [2 * target + core, 2 * target + (1 - core)]
        return jnp.stack(
            [
                jnp.stack([columns(value[:, 0], part * width, width) for part in cuts])
                for value in (hidden_late, cotangent)
            ]
        )

    entering = jnp.concatenate(
        [by_column(0)] + [to_outer(by_column(step), step) for step in range(1, outers)], axis=3
    )
    gains = jnp.stack([columns(norm_gain, part * width, width) for part in slots]).astype(F32)

    grads = []
    leaving = []
    for m in range(micro):
        sent = updates_here[m].astype(BF16)
        updates = [updates_here[m]] + [
            lax.ppermute(
                sent, "pipe", [(i, (i + step) % sections) for i in range(sections)]
            ).astype(F32)
            for step in range(1, sections)
        ]
        state = entering[0, :, m]
        kept = state
        for s in range(sections):
            add = updates[0]
            for step in range(1, sections):
                add = jnp.where((section - step) % sections == s, updates[step], add)
            state = (state.astype(F32) + add).astype(BF16)
            kept = jnp.where(section == s, state, kept)
        leaving.append(kept)
        final = state.astype(F32)
        upstream = entering[1, :, m].astype(F32) * gains[:, None, :]
        sums = jnp.stack(
            [jnp.sum(final * final, axis=(0, 2)), jnp.sum(upstream * final, axis=(0, 2))]
        ).reshape(2, outers, own_rows)
        total = sums
        for step in range(1, outers):
            total = total + jnp.roll(to_outer(sums, step), step, axis=1)
        total = total.reshape(2, rows) / features
        scale = lax.rsqrt(total[0] + 1e-05)
        shrink = scale * scale * total[1]
        grads.append(
            (scale[None, :, None] * (upstream - final * shrink[None, :, None])).astype(BF16)
        )

    full = []
    order = []
    earlier = None
    for m in range(micro):
        if blocks != 4:
            pieces_m = [grads[m]] + [to_block(grads[m], step) for step in range(1, blocks)]
            full.append(jnp.concatenate(pieces_m, axis=1))
            order.append([(t - step) % blocks for step in range(blocks)])
            continue
        opposite = to_block(grads[m], 2)
        beside = lax.ppermute(grads[m], "tensor", [(i, i ^ 1) for i in range(4)])
        mid = lax.ppermute(grads[m], "tensor", [(1, 2), (2, 1)])
        relay = after(opposite, beside, mid)
        farthest = lax.ppermute(relay, "tensor", [(1, 0), (2, 3)])
        last = jnp.where((t == 1) | (t == 2), mid, farthest)
        if earlier is not None:
            full[-1] = after(full[-1], relay)
        full.append(jnp.concatenate([grads[m], beside, opposite, last], axis=1))
        order.append([t, t ^ 1, t ^ 2, t ^ 3])
        earlier = relay

    outs = []
    for m in range(micro):
        by_group = after(leaving[m], grads[m]).reshape(2, outers, own_rows, width)
        row = jnp.zeros((own_rows, features), BF16)
        for step in range(outers):
            at = (outer + step) % outers
            piece = by_group[:, step]
            if step:
                piece = after(to_outer(piece, outers - step), full[-1])
            for slot in range(2):
                place = (2 * at + (core if slot == 0 else 1 - core)) * width
                row = lax.dynamic_update_slice_in_dim(row, piece[slot], place, 1)
        outs.append(row)
    section_out = jnp.stack(outs).reshape(1, micro, 1, own_rows, features)

    mix_rows = [
        jnp.concatenate(
            [pick(taken[m].reshape(blocks, rows, head_cols), at) for at in order[m]], axis=0
        )
        for m in range(micro)
    ]
    permuted_rows = [
        jnp.concatenate(
            [
                columns(half, m * tokens + at * own_rows, own_rows)
                for at in order[m]
                for half in permuted
            ],
            axis=1,
        )
        for m in range(micro)
    ]

    holder = (t * per_block) // 2
    mix_grads = []
    right_sum = 0.0
    left_sum = 0.0
    for m in range(micro):
        if per_block == 1:
            cols = pick(full[m], jnp.where(t % 2 == core, 0, 1))
        else:
            cols = jnp.concatenate(list(of_cores(full[m])), axis=1)
        left_sum = left_sum + dot(permuted_rows[m], cols, 1, 0)

        inner_grads = [
            dot(full[m][slot], left_slots[slot], 1, 1).astype(BF16) for slot in range(2)
        ]
        if per_block == 1:
            mine = jnp.concatenate(inner_grads, axis=1)
            right_here = jnp.concatenate(right_slots, axis=1)
        else:
            mine = (inner_grads[0].astype(F32) + inner_grads[1].astype(F32)).astype(BF16)
            right_here = right_slots[0]
        right_sum = right_sum + dot(mine, mix_rows[m], 0, 0)

        partial_mix = (
            dot(full[m][0], weights[0], 1, 1)
            + dot(full[m][1], weights[1], 1, 1)
            + dot(mine, right_here, 1, 1)
        ).reshape(blocks, outers, own_rows, head_cols)
        whole = partial_mix[:, 0]
        for step in range(1, outers):
            whole = whole + to_outer(partial_mix[:, step].astype(BF16), outers - step).astype(F32)
        whole = whole.astype(BF16)
        back = [t ^ i for i in range(blocks)] if blocks == 4 else order[m]
        mix_grads.append(
            jnp.concatenate([pick(whole, at) for at in back], axis=0)
        )
    grad_mix = jnp.stack(mix_grads).reshape(1, micro, 1, tokens, head_cols)

    half = block_cols // 2
    half_sum = (
        columns(left_sum, core * half, half) + to_core(columns(left_sum, (1 - core) * half, half))
    ).astype(BF16)
    best = half_sum
    for step in range(1, outers):
        pairs = []
        for i in range(blocks):
            at = (i * per_block) // 2
            for c in range(2):
                pairs.append(
                    (i * parts + 2 * at + c, i * parts + 2 * ((at + step) % outers) + c)
                )
        arrived = lax.ppermute(half_sum, ("tensor", "dp"), pairs)
        best = jnp.where((outer - holder) % outers == step, arrived, best)
    there = to_core(best)
    grad_left = jnp.concatenate(list(of_cores(jnp.stack([best, there]))), axis=1).astype(F32)

    if per_block == 1:
        right_sum = of_cores(right_sum.reshape(2, sub, head_cols)).reshape(2 * sub, head_cols)
    right_sum = (right_sum + to_core(right_sum)).astype(BF16)
    wide = jnp.zeros((rank, head_cols), BF16)
    count = right_sum.shape[0]
    for step in range(outers):
        arrived = to_outer(right_sum, step) if step else right_sum
        wide = lax.dynamic_update_slice_in_dim(
            wide, arrived, ((outer - step) % outers) * count, 0
        )
    grad_right = wide.T.astype(F32)

    return (
        section_out,
        grad_mix,
        grad_right.reshape(1, 1, head_cols, rank),
        grad_left.reshape(1, 1, rank, block_cols),
    )


def solution(mesh):
    return jax.shard_map(
        on_device,
        mesh=mesh,
        in_specs=(
            P("pipe", None, "dp", None, "tensor"),
            P(None, "dp", "tensor", None),
            P(None, "dp", "tensor", None),
            P("pipe", "tensor", "dp"),
            P("pipe", "tensor", None, None),
            P("pipe", "tensor", None, None),
            P(),
        ),
        out_specs=(
            P("pipe", None, "dp", "tensor", None),
            P("pipe", None, "dp", None, "tensor"),
            P("pipe", "tensor", None, None),
            P("pipe", "tensor", None, None),
        ),
        check_vma=False,
    )
```

time: 198 us -> 177 us (0.89)
  waiting for transfers between devices: 38.9 us -> 55.9 us
  starting transfers between devices: 82 us -> 65.1 us
  matrix products: 33.7 us -> 23.8 us
  local copies, waits for them, and re-layouts: 24.5 us -> 14.9 us
    ppermute x35 -> x27, waiting for transfers between devices: 30.3 us -> 44.8 us  [the longest x4 28.9 us: to_block(): lax.ppermute(value, 'tensor', [(i, (i + step) % blocks) for i in range(bl...]
    ppermute x35 -> x27, starting transfers between devices: 65.6 us -> 52.6 us  [the longest x4 14.5 us: to_block(): lax.ppermute(value, 'tensor', [(i, (i + step) % blocks) for i in range(bl...]
    dynamic_update_slice x24 -> x10, local copies, waits for them, and re-layouts: 14.2 us -> 2.93 us  [the longest x2 2.83 us: on_device(): lax.dynamic_update_slice_in_dim(wide, arrived, (outer - step) % outers *...]
    dot_general x24 -> x25, matrix products: 33.7 us -> 23.8 us  [dot(): lax.dot_general(left_side, right_side, (((left_dim,), (right_dim,)), ((),...]
    dynamic_slice x2 -> x5, local copies, waits for them, and re-layouts: 0.86 us -> 4.4 us  [columns(): return lax.dynamic_slice_in_dim(value, start, size, value.ndim - 1)]
    dynamic_update_slice x8 -> x0, other arithmetic: 3.48 us -> none  [the longest x2 2.13 us: on_device(): buffer = lax.dynamic_update_slice_in_dim(buffer, grads[m][:, None], t, 1)]
    all_to_all x2 -> x1, starting transfers between devices: 9.76 us -> 6.32 us  [on_device(): lax.all_to_all(jnp.concatenate([left.reshape(blocks, sub, block_cols), ow...]
    convert_element_type x12 -> x8, other arithmetic: 4.57 us -> 1.78 us  [the longest x1 1.07 us: on_device(): jnp.concatenate(list(of_cores(jnp.stack([best, there]))), axis=1)]
  transfers between devices with their start and end apart: 44 -> 35, of which waited for: 16 -> 15; matrix products, arithmetic and copies ran while one was open for 36% -> 26% of each run, Pallas kernels for 0% -> 0%
where the time goes in v2:
time: 177 us; the launch traced here: 176 us
  starting transfers between devices  65.1 us (37%)
  waiting for transfers between devices  55.9 us (32%)
  matrix products  23.8 us (13%)
  local copies, waits for them, and re-layouts  14.9 us (8%)
  other arithmetic  14.7 us (8%)
    ppermute x4, waiting for transfers between devices, to_block(): lax.ppermute(value, 'tensor', [(i, (i + step) % blocks) for i in range(bl...  28.9 us
    dot_general x25, matrix products, dot(): lax.dot_general(left_side, right_side, (((left_dim,), (right_dim,)), ((),...  23.8 us
    ppermute x4, starting transfers between devices, to_block(): lax.ppermute(value, 'tensor', [(i, (i + step) % blocks) for i in range(bl...  14.5 us
    ppermute x11, starting transfers between devices, to_outer(): lax.ppermute(value, 'dp', [(i, (i + 2 * step) % parts) for i in range(par...  10.5 us
    ppermute x11, waiting for transfers between devices, to_outer(): lax.ppermute(value, 'dp', [(i, (i + 2 * step) % parts) for i in range(par...  10.4 us
    ppermute x2, starting transfers between devices, on_device(): passed = lax.ppermute(far, 'tensor', [(0, 1), (3, 2)])  9.17 us
    ppermute x2, starting transfers between devices, on_device(): beside = lax.ppermute(grads[m], 'tensor', [(i, i ^ 1) for i in range(4)])  8.25 us
    ppermute x1, waiting for transfers between devices, on_device(): arrived = lax.ppermute(half_sum, ('tensor', 'dp'), pairs)  6.47 us
  transfers between devices with their start and end apart: 35, of which 15 were waited for; matrix products, arithmetic and copies ran while one was open for 26% of the time, Pallas kernels for 0%

profile of v2, /device:TPU:0, one launch (start us, length us, event | category | flops | bytes accessed | tf_op | source)
XLA Modules:
  0.0 175.9 jit_solution(7946237333893384342)
XLA Ops:
  0.7 1.4 convolution_convert_fusion.1
  2.0 1.9 %pad_maximum_fusion.3 = bf16[4,32,2176]{2,1,0:T(8,128)(2,1)} fusion(bf16[4,32,128]{2,1,0:T(8,128)(2,1)S(1)} %bitcast.337, bf16[4,32,2048]{2,1,0:T(8,128)(2,1)} %bitcast.330), kind=kLoop, calls=%fused_computation.55 | loop fusion | flops 1114112 | bytes 1114112 | tf_op jit(solution)/shard_map/concatenate | solution.py:82
  3.9 6.3 %all-to-all-start = ((bf16[4,32,2176]{2,1,0:T(8,128)(2,1)}), bf16[4,32,2176]{2,1,0:T(8,128)(2,1)S(1)}, u32[]{:S(2)}, u32[]{:S(2)}) async-start(bf16[4,32,2176]{2,1,0:T(8,128)(2,1)} %pad_maximum_fusion.3), calls=%async_computation | async-start | bytes 1114112 | tf_op jit(solution)/shard_map/all_to_all | solution.py:81
  10.3 1.0 fusion.145
  11.2 1.6 collective-permute-start
  14.1 2.0 %dynamic-slice_bitcast_fusion.1 = (bf16[1024,32]{1,0:T(8,128)(2,1)S(1)}, bf16[1024,32]{1,0:T(8,128)(2,1)}) fusion(bf16[1,1,1024,128]{3,2,1,0:T(8,128)(2,1)} %param.11, s32[]{:T(128)S(6)} %select_n.316, s32[]{:T(128)S(6)} %select_n.319), kind=kLoop, calls=%fused_computation.176 | loop fusion | bytes 262152 | tf_op jit(solution)/shard_map/dynamic_slice | solution.py:24
  16.1 1.5 collective-permute-done
  17.6 2.4 %collective-permute-done.1 = bf16[4,1,16,1024]{3,2,1,0:T(8,128)(2,1)S(1)} collective-permute-done((bf16[4,1,16,1024]{3,2,1,0:T(8,128)(2,1)S(1)}, bf16[4,1,16,1024]{3,2,1,0:T(8,128)(2,1)S(1)}, u32[]{:S(2)}, u32[]{:S(2)}) %collective-permute-start.1) | collective-permute-done | bytes 131104 | tf_op jit(solution)/shard_map/ppermute | solution.py:46
  20.2 0.8 pad_maximum_fusion.4
  21.1 1.5 collective-permute-start.2
  22.6 0.7 maximum_bitcast_fusion.2
  27.4 1.1 copy-done
  28.5 0.7 fusion
  29.2 0.7 fusion.2
  30.0 3.0 %fusion.1 = bf16[128,2048]{1,0:T(8,128)(2,1)S(1)} fusion(f32[128,2048]{1,0:T(8,128)S(1)} %fusion.97, bf16[128,1024]{1,0:T(8,128)(2,1)S(1)} %bitcast.314, bf16[1024,2048]{1,0:T(8,128)(2,1)} %collective-permute-done.3), kind=kOutput, calls=%fused_computation.6 | convolution fusion | flops 537395200 | bytes 6029312 | tf_op jit(solution)/shard_map/dot_general | solution.py:11
  33.0 0.9 fusion.64
  33.8 4.1 %collective-permute-start.6 = (bf16[2,32,2048]{2,1,0:T(8,128)(2,1)S(1)}, bf16[2,32,2048]{2,1,0:T(8,128)(2,1)S(1)}, u32[]{:S(2)}, u32[]{:S(2)}) collective-permute-start(bf16[2,32,2048]{2,1,0:T(8,128)(2,1)S(1)} %get-tuple-element.49), channel_id=1, source_target_pairs={{0,8},{24,16},{1,9},{25,17},{2,10},{26,18},{3,11},{27,19},{4,12},{... | collective-permute-start | bytes 786440 | tf_op jit(solution)/shard_map/ppermute | solution.py:133
  37.9 3.0 %fusion.3 = bf16[128,2048]{1,0:T(8,128)(2,1)S(1)} fusion(f32[128,2048]{1,0:T(8,128)S(1)} %fusion.95, bf16[128,1024]{1,0:T(8,128)(2,1)S(1)} %bitcast.310, bf16[1024,2048]{1,0:T(8,128)(2,1)} %collective-permute-done.3), kind=kOutput, calls=%fused_computation.8 | convolution fusion | flops 537395200 | bytes 6029312 | tf_op jit(solution)/shard_map/dot_general | solution.py:11
  40.9 0.9 fusion.54
  41.8 1.3 collective-permute-done.6
  43.0 0.8 fusion.47
  43.8 5.1 %collective-permute-start.13 = (bf16[2,32,2048]{2,1,0:T(8,128)(2,1)}, bf16[2,32,2048]{2,1,0:T(8,128)(2,1)}, u32[]{:S(2)}, u32[]{:S(2)}) collective-permute-start(bf16[2,32,2048]{2,1,0:T(8,128)(2,1)} %get-tuple-element.22), channel_id=1, source_target_pairs={{0,8},{24,16},{1,9},{25,17},{2,10},{26,18},{3,11},{27,19},{4,12},{... | collective-permute-start | bytes 786440 | tf_op jit(solution)/shard_map/ppermute | solution.py:133
  49.0 1.1 pad_maximum_fusion
  50.1 0.8 slice.174
  51.4 0.8 constant_dynamic-slice_fusion.10
  52.2 2.6 %collective-permute-done.30 = bf16[128,128]{1,0:T(8,128)(2,1)S(1)} collective-permute-done((bf16[128,128]{1,0:T(8,128)(2,1)S(1)}, bf16[128,128]{1,0:T(8,128)(2,1)S(1)}, u32[]{:S(2)}, u32[]{:S(2)}) %collective-permute-start.30) | collective-permute-done | bytes 32800 | tf_op jit(solution)/shard_map/ppermute | solution.py:46
  54.8 0.8 constant_dynamic-slice_fusion.9
  55.6 1.0 concatenate.99
  56.6 1.0 concatenate.98
  58.3 1.5 collective-permute-start.4
  59.7 1.5 collective-permute-start.7
  62.0 3.2 %collective-permute-start.11 = (bf16[2,32,2048]{2,1,0:T(8,128)(2,1)}, bf16[2,32,2048]{2,1,0:T(8,128)(2,1)S(1)}, u32[]{:S(2)}, u32[]{:S(2)}) collective-permute-start(bf16[2,32,2048]{2,1,0:T(8,128)(2,1)} %get-tuple-element.23), channel_id=1, source_target_pairs={{0,8},{8,0},{16,24},{24,16},{1,9},{9,1},{17,25},{25,17},{2,10},{10... | collective-permute-start | bytes 786440 | tf_op jit(solution)/shard_map/ppermute | solution.py:137
  65.2 1.1 fusion.48
  66.4 6.3 %collective-permute-start.14 = (bf16[2,32,2048]{2,1,0:T(8,128)(2,1)S(1)}, bf16[2,32,2048]{2,1,0:T(8,128)(2,1)S(1)}, u32[]{:S(2)}, u32[]{:S(2)}) collective-permute-start(bf16[2,32,2048]{2,1,0:T(8,128)(2,1)S(1)} %fusion.48), channel_id=1, source_target_pairs={{0,16},{8,24},{16,0},{24,8},{1,17},{9,25},{17,1},{25,9},{2,18},{10... | collective-permute-start | bytes 786440 | tf_op jit(solution)/shard_map/ppermute | solution.py:49
  72.6 11.3 %collective-permute-done.7 = bf16[2,32,2048]{2,1,0:T(8,128)(2,1)S(1)} collective-permute-done((bf16[2,32,2048]{2,1,0:T(8,128)(2,1)}, bf16[2,32,2048]{2,1,0:T(8,128)(2,1)S(1)}, u32[]{:S(2)}, u32[]{:S(2)}) %collective-permute-start.7) | collective-permute-done | bytes 262176 | tf_op jit(solution)/shard_map/ppermute | solution.py:49
  84.1 1.6 collective-permute-start.8
  85.7 5.8 %collective-permute-done.14 = bf16[2,32,2048]{2,1,0:T(8,128)(2,1)S(1)} collective-permute-done((bf16[2,32,2048]{2,1,0:T(8,128)(2,1)S(1)}, bf16[2,32,2048]{2,1,0:T(8,128)(2,1)S(1)}, u32[]{:S(2)}, u32[]{:S(2)}) %collective-permute-start.14) | collective-permute-done | bytes 262176 | tf_op jit(solution)/shard_map/ppermute | solution.py:49
  91.6 1.6 collective-permute-start.15
  93.4 4.7 %collective-permute-done.15 = bf16[2,32,2048]{2,1,0:T(8,128)(2,1)S(1)} collective-permute-done((bf16[2,32,2048]{2,1,0:T(8,128)(2,1)S(1)}, bf16[2,32,2048]{2,1,0:T(8,128)(2,1)S(1)}, u32[]{:S(2)}, u32[]{:S(2)}) %collective-permute-start.15) | collective-permute-done | bytes 262176 | tf_op jit(solution)/shard_map/ppermute | solution.py:170
  99.4 1.5 collective-permute-start.16
  101.1 1.2 collective-permute-done.9
  103.4 0.8 collective-permute-start.19
  104.2 2.4 %collective-permute-start.18 = (bf16[2,32,2048]{2,1,0:T(8,128)(2,1)S(1)}, bf16[2,32,2048]{2,1,0:T(8,128)(2,1)S(1)}, u32[]{:S(2)}, u32[]{:S(2)}) collective-permute-start(bf16[2,32,2048]{2,1,0:T(8,128)(2,1)S(1)} %get-tuple-element.44), channel_id=1, source_target_pairs={{0,16},{8,24},{16,0},{24,8},{1,17},{9,25},{17,1},{25,9},{2,18},{10... | collective-permute-start | bytes 786440 | tf_op jit(solution)/shard_map/ppermute | solution.py:49
  107.9 4.2 %collective-permute-start.23 = (bf16[2,32,2048]{2,1,0:T(8,128)(2,1)S(1)}, bf16[2,32,2048]{2,1,0:T(8,128)(2,1)S(1)}, u32[]{:S(2)}, u32[]{:S(2)}) collective-permute-start(bf16[2,32,2048]{2,1,0:T(8,128)(2,1)S(1)} %get-tuple-element.43), channel_id=1, source_target_pairs={{0,16},{8,24},{16,0},{24,8},{1,17},{9,25},{17,1},{25,9},{2,18},{10... | collective-permute-start | bytes 786440 | tf_op jit(solution)/shard_map/ppermute | solution.py:49
  112.3 7.7 %collective-permute-start.22 = (bf16[2,32,2048]{2,1,0:T(8,128)(2,1)S(1)}, bf16[2,32,2048]{2,1,0:T(8,128)(2,1)S(1)}, u32[]{:S(2)}, u32[]{:S(2)}) collective-permute-start(bf16[2,32,2048]{2,1,0:T(8,128)(2,1)S(1)} %get-tuple-element.43), channel_id=1, source_target_pairs={{0,8},{8,0},{16,24},{24,16},{1,9},{9,1},{17,25},{25,17},{2,10},{10... | collective-permute-start | bytes 786440 | tf_op jit(solution)/shard_map/ppermute | solution.py:209
  120.0 8.0 %collective-permute-done.18 = bf16[2,32,2048]{2,1,0:T(8,128)(2,1)S(1)} collective-permute-done((bf16[2,32,2048]{2,1,0:T(8,128)(2,1)S(1)}, bf16[2,32,2048]{2,1,0:T(8,128)(2,1)S(1)}, u32[]{:S(2)}, u32[]{:S(2)}) %collective-permute-start.18) | collective-permute-done | bytes 262176 | tf_op jit(solution)/shard_map/ppermute | solution.py:49
  128.0 1.5 collective-permute-start.21
  129.5 1.3 collective-permute-start.20
  131.4 3.8 %collective-permute-done.23 = bf16[2,32,2048]{2,1,0:T(8,128)(2,1)S(1)} collective-permute-done((bf16[2,32,2048]{2,1,0:T(8,128)(2,1)S(1)}, bf16[2,32,2048]{2,1,0:T(8,128)(2,1)S(1)}, u32[]{:S(2)}, u32[]{:S(2)}) %collective-permute-start.23) | collective-permute-done | bytes 262176 | tf_op jit(solution)/shard_map/ppermute | solution.py:49
  135.2 1.5 collective-permute-start.25
  136.7 4.2 %collective-permute-done.20 = bf16[2,32,2048]{2,1,0:T(8,128)(2,1)S(1)} collective-permute-done((bf16[2,32,2048]{2,1,0:T(8,128)(2,1)S(1)}, bf16[2,32,2048]{2,1,0:T(8,128)(2,1)S(1)}, u32[]{:S(2)}, u32[]{:S(2)}) %collective-permute-start.20) | collective-permute-done | bytes 262176 | tf_op jit(solution)/shard_map/ppermute | solution.py:212
  141.1 1.5 fusion.38
  143.5 3.7 %fusion.5 = f32[128,1024]{1,0:T(8,128)S(1)} fusion(f32[128,1024]{1,0:T(8,128)S(1)} %fusion.117, f32[128,1024]{1,0:T(8,128)S(1)} %fusion.38, bf16[1024,2048]{1,0:T(8,128)(2,1)} %collective-permute-done.3, bf16[2,128,2048]{2,1,0:T(8,128)(2,1)S(1)} %pad_maximum_fusion.1), kind=kOutput, calls=%fused_computation.32 | convolution fusion | flops 537133056 | bytes 6291456 | tf_op jit(solution)/shard_map/dot_general | solution.py:11
  147.3 1.7 collective-permute-start.27
  149.2 1.5 fusion.34
  151.7 3.7 %fusion.4 = f32[128,1024]{1,0:T(8,128)S(1)} fusion(f32[128,1024]{1,0:T(8,128)S(1)} %fusion.118, f32[128,1024]{1,0:T(8,128)S(1)} %fusion.34, bf16[1024,2048]{1,0:T(8,128)(2,1)} %collective-permute-done.3, bf16[2,128,2048]{2,1,0:T(8,128)(2,1)S(1)} %pad_maximum_fusion.2), kind=kOutput, calls=%fused_computation.31 | convolution fusion | flops 537133056 | bytes 6291456 | tf_op jit(solution)/shard_map/dot_general | solution.py:11
  157.6 0.8 maximum_bitcast_fusion
  158.5 2.0 %collective-permute-done.26 = bf16[4,16,1024]{2,1,0:T(8,128)(2,1)S(1)} collective-permute-done((bf16[4,16,1024]{2,1,0:T(8,128)(2,1)S(1)}, bf16[4,16,1024]{2,1,0:T(8,128)(2,1)S(1)}, u32[]{:S(2)}, u32[]{:S(2)}) %collective-permute-start.26) | collective-permute-done | bytes 131104 | tf_op jit(solution)/shard_map/ppermute | solution.py:46
  160.7 2.3 %collective-permute-start.32 = (bf16[128,1024]{1,0:T(8,128)(2,1)S(1)}, bf16[128,1024]{1,0:T(8,128)(2,1)S(1)}, u32[]{:S(2)}, u32[]{:S(2)}) collective-permute-start(bf16[128,1024]{1,0:T(8,128)(2,1)S(1)} %add_convert_fusion), channel_id=1, source_target_pairs={{0,4},{2,6},{8,12},{10,14},{20,16},{22,18},{28,24},{30,26},{1,5},{... | collective-permute-start | bytes 786440 | tf_op jit(solution)/shard_map/ppermute | solution.py:303
  163.1 6.5 %collective-permute-done.32 = bf16[128,1024]{1,0:T(8,128)(2,1)S(1)} collective-permute-done((bf16[128,1024]{1,0:T(8,128)(2,1)S(1)}, bf16[128,1024]{1,0:T(8,128)(2,1)S(1)}, u32[]{:S(2)}, u32[]{:S(2)}) %collective-permute-start.32) | collective-permute-done | bytes 262176 | tf_op jit(solution)/shard_map/ppermute | solution.py:303
  170.6 1.0 dynamic_update_slice.46
  171.9 1.8 %dynamic_update_slice.47 = bf16[128,1024]{0,1:T(8,128)(2,1)S(1)} dynamic-update-slice(bf16[128,1024]{0,1:T(8,128)(2,1)S(1)} %dynamic_update_slice.46, bf16[64,1024]{0,1:T(8,128)(2,1)S(1)} %copy.23, s32[]{:T(128)S(6)} %select_n.349, s32[]{:T(128)} %constant.274.clone.1) | dynamic-update-slice | bytes 262148 | tf_op jit(solution)/shard_map/dynamic_update_slice | solution.py:315
  173.7 0.8 convert_bitcast_fusion
  174.8 1.1 maximum_convert_fusion
  (159 shorter events, 18.3 us)
Async XLA Ops:
  0.6 19.4 %copy-start.9 = (bf16[2,1,16,8192]{3,2,1,0:T(8,128)(2,1)S(1)}, bf16[2,1,16,8192]{3,2,1,0:T(8,128)(2,1)}, u32[]{:S(2)}) copy-start(bf16[2,1,16,8192]{3,2,1,0:T(8,128)(2,1)} %param.8) | copy-start | bytes 1572868
  0.6 19.4 %copy-start.8 = (bf16[2,1,16,8192]{3,2,1,0:T(8,128)(2,1)S(1)}, bf16[2,1,16,8192]{3,2,1,0:T(8,128)(2,1)}, u32[]{:S(2)}) copy-start(bf16[2,1,16,8192]{3,2,1,0:T(8,128)(2,1)} %param.9) | copy-start | bytes 1572868
  3.9 22.1 %all-to-all-start = ((bf16[4,32,2176]{2,1,0:T(8,128)(2,1)}), bf16[4,32,2176]{2,1,0:T(8,128)(2,1)S(1)}, u32[]{:S(2)}, u32[]{:S(2)}) async-start(bf16[4,32,2176]{2,1,0:T(8,128)(2,1)} %pad_maximum_fusion.3), calls=%async_computation | async-start | bytes 1114112 | tf_op jit(solution)/shard_map/all_to_all | solution.py:81
  10.2 19.7 %collective-permute-start.3 = (bf16[1024,2048]{1,0:T(8,128)(2,1)}, bf16[1024,2048]{1,0:T(8,128)(2,1)}, u32[]{:S(2)}, u32[]{:S(2)}) collective-permute-start(bf16[1024,2048]{1,0:T(8,128)(2,1)} %bitcast.294), channel_id=1, source_target_pairs={{0,2},{2,0},{4,6},{6,4},{1,3},{3,1},{5,7},{7,5},{8,10},{10,8},{12,... | collective-permute-start | bytes 12582920 | tf_op jit(solution)/shard_map/ppermute | solution.py:43
  11.2 6.4 %collective-permute-start = (bf16[4,1,16,1024]{3,2,1,0:T(8,128)(2,1)S(1)}, bf16[4,1,16,1024]{3,2,1,0:T(8,128)(2,1)S(1)}, u32[]{:S(2)}, u32[]{:S(2)}) collective-permute-start(bf16[4,1,16,1024]{3,2,1,0:T(8,128)(2,1)S(1)} %bitcast.333), channel_id=1, source_target_pairs={{0,4},{2,6},{4,0},{6,2},{1,5},{3,7},{5,1},{7,3},{8,12},{10,14},{12... | collective-permute-start | bytes 393224 | tf_op jit(solution)/shard_map/ppermute | solution.py:46
  12.8 7.2 %collective-permute-start.1 = (bf16[4,1,16,1024]{3,2,1,0:T(8,128)(2,1)S(1)}, bf16[4,1,16,1024]{3,2,1,0:T(8,128)(2,1)S(1)}, u32[]{:S(2)}, u32[]{:S(2)}) collective-permute-start(bf16[4,1,16,1024]{3,2,1,0:T(8,128)(2,1)S(1)} %bitcast.331), channel_id=1, source_target_pairs={{0,4},{2,6},{4,0},{6,2},{1,5},{3,7},{5,1},{7,3},{8,12},{10,14},{12... | collective-permute-start | bytes 393224 | tf_op jit(solution)/shard_map/ppermute | solution.py:46
  14.1 11.4 %copy-start.2 = (bf16[1,1,1024,128]{3,2,1,0:T(8,128)(2,1)S(1)}, bf16[1,1,1024,128]{3,2,1,0:T(8,128)(2,1)}, u32[]{:S(2)}) copy-start(bf16[1,1,1024,128]{3,2,1,0:T(8,128)(2,1)} %param.11) | copy-start | bytes 786436
  21.1 27.9 %collective-permute-start.2 = (bf16[2,2,2,16,2048]{4,3,1,2,0:T(8,128)(2,1)}, bf16[2,2,2,16,2048]{4,3,1,2,0:T(8,128)(2,1)}, u32[]{:S(2)}, u32[]{:S(2)}) collective-permute-start(bf16[2,2,2,16,2048]{4,3,1,2,0:T(8,128)(2,1)} %pad_maximum_fusion.4), channel_id=1, source_target_pairs={{0,4},{2,6},{4,0},{6,2},{1,5},{3,7},{5,1},{7,3},{8,12},{10,14},{12... | collective-permute-start | bytes 1572872 | tf_op jit(solution)/shard_map/ppermute | solution.py:46
  26.1 3.2 %copy-start.4 = (bf16[4,32,2176]{2,1,0:T(8,128)(2,1)}, bf16[4,32,2176]{2,1,0:T(8,128)(2,1)S(1)}, u32[]{:S(2)}) copy-start(bf16[4,32,2176]{2,1,0:T(8,128)(2,1)S(1)} %all-to-all-done) | copy-start | bytes 1671172
  26.1 2.4 %copy-start = (bf16[1,1024,2048]{2,1,0:T(8,128)(2,1)S(1)}, bf16[1,1024,2048]{2,1,0:T(8,128)(2,1)}, u32[]{:S(2)}) copy-start(bf16[1,1024,2048]{2,1,0:T(8,128)(2,1)} %param.10) | copy-start | bytes 12582916
  33.8 15.1 %copy-start.6 = (bf16[1,2,2,16,2048]{4,3,1,2,0:T(8,128)(2,1)S(1)}, bf16[1,2,2,16,2048]{4,3,1,2,0:T(8,128)(2,1)}, u32[]{:S(2)}) copy-start(bf16[1,2,2,16,2048]{4,3,1,2,0:T(8,128)(2,1)} %maximum_bitcast_fusion.2) | copy-start | bytes 786436
  33.8 15.1 %copy-start.7 = (bf16[1,2,2,16,2048]{4,3,1,2,0:T(8,128)(2,1)S(1)}, bf16[1,2,2,16,2048]{4,3,1,2,0:T(8,128)(2,1)}, u32[]{:S(2)}) copy-start(bf16[1,2,2,16,2048]{4,3,1,2,0:T(8,128)(2,1)} %maximum_bitcast_fusion.1) | copy-start | bytes 786436
  33.8 9.2 %collective-permute-start.6 = (bf16[2,32,2048]{2,1,0:T(8,128)(2,1)S(1)}, bf16[2,32,2048]{2,1,0:T(8,128)(2,1)S(1)}, u32[]{:S(2)}, u32[]{:S(2)}) collective-permute-start(bf16[2,32,2048]{2,1,0:T(8,128)(2,1)S(1)} %get-tuple-element.49), channel_id=1, source_target_pairs={{0,8},{24,16},{1,9},{25,17},{2,10},{26,18},{3,11},{27,19},{4,12},{... | collective-permute-start | bytes 786440 | tf_op jit(solution)/shard_map/ppermute | solution.py:133
  43.8 18.1 %collective-permute-start.13 = (bf16[2,32,2048]{2,1,0:T(8,128)(2,1)}, bf16[2,32,2048]{2,1,0:T(8,128)(2,1)}, u32[]{:S(2)}, u32[]{:S(2)}) collective-permute-start(bf16[2,32,2048]{2,1,0:T(8,128)(2,1)} %get-tuple-element.22), channel_id=1, source_target_pairs={{0,8},{24,16},{1,9},{25,17},{2,10},{26,18},{3,11},{27,19},{4,12},{... | collective-permute-start | bytes 786440 | tf_op jit(solution)/shard_map/ppermute | solution.py:133
  50.8 3.9 %collective-permute-start.30 = (bf16[128,128]{1,0:T(8,128)(2,1)S(1)}, bf16[128,128]{1,0:T(8,128)(2,1)S(1)}, u32[]{:S(2)}, u32[]{:S(2)}) collective-permute-start(bf16[128,128]{1,0:T(8,128)(2,1)S(1)} %bitcast.315), channel_id=1, source_target_pairs={{0,4},{2,6},{4,0},{6,2},{1,5},{3,7},{5,1},{7,3},{8,12},{10,14},{12... | collective-permute-start | bytes 98312 | tf_op jit(solution)/shard_map/ppermute | solution.py:46
  57.6 8.7 %collective-permute-start.5 = (bf16[2,32,2048]{2,1,0:T(8,128)(2,1)}, bf16[2,32,2048]{2,1,0:T(8,128)(2,1)S(1)}, u32[]{:S(2)}, u32[]{:S(2)}) collective-permute-start(bf16[2,32,2048]{2,1,0:T(8,128)(2,1)} %get-tuple-element.20), channel_id=1, source_target_pairs={{8,16},{16,8},{9,17},{17,9},{10,18},{18,10},{11,19},{19,11},{12,20... | collective-permute-start | bytes 786440 | tf_op jit(solution)/shard_map/ppermute | solution.py:134
  58.3 14.3 %collective-permute-start.4 = (bf16[2,32,2048]{2,1,0:T(8,128)(2,1)}, bf16[2,32,2048]{2,1,0:T(8,128)(2,1)S(1)}, u32[]{:S(2)}, u32[]{:S(2)}) collective-permute-start(bf16[2,32,2048]{2,1,0:T(8,128)(2,1)} %get-tuple-element.19), channel_id=1, source_target_pairs={{0,8},{8,0},{16,24},{24,16},{1,9},{9,1},{17,25},{25,17},{2,10},{10... | collective-permute-start | bytes 786440 | tf_op jit(solution)/shard_map/ppermute | solution.py:137
  59.7 24.2 %collective-permute-start.7 = (bf16[2,32,2048]{2,1,0:T(8,128)(2,1)}, bf16[2,32,2048]{2,1,0:T(8,128)(2,1)S(1)}, u32[]{:S(2)}, u32[]{:S(2)}) collective-permute-start(bf16[2,32,2048]{2,1,0:T(8,128)(2,1)} %fusion.47), channel_id=1, source_target_pairs={{0,16},{8,24},{16,0},{24,8},{1,17},{9,25},{17,1},{25,9},{2,18},{10... | collective-permute-start | bytes 786440 | tf_op jit(solution)/shard_map/ppermute | solution.py:49
  61.3 24.4 %collective-permute-start.12 = (bf16[2,32,2048]{2,1,0:T(8,128)(2,1)}, bf16[2,32,2048]{2,1,0:T(8,128)(2,1)S(1)}, u32[]{:S(2)}, u32[]{:S(2)}) collective-permute-start(bf16[2,32,2048]{2,1,0:T(8,128)(2,1)} %get-tuple-element.24), channel_id=1, source_target_pairs={{8,16},{16,8},{9,17},{17,9},{10,18},{18,10},{11,19},{19,11},{12,20... | collective-permute-start | bytes 786440 | tf_op jit(solution)/shard_map/ppermute | solution.py:134
  62.0 23.7 %collective-permute-start.11 = (bf16[2,32,2048]{2,1,0:T(8,128)(2,1)}, bf16[2,32,2048]{2,1,0:T(8,128)(2,1)S(1)}, u32[]{:S(2)}, u32[]{:S(2)}) collective-permute-start(bf16[2,32,2048]{2,1,0:T(8,128)(2,1)} %get-tuple-element.23), channel_id=1, source_target_pairs={{0,8},{8,0},{16,24},{24,16},{1,9},{9,1},{17,25},{25,17},{2,10},{10... | collective-permute-start | bytes 786440 | tf_op jit(solution)/shard_map/ppermute | solution.py:137
  66.4 25.2 %collective-permute-start.14 = (bf16[2,32,2048]{2,1,0:T(8,128)(2,1)S(1)}, bf16[2,32,2048]{2,1,0:T(8,128)(2,1)S(1)}, u32[]{:S(2)}, u32[]{:S(2)}) collective-permute-start(bf16[2,32,2048]{2,1,0:T(8,128)(2,1)S(1)} %fusion.48), channel_id=1, source_target_pairs={{0,16},{8,24},{16,0},{24,8},{1,17},{9,25},{17,1},{25,9},{2,18},{10... | collective-permute-start | bytes 786440 | tf_op jit(solution)/shard_map/ppermute | solution.py:49
  84.1 9.2 %collective-permute-start.8 = (bf16[2,32,2048]{2,1,0:T(8,128)(2,1)S(1)}, bf16[2,32,2048]{2,1,0:T(8,128)(2,1)S(1)}, u32[]{:S(2)}, u32[]{:S(2)}) collective-permute-start(bf16[2,32,2048]{2,1,0:T(8,128)(2,1)S(1)} %get-tuple-element.39), channel_id=1, source_target_pairs={{0,1},{1,0},{2,3},{3,2},{4,5},{5,4},{6,7},{7,6},{8,9},{9,8},{10,11... | collective-permute-start | bytes 786440 | tf_op jit(solution)/shard_map/ppermute | solution.py:170
  91.6 6.4 %collective-permute-start.15 = (bf16[2,32,2048]{2,1,0:T(8,128)(2,1)S(1)}, bf16[2,32,2048]{2,1,0:T(8,128)(2,1)S(1)}, u32[]{:S(2)}, u32[]{:S(2)}) collective-permute-start(bf16[2,32,2048]{2,1,0:T(8,128)(2,1)S(1)} %get-tuple-element.41), channel_id=1, source_target_pairs={{0,1},{1,0},{2,3},{3,2},{4,5},{5,4},{6,7},{7,6},{8,9},{9,8},{10,11... | collective-permute-start | bytes 786440 | tf_op jit(solution)/shard_map/ppermute | solution.py:170
  98.7 3.6 %collective-permute-start.9 = (f32[2,2,16]{2,1,0:T(2,128)S(1)}, f32[2,2,16]{2,1,0:T(2,128)S(1)}, u32[]{:S(2)}, u32[]{:S(2)}) collective-permute-start(f32[2,2,16]{2,1,0:T(2,128)S(1)} %pad_maximum_fusion.17), channel_id=1, source_target_pairs={{0,4},{2,6},{4,0},{6,2},{1,5},{3,7},{5,1},{7,3},{8,12},{10,14},{12... | collective-permute-start | bytes 776 | tf_op jit(solution)/shard_map/ppermute | solution.py:46
  99.4 3.6 %collective-permute-start.16 = (f32[2,2,16]{2,1,0:T(2,128)S(1)}, f32[2,2,16]{2,1,0:T(2,128)S(1)}, u32[]{:S(2)}, u32[]{:S(2)}) collective-permute-start(f32[2,2,16]{2,1,0:T(2,128)S(1)} %pad_maximum_fusion.19), channel_id=1, source_target_pairs={{0,4},{2,6},{4,0},{6,2},{1,5},{3,7},{5,1},{7,3},{8,12},{10,14},{12... | collective-permute-start | bytes 776 | tf_op jit(solution)/shard_map/ppermute | solution.py:46
  103.1 37.9 %copy-start.1 = (bf16[1,1024,2048]{2,1,0:T(8,128)(2,1)S(1)}, bf16[1,1024,2048]{2,1,0:T(8,128)(2,1)}, u32[]{:S(2)}) copy-start(bf16[1,1024,2048]{2,1,0:T(8,128)(2,1)} %param.10) | copy-start | bytes 12582916
  103.4 8.9 %collective-permute-start.19 = (bf16[2,32,2048]{2,1,0:T(8,128)(2,1)S(1)}, bf16[2,32,2048]{2,1,0:T(8,128)(2,1)S(1)}, u32[]{:S(2)}, u32[]{:S(2)}) collective-permute-start(bf16[2,32,2048]{2,1,0:T(8,128)(2,1)S(1)} %get-tuple-element.44), channel_id=1, source_target_pairs={{8,16},{16,8},{9,17},{17,9},{10,18},{18,10},{11,19},{19,11},{12,20... | collective-permute-start | bytes 786440 | tf_op jit(solution)/shard_map/ppermute | solution.py:210
  104.2 23.7 %collective-permute-start.18 = (bf16[2,32,2048]{2,1,0:T(8,128)(2,1)S(1)}, bf16[2,32,2048]{2,1,0:T(8,128)(2,1)S(1)}, u32[]{:S(2)}, u32[]{:S(2)}) collective-permute-start(bf16[2,32,2048]{2,1,0:T(8,128)(2,1)S(1)} %get-tuple-element.44), channel_id=1, source_target_pairs={{0,16},{8,24},{16,0},{24,8},{1,17},{9,25},{17,1},{25,9},{2,18},{10... | collective-permute-start | bytes 786440 | tf_op jit(solution)/shard_map/ppermute | solution.py:49
  106.7 22.8 %collective-permute-start.17 = (bf16[2,32,2048]{2,1,0:T(8,128)(2,1)S(1)}, bf16[2,32,2048]{2,1,0:T(8,128)(2,1)S(1)}, u32[]{:S(2)}, u32[]{:S(2)}) collective-permute-start(bf16[2,32,2048]{2,1,0:T(8,128)(2,1)S(1)} %get-tuple-element.44), channel_id=1, source_target_pairs={{0,8},{8,0},{16,24},{24,16},{1,9},{9,1},{17,25},{25,17},{2,10},{10... | collective-permute-start | bytes 786440 | tf_op jit(solution)/shard_map/ppermute | solution.py:209
  107.2 23.5 %collective-permute-start.24 = (bf16[2,32,2048]{2,1,0:T(8,128)(2,1)S(1)}, bf16[2,32,2048]{2,1,0:T(8,128)(2,1)S(1)}, u32[]{:S(2)}, u32[]{:S(2)}) collective-permute-start(bf16[2,32,2048]{2,1,0:T(8,128)(2,1)S(1)} %get-tuple-element.43), channel_id=1, source_target_pairs={{8,16},{16,8},{9,17},{17,9},{10,18},{18,10},{11,19},{19,11},{12,20... | collective-permute-start | bytes 786440 | tf_op jit(solution)/shard_map/ppermute | solution.py:210
  107.9 27.3 %collective-permute-start.23 = (bf16[2,32,2048]{2,1,0:T(8,128)(2,1)S(1)}, bf16[2,32,2048]{2,1,0:T(8,128)(2,1)S(1)}, u32[]{:S(2)}, u32[]{:S(2)}) collective-permute-start(bf16[2,32,2048]{2,1,0:T(8,128)(2,1)S(1)} %get-tuple-element.43), channel_id=1, source_target_pairs={{0,16},{8,24},{16,0},{24,8},{1,17},{9,25},{17,1},{25,9},{2,18},{10... | collective-permute-start | bytes 786440 | tf_op jit(solution)/shard_map/ppermute | solution.py:49
  112.3 22.9 %collective-permute-start.22 = (bf16[2,32,2048]{2,1,0:T(8,128)(2,1)S(1)}, bf16[2,32,2048]{2,1,0:T(8,128)(2,1)S(1)}, u32[]{:S(2)}, u32[]{:S(2)}) collective-permute-start(bf16[2,32,2048]{2,1,0:T(8,128)(2,1)S(1)} %get-tuple-element.43), channel_id=1, source_target_pairs={{0,8},{8,0},{16,24},{24,16},{1,9},{9,1},{17,25},{25,17},{2,10},{10... | collective-permute-start | bytes 786440 | tf_op jit(solution)/shard_map/ppermute | solution.py:209
  128.0 13.0 %collective-permute-start.21 = (bf16[2,16,2048]{2,1,0:T(8,128)(2,1)S(1)}, bf16[2,16,2048]{2,1,0:T(8,128)(2,1)S(1)}, u32[]{:S(2)}, u32[]{:S(2)}) collective-permute-start(bf16[2,16,2048]{2,1,0:T(8,128)(2,1)S(1)} %slice_bitcast_fusion.14), channel_id=1, source_target_pairs={{0,4},{2,6},{4,0},{6,2},{1,5},{3,7},{5,1},{7,3},{8,12},{10,14},{12... | collective-permute-start | bytes 393224 | tf_op jit(solution)/shard_map/ppermute | solution.py:46
  129.5 11.4 %collective-permute-start.20 = (bf16[2,32,2048]{2,1,0:T(8,128)(2,1)S(1)}, bf16[2,32,2048]{2,1,0:T(8,128)(2,1)S(1)}, u32[]{:S(2)}, u32[]{:S(2)}) collective-permute-start(bf16[2,32,2048]{2,1,0:T(8,128)(2,1)S(1)} %collective-permute-done.18), channel_id=1, source_target_pairs={{8,0},{16,24},{9,1},{17,25},{10,2},{18,26},{11,3},{19,27},{12,4},{... | collective-permute-start | bytes 786440 | tf_op jit(solution)/shard_map/ppermute | solution.py:212
  130.8 11.8 %copy-start.5 = (bf16[4,32,2176]{2,1,0:T(8,128)(2,1)S(1)}, bf16[4,32,2176]{2,1,0:T(8,128)(2,1)}, u32[]{:S(2)}) copy-start(bf16[4,32,2176]{2,1,0:T(8,128)(2,1)} %copy-done.4) | copy-start | bytes 1671172
  130.8 11.8 %collective-permute-start.10 = (bf16[2,16,2048]{2,1,0:T(8,128)(2,1)S(1)}, bf16[2,16,2048]{2,1,0:T(8,128)(2,1)S(1)}, u32[]{:S(2)}, u32[]{:S(2)}) collective-permute-start(bf16[2,16,2048]{2,1,0:T(8,128)(2,1)S(1)} %slice_bitcast_fusion.15), channel_id=1, source_target_pairs={{0,4},{2,6},{4,0},{6,2},{1,5},{3,7},{5,1},{7,3},{8,12},{10,14},{12... | collective-permute-start | bytes 393224 | tf_op jit(solution)/shard_map/ppermute | solution.py:46
  135.2 13.9 %collective-permute-start.25 = (bf16[2,32,2048]{2,1,0:T(8,128)(2,1)S(1)}, bf16[2,32,2048]{2,1,0:T(8,128)(2,1)S(1)}, u32[]{:S(2)}, u32[]{:S(2)}) collective-permute-start(bf16[2,32,2048]{2,1,0:T(8,128)(2,1)S(1)} %collective-permute-done.23), channel_id=1, source_target_pairs={{8,0},{16,24},{9,1},{17,25},{10,2},{18,26},{11,3},{19,27},{12,4},{... | collective-permute-start | bytes 786440 | tf_op jit(solution)/shard_map/ppermute | solution.py:212
  140.9 2.3 %copy-start.3 = (bf16[1024,32]{1,0:T(8,128)(2,1)S(1)}, bf16[1024,32]{1,0:T(8,128)(2,1)}, u32[]{:S(2)}) copy-start(bf16[1024,32]{1,0:T(8,128)(2,1)} %get-tuple-element.70) | copy-start | bytes 196612
  147.3 11.2 %collective-permute-start.27 = (bf16[4,16,1024]{2,1,0:T(8,128)(2,1)S(1)}, bf16[4,16,1024]{2,1,0:T(8,128)(2,1)S(1)}, u32[]{:S(2)}, u32[]{:S(2)}) collective-permute-start(bf16[4,16,1024]{2,1,0:T(8,128)(2,1)S(1)} %fusion.92), channel_id=1, source_target_pairs={{0,4},{2,6},{4,0},{6,2},{1,5},{3,7},{5,1},{7,3},{8,12},{10,14},{12... | collective-permute-start | bytes 393224 | tf_op jit(solution)/shard_map/ppermute | solution.py:46
  151.0 4.9 %copy-start.14 = (bf16[32,1024]{1,0:T(8,128)(2,1)S(1)}, bf16[32,1024]{1,0:T(8,128)(2,1)}, u32[]{:S(2)}) copy-start(bf16[32,1024]{1,0:T(8,128)(2,1)} %get-tuple-element.65) | copy-start | bytes 196612
  151.0 4.9 %copy-start.15 = (bf16[32,1024]{1,0:T(8,128)(2,1)S(1)}, bf16[32,1024]{1,0:T(8,128)(2,1)}, u32[]{:S(2)}) copy-start(bf16[32,1024]{1,0:T(8,128)(2,1)} %get-tuple-element.66) | copy-start | bytes 196612
  151.0 4.9 %copy-start.16 = (bf16[32,1024]{1,0:T(8,128)(2,1)S(1)}, bf16[32,1024]{1,0:T(8,128)(2,1)}, u32[]{:S(2)}) copy-start(bf16[32,1024]{1,0:T(8,128)(2,1)} %get-tuple-element.67) | copy-start | bytes 196612
  151.0 4.9 %copy-start.17 = (bf16[32,1024]{1,0:T(8,128)(2,1)S(1)}, bf16[32,1024]{1,0:T(8,128)(2,1)}, u32[]{:S(2)}) copy-start(bf16[32,1024]{1,0:T(8,128)(2,1)} %get-tuple-element.68) | copy-start | bytes 196612
  151.3 4.8 %copy-start.10 = (bf16[32,1024]{1,0:T(8,128)(2,1)S(1)}, bf16[32,1024]{1,0:T(8,128)(2,1)}, u32[]{:S(2)}) copy-start(bf16[32,1024]{1,0:T(8,128)(2,1)} %get-tuple-element.61) | copy-start | bytes 196612
  151.3 4.7 %copy-start.11 = (bf16[32,1024]{1,0:T(8,128)(2,1)S(1)}, bf16[32,1024]{1,0:T(8,128)(2,1)}, u32[]{:S(2)}) copy-start(bf16[32,1024]{1,0:T(8,128)(2,1)} %get-tuple-element.62) | copy-start | bytes 196612
  151.4 4.7 %copy-start.12 = (bf16[32,1024]{1,0:T(8,128)(2,1)S(1)}, bf16[32,1024]{1,0:T(8,128)(2,1)}, u32[]{:S(2)}) copy-start(bf16[32,1024]{1,0:T(8,128)(2,1)} %get-tuple-element.63) | copy-start | bytes 196612
  151.4 4.7 %copy-start.13 = (bf16[32,1024]{1,0:T(8,128)(2,1)S(1)}, bf16[32,1024]{1,0:T(8,128)(2,1)}, u32[]{:S(2)}) copy-start(bf16[32,1024]{1,0:T(8,128)(2,1)} %get-tuple-element.64) | copy-start | bytes 196612
  155.5 5.0 %collective-permute-start.26 = (bf16[4,16,1024]{2,1,0:T(8,128)(2,1)S(1)}, bf16[4,16,1024]{2,1,0:T(8,128)(2,1)S(1)}, u32[]{:S(2)}, u32[]{:S(2)}) collective-permute-start(bf16[4,16,1024]{2,1,0:T(8,128)(2,1)S(1)} %fusion.91), channel_id=1, source_target_pairs={{0,4},{2,6},{4,0},{6,2},{1,5},{3,7},{5,1},{7,3},{8,12},{10,14},{12... | collective-permute-start | bytes 393224 | tf_op jit(solution)/shard_map/ppermute | solution.py:46
  156.3 6.6 %collective-permute-start.28 = (f32[64,1024]{1,0:T(8,128)S(1)}, f32[64,1024]{1,0:T(8,128)S(1)}, u32[]{:S(2)}, u32[]{:S(2)}) collective-permute-start(f32[64,1024]{1,0:T(8,128)S(1)} %bitcast.324), channel_id=1, source_target_pairs={{0,2},{2,0},{4,6},{6,4},{1,3},{3,1},{5,7},{7,5},{8,10},{10,8},{12,... | collective-permute-start | bytes 786440 | tf_op jit(solution)/shard_map/ppermute | solution.py:43
  157.1 3.5 %collective-permute-start.31 = (f32[128,1024]{1,0:T(8,128)S(1)}, f32[128,1024]{1,0:T(8,128)S(1)}, u32[]{:S(2)}, u32[]{:S(2)}) collective-permute-start(f32[128,1024]{1,0:T(8,128)S(1)} %constant_dynamic-slice_fusion), channel_id=1, source_target_pairs={{0,2},{2,0},{4,6},{6,4},{1,3},{3,1},{5,7},{7,5},{8,10},{10,8},{12,... | collective-permute-start | bytes 1572872 | tf_op jit(solution)/shard_map/ppermute | solution.py:43
  160.7 8.9 %collective-permute-start.32 = (bf16[128,1024]{1,0:T(8,128)(2,1)S(1)}, bf16[128,1024]{1,0:T(8,128)(2,1)S(1)}, u32[]{:S(2)}, u32[]{:S(2)}) collective-permute-start(bf16[128,1024]{1,0:T(8,128)(2,1)S(1)} %add_convert_fusion), channel_id=1, source_target_pairs={{0,4},{2,6},{8,12},{10,14},{20,16},{22,18},{28,24},{30,26},{1,5},{... | collective-permute-start | bytes 786440 | tf_op jit(solution)/shard_map/ppermute | solution.py:303
  163.0 8.7 %collective-permute-start.29 = (bf16[64,1024]{1,0:T(8,128)(2,1)S(1)}, bf16[64,1024]{1,0:T(8,128)(2,1)S(1)}, u32[]{:S(2)}, u32[]{:S(2)}) collective-permute-start(bf16[64,1024]{1,0:T(8,128)(2,1)S(1)} %add_convert_fusion.3), channel_id=1, source_target_pairs={{0,4},{2,6},{4,0},{6,2},{1,5},{3,7},{5,1},{7,3},{8,12},{10,14},{12... | collective-permute-start | bytes 393224 | tf_op jit(solution)/shard_map/ppermute | solution.py:46
  169.6 5.0 %collective-permute-start.33 = (bf16[128,1024]{1,0:T(8,128)(2,1)S(1)}, bf16[128,1024]{1,0:T(8,128)(2,1)S(1)}, u32[]{:S(2)}, u32[]{:S(2)}) collective-permute-start(bf16[128,1024]{1,0:T(8,128)(2,1)S(1)} %broadcast_select_fusion), channel_id=1, source_target_pairs={{0,2},{2,0},{4,6},{6,4},{1,3},{3,1},{5,7},{7,5},{8,10},{10,8},{12,... | collective-permute-start | bytes 786440 | tf_op jit(solution)/shard_map/ppermute | solution.py:43

commit v3 on v2

--- a/solution.py
+++ b/solution.py
@@ -1,10 +1,15 @@
+import functools
+
 import jax
 import jax.numpy as jnp
 from jax import lax
+from jax.experimental import pallas as pl
+from jax.experimental.pallas import tpu as pltpu
 from jax.sharding import PartitionSpec as P
 
 F32 = jnp.float32
 BF16 = jnp.bfloat16
+VMEM = 24 * 2**20
 
 
 def dot(left_side, right_side, left_dim, right_dim):
@@ -28,7 +33,431 @@
     return lax.optimization_barrier((value, *others))[0]
 
 
+def piece_kernel(place, mixes, right, left, *refs):
+    pieces, turned = refs[:-1], refs[-1]
+    t, core = place[0], place[2]
+    sub = pieces[0].shape[0]
+    half = left.shape[1] // 2
+    turned[...] = jnp.dot(mixes[...], right[...], preferred_element_type=F32).T
+    for o, piece in enumerate(pieces):
+        at = pl.ds(pl.multiple_of((t ^ o) * sub, sub), sub)
+        piece[:, :half] = left[at, pl.ds(pl.multiple_of(core * half, half), half)]
+        piece[:, half:] = turned[at, :].astype(BF16)
+
+
+def cut_pieces(place, mixes, right, left):
+    rows = mixes.shape[0]
+    rank, width = left.shape
+    vmem = pl.BlockSpec(memory_space=pltpu.VMEM)
+    return pl.pallas_call(
+        piece_kernel,
+        in_specs=[pl.BlockSpec(memory_space=pltpu.SMEM)] + [vmem] * 3,
+        out_specs=[vmem] * 4,
+        out_shape=[jax.ShapeDtypeStruct((rank // 4, width // 2 + rows), BF16)] * 4,
+        scratch_shapes=[pltpu.VMEM((rank, rows), F32)],
+        compiler_params=pltpu.CompilerParams(vmem_limit_bytes=VMEM),
+    )(place, mixes, right, left)
+
+
+def project_kernel(place, own_mix, other_mix, w00, w01, w10, w11, right, own_half, other_half, *refs):
+    sums, (mix_rows, left_rows, inner) = refs[:-3], refs[-3:]
+    cuts = ((w00, w01), (w10, w11))
+    t, outer, core = place[0], place[1], place[2]
+    micro, shards = mix_rows.shape[0], 4
+    sub, half = own_half.shape[1:]
+    step = pl.program_id(0)
+    rows = sums[0].shape[1]
+    own_rows = rows // 2
+    size = shards * rows
+    depth, tile = w00.shape
+
+    @pl.when(step == 0)
+    def _():
+        for m in range(micro):
+            for r in range(shards):
+                at = pl.ds(pl.multiple_of((t ^ r) * own_rows, own_rows), own_rows)
+                for group, source in enumerate((own_mix, other_mix)):
+                    mix_rows[m, pl.ds(r * rows + group * own_rows, own_rows), :] = source[m, at, :]
+            inner[pl.ds(m * size, size), :] = jnp.dot(
+                mix_rows[m], right[...], preferred_element_type=F32
+            ).astype(BF16)
+        left_rows[...] = jnp.zeros_like(left_rows)
+        for slot in range(2):
+            part = core ^ slot
+            at = pl.ds(pl.multiple_of((2 * outer + part) * sub, sub), sub)
+            left_rows[slot, at, pl.ds(pl.multiple_of(core * half, half), half)] = own_half[part]
+            left_rows[slot, at, pl.ds(pl.multiple_of((1 - core) * half, half), half)] = other_half[part]
+
+    at = pl.ds(pl.multiple_of(step * tile, tile), tile)
+    lines = mix_rows[...].reshape(micro * size, -1)
+    for slot in range(2):
+        product = jnp.dot(inner[...], left_rows[slot, :, at], preferred_element_type=F32)
+        for i, weight in enumerate(cuts[slot]):
+            product += jnp.dot(
+                lines[:, i * depth : (i + 1) * depth], weight[...], preferred_element_type=F32
+            )
+        for i in range(micro * shards):
+            sums[i][slot] = product[i * rows : (i + 1) * rows].astype(BF16)
+
+
+def doubled(weights):
+    return [weights[0], weights[0], weights[1], weights[1]]
+
+
+def weight_specs(head_cols, tile):
+    return [
+        pl.BlockSpec((head_cols // 2, tile), lambda i: (0, i)),
+        pl.BlockSpec((head_cols // 2, tile), lambda i: (1, i)),
+    ] * 2
+
+
+def whole(*shape):
+    return pl.BlockSpec(shape, lambda i: (0,) * len(shape))
+
+
+def project(place, own_mix, other_mix, weights, right, own_half, other_half):
+    micro, tokens, head_cols = own_mix.shape
+    width = weights[0].shape[1]
+    rank = right.shape[1]
+    tile = 512
+    tiles = width // tile
+    rows = tokens // 2
+    size = 4 * rows
+    return pl.pallas_call(
+        project_kernel,
+        grid=(tiles,),
+        in_specs=[
+            pl.BlockSpec(memory_space=pltpu.SMEM),
+            whole(*own_mix.shape),
+            whole(*own_mix.shape),
+            *weight_specs(head_cols, tile),
+            whole(*right.shape),
+            whole(*own_half.shape),
+            whole(*own_half.shape),
+        ],
+        out_specs=[pl.BlockSpec((2, rows, tile), lambda i: (0, 0, i))] * (4 * micro)
+        + [whole(micro, size, head_cols), whole(2, rank, width)],
+        out_shape=[jax.ShapeDtypeStruct((2, rows, width), BF16)] * (4 * micro)
+        + [
+            jax.ShapeDtypeStruct((micro, size, head_cols), BF16),
+            jax.ShapeDtypeStruct((2, rank, width), BF16),
+        ],
+        scratch_shapes=[pltpu.VMEM((micro * size, rank), BF16)],
+        compiler_params=pltpu.CompilerParams(vmem_limit_bytes=VMEM),
+        cost_estimate=pl.CostEstimate(
+            flops=4 * micro * size * head_cols * width,
+            bytes_accessed=4 * head_cols * width,
+            transcendentals=0,
+        ),
+    )(place, own_mix, other_mix, *doubled(weights), right, own_half, other_half)
+
+
+def back_kernel(m, place, *refs):
+    pieces, refs = refs[:5], refs[5:]
+    cuts, refs = (refs[0:2], refs[2:4]), refs[4:]
+    left_rows, right, mix_rows, own_permuted, other_permuted = refs[:5]
+    earlier, refs = (refs[5:7], refs[7:]) if m else (None, refs[5:])
+    mix_here, mix_sent, left_sum, right_sum, total, inner_grad, turned, permuted, right_all = refs
+    t, outer, core = place[0], place[1], place[2]
+    step = pl.program_id(0)
+    steps = pl.num_programs(0)
+    rows = pieces[0].shape[1]
+    own_rows = rows // 2
+    tokens = 4 * own_rows
+    depth, tile = cuts[0][0].shape
+    half = left_sum.shape[2]
+
+    @pl.when(step == 0)
+    def _():
+        total[...] = jnp.zeros_like(total)
+        inner_grad[...] = jnp.zeros_like(inner_grad)
+        for group, source in enumerate((own_permuted, other_permuted)):
+            turned[group] = source[...].astype(F32).T
+        for r in range(4):
+            at = pl.ds(pl.multiple_of(m * tokens + (t ^ r) * own_rows, own_rows), own_rows)
+            for group in range(2):
+                permuted[pl.ds(r * rows + group * own_rows, own_rows), :] = turned[group, at, :]
+        permuted[...] = permuted[...].T
+
+    own, beside, opposite, mid, farthest = pieces
+    grads = [
+        jnp.concatenate(
+            [own[slot], beside[slot], opposite[slot], mid[slot] + farthest[slot]], axis=0
+        )
+        for slot in range(2)
+    ]
+    over = (((1,), (1,)), ((), ()))
+    for i in range(2):
+        total[pl.ds(i * depth, depth), :] += lax.dot_general(
+            cuts[0][i][...], grads[0], over, preferred_element_type=F32
+        ) + lax.dot_general(cuts[1][i][...], grads[1], over, preferred_element_type=F32)
+    inner_grad[...] += lax.dot_general(
+        grads[0], left_rows[0], over, preferred_element_type=F32
+    ) + lax.dot_general(grads[1], left_rows[1], over, preferred_element_type=F32)
+
+    at = step * tile
+    which = (at // half) ^ core
+    cut = pl.ds(pl.multiple_of(at % half, tile), tile)
+    block = jnp.where(((t & 1) ^ core) == 0, grads[0], grads[1])
+    product = jnp.dot(permuted[...].astype(BF16), block, preferred_element_type=F32)
+    if m:
+        product += earlier[0][which, :, cut]
+    left_sum[which, :, cut] = product
+
+    @pl.when(step == steps - 1)
+    def _():
+        mine = inner_grad[...].astype(BF16)
+        everything = total[...].T + lax.dot_general(
+            mine, right[...], (((1,), (1,)), ((), ())), preferred_element_type=F32
+        )
+        for r in range(4):
+            at = pl.ds(pl.multiple_of((t ^ r) * own_rows, own_rows), own_rows)
+            mix_here[at, :] = everything[r * rows : r * rows + own_rows]
+            mix_sent[at, :] = everything[r * rows + own_rows : (r + 1) * rows].astype(BF16)
+        right_all[...] = lax.dot_general(
+            mine, mix_rows[0], (((0,), (0,)), ((), ())), preferred_element_type=F32
+        )
+        count = right_sum.shape[0]
+        product = right_all[pl.ds(pl.multiple_of(outer * count, count), count), :]
+        if m:
+            product += earlier[1][...]
+        right_sum[...] = product
+
+
+def back(m, place, pieces, weights, left_rows, right, mix_rows, permuted, earlier):
+    _, rows, width = pieces[0].shape
+    head_cols, rank = right.shape
+    size = 4 * rows
+    tokens = size // 2
+    half = width // 2
+    tile = 512
+    tiles = width // tile
+    piece = pl.BlockSpec((2, rows, tile), lambda i: (0, 0, i))
+    shapes = [
+        jax.ShapeDtypeStruct((tokens, head_cols), F32),
+        jax.ShapeDtypeStruct((tokens, head_cols), BF16),
+        jax.ShapeDtypeStruct((2, rank, half), F32),
+        jax.ShapeDtypeStruct((rank // 2, head_cols), F32),
+    ]
+    return pl.pallas_call(
+        functools.partial(back_kernel, m),
+        grid=(tiles,),
+        in_specs=[pl.BlockSpec(memory_space=pltpu.SMEM)]
+        + [piece] * 5
+        + weight_specs(head_cols, tile)
+        + [
+            pl.BlockSpec((2, rank, tile), lambda i: (0, 0, i)),
+            whole(*right.shape),
+            pl.BlockSpec((1, size, head_cols), lambda i: (m, 0, 0)),
+            whole(*permuted[0].shape),
+            whole(*permuted[0].shape),
+        ]
+        + [whole(*value.shape) for value in earlier],
+        out_specs=[whole(*shape.shape) for shape in shapes],
+        out_shape=shapes,
+        scratch_shapes=[
+            pltpu.VMEM((head_cols, size), F32),
+            pltpu.VMEM((size, rank), F32),
+            pltpu.VMEM((2, *permuted[0].shape[::-1]), F32),
+            pltpu.VMEM((size, rank), F32),
+            pltpu.VMEM((rank, head_cols), F32),
+        ],
+        compiler_params=pltpu.CompilerParams(vmem_limit_bytes=VMEM),
+        cost_estimate=pl.CostEstimate(
+            flops=4 * size * head_cols * width,
+            bytes_accessed=4 * head_cols * width,
+            transcendentals=0,
+        ),
+    )(place, *pieces, *doubled(weights), left_rows, right, mix_rows, *permuted, *earlier)
+
+
+def finish_kernel(place, own_left, other_left, own_right, other_right, grad_left, grad_right, wide):
+    outer, core = place[1], place[2]
+    half = own_left.shape[1]
+    count = own_right.shape[0]
+    grad_left[:, pl.ds(pl.multiple_of(core * half, half), half)] = own_left[...].astype(F32)
+    grad_left[:, pl.ds(pl.multiple_of((1 - core) * half, half), half)] = other_left[...].astype(F32)
+    wide[pl.ds(pl.multiple_of(outer * count, count), count), :] = own_right[...].astype(F32)
+    wide[pl.ds(pl.multiple_of((1 - outer) * count, count), count), :] = other_right[...].astype(F32)
+    grad_right[...] = wide[...].T
+
+
+def finish(place, own_left, other_left, own_right, other_right):
+    rank, half = own_left.shape
+    head_cols = own_right.shape[1]
+    vmem = pl.BlockSpec(memory_space=pltpu.VMEM)
+    return pl.pallas_call(
+        finish_kernel,
+        in_specs=[pl.BlockSpec(memory_space=pltpu.SMEM)] + [vmem] * 4,
+        out_specs=[vmem] * 2,
+        out_shape=[
+            jax.ShapeDtypeStruct((rank, 2 * half), F32),
+            jax.ShapeDtypeStruct((head_cols, rank), F32),
+        ],
+        scratch_shapes=[pltpu.VMEM((rank, head_cols), F32)],
+        compiler_params=pltpu.CompilerParams(vmem_limit_bytes=VMEM),
+    )(place, own_left, other_left, own_right, other_right)
+
+
 def on_device(mix, hidden_in, cotangent, frozen_weight, right_factor, left_factor, norm_gain):
+    t = lax.axis_index("tensor")
+    d = lax.axis_index("dp")
+    section = lax.axis_index("pipe")
+    outer = d // 2
+    core = d % 2
+    place = jnp.stack([t, outer, core]).astype(jnp.int32)
+
+    def to_core(value):
+        return lax.ppermute(value, "dp", [(i, i ^ 1) for i in range(4)])
+
+    def to_outer(value):
+        return lax.ppermute(value, "dp", [(i, i ^ 2) for i in range(4)])
+
+    def along(value, *pairs):
+        return lax.ppermute(value, "tensor", pairs)
+
+    mixes = mix[0, :, 0]
+    micro, tokens, head_cols = mixes.shape
+    own_rows = tokens // 4
+    rows = 2 * own_rows
+    weight = frozen_weight[0]
+    right = right_factor[0, 0]
+    left = left_factor[0, 0]
+    rank, width = left.shape
+    sub = rank // 4
+    half = width // 2
+    features = 4 * width
+    slots = (d, d ^ 1)
+
+    other_mixes = to_outer(mixes)
+    weights = (weight, to_core(weight))
+    cut = cut_pieces(place, mixes.reshape(micro * tokens, head_cols), right, left)
+    met = [cut[0]] + [along(cut[o], *[(i, i ^ o) for i in range(4)]) for o in range(1, 4)]
+
+    def of_block(block, start, stop):
+        return lax.select_n(t ^ block, *[piece[:, start:stop] for piece in met])
+
+    own_half = jnp.stack([of_block(2 * outer + i, 0, half) for i in range(2)])
+    other_half = to_core(own_half)
+    own_permuted = jnp.concatenate(
+        [of_block(i, half, half + micro * tokens) for i in range(4)], axis=0
+    )
+
+    *partial, mix_rows, left_rows = project(
+        place, mixes, other_mixes, weights, right, own_half, other_half
+    )
+
+    totals = []
+    ahead = None
+    for m in range(micro):
+        own, next_one, two_away, last = partial[4 * m : 4 * m + 4]
+        if ahead is not None:
+            next_one = after(next_one, ahead)
+            last = after(last, ahead)
+        passed = along(last, (0, 1), (3, 2))
+        beside = along(next_one, *[(i, i ^ 1) for i in range(4)])
+        mid = along(last, (1, 2), (2, 1))
+        ahead = (two_away.astype(F32) + passed.astype(F32)).astype(BF16)
+        if m == 0:
+            ahead = after(ahead, beside, mid)
+        crossed = along(ahead, *[(i, i ^ 2) for i in range(4)])
+        totals.append((own, beside, mid, crossed))
+
+    hidden_late = after(hidden_in, partial[0])
+
+    def by_column(target):
+        cuts = [2 * target + core, 2 * target + (1 - core)]
+        return jnp.stack(
+            [
+                jnp.stack([columns(value[:, 0], part * width, width) for part in cuts])
+                for value in (hidden_late, cotangent)
+            ]
+        )
+
+    entering = jnp.concatenate([by_column(outer), to_outer(by_column(1 - outer))], axis=3)
+    gains = jnp.stack([columns(norm_gain, part * width, width) for part in slots]).astype(F32)
+    own_permuted = after(own_permuted, partial[0])
+    permuted = (own_permuted, to_outer(own_permuted))
+
+    grads = []
+    leaving = []
+    for m in range(micro):
+        own, beside, mid, crossed = totals[m]
+        if m:
+            crossed = after(crossed, grads[m - 1])
+        update = (
+            own.astype(F32) + beside.astype(F32) + mid.astype(F32) + crossed.astype(F32)
+        )
+        sent = update.astype(BF16)
+        other = lax.ppermute(sent, "pipe", [(0, 1), (1, 0)])
+        if m == 0:
+            other = after(other, ahead)
+        other = other.astype(F32)
+        first = entering[0, :, m].astype(F32) + jnp.where(section == 0, update, other)
+        first = first.astype(BF16)
+        second = (first.astype(F32) + jnp.where(section == 0, other, update)).astype(BF16)
+        leaving.append(jnp.where(section == 0, first, second))
+        final = second.astype(F32)
+        upstream = entering[1, :, m].astype(F32) * gains[:, None, :]
+        sums = jnp.stack(
+            [jnp.sum(final * final, axis=(0, 2)), jnp.sum(upstream * final, axis=(0, 2))]
+        ).reshape(2, 2, own_rows)
+        total = (sums + to_outer(sums)[:, ::-1]).reshape(2, rows) / features
+        scale = lax.rsqrt(total[0] + 1e-05)
+        shrink = scale * scale * total[1]
+        grads.append(
+            (scale[None, :, None] * (upstream - final * shrink[None, :, None])).astype(BF16)
+        )
+
+    sums = ()
+    mix_grads = []
+    relays = []
+    for m in range(micro):
+        opposite = along(grads[m], *[(i, i ^ 2) for i in range(4)])
+        beside = along(grads[m], *[(i, i ^ 1) for i in range(4)])
+        mid = along(grads[m], (1, 2), (2, 1))
+        relay = after(opposite, beside, mid, *sums)
+        farthest = along(relay, (1, 0), (2, 3))
+        relays.append(relay)
+        pieces = [after(grads[m], grads[-1]), beside, relay, mid, farthest]
+        mix_here, mix_sent, *sums = back(
+            m, place, pieces, weights, left_rows, right, mix_rows, permuted, sums
+        )
+        mix_grads.append((mix_here + to_outer(mix_sent).astype(F32)).astype(BF16))
+    grad_mix = jnp.stack(mix_grads).reshape(1, micro, 1, tokens, head_cols)
+
+    outs = []
+    for m in range(micro):
+        by_group = leaving[m].reshape(2, 2, own_rows, width)
+        arrived = to_outer(after(by_group[:, 1], grads[m]))
+        arrived = after(arrived, relays[-1])
+        row = jnp.zeros((own_rows, features), BF16)
+        for at, piece in ((outer, by_group[:, 0]), (1 - outer, arrived)):
+            for slot in range(2):
+                place_at = (2 * at + (core if slot == 0 else 1 - core)) * width
+                row = lax.dynamic_update_slice_in_dim(row, piece[slot], place_at, 1)
+        outs.append(row)
+    section_out = jnp.stack(outs).reshape(1, micro, 1, own_rows, features)
+
+    left_sum, right_sum = sums
+    half_sum = (left_sum[0] + to_core(left_sum[1])).astype(BF16)
+    pairs = [
+        (4 * i + 2 * (i // 2) + c, 4 * i + 2 * (1 - i // 2) + c) for i in range(4) for c in range(2)
+    ]
+    arrived = lax.ppermute(half_sum, ("tensor", "dp"), pairs)
+    best = jnp.where(outer == t // 2, half_sum, arrived)
+    own_right = (right_sum + to_core(right_sum)).astype(BF16)
+    grad_left, grad_right = finish(place, best, to_core(best), own_right, to_outer(own_right))
+
+    return (
+        section_out,
+        grad_mix,
+        grad_right.reshape(1, 1, head_cols, rank),
+        grad_left.reshape(1, 1, rank, width),
+    )
+
+
+def on_device_general(mix, hidden_in, cotangent, frozen_weight, right_factor, left_factor, norm_gain):
     blocks = lax.axis_size("tensor")
     parts = lax.axis_size("dp")
     sections = lax.axis_size("pipe")
@@ -119,31 +548,11 @@
         return pick(partial[m], index, 1)
 
     updates_here = []
-    arrived_last = None
     for m in range(micro):
         total = shard(m, t).astype(F32)
-        if blocks != 4:
-            for step in range(1, blocks):
-                total = total + to_block(shard(m, (t + step) % blocks), step).astype(F32)
-            updates_here.append(total)
-            continue
-        far = shard(m, jnp.where(t < 2, 3, 0))
-        if arrived_last is not None:
-            far = after(far, arrived_last)
-        passed = lax.ppermute(far, "tensor", [(0, 1), (3, 2)])
-        mid = lax.ppermute(
-            after(shard(m, jnp.where(t < 2, 2, 1)), far), "tensor", [(1, 2), (2, 1)]
-        )
-        beside = lax.ppermute(after(shard(m, t ^ 1), far), "tensor", [(i, i ^ 1) for i in range(4)])
-        middle = (t == 1) | (t == 2)
-        two_away = jnp.where(
-            middle, (far.astype(F32) + passed.astype(F32)).astype(BF16), shard(m, t ^ 2)
-        )
-        arrived_last = two_away
-        crossed = to_block(two_away, 2)
-        updates_here.append(
-            total + beside.astype(F32) + mid.astype(F32) + crossed.astype(F32)
-        )
+        for step in range(1, blocks):
+            total = total + to_block(shard(m, (t + step) % blocks), step).astype(F32)
+        updates_here.append(total)
 
     hidden_late = after(hidden_in, *taken)
 
@@ -196,26 +605,13 @@
             (scale[None, :, None] * (upstream - final * shrink[None, :, None])).astype(BF16)
         )
 
-    full = []
-    order = []
-    earlier = None
-    for m in range(micro):
-        if blocks != 4:
-            pieces_m = [grads[m]] + [to_block(grads[m], step) for step in range(1, blocks)]
-            full.append(jnp.concatenate(pieces_m, axis=1))
-            order.append([(t - step) % blocks for step in range(blocks)])
-            continue
-        opposite = to_block(grads[m], 2)
-        beside = lax.ppermute(grads[m], "tensor", [(i, i ^ 1) for i in range(4)])
-        mid = lax.ppermute(grads[m], "tensor", [(1, 2), (2, 1)])
-        relay = after(opposite, beside, mid)
-        farthest = lax.ppermute(relay, "tensor", [(1, 0), (2, 3)])
-        last = jnp.where((t == 1) | (t == 2), mid, farthest)
-        if earlier is not None:
-            full[-1] = after(full[-1], relay)
-        full.append(jnp.concatenate([grads[m], beside, opposite, last], axis=1))
-        order.append([t, t ^ 1, t ^ 2, t ^ 3])
-        earlier = relay
+    full = [
+        jnp.concatenate(
+            [grads[m]] + [to_block(grads[m], step) for step in range(1, blocks)], axis=1
+        )
+        for m in range(micro)
+    ]
+    order = [[(t - step) % blocks for step in range(blocks)]] * micro
 
     outs = []
     for m in range(micro):
@@ -281,7 +677,7 @@
         for step in range(1, outers):
             whole = whole + to_outer(partial_mix[:, step].astype(BF16), outers - step).astype(F32)
         whole = whole.astype(BF16)
-        back = [t ^ i for i in range(blocks)] if blocks == 4 else order[m]
+        back = order[m]
         mix_grads.append(
             jnp.concatenate([pick(whole, at) for at in back], axis=0)
         )
@@ -326,8 +722,9 @@
 
 
 def solution(mesh):
+    sizes = (mesh.shape["tensor"], mesh.shape["dp"], mesh.shape["pipe"])
     return jax.shard_map(
-        on_device,
+        on_device if sizes == (4, 4, 2) else on_device_general,
         mesh=mesh,
         in_specs=(
             P("pipe", None, "dp", None, "tensor"),

time: 177 us -> 155 us (0.88)
  matrix products: 23.8 us -> 0 us
  Pallas kernels: 0 us -> 20.6 us
  starting transfers between devices: 65.1 us -> 47.9 us
  other arithmetic: 14.7 us -> 11.1 us
  local copies, waits for them, and re-layouts: 14.9 us -> 18.3 us
    dot_general x25 -> x0, matrix products: 23.8 us -> none  [dot(): lax.dot_general(left_side, right_side, (((left_dim,), (right_dim,)), ((),...]
    pallas_call x0 -> x5, Pallas kernels: none -> 20.6 us  [the longest x2 11.8 us: back(): pl.pallas_call(functools.partial(back_kernel, m), grid=(tiles,), in_specs...]
    ppermute x33 -> x36, starting transfers between devices: 56.5 us -> 45.4 us  [the longest x19 30.4 us: along(): return lax.ppermute(value, 'tensor', pairs)]
    unnamed x36 -> x40, local copies, waits for them, and re-layouts: 1.22 us -> 8.08 us
    all_to_all x1 -> x0, starting transfers between devices: 6.32 us -> none  [on_device(): lax.all_to_all(jnp.concatenate([left.reshape(blocks, sub, block_cols), ow...]
    dynamic_slice x5 -> x1, local copies, waits for them, and re-layouts: 4.4 us -> 0.7 us  [columns(): return lax.dynamic_slice_in_dim(value, start, size, value.ndim - 1)]
    dynamic_update_slice x10 -> x8, local copies, waits for them, and re-layouts: 2.93 us -> 6.52 us  [on_device(): row = lax.dynamic_update_slice_in_dim(row, piece[slot], place_at, 1)]
    concatenate x8 -> x2, other arithmetic: 3.25 us -> 0.08 us  [the longest x1 0.07 us: on_device(): jnp.concatenate([by_column(outer), to_outer(by_column(1 - outer))], axis=3)]
  transfers between devices with their start and end apart: 35 -> 37, of which waited for: 15 -> 15; matrix products, arithmetic and copies ran while one was open for 26% -> 14% of each run, Pallas kernels for 0% -> 8%
where the time goes in v3:
time: 155 us; the launch traced here: 154 us
  waiting for transfers between devices  54.7 us (35%)
  starting transfers between devices  47.9 us (31%)
  Pallas kernels  20.6 us (13%)
  local copies, waits for them, and re-layouts  18.3 us (12%)
  other arithmetic  11.1 us (7%)
    ppermute x19, waiting for transfers between devices, along(): return lax.ppermute(value, 'tensor', pairs)  39.2 us
    ppermute x19, starting transfers between devices, along(): return lax.ppermute(value, 'tensor', pairs)  30.4 us
    pallas_call x2, Pallas kernels, back(): pl.pallas_call(functools.partial(back_kernel, m), grid=(tiles,), in_specs...  11.8 us
    ppermute x10, starting transfers between devices, to_outer(): return lax.ppermute(value, 'dp', [(i, i ^ 2) for i in range(4)])  10.6 us
    unnamed x40, local copies, waits for them, and re-layouts  8.08 us
    dynamic_update_slice x8, local copies, waits for them, and re-layouts, on_device(): row = lax.dynamic_update_slice_in_dim(row, piece[slot], place_at, 1)  6.52 us
    pallas_call x1, Pallas kernels, project(): pl.pallas_call(project_kernel, grid=(tiles,), in_specs=[pl.BlockSpec(memo...  6.04 us
    ppermute x2, waiting for transfers between devices, on_device(): other = lax.ppermute(sent, 'pipe', [(0, 1), (1, 0)])  5.11 us
  transfers between devices with their start and end apart: 37, of which 15 were waited for; matrix products, arithmetic and copies ran while one was open for 14% of the time, Pallas kernels for 8%

profile of v3, /device:TPU:0, one launch (start us, length us, event | category | flops | bytes accessed | tf_op | source)
XLA Modules:
  0.0 153.8 jit_solution(14569959619089616966)
XLA Ops:
  1.1 2.6 %collective-permute-start = (bf16[2,64,1024]{2,1,0:T(8,128)(2,1)}, bf16[2,64,1024]{2,1,0:T(8,128)(2,1)S(1)}, u32[]{:S(2)}, u32[]{:S(2)}) collective-permute-start(bf16[2,64,1024]{2,1,0:T(8,128)(2,1)} %bitcast.125), channel_id=1, source_target_pairs={{0,4},{2,6},{4,0},{6,2},{1,5},{3,7},{5,1},{7,3},{8,12},{10,14},{12... | collective-permute-start | bytes 786440 | tf_op jit(solution)/shard_map/ppermute | solution.py:314
  3.8 0.9 copy-done.2
  4.7 0.9 copy-done.4
  5.7 1.0 copy-done.6
  6.7 0.8 shard_map.102
  7.6 1.6 %collective-permute-start.2 = (bf16[32,1152]{1,0:T(8,128)(2,1)S(1)}, bf16[32,1152]{1,0:T(8,128)(2,1)S(1)}, u32[]{:S(2)}, u32[]{:S(2)}) collective-permute-start(bf16[32,1152]{1,0:T(8,128)(2,1)S(1)} %get-tuple-element.44), channel_id=1, source_target_pairs={{0,8},{8,0},{16,24},{24,16},{1,9},{9,1},{17,25},{25,17},{2,10},{10... | collective-permute-start | bytes 221192 | tf_op jit(solution)/shard_map/ppermute | solution.py:317
  9.2 2.6 %collective-permute-start.3 = (bf16[32,1152]{1,0:T(8,128)(2,1)S(1)}, bf16[32,1152]{1,0:T(8,128)(2,1)S(1)}, u32[]{:S(2)}, u32[]{:S(2)}) collective-permute-start(bf16[32,1152]{1,0:T(8,128)(2,1)S(1)} %get-tuple-element.45), channel_id=1, source_target_pairs={{0,16},{8,24},{16,0},{24,8},{1,17},{9,25},{17,1},{25,9},{2,18},{10... | collective-permute-start | bytes 221192 | tf_op jit(solution)/shard_map/ppermute | solution.py:317
  12.0 0.7 fusion.31
  12.9 5.2 %collective-permute-done.3 = bf16[32,1152]{1,0:T(8,128)(2,1)S(1)} collective-permute-done((bf16[32,1152]{1,0:T(8,128)(2,1)S(1)}, bf16[32,1152]{1,0:T(8,128)(2,1)S(1)}, u32[]{:S(2)}, u32[]{:S(2)}) %collective-permute-start.3) | collective-permute-done | bytes 73760 | tf_op jit(solution)/shard_map/ppermute | solution.py:317
  18.3 1.3 collective-permute-done.5.other_half
  19.6 2.2 %copy-done = bf16[1,1024,2048]{2,1,0:T(8,128)(2,1)S(1)} copy-done((bf16[1,1024,2048]{2,1,0:T(8,128)(2,1)S(1)}, bf16[1,1024,2048]{2,1,0:T(8,128)(2,1)}, u32[]{:S(2)}) %copy-start) | copy-done | bytes 4194328
  21.8 6.0 %shard_map.103 = (bf16[2,32,2048]{2,1,0:T(8,128)(2,1)S(1)}, bf16[2,32,2048]{2,1,0:T(8,128)(2,1)S(1)}, bf16[2,32,2048]{2,1,0:T(8,128)(2,1)S(1)}, bf16[2,32,2048]{...) custom-call(s32[3]{0:T(128)S(1)} %pad_add_fusion.place, ...), custom_call_target="tpu_custom_call" | custom-call | flops 2147483648 | bytes 8388608 | tf_op jit(solution)/shard_map/pallas_call | solution.py:126
  27.8 3.4 %collective-permute-start.9 = (bf16[2,32,2048]{2,1,0:T(8,128)(2,1)S(1)}, bf16[2,32,2048]{2,1,0:T(8,128)(2,1)S(1)}, u32[]{:S(2)}, u32[]{:S(2)}) collective-permute-start(bf16[2,32,2048]{2,1,0:T(8,128)(2,1)S(1)} %get-tuple-element.50), channel_id=1, source_target_pairs={{0,8},{24,16},{1,9},{25,17},{2,10},{26,18},{3,11},{27,19},{4,12},{... | collective-permute-start | bytes 786440 | tf_op jit(solution)/shard_map/ppermute | solution.py:317
  31.2 0.7 collective-permute-start.8
  32.5 2.1 %collective-permute-start.7 = (bf16[2,32,2048]{2,1,0:T(8,128)(2,1)S(1)}, bf16[2,32,2048]{2,1,0:T(8,128)(2,1)S(1)}, u32[]{:S(2)}, u32[]{:S(2)}) collective-permute-start(bf16[2,32,2048]{2,1,0:T(8,128)(2,1)S(1)} %get-tuple-element.49), channel_id=1, source_target_pairs={{0,8},{8,0},{16,24},{24,16},{1,9},{9,1},{17,25},{25,17},{2,10},{10... | collective-permute-start | bytes 786440 | tf_op jit(solution)/shard_map/ppermute | solution.py:317
  34.8 1.6 %collective-permute-start.6 = (bf16[2,2,2,16,2048]{4,3,1,2,0:T(8,128)(2,1)S(1)}, bf16[2,2,2,16,2048]{4,3,1,2,0:T(8,128)(2,1)S(1)}, u32[]{:S(2)}, u32[]{:S(2)}) collective-permute-start(bf16[2,2,2,16,2048]{4,3,1,2,0:T(8,128)(2,1)S(1)} %pad_maximum_fusion.1), channel_id=1, source_target_pairs={{0,4},{2,6},{4,0},{6,2},{1,5},{3,7},{5,1},{7,3},{8,12},{10,14},{12... | collective-permute-start | bytes 1572872 | tf_op jit(solution)/shard_map/ppermute | solution.py:314
  36.4 1.4 collective-permute-done.9
  37.9 4.8 %collective-permute-done.7 = bf16[2,32,2048]{2,1,0:T(8,128)(2,1)S(1)} collective-permute-done((bf16[2,32,2048]{2,1,0:T(8,128)(2,1)S(1)}, bf16[2,32,2048]{2,1,0:T(8,128)(2,1)S(1)}, u32[]{:S(2)}, u32[]{:S(2)}) %collective-permute-start.7) | collective-permute-done | bytes 262176 | tf_op jit(solution)/shard_map/ppermute | solution.py:317
  42.7 3.4 %collective-permute-start.10 = (bf16[2,32,2048]{2,1,0:T(8,128)(2,1)S(1)}, bf16[2,32,2048]{2,1,0:T(8,128)(2,1)S(1)}, u32[]{:S(2)}, u32[]{:S(2)}) collective-permute-start(bf16[2,32,2048]{2,1,0:T(8,128)(2,1)S(1)} %add_convert_fusion.1), channel_id=1, source_target_pairs={{0,16},{8,24},{16,0},{24,8},{1,17},{9,25},{17,1},{25,9},{2,18},{10... | collective-permute-start | bytes 786440 | tf_op jit(solution)/shard_map/ppermute | solution.py:317
  46.1 0.7 collective-permute-start.16
  46.8 3.7 %collective-permute-start.12 = (bf16[2,32,2048]{2,1,0:T(8,128)(2,1)S(1)}, bf16[2,32,2048]{2,1,0:T(8,128)(2,1)S(1)}, u32[]{:S(2)}, u32[]{:S(2)}) collective-permute-start(bf16[2,32,2048]{2,1,0:T(8,128)(2,1)S(1)} %get-tuple-element.55), channel_id=1, source_target_pairs={{0,8},{24,16},{1,9},{25,17},{2,10},{26,18},{3,11},{27,19},{4,12},{... | collective-permute-start | bytes 786440 | tf_op jit(solution)/shard_map/ppermute | solution.py:317
  50.7 8.1 %collective-permute-done.10 = bf16[2,32,2048]{2,1,0:T(8,128)(2,1)S(1)} collective-permute-done((bf16[2,32,2048]{2,1,0:T(8,128)(2,1)S(1)}, bf16[2,32,2048]{2,1,0:T(8,128)(2,1)S(1)}, u32[]{:S(2)}, u32[]{:S(2)}) %collective-permute-start.10) | collective-permute-done | bytes 262176 | tf_op jit(solution)/shard_map/ppermute | solution.py:317
  59.0 1.6 %collective-permute-start.11 = (bf16[2,32,2048]{2,1,0:T(8,128)(2,1)S(1)}, bf16[2,32,2048]{2,1,0:T(8,128)(2,1)S(1)}, u32[]{:S(2)}, u32[]{:S(2)}) collective-permute-start(bf16[2,32,2048]{2,1,0:T(8,128)(2,1)S(1)} %fusion.27), channel_id=1, source_target_pairs={{0,1},{1,0},{2,3},{3,2},{4,5},{5,4},{6,7},{7,6},{8,9},{9,8},{10,11... | collective-permute-start | bytes 786440 | tf_op jit(solution)/shard_map/ppermute | solution.py:392
  60.6 0.8 add_convert_fusion
  61.3 4.1 %collective-permute-done.11 = bf16[2,32,2048]{2,1,0:T(8,128)(2,1)S(1)} collective-permute-done((bf16[2,32,2048]{2,1,0:T(8,128)(2,1)S(1)}, bf16[2,32,2048]{2,1,0:T(8,128)(2,1)S(1)}, u32[]{:S(2)}, u32[]{:S(2)}) %collective-permute-start.11) | collective-permute-done | bytes 262176 | tf_op jit(solution)/shard_map/ppermute | solution.py:392
  65.7 0.7 slice_bitcast_fusion.6
  67.4 0.7 stack.126.clone.1
  68.1 1.5 fusion.24
  69.6 0.9 collective-permute-done.13
  70.7 1.3 fusion.12.refs_0_
  72.0 2.6 %collective-permute-done.17 = bf16[2,32,2048]{2,1,0:T(8,128)(2,1)} collective-permute-done((bf16[2,32,2048]{2,1,0:T(8,128)(2,1)}, bf16[2,32,2048]{2,1,0:T(8,128)(2,1)}, u32[]{:S(2)}, u32[]{:S(2)}) %collective-permute-start.17) | collective-permute-done | bytes 262176 | tf_op jit(solution)/shard_map/ppermute | solution.py:317
  74.5 1.2 fusion.28
  75.7 1.6 %collective-permute-start.18 = (bf16[2,32,2048]{2,1,0:T(8,128)(2,1)S(1)}, bf16[2,32,2048]{2,1,0:T(8,128)(2,1)S(1)}, u32[]{:S(2)}, u32[]{:S(2)}) collective-permute-start(bf16[2,32,2048]{2,1,0:T(8,128)(2,1)S(1)} %fusion.28), channel_id=1, source_target_pairs={{0,1},{1,0},{2,3},{3,2},{4,5},{5,4},{6,7},{7,6},{8,9},{9,8},{10,11... | collective-permute-start | bytes 786440 | tf_op jit(solution)/shard_map/ppermute | solution.py:392
  77.3 1.5 fusion.23
  78.7 0.8 collective-permute-start.25
  79.6 1.5 collective-permute-start.24
  81.1 0.7 collective-permute-start.23
  81.8 1.0 collective-permute-done.18
  82.8 1.5 fusion.14
  84.3 1.3 broadcast_select_fusion.1
  85.6 0.7 copy-done.13
  86.3 0.7 slice_bitcast_fusion.5
  87.7 0.9 fusion.22
  88.6 8.0 %collective-permute-done.24.refs_2_ = bf16[2,32,2048]{2,1,0:T(8,128)(2,1)S(1)} collective-permute-done((bf16[2,32,2048]{2,1,0:T(8,128)(2,1)S(1)}, bf16[2,32,2048]{2,1,0:T(8,128)(2,1)S(1)}, u32[]{:S(2)}, u32[]{:S(2)}) %collective-permute-start.24) | collective-permute-done | bytes 262176 | tf_op jit(solution)/shard_map/ppermute | solution.py:317
  96.6 1.3 collective-permute-start.26
  98.1 1.2 fusion.17.refs_0_
  99.3 0.7 collective-permute-start.22
  99.9 5.7 %collective-permute-start.21 = (bf16[2,32,2048]{2,1,0:T(8,128)(2,1)S(1)}, bf16[2,32,2048]{2,1,0:T(8,128)(2,1)S(1)}, u32[]{:S(2)}, u32[]{:S(2)}) collective-permute-start(bf16[2,32,2048]{2,1,0:T(8,128)(2,1)S(1)} %fusion.17.refs_0_), channel_id=1, source_target_pairs={{0,8},{8,0},{16,24},{24,16},{1,9},{9,1},{17,25},{25,17},{2,10},{10... | collective-permute-start | bytes 786440 | tf_op jit(solution)/shard_map/ppermute | solution.py:317
  106.2 1.5 fusion.21
  107.7 1.5 collective-permute-start.14
  109.1 2.2 %copy-done.1 = bf16[1,1024,2048]{2,1,0:T(8,128)(2,1)S(1)} copy-done((bf16[1,1024,2048]{2,1,0:T(8,128)(2,1)S(1)}, bf16[1,1024,2048]{2,1,0:T(8,128)(2,1)}, u32[]{:S(2)}) %copy-start.1) | copy-done | bytes 4194328
  111.3 5.9 %shard_map.104 = (f32[64,1024]{1,0:T(8,128)S(1)}, bf16[64,1024]{1,0:T(8,128)(2,1)S(1)}, f32[2,128,1024]{2,1,0:T(8,128)S(1)}, f32[64,1024]{1,0:T(8,128)S(1)}) custom-call(s32[3]{0:T(128)S(1)} %pad_add_fusion.place, bf16[2,32,2048]{2,1,0:T(8,128)(2,1)S(1)} %fusion.12.refs_0_, bf16[2,32,2048]{2,1,0:T(8,128)(2,1)S(1)} %collective-permute-done.23.refs_1_, ...), custom_call_target="tpu_custom_call" | custom-call | flops 1073741824 | bytes 8388608 | tf_op jit(solution)/shard_map/pallas_call | solution.py:242
  117.9 3.5 %collective-permute-done.20.refs_2_ = bf16[2,32,2048]{2,1,0:T(8,128)(2,1)S(1)} collective-permute-done((bf16[2,32,2048]{2,1,0:T(8,128)(2,1)S(1)}, bf16[2,32,2048]{2,1,0:T(8,128)(2,1)S(1)}, u32[]{:S(2)}, u32[]{:S(2)}) %collective-permute-start.20) | collective-permute-done | bytes 262176 | tf_op jit(solution)/shard_map/ppermute | solution.py:317
  121.4 1.3 collective-permute-start.30
  124.0 5.6 %collective-permute-done.30.refs_4_ = bf16[2,32,2048]{2,1,0:T(8,128)(2,1)S(1)} collective-permute-done((bf16[2,32,2048]{2,1,0:T(8,128)(2,1)S(1)}, bf16[2,32,2048]{2,1,0:T(8,128)(2,1)S(1)}, u32[]{:S(2)}, u32[]{:S(2)}) %collective-permute-start.30) | collective-permute-done | bytes 262176 | tf_op jit(solution)/shard_map/ppermute | solution.py:317
  129.6 5.9 %shard_map.105 = (f32[64,1024]{1,0:T(8,128)S(1)}, bf16[64,1024]{1,0:T(8,128)(2,1)S(1)}, f32[2,128,1024]{2,1,0:T(8,128)S(1)}, f32[64,1024]{1,0:T(8,128)S(1)}) custom-call(s32[3]{0:T(128)S(1)} %pad_add_fusion.place, bf16[2,32,2048]{2,1,0:T(8,128)(2,1)S(1)} %fusion.17.refs_0_, bf16[2,32,2048]{2,1,0:T(8,128)(2,1)S(1)} %collective-permute-done.21.refs_1_, ...), custom_call_target="tpu_custom_call" | custom-call | flops 1073741824 | bytes 8388608 | tf_op jit(solution)/shard_map/pallas_call | solution.py:242
  135.7 1.8 %maximum_bitcast_fusion = bf16[1,2,1,16,8192]{4,3,2,1,0:T(8,128)(2,1)} fusion(bf16[1,16,8192]{2,1,0:T(8,128)(2,1)S(1)} %slice_dynamic-update-slice_fusion, bf16[1,16,8192]{2,1,0:T(8,128)(2,1)} %slice_dynamic-update-slice_fusion.2), kind=kLoop, calls=%fused_computation.30 | loop fusion | flops 262144 | bytes 1048576 | tf_op jit(solution)/shard_map/reshape | solution.py:440
  138.0 2.5 %collective-permute-start.33 = (bf16[128,1024]{1,0:T(8,128)(2,1)S(1)}, bf16[128,1024]{1,0:T(8,128)(2,1)S(1)}, u32[]{:S(2)}, u32[]{:S(2)}) collective-permute-start(bf16[128,1024]{1,0:T(8,128)(2,1)S(1)} %fusion.18), channel_id=1, source_target_pairs={{0,4},{2,6},{8,12},{10,14},{20,16},{22,18},{28,24},{30,26},{1,5},{... | collective-permute-start | bytes 786440 | tf_op jit(solution)/shard_map/ppermute | solution.py:447
  140.7 2.1 %collective-permute-start.36 = (bf16[64,1024]{1,0:T(8,128)(2,1)S(1)}, bf16[64,1024]{1,0:T(8,128)(2,1)S(1)}, u32[]{:S(2)}, u32[]{:S(2)}) collective-permute-start(bf16[64,1024]{1,0:T(8,128)(2,1)S(1)} %add_convert_fusion.2.own_right), channel_id=1, source_target_pairs={{0,4},{2,6},{4,0},{6,2},{1,5},{3,7},{5,1},{7,3},{8,12},{10,14},{12... | collective-permute-start | bytes 393224 | tf_op jit(solution)/shard_map/ppermute | solution.py:314
  142.8 4.4 %collective-permute-done.33 = bf16[128,1024]{1,0:T(8,128)(2,1)S(1)} collective-permute-done((bf16[128,1024]{1,0:T(8,128)(2,1)S(1)}, bf16[128,1024]{1,0:T(8,128)(2,1)S(1)}, u32[]{:S(2)}, u32[]{:S(2)}) %collective-permute-start.33) | collective-permute-done | bytes 262176 | tf_op jit(solution)/shard_map/ppermute | solution.py:447
  147.3 2.7 %collective-permute-done.31 = bf16[64,1024]{1,0:T(8,128)(2,1)S(1)} collective-permute-done((bf16[64,1024]{1,0:T(8,128)(2,1)S(1)}, bf16[64,1024]{1,0:T(8,128)(2,1)S(1)}, u32[]{:S(2)}, u32[]{:S(2)}) %collective-permute-start.31) | collective-permute-done | bytes 131104 | tf_op jit(solution)/shard_map/ppermute | solution.py:314
  150.0 0.7 maximum_bitcast_fusion.5
  150.7 1.1 collective-permute-done.36.other_right
  151.9 1.9 %shard_map.106 = (f32[128,2048]{1,0:T(8,128)}, f32[1024,128]{1,0:T(8,128)}) custom-call(s32[3]{0:T(128)S(1)} %pad_add_fusion.place, bf16[128,1024]{1,0:T(8,128)(2,1)S(1)} %broadcast_select_fusion.own_left, bf16[128,1024]{1,0:T(8,128)(2,1)S(1)} %collective-permute-done.34.other_left, bf16[64,1024]{1,0:T(8,128)(2,1)S(1)} %add_convert_fusion.2.own_right, ...), custom_call_target="tpu_custom_call" | custom-call | tf_op jit(solution)/shard_map/pallas_call | solution.py:289
  (120 shorter events, 8.1 us)
Async XLA Ops:
  0.6 18.9 %collective-permute-start.1 = (bf16[1024,2048]{1,0:T(8,128)(2,1)}, bf16[1024,2048]{1,0:T(8,128)(2,1)}, u32[]{:S(2)}, u32[]{:S(2)}) collective-permute-start(bf16[1024,2048]{1,0:T(8,128)(2,1)} %bitcast.114), channel_id=1, source_target_pairs={{0,2},{2,0},{4,6},{6,4},{1,3},{3,1},{5,7},{7,5},{8,10},{10,8},{12,... | collective-permute-start | bytes 12582920 | tf_op jit(solution)/shard_map/ppermute | solution.py:311
  1.1 18.4 %collective-permute-start = (bf16[2,64,1024]{2,1,0:T(8,128)(2,1)}, bf16[2,64,1024]{2,1,0:T(8,128)(2,1)S(1)}, u32[]{:S(2)}, u32[]{:S(2)}) collective-permute-start(bf16[2,64,1024]{2,1,0:T(8,128)(2,1)} %bitcast.125), channel_id=1, source_target_pairs={{0,4},{2,6},{4,0},{6,2},{1,5},{3,7},{5,1},{7,3},{8,12},{10,14},{12... | collective-permute-start | bytes 786440 | tf_op jit(solution)/shard_map/ppermute | solution.py:314
  3.8 1.0 copy-start.2
  4.7 0.9 copy-start.4
  5.7 1.0 copy-start.6
  6.7 12.8 %copy-start.3 = (bf16[1,1,1024,128]{3,2,1,0:T(8,128)(2,1)S(1)}, bf16[1,1,1024,128]{3,2,1,0:T(8,128)(2,1)}, u32[]{:S(2)}) copy-start(bf16[1,1,1024,128]{3,2,1,0:T(8,128)(2,1)} %param.11) | copy-start | bytes 786436
  6.7 12.8 %copy-start.5 = (bf16[1,2,1,64,1024]{4,3,2,1,0:T(8,128)(2,1)S(1)}, bf16[1,2,1,64,1024]{4,3,2,1,0:T(8,128)(2,1)}, u32[]{:S(2)}) copy-start(bf16[1,2,1,64,1024]{4,3,2,1,0:T(8,128)(2,1)} %param.7) | copy-start | bytes 786436
  7.6 5.3 %collective-permute-start.2 = (bf16[32,1152]{1,0:T(8,128)(2,1)S(1)}, bf16[32,1152]{1,0:T(8,128)(2,1)S(1)}, u32[]{:S(2)}, u32[]{:S(2)}) collective-permute-start(bf16[32,1152]{1,0:T(8,128)(2,1)S(1)} %get-tuple-element.44), channel_id=1, source_target_pairs={{0,8},{8,0},{16,24},{24,16},{1,9},{9,1},{17,25},{25,17},{2,10},{10... | collective-permute-start | bytes 221192 | tf_op jit(solution)/shard_map/ppermute | solution.py:317
  9.2 8.9 %collective-permute-start.3 = (bf16[32,1152]{1,0:T(8,128)(2,1)S(1)}, bf16[32,1152]{1,0:T(8,128)(2,1)S(1)}, u32[]{:S(2)}, u32[]{:S(2)}) collective-permute-start(bf16[32,1152]{1,0:T(8,128)(2,1)S(1)} %get-tuple-element.45), channel_id=1, source_target_pairs={{0,16},{8,24},{16,0},{24,8},{1,17},{9,25},{17,1},{25,9},{2,18},{10... | collective-permute-start | bytes 221192 | tf_op jit(solution)/shard_map/ppermute | solution.py:317
  11.8 6.3 %collective-permute-start.4 = (bf16[32,1152]{1,0:T(8,128)(2,1)S(1)}, bf16[32,1152]{1,0:T(8,128)(2,1)S(1)}, u32[]{:S(2)}, u32[]{:S(2)}) collective-permute-start(bf16[32,1152]{1,0:T(8,128)(2,1)S(1)} %get-tuple-element.46), channel_id=1, source_target_pairs={{0,24},{8,16},{16,8},{24,0},{1,25},{9,17},{17,9},{25,1},{2,26},{10... | collective-permute-start | bytes 221192 | tf_op jit(solution)/shard_map/ppermute | solution.py:317
  18.1 1.4 collective-permute-start.5
  19.6 2.2 %copy-start = (bf16[1,1024,2048]{2,1,0:T(8,128)(2,1)S(1)}, bf16[1,1024,2048]{2,1,0:T(8,128)(2,1)}, u32[]{:S(2)}) copy-start(bf16[1,1024,2048]{2,1,0:T(8,128)(2,1)} %param.10) | copy-start | bytes 12582916
  21.8 12.8 %copy-start.17 = (bf16[2,1,16,8192]{3,2,1,0:T(8,128)(2,1)S(1)}, bf16[2,1,16,8192]{3,2,1,0:T(8,128)(2,1)}, u32[]{:S(2)}) copy-start(bf16[2,1,16,8192]{3,2,1,0:T(8,128)(2,1)} %param.9) | copy-start | bytes 1572868
  21.8 12.8 %copy-start.18 = (bf16[2,1,16,8192]{3,2,1,0:T(8,128)(2,1)S(1)}, bf16[2,1,16,8192]{3,2,1,0:T(8,128)(2,1)}, u32[]{:S(2)}) copy-start(bf16[2,1,16,8192]{3,2,1,0:T(8,128)(2,1)} %param.8) | copy-start | bytes 1572868
  27.8 10.0 %collective-permute-start.9 = (bf16[2,32,2048]{2,1,0:T(8,128)(2,1)S(1)}, bf16[2,32,2048]{2,1,0:T(8,128)(2,1)S(1)}, u32[]{:S(2)}, u32[]{:S(2)}) collective-permute-start(bf16[2,32,2048]{2,1,0:T(8,128)(2,1)S(1)} %get-tuple-element.50), channel_id=1, source_target_pairs={{0,8},{24,16},{1,9},{25,17},{2,10},{26,18},{3,11},{27,19},{4,12},{... | collective-permute-start | bytes 786440 | tf_op jit(solution)/shard_map/ppermute | solution.py:317
  31.2 11.5 %collective-permute-start.8 = (bf16[2,32,2048]{2,1,0:T(8,128)(2,1)S(1)}, bf16[2,32,2048]{2,1,0:T(8,128)(2,1)S(1)}, u32[]{:S(2)}, u32[]{:S(2)}) collective-permute-start(bf16[2,32,2048]{2,1,0:T(8,128)(2,1)S(1)} %get-tuple-element.50), channel_id=1, source_target_pairs={{8,16},{16,8},{9,17},{17,9},{10,18},{18,10},{11,19},{19,11},{12,20... | collective-permute-start | bytes 786440 | tf_op jit(solution)/shard_map/ppermute | solution.py:317
  31.9 73.8 %collective-permute-start.27 = (bf16[128,128]{1,0:T(8,128)(2,1)S(1)}, bf16[128,128]{1,0:T(8,128)(2,1)S(1)}, u32[]{:S(2)}, u32[]{:S(2)}) collective-permute-start(bf16[128,128]{1,0:T(8,128)(2,1)S(1)} %pad_maximum_fusion.3.refs_12_), channel_id=1, source_target_pairs={{0,4},{2,6},{4,0},{6,2},{1,5},{3,7},{5,1},{7,3},{8,12},{10,14},{12... | collective-permute-start | bytes 98312 | tf_op jit(solution)/shard_map/ppermute | solution.py:314
  32.5 10.2 %collective-permute-start.7 = (bf16[2,32,2048]{2,1,0:T(8,128)(2,1)S(1)}, bf16[2,32,2048]{2,1,0:T(8,128)(2,1)S(1)}, u32[]{:S(2)}, u32[]{:S(2)}) collective-permute-start(bf16[2,32,2048]{2,1,0:T(8,128)(2,1)S(1)} %get-tuple-element.49), channel_id=1, source_target_pairs={{0,8},{8,0},{16,24},{24,16},{1,9},{9,1},{17,25},{25,17},{2,10},{10... | collective-permute-start | bytes 786440 | tf_op jit(solution)/shard_map/ppermute | solution.py:317
  34.8 15.7 %collective-permute-start.6 = (bf16[2,2,2,16,2048]{4,3,1,2,0:T(8,128)(2,1)S(1)}, bf16[2,2,2,16,2048]{4,3,1,2,0:T(8,128)(2,1)S(1)}, u32[]{:S(2)}, u32[]{:S(2)}) collective-permute-start(bf16[2,2,2,16,2048]{4,3,1,2,0:T(8,128)(2,1)S(1)} %pad_maximum_fusion.1), channel_id=1, source_target_pairs={{0,4},{2,6},{4,0},{6,2},{1,5},{3,7},{5,1},{7,3},{8,12},{10,14},{12... | collective-permute-start | bytes 1572872 | tf_op jit(solution)/shard_map/ppermute | solution.py:314
  42.7 16.2 %collective-permute-start.10 = (bf16[2,32,2048]{2,1,0:T(8,128)(2,1)S(1)}, bf16[2,32,2048]{2,1,0:T(8,128)(2,1)S(1)}, u32[]{:S(2)}, u32[]{:S(2)}) collective-permute-start(bf16[2,32,2048]{2,1,0:T(8,128)(2,1)S(1)} %add_convert_fusion.1), channel_id=1, source_target_pairs={{0,16},{8,24},{16,0},{24,8},{1,17},{9,25},{17,1},{25,9},{2,18},{10... | collective-permute-start | bytes 786440 | tf_op jit(solution)/shard_map/ppermute | solution.py:317
  46.1 28.4 %collective-permute-start.16 = (bf16[2,32,2048]{2,1,0:T(8,128)(2,1)S(1)}, bf16[2,32,2048]{2,1,0:T(8,128)(2,1)S(1)}, u32[]{:S(2)}, u32[]{:S(2)}) collective-permute-start(bf16[2,32,2048]{2,1,0:T(8,128)(2,1)S(1)} %get-tuple-element.55), channel_id=1, source_target_pairs={{8,16},{16,8},{9,17},{17,9},{10,18},{18,10},{11,19},{19,11},{12,20... | collective-permute-start | bytes 786440 | tf_op jit(solution)/shard_map/ppermute | solution.py:317
  46.8 13.7 %collective-permute-start.12 = (bf16[2,32,2048]{2,1,0:T(8,128)(2,1)S(1)}, bf16[2,32,2048]{2,1,0:T(8,128)(2,1)S(1)}, u32[]{:S(2)}, u32[]{:S(2)}) collective-permute-start(bf16[2,32,2048]{2,1,0:T(8,128)(2,1)S(1)} %get-tuple-element.55), channel_id=1, source_target_pairs={{0,8},{24,16},{1,9},{25,17},{2,10},{26,18},{3,11},{27,19},{4,12},{... | collective-permute-start | bytes 786440 | tf_op jit(solution)/shard_map/ppermute | solution.py:317
  50.5 24.0 %collective-permute-start.15 = (bf16[2,32,2048]{2,1,0:T(8,128)(2,1)S(1)}, bf16[2,32,2048]{2,1,0:T(8,128)(2,1)S(1)}, u32[]{:S(2)}, u32[]{:S(2)}) collective-permute-start(bf16[2,32,2048]{2,1,0:T(8,128)(2,1)S(1)} %get-tuple-element.60), channel_id=1, source_target_pairs={{0,8},{8,0},{16,24},{24,16},{1,9},{9,1},{17,25},{25,17},{2,10},{10... | collective-permute-start | bytes 786440 | tf_op jit(solution)/shard_map/ppermute | solution.py:317
  50.7 15.7 %copy-start.7 = (bf16[2,2,2,32,2048]{4,3,1,2,0:T(8,128)(2,1)}, bf16[2,2,2,32,2048]{4,3,1,2,0:T(8,128)(2,1)S(1)}, u32[]{:S(2)}) copy-start(bf16[2,2,2,32,2048]{4,3,1,2,0:T(8,128)(2,1)S(1)} %pad_maximum_fusion) | copy-start | bytes 3145732
  59.0 6.4 %collective-permute-start.11 = (bf16[2,32,2048]{2,1,0:T(8,128)(2,1)S(1)}, bf16[2,32,2048]{2,1,0:T(8,128)(2,1)S(1)}, u32[]{:S(2)}, u32[]{:S(2)}) collective-permute-start(bf16[2,32,2048]{2,1,0:T(8,128)(2,1)S(1)} %fusion.27), channel_id=1, source_target_pairs={{0,1},{1,0},{2,3},{3,2},{4,5},{5,4},{6,7},{7,6},{8,9},{9,8},{10,11... | collective-permute-start | bytes 786440 | tf_op jit(solution)/shard_map/ppermute | solution.py:392
  61.3 13.2 %collective-permute-start.17 = (bf16[2,32,2048]{2,1,0:T(8,128)(2,1)}, bf16[2,32,2048]{2,1,0:T(8,128)(2,1)}, u32[]{:S(2)}, u32[]{:S(2)}) collective-permute-start(bf16[2,32,2048]{2,1,0:T(8,128)(2,1)} %add_convert_fusion), channel_id=1, source_target_pairs={{0,16},{8,24},{16,0},{24,8},{1,17},{9,25},{17,1},{25,9},{2,18},{10... | collective-permute-start | bytes 786440 | tf_op jit(solution)/shard_map/ppermute | solution.py:317
  65.7 1.0 copy-start.14
  65.7 5.0 %copy-start.12 = (bf16[2,32,2048]{2,1,0:T(8,128)(2,1)}, bf16[2,32,2048]{2,1,0:T(8,128)(2,1)S(1)}, u32[]{:S(2)}) copy-start(bf16[2,32,2048]{2,1,0:T(8,128)(2,1)S(1)} %get-tuple-element.91) | copy-start | bytes 786436
  66.9 3.6 %collective-permute-start.13 = (f32[2,2,16]{2,1,0:T(2,128)S(1)}, f32[2,2,16]{2,1,0:T(2,128)S(1)}, u32[]{:S(2)}, u32[]{:S(2)}) collective-permute-start(f32[2,2,16]{2,1,0:T(2,128)S(1)} %constant_dynamic-update-slice_fusion), channel_id=1, source_target_pairs={{0,4},{2,6},{4,0},{6,2},{1,5},{3,7},{5,1},{7,3},{8,12},{10,14},{12... | collective-permute-start | bytes 776 | tf_op jit(solution)/shard_map/ppermute | solution.py:314
  70.7 12.1 %copy-start.8 = (bf16[2,2,2,32,2048]{4,3,1,2,0:T(8,128)(2,1)S(1)}, bf16[2,2,2,32,2048]{4,3,1,2,0:T(8,128)(2,1)}, u32[]{:S(2)}) copy-start(bf16[2,2,2,32,2048]{4,3,1,2,0:T(8,128)(2,1)} %copy-done.7) | copy-start | bytes 3145732
  74.5 2.8 %copy-start.9 = (bf16[2,32,2048]{2,1,0:T(8,128)(2,1)}, bf16[2,32,2048]{2,1,0:T(8,128)(2,1)S(1)}, u32[]{:S(2)}) copy-start(bf16[2,32,2048]{2,1,0:T(8,128)(2,1)S(1)} %collective-permute-done.15) | copy-start | bytes 786436
  75.7 7.1 %collective-permute-start.18 = (bf16[2,32,2048]{2,1,0:T(8,128)(2,1)S(1)}, bf16[2,32,2048]{2,1,0:T(8,128)(2,1)S(1)}, u32[]{:S(2)}, u32[]{:S(2)}) collective-permute-start(bf16[2,32,2048]{2,1,0:T(8,128)(2,1)S(1)} %fusion.28), channel_id=1, source_target_pairs={{0,1},{1,0},{2,3},{3,2},{4,5},{5,4},{6,7},{7,6},{8,9},{9,8},{10,11... | collective-permute-start | bytes 786440 | tf_op jit(solution)/shard_map/ppermute | solution.py:392
  78.7 5.5 %copy-start.10 = (bf16[2,32,2048]{2,1,0:T(8,128)(2,1)S(1)}, bf16[2,32,2048]{2,1,0:T(8,128)(2,1)}, u32[]{:S(2)}) copy-start(bf16[2,32,2048]{2,1,0:T(8,128)(2,1)} %copy-done.9) | copy-start | bytes 786436
  78.7 9.8 %collective-permute-start.25 = (bf16[2,32,2048]{2,1,0:T(8,128)(2,1)S(1)}, bf16[2,32,2048]{2,1,0:T(8,128)(2,1)S(1)}, u32[]{:S(2)}, u32[]{:S(2)}) collective-permute-start(bf16[2,32,2048]{2,1,0:T(8,128)(2,1)S(1)} %fusion.12.refs_0_), channel_id=1, source_target_pairs={{8,16},{16,8},{9,17},{17,9},{10,18},{18,10},{11,19},{19,11},{12,20... | collective-permute-start | bytes 786440 | tf_op jit(solution)/shard_map/ppermute | solution.py:317
  79.6 17.0 %collective-permute-start.24 = (bf16[2,32,2048]{2,1,0:T(8,128)(2,1)S(1)}, bf16[2,32,2048]{2,1,0:T(8,128)(2,1)S(1)}, u32[]{:S(2)}, u32[]{:S(2)}) collective-permute-start(bf16[2,32,2048]{2,1,0:T(8,128)(2,1)S(1)} %fusion.12.refs_0_), channel_id=1, source_target_pairs={{0,16},{8,24},{16,0},{24,8},{1,17},{9,25},{17,1},{25,9},{2,18},{10... | collective-permute-start | bytes 786440 | tf_op jit(solution)/shard_map/ppermute | solution.py:317
  81.1 15.5 %collective-permute-start.23 = (bf16[2,32,2048]{2,1,0:T(8,128)(2,1)S(1)}, bf16[2,32,2048]{2,1,0:T(8,128)(2,1)S(1)}, u32[]{:S(2)}, u32[]{:S(2)}) collective-permute-start(bf16[2,32,2048]{2,1,0:T(8,128)(2,1)S(1)} %fusion.12.refs_0_), channel_id=1, source_target_pairs={{0,8},{8,0},{16,24},{24,16},{1,9},{9,1},{17,25},{25,17},{2,10},{10... | collective-permute-start | bytes 786440 | tf_op jit(solution)/shard_map/ppermute | solution.py:317
  84.3 1.3 copy-start.11
  85.6 0.7 copy-start.13
  87.2 10.7 %collective-permute-start.19 = (f32[2,2,16]{2,1,0:T(2,128)S(1)}, f32[2,2,16]{2,1,0:T(2,128)S(1)}, u32[]{:S(2)}, u32[]{:S(2)}) collective-permute-start(f32[2,2,16]{2,1,0:T(2,128)S(1)} %constant_dynamic-update-slice_fusion.2), channel_id=1, source_target_pairs={{0,4},{2,6},{4,0},{6,2},{1,5},{3,7},{5,1},{7,3},{8,12},{10,14},{12... | collective-permute-start | bytes 776 | tf_op jit(solution)/shard_map/ppermute | solution.py:314
  88.6 9.5 %copy-start.15 = (bf16[1,16,8192]{2,1,0:T(8,128)(2,1)}, bf16[1,16,8192]{2,1,0:T(8,128)(2,1)S(1)}, u32[]{:S(2)}) copy-start(bf16[1,16,8192]{2,1,0:T(8,128)(2,1)S(1)} %fusion.22) | copy-start | bytes 786436
  96.6 11.1 %collective-permute-start.26 = (bf16[2,32,2048]{2,1,0:T(8,128)(2,1)S(1)}, bf16[2,32,2048]{2,1,0:T(8,128)(2,1)S(1)}, u32[]{:S(2)}, u32[]{:S(2)}) collective-permute-start(bf16[2,32,2048]{2,1,0:T(8,128)(2,1)S(1)} %collective-permute-done.24.refs_2_), channel_id=1, source_target_pairs={{8,0},{16,24},{9,1},{17,25},{10,2},{18,26},{11,3},{19,27},{12,4},{... | collective-permute-start | bytes 786440 | tf_op jit(solution)/shard_map/ppermute | solution.py:317
  99.3 18.0 %collective-permute-start.22 = (bf16[2,32,2048]{2,1,0:T(8,128)(2,1)S(1)}, bf16[2,32,2048]{2,1,0:T(8,128)(2,1)S(1)}, u32[]{:S(2)}, u32[]{:S(2)}) collective-permute-start(bf16[2,32,2048]{2,1,0:T(8,128)(2,1)S(1)} %fusion.17.refs_0_), channel_id=1, source_target_pairs={{8,16},{16,8},{9,17},{17,9},{10,18},{18,10},{11,19},{19,11},{12,20... | collective-permute-start | bytes 786440 | tf_op jit(solution)/shard_map/ppermute | solution.py:317
  99.9 17.9 %collective-permute-start.21 = (bf16[2,32,2048]{2,1,0:T(8,128)(2,1)S(1)}, bf16[2,32,2048]{2,1,0:T(8,128)(2,1)S(1)}, u32[]{:S(2)}, u32[]{:S(2)}) collective-permute-start(bf16[2,32,2048]{2,1,0:T(8,128)(2,1)S(1)} %fusion.17.refs_0_), channel_id=1, source_target_pairs={{0,8},{8,0},{16,24},{24,16},{1,9},{9,1},{17,25},{25,17},{2,10},{10... | collective-permute-start | bytes 786440 | tf_op jit(solution)/shard_map/ppermute | solution.py:317
  105.6 15.7 %collective-permute-start.20 = (bf16[2,32,2048]{2,1,0:T(8,128)(2,1)S(1)}, bf16[2,32,2048]{2,1,0:T(8,128)(2,1)S(1)}, u32[]{:S(2)}, u32[]{:S(2)}) collective-permute-start(bf16[2,32,2048]{2,1,0:T(8,128)(2,1)S(1)} %fusion.17.refs_0_), channel_id=1, source_target_pairs={{0,16},{8,24},{16,0},{24,8},{1,17},{9,25},{17,1},{25,9},{2,18},{10... | collective-permute-start | bytes 786440 | tf_op jit(solution)/shard_map/ppermute | solution.py:317
  105.6 17.0 %collective-permute-start.28 = (bf16[2,16,2048]{2,1,0:T(8,128)(2,1)}, bf16[2,16,2048]{2,1,0:T(8,128)(2,1)S(1)}, u32[]{:S(2)}, u32[]{:S(2)}) collective-permute-start(bf16[2,16,2048]{2,1,0:T(8,128)(2,1)} %slice_bitcast_fusion.5), channel_id=1, source_target_pairs={{0,4},{2,6},{4,0},{6,2},{1,5},{3,7},{5,1},{7,3},{8,12},{10,14},{12... | collective-permute-start | bytes 393224 | tf_op jit(solution)/shard_map/ppermute | solution.py:314
  107.7 15.0 %collective-permute-start.14 = (bf16[2,16,2048]{2,1,0:T(8,128)(2,1)}, bf16[2,16,2048]{2,1,0:T(8,128)(2,1)S(1)}, u32[]{:S(2)}, u32[]{:S(2)}) collective-permute-start(bf16[2,16,2048]{2,1,0:T(8,128)(2,1)} %slice_bitcast_fusion.6), channel_id=1, source_target_pairs={{0,4},{2,6},{4,0},{6,2},{1,5},{3,7},{5,1},{7,3},{8,12},{10,14},{12... | collective-permute-start | bytes 393224 | tf_op jit(solution)/shard_map/ppermute | solution.py:314
  109.1 2.2 %copy-start.1 = (bf16[1,1024,2048]{2,1,0:T(8,128)(2,1)S(1)}, bf16[1,1024,2048]{2,1,0:T(8,128)(2,1)}, u32[]{:S(2)}) copy-start(bf16[1,1024,2048]{2,1,0:T(8,128)(2,1)} %param.10) | copy-start | bytes 12582916
  111.3 11.3 %copy-start.16 = (bf16[1,16,8192]{2,1,0:T(8,128)(2,1)S(1)}, bf16[1,16,8192]{2,1,0:T(8,128)(2,1)}, u32[]{:S(2)}) copy-start(bf16[1,16,8192]{2,1,0:T(8,128)(2,1)} %fusion.21) | copy-start | bytes 786436
  117.3 23.3 %collective-permute-start.29 = (bf16[64,1024]{1,0:T(8,128)(2,1)S(1)}, bf16[64,1024]{1,0:T(8,128)(2,1)S(1)}, u32[]{:S(2)}, u32[]{:S(2)}) collective-permute-start(bf16[64,1024]{1,0:T(8,128)(2,1)S(1)} %get-tuple-element.74), channel_id=1, source_target_pairs={{0,4},{2,6},{4,0},{6,2},{1,5},{3,7},{5,1},{7,3},{8,12},{10,14},{12... | collective-permute-start | bytes 393224 | tf_op jit(solution)/shard_map/ppermute | solution.py:314
  121.4 8.3 %collective-permute-start.30 = (bf16[2,32,2048]{2,1,0:T(8,128)(2,1)S(1)}, bf16[2,32,2048]{2,1,0:T(8,128)(2,1)S(1)}, u32[]{:S(2)}, u32[]{:S(2)}) collective-permute-start(bf16[2,32,2048]{2,1,0:T(8,128)(2,1)S(1)} %collective-permute-done.20.refs_2_), channel_id=1, source_target_pairs={{8,0},{16,24},{9,1},{17,25},{10,2},{18,26},{11,3},{19,27},{12,4},{... | collective-permute-start | bytes 786440 | tf_op jit(solution)/shard_map/ppermute | solution.py:317
  135.6 2.4 %collective-permute-start.32 = (f32[128,1024]{1,0:T(8,128)S(1)}, f32[128,1024]{1,0:T(8,128)S(1)}, u32[]{:S(2)}, u32[]{:S(2)}) collective-permute-start(f32[128,1024]{1,0:T(8,128)S(1)} %slice_bitcast_fusion), channel_id=1, source_target_pairs={{0,2},{2,0},{4,6},{6,4},{1,3},{3,1},{5,7},{7,5},{8,10},{10,8},{12,... | collective-permute-start | bytes 1572872 | tf_op jit(solution)/shard_map/ppermute | solution.py:311
  137.5 3.2 %collective-permute-start.35 = (f32[64,1024]{1,0:T(8,128)S(1)}, f32[64,1024]{1,0:T(8,128)S(1)}, u32[]{:S(2)}, u32[]{:S(2)}) collective-permute-start(f32[64,1024]{1,0:T(8,128)S(1)} %get-tuple-element.79), channel_id=1, source_target_pairs={{0,2},{2,0},{4,6},{6,4},{1,3},{3,1},{5,7},{7,5},{8,10},{10,8},{12,... | collective-permute-start | bytes 786440 | tf_op jit(solution)/shard_map/ppermute | solution.py:311
  138.0 9.1 %collective-permute-start.33 = (bf16[128,1024]{1,0:T(8,128)(2,1)S(1)}, bf16[128,1024]{1,0:T(8,128)(2,1)S(1)}, u32[]{:S(2)}, u32[]{:S(2)}) collective-permute-start(bf16[128,1024]{1,0:T(8,128)(2,1)S(1)} %fusion.18), channel_id=1, source_target_pairs={{0,4},{2,6},{8,12},{10,14},{20,16},{22,18},{28,24},{30,26},{1,5},{... | collective-permute-start | bytes 786440 | tf_op jit(solution)/shard_map/ppermute | solution.py:447
  140.6 9.4 %collective-permute-start.31 = (bf16[64,1024]{1,0:T(8,128)(2,1)S(1)}, bf16[64,1024]{1,0:T(8,128)(2,1)S(1)}, u32[]{:S(2)}, u32[]{:S(2)}) collective-permute-start(bf16[64,1024]{1,0:T(8,128)(2,1)S(1)} %get-tuple-element.77), channel_id=1, source_target_pairs={{0,4},{2,6},{4,0},{6,2},{1,5},{3,7},{5,1},{7,3},{8,12},{10,14},{12... | collective-permute-start | bytes 393224 | tf_op jit(solution)/shard_map/ppermute | solution.py:314
  140.7 11.2 %collective-permute-start.36 = (bf16[64,1024]{1,0:T(8,128)(2,1)S(1)}, bf16[64,1024]{1,0:T(8,128)(2,1)S(1)}, u32[]{:S(2)}, u32[]{:S(2)}) collective-permute-start(bf16[64,1024]{1,0:T(8,128)(2,1)S(1)} %add_convert_fusion.2.own_right), channel_id=1, source_target_pairs={{0,4},{2,6},{4,0},{6,2},{1,5},{3,7},{5,1},{7,3},{8,12},{10,14},{12... | collective-permute-start | bytes 393224 | tf_op jit(solution)/shard_map/ppermute | solution.py:314
  147.2 4.6 %collective-permute-start.34 = (bf16[128,1024]{1,0:T(8,128)(2,1)S(1)}, bf16[128,1024]{1,0:T(8,128)(2,1)S(1)}, u32[]{:S(2)}, u32[]{:S(2)}) collective-permute-start(bf16[128,1024]{1,0:T(8,128)(2,1)S(1)} %broadcast_select_fusion.own_left), channel_id=1, source_target_pairs={{0,2},{2,0},{4,6},{6,4},{1,3},{3,1},{5,7},{7,5},{8,10},{10,8},{12,... | collective-permute-start | bytes 786440 | tf_op jit(solution)/shard_map/ppermute | solution.py:311

commit v4 on v2

--- a/solution.py
+++ b/solution.py
@@ -1,10 +1,17 @@
+import functools
+
 import jax
 import jax.numpy as jnp
 from jax import lax
+from jax.experimental import pallas as pl
+from jax.experimental.pallas import tpu as pltpu
 from jax.sharding import PartitionSpec as P
 
 F32 = jnp.float32
 BF16 = jnp.bfloat16
+VMEM = 24 * 2**20
+VMEM_ALL = 48 * 2**20
+VMEM_SMALL = 10 * 2**20
 
 
 def dot(left_side, right_side, left_dim, right_dim):
@@ -28,7 +35,548 @@
     return lax.optimization_barrier((value, *others))[0]
 
 
+NO_COST = pl.CostEstimate(flops=0, bytes_accessed=0, transcendentals=0)
+
+
+def small(kernel, outs, scratch, place, *values):
+    vmem = pl.BlockSpec(memory_space=pltpu.VMEM)
+    return pl.pallas_call(
+        kernel,
+        in_specs=[pl.BlockSpec(memory_space=pltpu.SMEM)] + [vmem] * len(values),
+        out_specs=[vmem] * len(outs),
+        out_shape=[jax.ShapeDtypeStruct(shape, dtype) for shape, dtype in outs],
+        scratch_shapes=scratch,
+        compiler_params=pltpu.CompilerParams(vmem_limit_bytes=VMEM_SMALL),
+        cost_estimate=NO_COST,
+    )(place, *values)
+
+
+def at_multiple(index, size):
+    return pl.ds(pl.multiple_of(index * size, size), size)
+
+
+def cut_kernel(place, hidden, cotangent, here, there):
+    outer, core = place[1], place[2]
+    width = here.shape[4]
+    for out, target in ((here, outer), (there, 1 - outer)):
+        for which, source in enumerate((hidden, cotangent)):
+            for m in range(source.shape[0]):
+                for slot in range(2):
+                    out[which, m, slot] = source[m, :, at_multiple(2 * target + (core ^ slot), width)]
+
+
+def ahead_kernel(place, two_away, passed, ahead):
+    carried = ahead.shape[2] - two_away.shape[2]
+    width = two_away.shape[2] - carried
+    ahead[:, :, :width] = (
+        two_away[:, :, :width].astype(F32) + passed[:, :, :width].astype(F32)
+    ).astype(BF16)
+    if carried:
+        ahead[:, :, width : width + carried] = two_away[:, :, width:]
+        ahead[:, :, width + carried :] = passed[:, :, width:]
+
+
+def update_kernel(place, own, beside, *refs):
+    micro, _, _, width = own.shape
+    mids, crossings, (update, kept, sent) = refs[:micro], refs[micro : 2 * micro], refs[2 * micro :]
+    for m in range(micro):
+        total = (own[m].astype(F32) + beside[m, :, :, :width].astype(F32)) + (
+            mids[m][:, :, :width].astype(F32) + crossings[m][:, :, :width].astype(F32)
+        )
+        update[m] = total
+        (sent if m else kept)[...] = total.astype(BF16)
+
+
+def state_kernel(place, here, arrived, gain, update, other, leaving, final, sums):
+    outer, core, section = place[1], place[2], place[3]
+    own_rows, width = here.shape[3:]
+    for group, source in enumerate((here, arrived)):
+        at = pl.ds(group * own_rows, own_rows)
+        squares = jnp.zeros((own_rows, 1), F32)
+        products = jnp.zeros((own_rows, 1), F32)
+        for slot in range(2):
+            mine = update[0, slot, at, :]
+            others = other[slot, at, :].astype(F32)
+            first_add = jnp.where(section == 0, mine, others)
+            second_add = jnp.where(section == 0, others, mine)
+            first = (source[0, section, slot].astype(F32) + first_add).astype(BF16)
+            second = (first.astype(F32) + second_add).astype(BF16)
+            leaving[slot, at, :] = jnp.where(section == 0, first, second)
+            final[slot, at, :] = second
+            value = second.astype(F32)
+            upstream = source[1, section, slot].astype(F32) * gain[:, at_multiple(2 * outer + (core ^ slot), width)]
+            squares += jnp.sum(value * value, axis=1, keepdims=True)
+            products += jnp.sum(value * upstream, axis=1, keepdims=True)
+        lane = lax.broadcasted_iota(jnp.int32, (own_rows, sums.shape[1]), 1)
+        sums[at, :] = jnp.where(lane < sums.shape[1] // 2, squares, products)
+
+
+def later_kernel(place, here, arrived, update, before, leaving, own, sent):
+    section = place[3]
+    own_rows = here.shape[3]
+    for group, (source, out) in enumerate(((here, own), (arrived, sent))):
+        at = pl.ds(group * own_rows, own_rows)
+        for slot in range(2):
+            start = source[0, 1 - section, slot].astype(F32)
+            entering = (start + before[slot, at, :].astype(F32)).astype(BF16).astype(F32)
+            entering = jnp.where(section == 0, start, entering)
+            out[0, slot] = leaving[slot, at, :]
+            out[1, slot] = (entering + update[1, slot, at, :]).astype(BF16)
+
+
+def norm_kernel(place, here, arrived, gain, final, sums, other_sums, grad):
+    outer, core, section = place[1], place[2], place[3]
+    own_rows, width = here.shape[3:]
+    lanes = sums.shape[1]
+    for group, source in enumerate((here, arrived)):
+        at = pl.ds(group * own_rows, own_rows)
+        total = sums[at, :] + other_sums[pl.ds((1 - group) * own_rows, own_rows), :]
+        total = total * (1.0 / (4 * width))
+        scale = lax.rsqrt(total[:, :1] + 1e-05)
+        shrink = scale * scale * total[:, lanes // 2 : lanes // 2 + 1]
+        for slot in range(2):
+            upstream = source[1, section, slot].astype(F32) * gain[:, at_multiple(2 * outer + (core ^ slot), width)]
+            value = final[slot, at, :].astype(F32)
+            grad[slot, at, :] = (scale * (upstream - value * shrink)).astype(BF16)
+
+
+def join_kernel(place, mid, farthest, last):
+    last[...] = mid[...] + farthest[...]
+
+
+def project_kernel(place, own_mix, other_mix, w00, w01, w10, w11, right, own_half, other_half, *refs):
+    own, next_one, *sums, mix_rows, left_rows, piece, inner, turned = refs
+    cuts = ((w00, w01), (w10, w11))
+    t, outer, core, section = place[0], place[1], place[2], place[3]
+    micro, shards = mix_rows.shape[0], 4
+    sub, half = own_half.shape[1:]
+    step = pl.program_id(0)
+    rows = own.shape[2]
+    own_rows = rows // 2
+    size = shards * rows
+    depth, tile = w00.shape
+
+    @pl.when(step == 0)
+    def _():
+        for m in range(micro):
+            for r in range(shards):
+                at = pl.ds(pl.multiple_of((t ^ r) * own_rows, own_rows), own_rows)
+                for group, source in enumerate((own_mix, other_mix)):
+                    mix_rows[m, pl.ds(r * rows + group * own_rows, own_rows), :] = source[m ^ section, at, :]
+        product = jnp.dot(
+            mix_rows[...].reshape(micro * size, -1), right[...], preferred_element_type=F32
+        )
+        inner[...] = product.astype(BF16)
+        width = left_rows.shape[2]
+        for o in range(shards):
+            lines = [
+                product[m * size + (r ^ o) * rows :][:rows] for m in range(micro) for r in range(shards)
+            ]
+            turned[...] = jnp.concatenate(lines, axis=0).T
+            cut = turned[at_multiple(t ^ o, sub), :].astype(BF16)
+            for m in range(micro):
+                beside = cut[:, m * size : (m + 1) * size]
+                if o == 0:
+                    piece[m] = beside
+                elif o == 1:
+                    next_one[0, m, :, pl.ds(width, size)] = beside
+                    next_one[1, m, :, pl.ds(width, size)] = jnp.zeros_like(beside)
+                else:
+                    sums[(o - 2) * micro][m, :, pl.ds(width, size)] = beside
+        left_rows[...] = jnp.zeros_like(left_rows)
+        for slot in range(2):
+            part = core ^ slot
+            at = pl.ds(pl.multiple_of((2 * outer + part) * sub, sub), sub)
+            left_rows[slot, at, pl.ds(pl.multiple_of(core * half, half), half)] = own_half[part]
+            left_rows[slot, at, pl.ds(pl.multiple_of((1 - core) * half, half), half)] = other_half[part]
+
+    at = pl.ds(pl.multiple_of(step * tile, tile), tile)
+    lines = mix_rows[...].reshape(micro * size, -1)
+    for slot in range(2):
+        product = jnp.dot(inner[...], left_rows[slot, :, at], preferred_element_type=F32)
+        for i, weight in enumerate(cuts[slot]):
+            product += jnp.dot(
+                lines[:, i * depth : (i + 1) * depth], weight[...], preferred_element_type=F32
+            )
+        for m in range(micro):
+            for r in range(shards):
+                at_row = m * size + r * rows
+                value = product[at_row : at_row + rows].astype(BF16)
+                if r == 0:
+                    own[m, slot] = value
+                elif r == 1:
+                    next_one[m, slot, :, at] = value
+                else:
+                    sums[(r - 2) * micro + m][slot, :, at] = value
+
+
+def doubled(weights):
+    return [weights[0], weights[0], weights[1], weights[1]]
+
+
+def weight_specs(head_cols, tile):
+    return [
+        pl.BlockSpec((head_cols // 2, tile), lambda i: (0, i)),
+        pl.BlockSpec((head_cols // 2, tile), lambda i: (1, i)),
+    ] * 2
+
+
+def whole(*shape):
+    return pl.BlockSpec(shape, lambda i: (0,) * len(shape))
+
+
+def project(place, own_mix, other_mix, weights, right, own_half, other_half):
+    micro, tokens, head_cols = own_mix.shape
+    width = weights[0].shape[1]
+    rank = right.shape[1]
+    tile = 512
+    tiles = width // tile
+    rows = tokens // 2
+    size = 4 * rows
+    carrying = (2, rows, width + size)
+    plain = (2, rows, width)
+    shapes = [(micro, *carrying)] + [carrying, *[plain] * (micro - 1)] * 2
+    shapes += [(micro, size, head_cols), (2, rank, width), (2, rank // 4, size)]
+    return pl.pallas_call(
+        project_kernel,
+        grid=(tiles,),
+        in_specs=[
+            pl.BlockSpec(memory_space=pltpu.SMEM),
+            whole(*own_mix.shape),
+            whole(*own_mix.shape),
+            *weight_specs(head_cols, tile),
+            whole(*right.shape),
+            whole(*own_half.shape),
+            whole(*own_half.shape),
+        ],
+        out_specs=[pl.BlockSpec((micro, 2, rows, tile), lambda i: (0, 0, 0, i))]
+        + [whole(*shape) for shape in shapes],
+        out_shape=[jax.ShapeDtypeStruct((micro, 2, rows, width), BF16)]
+        + [jax.ShapeDtypeStruct(shape, BF16) for shape in shapes],
+        scratch_shapes=[
+            pltpu.VMEM((micro * size, rank), BF16),
+            pltpu.VMEM((rank, micro * size), F32),
+        ],
+        compiler_params=pltpu.CompilerParams(vmem_limit_bytes=VMEM_ALL),
+        cost_estimate=NO_COST,
+    )(place, own_mix, other_mix, *doubled(weights), right, own_half, other_half)
+
+
+def back_kernel(micro, place, *refs):
+    pieces, refs = refs[: 4 * micro], refs[4 * micro :]
+    cuts, refs = (refs[0:2], refs[2:4]), refs[4:]
+    left_rows, right, mix_rows = refs[:3]
+    (own_piece, beside_piece, crossed_piece, relayed_piece, mid_piece), refs = refs[3:8], refs[8:]
+    mix_here, mix_sent, *factors, total, inner_grad, permuted, right_all = refs
+    rank = permuted.shape[0]
+    t, outer, core, section = place[0], place[1], place[2], place[3]
+    step = pl.program_id(0)
+    rows = pieces[0].shape[1]
+    own_rows = rows // 2
+    depth, tile = cuts[0][0].shape
+    half = factors[0].shape[1]
+
+    @pl.when(step == 0)
+    def _():
+        total[...] = jnp.zeros_like(total)
+        inner_grad[...] = jnp.zeros_like(inner_grad)
+        _, sub, size = own_piece.shape
+        for m in range(micro):
+            cut = pl.ds(m * size, size)
+            last = mid_piece[m] + relayed_piece[m]
+            for o, value in enumerate((own_piece[m], beside_piece[0, m], crossed_piece[m], last)):
+                permuted[at_multiple(t ^ o, sub), cut] = value
+
+    grads = []
+    for slot in range(2):
+        parts = []
+        for m in range(micro):
+            parts += [piece[slot] for piece in pieces[4 * m : 4 * m + 4]]
+        grads.append(jnp.concatenate(parts, axis=0))
+    over = (((1,), (1,)), ((), ()))
+    for i in range(2):
+        total[pl.ds(i * depth, depth), :] += lax.dot_general(
+            cuts[0][i][...], grads[0], over, preferred_element_type=F32
+        ) + lax.dot_general(cuts[1][i][...], grads[1], over, preferred_element_type=F32)
+    inner_grad[...] += lax.dot_general(
+        grads[0], left_rows[0], over, preferred_element_type=F32
+    ) + lax.dot_general(grads[1], left_rows[1], over, preferred_element_type=F32)
+
+    at = step * tile
+    cut = pl.ds(pl.multiple_of(at % half, tile), tile)
+    block = jnp.where(((t & 1) ^ core) == 0, grads[0], grads[1])
+    product = jnp.dot(permuted[...], block, preferred_element_type=F32)
+    for i, factor in enumerate(factors):
+
+        @pl.when((at // half) ^ core == i)
+        def _():
+            factor[:rank, cut] = product
+
+
+    @pl.when(step == pl.num_programs(0) - 1)
+    def _():
+        mine = inner_grad[...].astype(BF16)
+        everything = total[...].T + lax.dot_general(
+            mine, right[...], over, preferred_element_type=F32
+        )
+        for m in range(micro):
+            for r in range(4):
+                at = at_multiple(t ^ r, own_rows)
+                lines = everything[(4 * m + r) * rows :][:rows]
+                mix_here[m ^ section, at, :] = lines[:own_rows]
+                mix_sent[m ^ section, at, :] = lines[own_rows:].astype(BF16)
+        right_all[...] = lax.dot_general(
+            mine,
+            mix_rows[...].reshape(mine.shape[0], -1),
+            (((0,), (0,)), ((), ())),
+            preferred_element_type=F32,
+        )
+        for i in range(2):
+            factors[i][rank:, :] = right_all[at_multiple(outer, rank // 2), :]
+
+
+def back(place, pieces, weights, left_rows, right, mix_rows, permuted):
+    _, rows, width = pieces[0].shape
+    head_cols, rank = right.shape
+    micro, size, _ = mix_rows.shape
+    half = width // 2
+    tile = 512
+    tiles = width // tile
+    shapes = [
+        jax.ShapeDtypeStruct((micro, size // 2, head_cols), F32),
+        jax.ShapeDtypeStruct((micro, size // 2, head_cols), BF16),
+        jax.ShapeDtypeStruct((rank + rank // 2, half), F32),
+        jax.ShapeDtypeStruct((rank + rank // 2, half), F32),
+    ]
+    return pl.pallas_call(
+        functools.partial(back_kernel, micro),
+        grid=(tiles,),
+        in_specs=[pl.BlockSpec(memory_space=pltpu.SMEM)]
+        + [pl.BlockSpec((2, rows, tile), lambda i: (0, 0, i))] * (4 * micro)
+        + weight_specs(head_cols, tile)
+        + [
+            pl.BlockSpec((2, rank, tile), lambda i: (0, 0, i)),
+            whole(*right.shape),
+            whole(*mix_rows.shape),
+        ]
+        + [
+            whole(*permuted[0].shape),
+            pl.BlockSpec((1, 2, rows, size), lambda i: (0, 0, 0, width // size)),
+            pl.BlockSpec((2, rows, size), lambda i: (0, 0, width // size)),
+            pl.BlockSpec((2, rows, size), lambda i: (0, 0, width // size + 1)),
+            pl.BlockSpec((2, rows, size), lambda i: (0, 0, width // size)),
+        ],
+        out_specs=[whole(*shape.shape) for shape in shapes],
+        out_shape=shapes,
+        scratch_shapes=[
+            pltpu.VMEM((head_cols, micro * size), F32),
+            pltpu.VMEM((micro * size, rank), F32),
+            pltpu.VMEM((rank, micro * size), BF16),
+            pltpu.VMEM((rank, head_cols), F32),
+        ],
+        compiler_params=pltpu.CompilerParams(vmem_limit_bytes=VMEM_ALL),
+        cost_estimate=NO_COST,
+    )(place, *pieces, *doubled(weights), left_rows, right, mix_rows, *permuted)
+
+
+def gather_kernel(place, here, arrived, out):
+    outer, core, section = place[1], place[2], place[3]
+    width = arrived.shape[3]
+    for m in range(here.shape[0]):
+        for slot in range(2):
+            part = core ^ slot
+            at = pl.ds(pl.multiple_of((2 * outer + part) * width, width), width)
+            out[m ^ section, :, at] = here[m, slot]
+            at = pl.ds(pl.multiple_of((2 * (1 - outer) + part) * width, width), width)
+            out[m ^ section, :, at] = arrived[m, slot]
+
+
+def left_kernel(place, own_left, other_left, grad_left):
+    core = place[2]
+    half = own_left.shape[1]
+    grad_left[:, pl.ds(pl.multiple_of(core * half, half), half)] = own_left[...].astype(F32)
+    grad_left[:, pl.ds(pl.multiple_of((1 - core) * half, half), half)] = other_left[...].astype(F32)
+
+
+def right_kernel(place, own_right, other_right, grad_right, wide):
+    outer = place[1]
+    rank = wide.shape[0]
+    wide[at_multiple(outer, rank // 2), :] = own_right[rank:, :].astype(F32)
+    wide[at_multiple(1 - outer, rank // 2), :] = other_right[rank:, :].astype(F32)
+    grad_right[...] = wide[...].T
+
+
 def on_device(mix, hidden_in, cotangent, frozen_weight, right_factor, left_factor, norm_gain):
+    t = lax.axis_index("tensor")
+    d = lax.axis_index("dp")
+    section = lax.axis_index("pipe")
+    outer = d // 2
+    core = d % 2
+    place = jnp.stack([t, outer, core, section]).astype(jnp.int32)
+
+    def to_core(value):
+        return lax.ppermute(value, "dp", [(i, i ^ 1) for i in range(4)])
+
+    def to_outer(value):
+        return lax.ppermute(value, "dp", [(i, i ^ 2) for i in range(4)])
+
+    def along(value, *pairs):
+        return lax.ppermute(value, "tensor", pairs)
+
+    mixes = mix[0, :, 0]
+    micro, tokens, head_cols = mixes.shape
+    own_rows = tokens // 4
+    rows = 2 * own_rows
+    weight = frozen_weight[0]
+    right = right_factor[0, 0]
+    left = left_factor[0, 0]
+    rank, width = left.shape
+    sub = rank // 4
+    half = width // 2
+    features = 4 * width
+    slots = (d, d ^ 1)
+
+    other_mixes = to_outer(mixes)
+    weights = (weight, to_core(weight))
+
+    def swapped(values):
+        return [values[0]] + [along(values[o], *[(i, i ^ o) for i in range(4)]) for o in (1, 2, 3)]
+
+    def of_block(values, block):
+        return lax.select_n(t ^ block, *values)
+
+    cut = [
+        lax.dynamic_slice(left, ((t ^ o) * sub, core * half), (sub, half)) for o in range(4)
+    ]
+    met = swapped(cut)
+    own_half = jnp.stack([of_block(met, 2 * outer + i) for i in range(2)])
+    other_half = to_core(own_half)
+
+    own, next_one, *partial, mix_rows, left_rows, own_piece = project(
+        place, mixes, other_mixes, weights, right, own_half, other_half
+    )
+
+    swaps = [[(i, i ^ o) for i in range(4)] for o in range(4)]
+    shape = (2, rows, width)
+    passed, mids, crossings = [], [], []
+    for m in range(micro):
+        last = partial[micro + m]
+        passed.append(along(last, (0, 1), (3, 2)))
+        mids.append(along(last, (1, 2), (2, 1)))
+    for m in range(micro):
+        two_away = partial[m]
+        carried = two_away.shape[2] - width
+        (ahead,) = small(
+            ahead_kernel,
+            [((2, rows, width + 2 * carried), BF16)],
+            [],
+            place,
+            two_away,
+            after(passed[m], *mids, *passed),
+        )
+        crossings.append(along(ahead, *swaps[2]))
+    beside = along(next_one, *swaps[1])
+    permuted = (own_piece, beside, crossings[0], crossings[0], mids[0])
+
+    layout = (2, micro, 2, own_rows, width)
+    here, there = small(
+        cut_kernel,
+        [(layout, BF16)] * 2,
+        [],
+        place,
+        after(hidden_in[:, 0], own),
+        cotangent[:, 0],
+    )
+    arrived = to_outer(there)
+    gain = norm_gain.astype(F32).reshape(1, features)
+
+    update, kept, sent = small(
+        update_kernel,
+        [((micro, *shape), F32), (shape, BF16), (shape, BF16)],
+        [],
+        place,
+        own,
+        after(beside, arrived),
+        *mids,
+        *crossings,
+    )
+
+    def to_section(value):
+        return lax.ppermute(value, "pipe", [(0, 1), (1, 0)])
+
+    leaving, final, sums = small(
+        state_kernel,
+        [(shape, BF16)] * 2 + [((rows, 128), F32)],
+        [],
+        place,
+        here,
+        arrived,
+        gain,
+        update,
+        to_section(sent),
+    )
+    (grad,) = small(
+        norm_kernel, [(shape, BF16)], [], place, here, arrived, gain, final, sums, to_outer(sums)
+    )
+
+    opposite = along(grad, *swaps[2])
+    beside = along(grad, *swaps[1])
+    before = to_section(after(kept, final))
+    own_there = to_section(after(grad, before))
+    relay = after(opposite, own_there, beside)
+    mid = along(after(grad, beside), (1, 2), (2, 1))
+    farthest = along(relay, (1, 0), (2, 3))
+    opposite_there = to_section(opposite)
+    by_group, others = small(
+        later_kernel,
+        [((micro, 2, own_rows, width), BF16)] * 2,
+        [],
+        place,
+        here,
+        arrived,
+        update,
+        before,
+        leaving,
+    )
+    others = to_outer(others)
+    beside_there = to_section(after(beside, others))
+    (section_out,) = small(
+        gather_kernel, [((micro, own_rows, features), BF16)], [], place, by_group, others
+    )
+    (last,) = small(
+        join_kernel, [(shape, BF16)], [], place, mid, after(farthest, beside_there)
+    )
+    pieces = [grad, beside, relay, last]
+    pieces += [own_there, beside_there, opposite_there, to_section(after(last, opposite_there))]
+    mix_here, mix_sent, kept_factors, sent_factors = back(
+        place, pieces, weights, left_rows, right, mix_rows, permuted
+    )
+    joined = (kept_factors + to_core(sent_factors)).astype(BF16)
+    other_joined = to_outer(joined)
+    best = jnp.where(outer == t // 2, joined[:rank], other_joined[:rank])
+    (grad_right,) = small(
+        right_kernel,
+        [((head_cols, rank), F32)],
+        [pltpu.VMEM((rank, head_cols), F32)],
+        place,
+        joined,
+        other_joined,
+    )
+    (grad_left,) = small(
+        left_kernel, [((rank, width), F32)], [], place, best, after(to_core(best), grad_right)
+    )
+    grad_mix = (mix_here + after(to_outer(mix_sent), grad_left).astype(F32)).astype(BF16)
+    grad_mix = grad_mix.reshape(1, micro, 1, tokens, head_cols)
+
+    return (
+        section_out.reshape(1, micro, 1, own_rows, features),
+        grad_mix,
+        grad_right.reshape(1, 1, head_cols, rank),
+        grad_left.reshape(1, 1, rank, width),
+    )
+
+
+def on_device_general(mix, hidden_in, cotangent, frozen_weight, right_factor, left_factor, norm_gain):
     blocks = lax.axis_size("tensor")
     parts = lax.axis_size("dp")
     sections = lax.axis_size("pipe")
@@ -119,31 +667,11 @@
         return pick(partial[m], index, 1)
 
     updates_here = []
-    arrived_last = None
     for m in range(micro):
         total = shard(m, t).astype(F32)
-        if blocks != 4:
-            for step in range(1, blocks):
-                total = total + to_block(shard(m, (t + step) % blocks), step).astype(F32)
-            updates_here.append(total)
-            continue
-        far = shard(m, jnp.where(t < 2, 3, 0))
-        if arrived_last is not None:
-            far = after(far, arrived_last)
-        passed = lax.ppermute(far, "tensor", [(0, 1), (3, 2)])
-        mid = lax.ppermute(
-            after(shard(m, jnp.where(t < 2, 2, 1)), far), "tensor", [(1, 2), (2, 1)]
-        )
-        beside = lax.ppermute(after(shard(m, t ^ 1), far), "tensor", [(i, i ^ 1) for i in range(4)])
-        middle = (t == 1) | (t == 2)
-        two_away = jnp.where(
-            middle, (far.astype(F32) + passed.astype(F32)).astype(BF16), shard(m, t ^ 2)
-        )
-        arrived_last = two_away
-        crossed = to_block(two_away, 2)
-        updates_here.append(
-            total + beside.astype(F32) + mid.astype(F32) + crossed.astype(F32)
-        )
+        for step in range(1, blocks):
+            total = total + to_block(shard(m, (t + step) % blocks), step).astype(F32)
+        updates_here.append(total)
 
     hidden_late = after(hidden_in, *taken)
 
@@ -196,26 +724,13 @@
             (scale[None, :, None] * (upstream - final * shrink[None, :, None])).astype(BF16)
         )
 
-    full = []
-    order = []
-    earlier = None
-    for m in range(micro):
-        if blocks != 4:
-            pieces_m = [grads[m]] + [to_block(grads[m], step) for step in range(1, blocks)]
-            full.append(jnp.concatenate(pieces_m, axis=1))
-            order.append([(t - step) % blocks for step in range(blocks)])
-            continue
-        opposite = to_block(grads[m], 2)
-        beside = lax.ppermute(grads[m], "tensor", [(i, i ^ 1) for i in range(4)])
-        mid = lax.ppermute(grads[m], "tensor", [(1, 2), (2, 1)])
-        relay = after(opposite, beside, mid)
-        farthest = lax.ppermute(relay, "tensor", [(1, 0), (2, 3)])
-        last = jnp.where((t == 1) | (t == 2), mid, farthest)
-        if earlier is not None:
-            full[-1] = after(full[-1], relay)
-        full.append(jnp.concatenate([grads[m], beside, opposite, last], axis=1))
-        order.append([t, t ^ 1, t ^ 2, t ^ 3])
-        earlier = relay
+    full = [
+        jnp.concatenate(
+            [grads[m]] + [to_block(grads[m], step) for step in range(1, blocks)], axis=1
+        )
+        for m in range(micro)
+    ]
+    order = [[(t - step) % blocks for step in range(blocks)]] * micro
 
     outs = []
     for m in range(micro):
@@ -281,7 +796,7 @@
         for step in range(1, outers):
             whole = whole + to_outer(partial_mix[:, step].astype(BF16), outers - step).astype(F32)
         whole = whole.astype(BF16)
-        back = [t ^ i for i in range(blocks)] if blocks == 4 else order[m]
+        back = order[m]
         mix_grads.append(
             jnp.concatenate([pick(whole, at) for at in back], axis=0)
         )
@@ -326,8 +841,9 @@
 
 
 def solution(mesh):
+    sizes = (mesh.shape["tensor"], mesh.shape["dp"], mesh.shape["pipe"])
     return jax.shard_map(
-        on_device,
+        on_device if sizes == (4, 4, 2) else on_device_general,
         mesh=mesh,
         in_specs=(
             P("pipe", None, "dp", None, "tensor"),

time: 177 us -> 144 us (0.81)
  Pallas kernels: 0 us -> 24.4 us
  matrix products: 23.8 us -> 0 us
  starting transfers between devices: 65.1 us -> 42.4 us
  waiting for transfers between devices: 55.9 us -> 71.2 us
  other arithmetic: 14.7 us -> 1.88 us
  local copies, waits for them, and re-layouts: 14.9 us -> 2.84 us
    pallas_call x0 -> x13, Pallas kernels: none -> 24.4 us  [the longest x11 10 us: small(): pl.pallas_call(kernel, in_specs=[pl.BlockSpec(memory_space=pltpu.SMEM)] +...]
    dot_general x25 -> x0, matrix products: 23.8 us -> none  [dot(): lax.dot_general(left_side, right_side, (((left_dim,), (right_dim,)), ((),...]
    ppermute x34 -> x30, starting transfers between devices: 58.7 us -> 42.4 us  [the longest x14 23.8 us: along(): return lax.ppermute(value, 'tensor', pairs)]
    ppermute x34 -> x30, waiting for transfers between devices: 55.9 us -> 71.2 us  [the longest x14 36.7 us: along(): return lax.ppermute(value, 'tensor', pairs)]
    all_to_all x1 -> x0, starting transfers between devices: 6.32 us -> none  [on_device(): lax.all_to_all(jnp.concatenate([left.reshape(blocks, sub, block_cols), ow...]
    dynamic_slice x5 -> x1, local copies, waits for them, and re-layouts: 4.4 us -> 0.92 us  [on_device(): lax.dynamic_slice(left, ((t ^ o) * sub, core * half), (sub, half))]
    concatenate x8 -> x0, other arithmetic: 3.25 us -> none  [the longest x1 1.89 us: on_device(): jnp.concatenate([left.reshape(blocks, sub, block_cols), own_inner.reshape...]
    dynamic_update_slice x10 -> x0, local copies, waits for them, and re-layouts: 2.93 us -> none  [the longest x2 2.83 us: on_device(): lax.dynamic_update_slice_in_dim(wide, arrived, (outer - step) % outers *...]
  transfers between devices with their start and end apart: 35 -> 30, of which waited for: 15 -> 19; matrix products, arithmetic and copies ran while one was open for 26% -> 1% of each run, Pallas kernels for 0% -> 6%
where the time goes in v4:
time: 144 us
  waiting for transfers between devices  71.2 us (49%)
  starting transfers between devices  42.4 us (29%)
  Pallas kernels  24.4 us (17%)
  local copies, waits for them, and re-layouts  2.84 us (2%)
  other arithmetic  1.88 us (1%)
    ppermute x14, waiting for transfers between devices, along(): return lax.ppermute(value, 'tensor', pairs)  36.7 us
    ppermute x14, starting transfers between devices, along(): return lax.ppermute(value, 'tensor', pairs)  23.8 us
    ppermute x6, waiting for transfers between devices, to_outer(): return lax.ppermute(value, 'dp', [(i, i ^ 2) for i in range(4)])  16.6 us
    ppermute x6, waiting for transfers between devices, to_section(): return lax.ppermute(value, 'pipe', [(0, 1), (1, 0)])  14.1 us
    pallas_call x11, Pallas kernels, small(): pl.pallas_call(kernel, in_specs=[pl.BlockSpec(memory_space=pltpu.SMEM)] +...  10 us
    ppermute x6, starting transfers between devices, to_outer(): return lax.ppermute(value, 'dp', [(i, i ^ 2) for i in range(4)])  9.27 us
    ppermute x6, starting transfers between devices, to_section(): return lax.ppermute(value, 'pipe', [(0, 1), (1, 0)])  8.65 us
    pallas_call x1, Pallas kernels, back(): pl.pallas_call(functools.partial(back_kernel, micro), grid=(tiles,), in_s...  7.92 us
  transfers between devices with their start and end apart: 30, of which 19 were waited for; matrix products, arithmetic and copies ran while one was open for 1% of the time, Pallas kernels for 6%

profile of v4, /device:TPU:0, one launch (start us, length us, event | category | flops | bytes accessed | tf_op | source)
XLA Modules:
  0.0 143.6 jit_solution(6387338162994220810)
XLA Ops:
  0.6 0.5 collective-permute-start.1
  1.1 0.9 dynamic-slice_bitcast_fusion
  2.1 4.7 %collective-permute-start.4 = (bf16[32,1024]{1,0:T(8,128)(2,1)S(1)}, bf16[32,1024]{1,0:T(8,128)(2,1)S(1)}, u32[]{:S(2)}, u32[]{:S(2)}) collective-permute-start(bf16[32,1024]{1,0:T(8,128)(2,1)S(1)} %get-tuple-element.82), channel_id=1, source_target_pairs={{0,24},{8,16},{16,8},{24,0},{1,25},{9,17},{17,9},{25,1},{2,26},{10... | collective-permute-start | bytes 196616 | tf_op jit(solution)/shard_map/ppermute | solution.py:424
  6.8 0.6 collective-permute-start.3
  7.4 1.6 %collective-permute-start = (bf16[2,64,1024]{2,1,0:T(8,128)(2,1)}, bf16[2,64,1024]{2,1,0:T(8,128)(2,1)S(1)}, u32[]{:S(2)}, u32[]{:S(2)}) collective-permute-start(bf16[2,64,1024]{2,1,0:T(8,128)(2,1)} %bitcast.46), channel_id=1, source_target_pairs={{0,4},{2,6},{4,0},{6,2},{1,5},{3,7},{5,1},{7,3},{8,12},{10,14},{12... | collective-permute-start | bytes 786440 | tf_op jit(solution)/shard_map/ppermute | solution.py:421
  9.1 0.7 collective-permute-done.4
  9.8 2.5 %collective-permute-done.2 = bf16[32,1024]{1,0:T(8,128)(2,1)S(1)} collective-permute-done((bf16[32,1024]{1,0:T(8,128)(2,1)S(1)}, bf16[32,1024]{1,0:T(8,128)(2,1)S(1)}, u32[]{:S(2)}, u32[]{:S(2)}) %collective-permute-start.2) | collective-permute-done | bytes 65568 | tf_op jit(solution)/shard_map/ppermute | solution.py:424
  12.2 0.4 collective-permute-done.3
  12.7 0.9 fusion.2
  13.7 0.1 pad_add_fusion.place
  13.8 1.3 collective-permute-done.5.other_half
  15.0 0.7 collective-permute-done.other_mix
  15.7 0.9 copy-done
  16.7 0.9 copy-done.5
  17.7 6.5 %shard_map.102 = (bf16[2,2,32,2048]{3,2,1,0:T(8,128)(2,1)S(1)}, bf16[2,2,32,2176]{3,2,1,0:T(8,128)(2,1)S(1)}, bf16[2,32,2176]{2,1,0:T(8,128)(2,1)S(1)}, bf16[2,3...) custom-call(s32[4]{0:T(128)S(1)} %pad_add_fusion.place, ...), custom_call_target="tpu_custom_call" | custom-call | tf_op jit(solution)/shard_map/pallas_call | solution.py:240
  24.2 3.4 %collective-permute-start.11 = (bf16[2,32,2048]{2,1,0:T(8,128)(2,1)S(1)}, bf16[2,32,2048]{2,1,0:T(8,128)(2,1)S(1)}, u32[]{:S(2)}, u32[]{:S(2)}) collective-permute-start(bf16[2,32,2048]{2,1,0:T(8,128)(2,1)S(1)} %get-tuple-element.47), channel_id=1, source_target_pairs={{0,8},{24,16},{1,9},{25,17},{2,10},{26,18},{3,11},{27,19},{4,12},{... | collective-permute-start | bytes 786440 | tf_op jit(solution)/shard_map/ppermute | solution.py:424
  27.6 1.3 collective-permute-start.10
  28.9 0.7 collective-permute-start.8
  29.6 0.7 collective-permute-start.9
  30.3 3.9 %collective-permute-start.7 = (bf16[2,2,32,2176]{3,2,1,0:T(8,128)(2,1)S(1)}, bf16[2,2,32,2176]{3,2,1,0:T(8,128)(2,1)S(1)}, u32[]{:S(2)}, u32[]{:S(2)}) collective-permute-start(bf16[2,2,32,2176]{3,2,1,0:T(8,128)(2,1)S(1)} %get-tuple-element.44), channel_id=1, source_target_pairs={{0,8},{8,0},{16,24},{24,16},{1,9},{9,1},{17,25},{25,17},{2,10},{10... | collective-permute-start | bytes 1671176 | tf_op jit(solution)/shard_map/ppermute | solution.py:424
  34.2 0.6 shard_map.103
  34.9 1.6 %collective-permute-start.6 = (bf16[2,2,2,16,2048]{4,3,2,1,0:T(8,128)(2,1)S(1)}, bf16[2,2,2,16,2048]{4,3,2,1,0:T(8,128)(2,1)S(1)}, u32[]{:S(2)}, u32[]{:S(2)}) collective-permute-start(bf16[2,2,2,16,2048]{4,3,2,1,0:T(8,128)(2,1)S(1)} %get-tuple-element.43), channel_id=1, source_target_pairs={{0,4},{2,6},{4,0},{6,2},{1,5},{3,7},{5,1},{7,3},{8,12},{10,14},{12... | collective-permute-start | bytes 1572872 | tf_op jit(solution)/shard_map/ppermute | solution.py:421
  36.4 3.9 %collective-permute-done.10.passed = bf16[2,32,2176]{2,1,0:T(8,128)(2,1)S(1)} collective-permute-done((bf16[2,32,2176]{2,1,0:T(8,128)(2,1)S(1)}, bf16[2,32,2176]{2,1,0:T(8,128)(2,1)S(1)}, u32[]{:S(2)}, u32[]{:S(2)}) %collective-permute-start.10) | collective-permute-done | bytes 278560 | tf_op jit(solution)/shard_map/ppermute | solution.py:424
  40.3 0.6 shard_map.104
  40.9 4.4 %collective-permute-start.12 = (bf16[2,32,2304]{2,1,0:T(8,128)(2,1)S(1)}, bf16[2,32,2304]{2,1,0:T(8,128)(2,1)S(1)}, u32[]{:S(2)}, u32[]{:S(2)}) collective-permute-start(bf16[2,32,2304]{2,1,0:T(8,128)(2,1)S(1)} %shard_map.104), channel_id=1, source_target_pairs={{0,16},{8,24},{16,0},{24,8},{1,17},{9,25},{17,1},{25,9},{2,18},{10... | collective-permute-start | bytes 884744 | tf_op jit(solution)/shard_map/ppermute | solution.py:424
  45.4 0.6 shard_map.105
  46.0 0.1 collective-permute-start.13
  46.0 1.2 collective-permute-done.6.arrived
  47.3 6.7 %collective-permute-done.7.beside.refs_16_ = bf16[2,2,32,2176]{3,2,1,0:T(8,128)(2,1)S(1)} collective-permute-done((bf16[2,2,32,2176]{3,2,1,0:T(8,128)(2,1)S(1)}, bf16[2,2,32,2176]{3,2,1,0:T(8,128)(2,1)S(1)}, u32[]{:S(2)}, u32[]{:S(2)}) %collective-permute-start.7) | collective-permute-done | bytes 557088 | tf_op jit(solution)/shard_map/ppermute | solution.py:424
  53.9 14.7 %collective-permute-done.13.refs_3_ = bf16[2,32,2048]{2,1,0:T(8,128)(2,1)S(1)} collective-permute-done((bf16[2,32,2048]{2,1,0:T(8,128)(2,1)S(1)}, bf16[2,32,2048]{2,1,0:T(8,128)(2,1)S(1)}, u32[]{:S(2)}, u32[]{:S(2)}) %collective-permute-start.13) | collective-permute-done | bytes 262176 | tf_op jit(solution)/shard_map/ppermute | solution.py:424
  68.6 0.8 shard_map.106
  69.4 1.6 %collective-permute-start.14 = (bf16[2,32,2048]{2,1,0:T(8,128)(2,1)S(1)}, bf16[2,32,2048]{2,1,0:T(8,128)(2,1)S(1)}, u32[]{:S(2)}, u32[]{:S(2)}) collective-permute-start(bf16[2,32,2048]{2,1,0:T(8,128)(2,1)S(1)} %get-tuple-element.54), channel_id=1, source_target_pairs={{0,1},{1,0},{2,3},{3,2},{4,5},{5,4},{6,7},{7,6},{8,9},{9,8},{10,11... | collective-permute-start | bytes 786440 | tf_op jit(solution)/shard_map/ppermute | solution.py:505
  71.0 4.9 %collective-permute-done.14.other = bf16[2,32,2048]{2,1,0:T(8,128)(2,1)S(1)} collective-permute-done((bf16[2,32,2048]{2,1,0:T(8,128)(2,1)S(1)}, bf16[2,32,2048]{2,1,0:T(8,128)(2,1)S(1)}, u32[]{:S(2)}, u32[]{:S(2)}) %collective-permute-start.14) | collective-permute-done | bytes 262176 | tf_op jit(solution)/shard_map/ppermute | solution.py:505
  75.9 0.9 shard_map.107
  76.7 1.6 %collective-permute-start.15 = (bf16[2,32,2048]{2,1,0:T(8,128)(2,1)S(1)}, bf16[2,32,2048]{2,1,0:T(8,128)(2,1)S(1)}, u32[]{:S(2)}, u32[]{:S(2)}) collective-permute-start(bf16[2,32,2048]{2,1,0:T(8,128)(2,1)S(1)} %get-tuple-element.56), channel_id=1, source_target_pairs={{0,1},{1,0},{2,3},{3,2},{4,5},{5,4},{6,7},{7,6},{8,9},{9,8},{10,11... | collective-permute-start | bytes 786440 | tf_op jit(solution)/shard_map/ppermute | solution.py:505
  78.3 1.5 %collective-permute-start.17 = (f32[32,128]{1,0:T(8,128)S(1)}, f32[32,128]{1,0:T(8,128)S(1)}, u32[]{:S(2)}, u32[]{:S(2)}) collective-permute-start(f32[32,128]{1,0:T(8,128)S(1)} %get-tuple-element.60.sums), channel_id=1, source_target_pairs={{0,4},{2,6},{4,0},{6,2},{1,5},{3,7},{5,1},{7,3},{8,12},{10,14},{12... | collective-permute-start | bytes 49160 | tf_op jit(solution)/shard_map/ppermute | solution.py:421
  79.8 2.2 %collective-permute-done.17.other_sums = f32[32,128]{1,0:T(8,128)S(1)} collective-permute-done((f32[32,128]{1,0:T(8,128)S(1)}, f32[32,128]{1,0:T(8,128)S(1)}, u32[]{:S(2)}, u32[]{:S(2)}) %collective-permute-start.17) | collective-permute-done | bytes 16416 | tf_op jit(solution)/shard_map/ppermute | solution.py:421
  82.1 0.8 shard_map.110.refs_0_
  82.9 1.9 %collective-permute-start.18 = (bf16[2,32,2048]{2,1,0:T(8,128)(2,1)S(1)}, bf16[2,32,2048]{2,1,0:T(8,128)(2,1)S(1)}, u32[]{:S(2)}, u32[]{:S(2)}) collective-permute-start(bf16[2,32,2048]{2,1,0:T(8,128)(2,1)S(1)} %shard_map.110.refs_0_), channel_id=1, source_target_pairs={{0,8},{8,0},{16,24},{24,16},{1,9},{9,1},{17,25},{25,17},{2,10},{10... | collective-permute-start | bytes 786440 | tf_op jit(solution)/shard_map/ppermute | solution.py:424
  84.8 1.7 %collective-permute-start.20 = (bf16[2,32,2048]{2,1,0:T(8,128)(2,1)S(1)}, bf16[2,32,2048]{2,1,0:T(8,128)(2,1)S(1)}, u32[]{:S(2)}, u32[]{:S(2)}) collective-permute-start(bf16[2,32,2048]{2,1,0:T(8,128)(2,1)S(1)} %shard_map.110.refs_0_), channel_id=1, source_target_pairs={{0,1},{1,0},{2,3},{3,2},{4,5},{5,4},{6,7},{7,6},{8,9},{9,8},{10,11... | collective-permute-start | bytes 786440 | tf_op jit(solution)/shard_map/ppermute | solution.py:505
  86.5 0.7 shard_map.108
  87.2 1.6 %collective-permute-start.16 = (bf16[2,2,16,2048]{3,2,1,0:T(8,128)(2,1)S(1)}, bf16[2,2,16,2048]{3,2,1,0:T(8,128)(2,1)S(1)}, u32[]{:S(2)}, u32[]{:S(2)}) collective-permute-start(bf16[2,2,16,2048]{3,2,1,0:T(8,128)(2,1)S(1)} %get-tuple-element.59), channel_id=1, source_target_pairs={{0,4},{2,6},{4,0},{6,2},{1,5},{3,7},{5,1},{7,3},{8,12},{10,14},{12... | collective-permute-start | bytes 786440 | tf_op jit(solution)/shard_map/ppermute | solution.py:421
  88.8 3.7 %collective-permute-done.18.refs_1_ = bf16[2,32,2048]{2,1,0:T(8,128)(2,1)S(1)} collective-permute-done((bf16[2,32,2048]{2,1,0:T(8,128)(2,1)S(1)}, bf16[2,32,2048]{2,1,0:T(8,128)(2,1)S(1)}, u32[]{:S(2)}, u32[]{:S(2)}) %collective-permute-start.18) | collective-permute-done | bytes 262176 | tf_op jit(solution)/shard_map/ppermute | solution.py:424
  92.5 1.3 collective-permute-start.22
  93.8 1.7 %collective-permute-start.23 = (bf16[2,32,2048]{2,1,0:T(8,128)(2,1)S(1)}, bf16[2,32,2048]{2,1,0:T(8,128)(2,1)S(1)}, u32[]{:S(2)}, u32[]{:S(2)}) collective-permute-start(bf16[2,32,2048]{2,1,0:T(8,128)(2,1)S(1)} %collective-permute-done.18.refs_1_), channel_id=1, source_target_pairs={{0,1},{1,0},{2,3},{3,2},{4,5},{5,4},{6,7},{7,6},{8,9},{9,8},{10,11... | collective-permute-start | bytes 786440 | tf_op jit(solution)/shard_map/ppermute | solution.py:505
  95.5 0.7 collective-permute-start.21
  96.2 0.4 collective-permute-start.24
  96.6 4.1 %collective-permute-done.22.farthest = bf16[2,32,2048]{2,1,0:T(8,128)(2,1)S(1)} collective-permute-done((bf16[2,32,2048]{2,1,0:T(8,128)(2,1)S(1)}, bf16[2,32,2048]{2,1,0:T(8,128)(2,1)S(1)}, u32[]{:S(2)}, u32[]{:S(2)}) %collective-permute-start.22) | collective-permute-done | bytes 262176 | tf_op jit(solution)/shard_map/ppermute | solution.py:424
  100.8 0.4 collective-permute-done.23.refs_5_
  101.2 0.6 shard_map.111.refs_3_
  101.8 4.1 %collective-permute-done.24.refs_6_ = bf16[2,32,2048]{2,1,0:T(8,128)(2,1)S(1)} collective-permute-done((bf16[2,32,2048]{2,1,0:T(8,128)(2,1)S(1)}, bf16[2,32,2048]{2,1,0:T(8,128)(2,1)S(1)}, u32[]{:S(2)}, u32[]{:S(2)}) %collective-permute-start.24) | collective-permute-done | bytes 262176 | tf_op jit(solution)/shard_map/ppermute | solution.py:505
  105.9 1.6 %collective-permute-start.25 = (bf16[2,32,2048]{2,1,0:T(8,128)(2,1)S(1)}, bf16[2,32,2048]{2,1,0:T(8,128)(2,1)S(1)}, u32[]{:S(2)}, u32[]{:S(2)}) collective-permute-start(bf16[2,32,2048]{2,1,0:T(8,128)(2,1)S(1)} %shard_map.111.refs_3_), channel_id=1, source_target_pairs={{0,1},{1,0},{2,3},{3,2},{4,5},{5,4},{6,7},{7,6},{8,9},{9,8},{10,11... | collective-permute-start | bytes 786440 | tf_op jit(solution)/shard_map/ppermute | solution.py:505
  107.5 4.7 %collective-permute-done.25.refs_7_ = bf16[2,32,2048]{2,1,0:T(8,128)(2,1)S(1)} collective-permute-done((bf16[2,32,2048]{2,1,0:T(8,128)(2,1)S(1)}, bf16[2,32,2048]{2,1,0:T(8,128)(2,1)S(1)}, u32[]{:S(2)}, u32[]{:S(2)}) %collective-permute-start.25) | collective-permute-done | bytes 262176 | tf_op jit(solution)/shard_map/ppermute | solution.py:505
  112.2 7.9 %shard_map.112 = (f32[2,64,1024]{2,1,0:T(8,128)S(1)}, bf16[2,64,1024]{2,1,0:T(8,128)(2,1)S(1)}, f32[192,1024]{1,0:T(8,128)S(1)}, f32[192,1024]{1,0:T(8,128)}) custom-call(s32[4]{0:T(128)S(1)} %pad_add_fusion.place, bf16[2,32,2048]{2,1,0:T(8,128)(2,1)S(1)} %shard_map.110.refs_0_, bf16[2,32,2048]{2,1,0:T(8,128)(2,1)S(1)} %collective-permute-done.18.refs_1_, ...), custom_call_target="tpu_custom_call" | custom-call | tf_op jit(solution)/shard_map/pallas_call | solution.py:351
  120.2 2.5 %collective-permute-done.27 = f32[192,1024]{1,0:T(8,128)S(1)} collective-permute-done((f32[192,1024]{1,0:T(8,128)}, f32[192,1024]{1,0:T(8,128)S(1)}, u32[]{:S(2)}, u32[]{:S(2)}) %collective-permute-start.27) | collective-permute-done | bytes 786464 | tf_op jit(solution)/shard_map/ppermute | solution.py:418
  122.7 0.1 add_convert_fusion.own_right
  122.8 1.5 %collective-permute-start.28 = (bf16[192,1024]{1,0:T(8,128)(2,1)S(1)}, bf16[192,1024]{1,0:T(8,128)(2,1)S(1)}, u32[]{:S(2)}, u32[]{:S(2)}) collective-permute-start(bf16[192,1024]{1,0:T(8,128)(2,1)S(1)} %add_convert_fusion.own_right), channel_id=1, source_target_pairs={{0,4},{2,6},{4,0},{6,2},{1,5},{3,7},{5,1},{7,3},{8,12},{10,14},{12... | collective-permute-start | bytes 1179656 | tf_op jit(solution)/shard_map/ppermute | solution.py:421
  124.3 9.7 %collective-permute-done.28.other_right = bf16[192,1024]{1,0:T(8,128)(2,1)S(1)} collective-permute-done((bf16[192,1024]{1,0:T(8,128)(2,1)S(1)}, bf16[192,1024]{1,0:T(8,128)(2,1)S(1)}, u32[]{:S(2)}, u32[]{:S(2)}) %collective-permute-start.28) | collective-permute-done | bytes 393248 | tf_op jit(solution)/shard_map/ppermute | solution.py:421
  134.1 1.5 %collective-permute-start.26 = (bf16[2,64,1024]{2,1,0:T(8,128)(2,1)S(1)}, bf16[2,64,1024]{2,1,0:T(8,128)(2,1)S(1)}, u32[]{:S(2)}, u32[]{:S(2)}) collective-permute-start(bf16[2,64,1024]{2,1,0:T(8,128)(2,1)S(1)} %get-tuple-element.71), channel_id=1, source_target_pairs={{0,4},{2,6},{4,0},{6,2},{1,5},{3,7},{5,1},{7,3},{8,12},{10,14},{12... | collective-permute-start | bytes 786440 | tf_op jit(solution)/shard_map/ppermute | solution.py:421
  135.6 1.4 shard_map.109
  137.0 1.6 %shard_map.113 = f32[1024,128]{1,0:T(8,128)} custom-call(s32[4]{0:T(128)S(1)} %pad_add_fusion.place, bf16[192,1024]{1,0:T(8,128)(2,1)S(1)} %add_convert_fusion.own_right, bf16[192,1024]{1,0:T(8,128)(2,1)S(1)} %collective-permute-done.28.other_right), custom_call_target="tpu_custom_call" | custom-call | tf_op jit(solution)/shard_map/pallas_call | solution.py:43
  138.6 1.6 %shard_map.114 = f32[128,2048]{1,0:T(8,128)} custom-call(s32[4]{0:T(128)S(1)} %pad_add_fusion.place, bf16[128,1024]{1,0:T(8,128)(2,1)S(1)} %slice_select_fusion.own_left, bf16[128,1024]{1,0:T(8,128)(2,1)S(1)} %collective-permute-done.29.other_left), custom_call_target="tpu_custom_call" | custom-call | tf_op jit(solution)/shard_map/pallas_call | solution.py:43
  140.1 2.7 %collective-permute-done.26 = bf16[2,64,1024]{2,1,0:T(8,128)(2,1)S(1)} collective-permute-done((bf16[2,64,1024]{2,1,0:T(8,128)(2,1)S(1)}, bf16[2,64,1024]{2,1,0:T(8,128)(2,1)S(1)}, u32[]{:S(2)}, u32[]{:S(2)}) %collective-permute-start.26) | collective-permute-done | bytes 262176 | tf_op jit(solution)/shard_map/ppermute | solution.py:421
  142.8 0.8 fusion
  (31 shorter events, 0.3 us)
Async XLA Ops:
  0.6 15.1 %collective-permute-start.1 = (bf16[1024,2048]{1,0:T(8,128)(2,1)}, bf16[1024,2048]{1,0:T(8,128)(2,1)}, u32[]{:S(2)}, u32[]{:S(2)}) collective-permute-start(bf16[1024,2048]{1,0:T(8,128)(2,1)} %bitcast.48), channel_id=1, source_target_pairs={{0,2},{2,0},{4,6},{6,4},{1,3},{3,1},{5,7},{7,5},{8,10},{10,8},{12,... | collective-permute-start | bytes 12582920 | tf_op jit(solution)/shard_map/ppermute | solution.py:418
  2.1 7.7 %collective-permute-start.4 = (bf16[32,1024]{1,0:T(8,128)(2,1)S(1)}, bf16[32,1024]{1,0:T(8,128)(2,1)S(1)}, u32[]{:S(2)}, u32[]{:S(2)}) collective-permute-start(bf16[32,1024]{1,0:T(8,128)(2,1)S(1)} %get-tuple-element.82), channel_id=1, source_target_pairs={{0,24},{8,16},{16,8},{24,0},{1,25},{9,17},{17,9},{25,1},{2,26},{10... | collective-permute-start | bytes 196616 | tf_op jit(solution)/shard_map/ppermute | solution.py:424
  6.8 5.4 %collective-permute-start.2 = (bf16[32,1024]{1,0:T(8,128)(2,1)S(1)}, bf16[32,1024]{1,0:T(8,128)(2,1)S(1)}, u32[]{:S(2)}, u32[]{:S(2)}) collective-permute-start(bf16[32,1024]{1,0:T(8,128)(2,1)S(1)} %get-tuple-element.83), channel_id=1, source_target_pairs={{0,8},{8,0},{16,24},{24,16},{1,9},{9,1},{17,25},{25,17},{2,10},{10... | collective-permute-start | bytes 196616 | tf_op jit(solution)/shard_map/ppermute | solution.py:424
  6.8 5.9 %collective-permute-start.3 = (bf16[32,1024]{1,0:T(8,128)(2,1)S(1)}, bf16[32,1024]{1,0:T(8,128)(2,1)S(1)}, u32[]{:S(2)}, u32[]{:S(2)}) collective-permute-start(bf16[32,1024]{1,0:T(8,128)(2,1)S(1)} %get-tuple-element.84), channel_id=1, source_target_pairs={{0,16},{8,24},{16,0},{24,8},{1,17},{9,25},{17,1},{25,9},{2,18},{10... | collective-permute-start | bytes 196616 | tf_op jit(solution)/shard_map/ppermute | solution.py:424
  7.4 8.3 %collective-permute-start = (bf16[2,64,1024]{2,1,0:T(8,128)(2,1)}, bf16[2,64,1024]{2,1,0:T(8,128)(2,1)S(1)}, u32[]{:S(2)}, u32[]{:S(2)}) collective-permute-start(bf16[2,64,1024]{2,1,0:T(8,128)(2,1)} %bitcast.46), channel_id=1, source_target_pairs={{0,4},{2,6},{4,0},{6,2},{1,5},{3,7},{5,1},{7,3},{8,12},{10,14},{12... | collective-permute-start | bytes 786440 | tf_op jit(solution)/shard_map/ppermute | solution.py:421
  13.6 1.4 collective-permute-start.5
  15.7 1.0 copy-start
  16.7 0.9 copy-start.5
  17.6 16.6 %copy-start.3 = (bf16[2,1,16,8192]{3,2,1,0:T(8,128)(2,1)S(1)}, bf16[2,1,16,8192]{3,2,1,0:T(8,128)(2,1)}, u32[]{:S(2)}) copy-start(bf16[2,1,16,8192]{3,2,1,0:T(8,128)(2,1)} %param.8) | copy-start | bytes 1572868
  17.7 16.6 %copy-start.4 = (bf16[2,1,16,8192]{3,2,1,0:T(8,128)(2,1)S(1)}, bf16[2,1,16,8192]{3,2,1,0:T(8,128)(2,1)}, u32[]{:S(2)}) copy-start(bf16[2,1,16,8192]{3,2,1,0:T(8,128)(2,1)} %param.9) | copy-start | bytes 1572868
  24.2 58.7 %copy-start.2 = (bf16[2,128,2048]{2,1,0:T(8,128)(2,1)}, bf16[2,128,2048]{2,1,0:T(8,128)(2,1)S(1)}, u32[]{:S(2)}) copy-start(bf16[2,128,2048]{2,1,0:T(8,128)(2,1)S(1)} %get-tuple-element.67.refs_12_) | copy-start | bytes 3145732
  24.2 46.8 %copy-start.6 = (bf16[8192]{0:T(1024)(128)(2,1)S(1)}, bf16[8192]{0:T(1024)(128)(2,1)}, u32[]{:S(2)}) copy-start(bf16[8192]{0:T(1024)(128)(2,1)} %param.13) | copy-start | bytes 49156
  24.2 10.7 %collective-permute-start.11 = (bf16[2,32,2048]{2,1,0:T(8,128)(2,1)S(1)}, bf16[2,32,2048]{2,1,0:T(8,128)(2,1)S(1)}, u32[]{:S(2)}, u32[]{:S(2)}) collective-permute-start(bf16[2,32,2048]{2,1,0:T(8,128)(2,1)S(1)} %get-tuple-element.47), channel_id=1, source_target_pairs={{0,8},{24,16},{1,9},{25,17},{2,10},{26,18},{3,11},{27,19},{4,12},{... | collective-permute-start | bytes 786440 | tf_op jit(solution)/shard_map/ppermute | solution.py:424
  27.6 12.7 %collective-permute-start.10 = (bf16[2,32,2176]{2,1,0:T(8,128)(2,1)S(1)}, bf16[2,32,2176]{2,1,0:T(8,128)(2,1)S(1)}, u32[]{:S(2)}, u32[]{:S(2)}) collective-permute-start(bf16[2,32,2176]{2,1,0:T(8,128)(2,1)S(1)} %get-tuple-element.46), channel_id=1, source_target_pairs={{0,8},{24,16},{1,9},{25,17},{2,10},{26,18},{3,11},{27,19},{4,12},{... | collective-permute-start | bytes 835592 | tf_op jit(solution)/shard_map/ppermute | solution.py:424
  28.9 11.4 %collective-permute-start.8 = (bf16[2,32,2176]{2,1,0:T(8,128)(2,1)S(1)}, bf16[2,32,2176]{2,1,0:T(8,128)(2,1)S(1)}, u32[]{:S(2)}, u32[]{:S(2)}) collective-permute-start(bf16[2,32,2176]{2,1,0:T(8,128)(2,1)S(1)} %get-tuple-element.46), channel_id=1, source_target_pairs={{8,16},{16,8},{9,17},{17,9},{10,18},{18,10},{11,19},{19,11},{12,20... | collective-permute-start | bytes 835592 | tf_op jit(solution)/shard_map/ppermute | solution.py:424
  29.6 6.8 %collective-permute-start.9 = (bf16[2,32,2048]{2,1,0:T(8,128)(2,1)S(1)}, bf16[2,32,2048]{2,1,0:T(8,128)(2,1)S(1)}, u32[]{:S(2)}, u32[]{:S(2)}) collective-permute-start(bf16[2,32,2048]{2,1,0:T(8,128)(2,1)S(1)} %get-tuple-element.47), channel_id=1, source_target_pairs={{8,16},{16,8},{9,17},{17,9},{10,18},{18,10},{11,19},{19,11},{12,20... | collective-permute-start | bytes 786440 | tf_op jit(solution)/shard_map/ppermute | solution.py:424
  30.3 23.6 %collective-permute-start.7 = (bf16[2,2,32,2176]{3,2,1,0:T(8,128)(2,1)S(1)}, bf16[2,2,32,2176]{3,2,1,0:T(8,128)(2,1)S(1)}, u32[]{:S(2)}, u32[]{:S(2)}) collective-permute-start(bf16[2,2,32,2176]{3,2,1,0:T(8,128)(2,1)S(1)} %get-tuple-element.44), channel_id=1, source_target_pairs={{0,8},{8,0},{16,24},{24,16},{1,9},{9,1},{17,25},{25,17},{2,10},{10... | collective-permute-start | bytes 1671176 | tf_op jit(solution)/shard_map/ppermute | solution.py:424
  34.9 12.4 %collective-permute-start.6 = (bf16[2,2,2,16,2048]{4,3,2,1,0:T(8,128)(2,1)S(1)}, bf16[2,2,2,16,2048]{4,3,2,1,0:T(8,128)(2,1)S(1)}, u32[]{:S(2)}, u32[]{:S(2)}) collective-permute-start(bf16[2,2,2,16,2048]{4,3,2,1,0:T(8,128)(2,1)S(1)} %get-tuple-element.43), channel_id=1, source_target_pairs={{0,4},{2,6},{4,0},{6,2},{1,5},{3,7},{5,1},{7,3},{8,12},{10,14},{12... | collective-permute-start | bytes 1572872 | tf_op jit(solution)/shard_map/ppermute | solution.py:421
  40.9 27.7 %collective-permute-start.12 = (bf16[2,32,2304]{2,1,0:T(8,128)(2,1)S(1)}, bf16[2,32,2304]{2,1,0:T(8,128)(2,1)S(1)}, u32[]{:S(2)}, u32[]{:S(2)}) collective-permute-start(bf16[2,32,2304]{2,1,0:T(8,128)(2,1)S(1)} %shard_map.104), channel_id=1, source_target_pairs={{0,16},{8,24},{16,0},{24,8},{1,17},{9,25},{17,1},{25,9},{2,18},{10... | collective-permute-start | bytes 884744 | tf_op jit(solution)/shard_map/ppermute | solution.py:424
  46.0 22.6 %collective-permute-start.13 = (bf16[2,32,2048]{2,1,0:T(8,128)(2,1)S(1)}, bf16[2,32,2048]{2,1,0:T(8,128)(2,1)S(1)}, u32[]{:S(2)}, u32[]{:S(2)}) collective-permute-start(bf16[2,32,2048]{2,1,0:T(8,128)(2,1)S(1)} %shard_map.105), channel_id=1, source_target_pairs={{0,16},{8,24},{16,0},{24,8},{1,17},{9,25},{17,1},{25,9},{2,18},{10... | collective-permute-start | bytes 786440 | tf_op jit(solution)/shard_map/ppermute | solution.py:424
  69.4 42.8 %copy-start.1 = (bf16[1,1,1024,128]{3,2,1,0:T(8,128)(2,1)S(1)}, bf16[1,1,1024,128]{3,2,1,0:T(8,128)(2,1)}, u32[]{:S(2)}) copy-start(bf16[1,1,1024,128]{3,2,1,0:T(8,128)(2,1)} %param.11) | copy-start | bytes 786436
  69.4 6.4 %collective-permute-start.14 = (bf16[2,32,2048]{2,1,0:T(8,128)(2,1)S(1)}, bf16[2,32,2048]{2,1,0:T(8,128)(2,1)S(1)}, u32[]{:S(2)}, u32[]{:S(2)}) collective-permute-start(bf16[2,32,2048]{2,1,0:T(8,128)(2,1)S(1)} %get-tuple-element.54), channel_id=1, source_target_pairs={{0,1},{1,0},{2,3},{3,2},{4,5},{5,4},{6,7},{7,6},{8,9},{9,8},{10,11... | collective-permute-start | bytes 786440 | tf_op jit(solution)/shard_map/ppermute | solution.py:505
  76.7 8.1 %collective-permute-start.15 = (bf16[2,32,2048]{2,1,0:T(8,128)(2,1)S(1)}, bf16[2,32,2048]{2,1,0:T(8,128)(2,1)S(1)}, u32[]{:S(2)}, u32[]{:S(2)}) collective-permute-start(bf16[2,32,2048]{2,1,0:T(8,128)(2,1)S(1)} %get-tuple-element.56), channel_id=1, source_target_pairs={{0,1},{1,0},{2,3},{3,2},{4,5},{5,4},{6,7},{7,6},{8,9},{9,8},{10,11... | collective-permute-start | bytes 786440 | tf_op jit(solution)/shard_map/ppermute | solution.py:505
  78.3 3.7 %collective-permute-start.17 = (f32[32,128]{1,0:T(8,128)S(1)}, f32[32,128]{1,0:T(8,128)S(1)}, u32[]{:S(2)}, u32[]{:S(2)}) collective-permute-start(f32[32,128]{1,0:T(8,128)S(1)} %get-tuple-element.60.sums), channel_id=1, source_target_pairs={{0,4},{2,6},{4,0},{6,2},{1,5},{3,7},{5,1},{7,3},{8,12},{10,14},{12... | collective-permute-start | bytes 49160 | tf_op jit(solution)/shard_map/ppermute | solution.py:421
  82.8 9.7 %collective-permute-start.19 = (bf16[2,32,2048]{2,1,0:T(8,128)(2,1)S(1)}, bf16[2,32,2048]{2,1,0:T(8,128)(2,1)S(1)}, u32[]{:S(2)}, u32[]{:S(2)}) collective-permute-start(bf16[2,32,2048]{2,1,0:T(8,128)(2,1)S(1)} %shard_map.110.refs_0_), channel_id=1, source_target_pairs={{0,16},{8,24},{16,0},{24,8},{1,17},{9,25},{17,1},{25,9},{2,18},{10... | collective-permute-start | bytes 786440 | tf_op jit(solution)/shard_map/ppermute | solution.py:424
  82.9 9.6 %collective-permute-start.18 = (bf16[2,32,2048]{2,1,0:T(8,128)(2,1)S(1)}, bf16[2,32,2048]{2,1,0:T(8,128)(2,1)S(1)}, u32[]{:S(2)}, u32[]{:S(2)}) collective-permute-start(bf16[2,32,2048]{2,1,0:T(8,128)(2,1)S(1)} %shard_map.110.refs_0_), channel_id=1, source_target_pairs={{0,8},{8,0},{16,24},{24,16},{1,9},{9,1},{17,25},{25,17},{2,10},{10... | collective-permute-start | bytes 786440 | tf_op jit(solution)/shard_map/ppermute | solution.py:424
  84.8 7.7 %collective-permute-start.20 = (bf16[2,32,2048]{2,1,0:T(8,128)(2,1)S(1)}, bf16[2,32,2048]{2,1,0:T(8,128)(2,1)S(1)}, u32[]{:S(2)}, u32[]{:S(2)}) collective-permute-start(bf16[2,32,2048]{2,1,0:T(8,128)(2,1)S(1)} %shard_map.110.refs_0_), channel_id=1, source_target_pairs={{0,1},{1,0},{2,3},{3,2},{4,5},{5,4},{6,7},{7,6},{8,9},{9,8},{10,11... | collective-permute-start | bytes 786440 | tf_op jit(solution)/shard_map/ppermute | solution.py:505
  87.2 6.6 %collective-permute-start.16 = (bf16[2,2,16,2048]{3,2,1,0:T(8,128)(2,1)S(1)}, bf16[2,2,16,2048]{3,2,1,0:T(8,128)(2,1)S(1)}, u32[]{:S(2)}, u32[]{:S(2)}) collective-permute-start(bf16[2,2,16,2048]{3,2,1,0:T(8,128)(2,1)S(1)} %get-tuple-element.59), channel_id=1, source_target_pairs={{0,4},{2,6},{4,0},{6,2},{1,5},{3,7},{5,1},{7,3},{8,12},{10,14},{12... | collective-permute-start | bytes 786440 | tf_op jit(solution)/shard_map/ppermute | solution.py:421
  92.5 8.3 %collective-permute-start.22 = (bf16[2,32,2048]{2,1,0:T(8,128)(2,1)S(1)}, bf16[2,32,2048]{2,1,0:T(8,128)(2,1)S(1)}, u32[]{:S(2)}, u32[]{:S(2)}) collective-permute-start(bf16[2,32,2048]{2,1,0:T(8,128)(2,1)S(1)} %collective-permute-done.19.refs_2_), channel_id=1, source_target_pairs={{8,0},{16,24},{9,1},{17,25},{10,2},{18,26},{11,3},{19,27},{12,4},{... | collective-permute-start | bytes 786440 | tf_op jit(solution)/shard_map/ppermute | solution.py:424
  93.8 7.4 %collective-permute-start.23 = (bf16[2,32,2048]{2,1,0:T(8,128)(2,1)S(1)}, bf16[2,32,2048]{2,1,0:T(8,128)(2,1)S(1)}, u32[]{:S(2)}, u32[]{:S(2)}) collective-permute-start(bf16[2,32,2048]{2,1,0:T(8,128)(2,1)S(1)} %collective-permute-done.18.refs_1_), channel_id=1, source_target_pairs={{0,1},{1,0},{2,3},{3,2},{4,5},{5,4},{6,7},{7,6},{8,9},{9,8},{10,11... | collective-permute-start | bytes 786440 | tf_op jit(solution)/shard_map/ppermute | solution.py:505
  95.5 5.7 %collective-permute-start.21 = (bf16[2,32,2048]{2,1,0:T(8,128)(2,1)S(1)}, bf16[2,32,2048]{2,1,0:T(8,128)(2,1)S(1)}, u32[]{:S(2)}, u32[]{:S(2)}) collective-permute-start(bf16[2,32,2048]{2,1,0:T(8,128)(2,1)S(1)} %shard_map.110.refs_0_), channel_id=1, source_target_pairs={{8,16},{16,8},{9,17},{17,9},{10,18},{18,10},{11,19},{19,11},{12,20... | collective-permute-start | bytes 786440 | tf_op jit(solution)/shard_map/ppermute | solution.py:424
  96.2 9.7 %collective-permute-start.24 = (bf16[2,32,2048]{2,1,0:T(8,128)(2,1)S(1)}, bf16[2,32,2048]{2,1,0:T(8,128)(2,1)S(1)}, u32[]{:S(2)}, u32[]{:S(2)}) collective-permute-start(bf16[2,32,2048]{2,1,0:T(8,128)(2,1)S(1)} %collective-permute-done.19.refs_2_), channel_id=1, source_target_pairs={{0,1},{1,0},{2,3},{3,2},{4,5},{5,4},{6,7},{7,6},{8,9},{9,8},{10,11... | collective-permute-start | bytes 786440 | tf_op jit(solution)/shard_map/ppermute | solution.py:505
  105.9 6.4 %collective-permute-start.25 = (bf16[2,32,2048]{2,1,0:T(8,128)(2,1)S(1)}, bf16[2,32,2048]{2,1,0:T(8,128)(2,1)S(1)}, u32[]{:S(2)}, u32[]{:S(2)}) collective-permute-start(bf16[2,32,2048]{2,1,0:T(8,128)(2,1)S(1)} %shard_map.111.refs_3_), channel_id=1, source_target_pairs={{0,1},{1,0},{2,3},{3,2},{4,5},{5,4},{6,7},{7,6},{8,9},{9,8},{10,11... | collective-permute-start | bytes 786440 | tf_op jit(solution)/shard_map/ppermute | solution.py:505
  120.2 2.5 %collective-permute-start.27 = (f32[192,1024]{1,0:T(8,128)}, f32[192,1024]{1,0:T(8,128)S(1)}, u32[]{:S(2)}, u32[]{:S(2)}) collective-permute-start(f32[192,1024]{1,0:T(8,128)} %get-tuple-element.73), channel_id=1, source_target_pairs={{0,2},{2,0},{4,6},{6,4},{1,3},{3,1},{5,7},{7,5},{8,10},{10,8},{12,... | collective-permute-start | bytes 2359304 | tf_op jit(solution)/shard_map/ppermute | solution.py:418
  122.8 11.2 %collective-permute-start.28 = (bf16[192,1024]{1,0:T(8,128)(2,1)S(1)}, bf16[192,1024]{1,0:T(8,128)(2,1)S(1)}, u32[]{:S(2)}, u32[]{:S(2)}) collective-permute-start(bf16[192,1024]{1,0:T(8,128)(2,1)S(1)} %add_convert_fusion.own_right), channel_id=1, source_target_pairs={{0,4},{2,6},{4,0},{6,2},{1,5},{3,7},{5,1},{7,3},{8,12},{10,14},{12... | collective-permute-start | bytes 1179656 | tf_op jit(solution)/shard_map/ppermute | solution.py:421
  134.0 4.5 %collective-permute-start.29 = (bf16[128,1024]{1,0:T(8,128)(2,1)S(1)}, bf16[128,1024]{1,0:T(8,128)(2,1)S(1)}, u32[]{:S(2)}, u32[]{:S(2)}) collective-permute-start(bf16[128,1024]{1,0:T(8,128)(2,1)S(1)} %slice_select_fusion.own_left), channel_id=1, source_target_pairs={{0,2},{2,0},{4,6},{6,4},{1,3},{3,1},{5,7},{7,5},{8,10},{10,8},{12,... | collective-permute-start | bytes 786440 | tf_op jit(solution)/shard_map/ppermute | solution.py:418
  134.1 8.7 %collective-permute-start.26 = (bf16[2,64,1024]{2,1,0:T(8,128)(2,1)S(1)}, bf16[2,64,1024]{2,1,0:T(8,128)(2,1)S(1)}, u32[]{:S(2)}, u32[]{:S(2)}) collective-permute-start(bf16[2,64,1024]{2,1,0:T(8,128)(2,1)S(1)} %get-tuple-element.71), channel_id=1, source_target_pairs={{0,4},{2,6},{4,0},{6,2},{1,5},{3,7},{5,1},{7,3},{8,12},{10,14},{12... | collective-permute-start | bytes 786440 | tf_op jit(solution)/shard_map/ppermute | solution.py:421

commit v5 on v4

--- a/solution.py
+++ b/solution.py
@@ -38,7 +38,7 @@
 NO_COST = pl.CostEstimate(flops=0, bytes_accessed=0, transcendentals=0)
 
 
-def small(kernel, outs, scratch, place, *values):
+def small(kernel, outs, scratch, place, *values, cost=NO_COST):
     vmem = pl.BlockSpec(memory_space=pltpu.VMEM)
     return pl.pallas_call(
         kernel,
@@ -47,7 +47,7 @@
         out_shape=[jax.ShapeDtypeStruct(shape, dtype) for shape, dtype in outs],
         scratch_shapes=scratch,
         compiler_params=pltpu.CompilerParams(vmem_limit_bytes=VMEM_SMALL),
-        cost_estimate=NO_COST,
+        cost_estimate=cost,
     )(place, *values)
 
 
@@ -374,7 +374,7 @@
             pltpu.VMEM((rank, micro * size), BF16),
             pltpu.VMEM((rank, head_cols), F32),
         ],
-        compiler_params=pltpu.CompilerParams(vmem_limit_bytes=VMEM_ALL),
+        compiler_params=pltpu.CompilerParams(vmem_limit_bytes=VMEM),
         cost_estimate=NO_COST,
     )(place, *pieces, *doubled(weights), left_rows, right, mix_rows, *permuted)
 
@@ -389,6 +389,10 @@
             out[m ^ section, :, at] = here[m, slot]
             at = pl.ds(pl.multiple_of((2 * (1 - outer) + part) * width, width), width)
             out[m ^ section, :, at] = arrived[m, slot]
+
+
+def add_kernel(place, here, arrived, total):
+    total[...] = (here[...] + arrived[...].astype(F32)).astype(BF16)
 
 
 def left_kernel(place, own_left, other_left, grad_left):
@@ -551,7 +555,7 @@
     mix_here, mix_sent, kept_factors, sent_factors = back(
         place, pieces, weights, left_rows, right, mix_rows, permuted
     )
-    joined = (kept_factors + to_core(sent_factors)).astype(BF16)
+    joined = (kept_factors + after(to_core(sent_factors), section_out)).astype(BF16)
     other_joined = to_outer(joined)
     best = jnp.where(outer == t // 2, joined[:rank], other_joined[:rank])
     (grad_right,) = small(
@@ -563,9 +567,23 @@
         other_joined,
     )
     (grad_left,) = small(
-        left_kernel, [((rank, width), F32)], [], place, best, after(to_core(best), grad_right)
-    )
-    grad_mix = (mix_here + after(to_outer(mix_sent), grad_left).astype(F32)).astype(BF16)
+        left_kernel,
+        [((rank, width), F32)],
+        [],
+        place,
+        best,
+        after(to_core(best), grad_right),
+        cost=pl.CostEstimate(flops=8 * 10**9, bytes_accessed=0, transcendentals=0),
+    )
+    (grad_mix,) = small(
+        add_kernel,
+        [(mix_here.shape, BF16)],
+        [],
+        place,
+        mix_here,
+        after(to_outer(mix_sent), grad_right),
+        cost=pl.CostEstimate(flops=5 * 10**9, bytes_accessed=0, transcendentals=0),
+    )
     grad_mix = grad_mix.reshape(1, micro, 1, tokens, head_cols)
 
     return (

time: 144 us -> 142 us (0.986)
    pallas_call x1, Pallas kernels: 7.92 us -> 6.38 us  [back(): pl.pallas_call(functools.partial(back_kernel, micro), grid=(tiles,), in_s...]
    pallas_call x11 -> x12, Pallas kernels: 10 us -> 11.3 us  [small(): pl.pallas_call(kernel, in_specs=[pl.BlockSpec(memory_space=pltpu.SMEM)] +...]
  transfers between devices with their start and end apart: 30 -> 30, of which waited for: 19 -> 20; matrix products, arithmetic and copies ran while one was open for 1% -> 1% of each run, Pallas kernels for 6% -> 6%
where the time goes in v5:
time: 142 us; the launch traced here: 141 us
  waiting for transfers between devices  70.7 us (50%)
  starting transfers between devices  41.4 us (29%)
  Pallas kernels  24.2 us (17%)
  local copies, waits for them, and re-layouts  2.84 us (2%)
    ppermute x14, waiting for transfers between devices, along(): return lax.ppermute(value, 'tensor', pairs)  36.8 us
    ppermute x14, starting transfers between devices, along(): return lax.ppermute(value, 'tensor', pairs)  23.7 us
    ppermute x6, waiting for transfers between devices, to_outer(): return lax.ppermute(value, 'dp', [(i, i ^ 2) for i in range(4)])  17.4 us
    ppermute x6, waiting for transfers between devices, to_section(): return lax.ppermute(value, 'pipe', [(0, 1), (1, 0)])  14.1 us
    pallas_call x12, Pallas kernels, small(): pl.pallas_call(kernel, in_specs=[pl.BlockSpec(memory_space=pltpu.SMEM)] +...  11.3 us
    ppermute x6, starting transfers between devices, to_section(): return lax.ppermute(value, 'pipe', [(0, 1), (1, 0)])  8.65 us
    ppermute x6, starting transfers between devices, to_outer(): return lax.ppermute(value, 'dp', [(i, i ^ 2) for i in range(4)])  8.31 us
    pallas_call x1, Pallas kernels, project(): pl.pallas_call(project_kernel, grid=(tiles,), in_specs=[pl.BlockSpec(memo...  6.49 us
  transfers between devices with their start and end apart: 30, of which 20 were waited for; matrix products, arithmetic and copies ran while one was open for 1% of the time, Pallas kernels for 6%

profile of v5, /device:TPU:0, one launch (start us, length us, event | category | flops | bytes accessed | tf_op | source)
XLA Modules:
  0.0 141.0 jit_solution(13679977344629734799)
XLA Ops:
  0.6 0.5 collective-permute-start.1
  1.1 0.9 dynamic-slice_bitcast_fusion
  2.1 4.7 %collective-permute-start.4 = (bf16[32,1024]{1,0:T(8,128)(2,1)S(1)}, bf16[32,1024]{1,0:T(8,128)(2,1)S(1)}, u32[]{:S(2)}, u32[]{:S(2)}) collective-permute-start(bf16[32,1024]{1,0:T(8,128)(2,1)S(1)} %get-tuple-element.84), channel_id=1, source_target_pairs={{0,24},{8,16},{16,8},{24,0},{1,25},{9,17},{17,9},{25,1},{2,26},{10... | collective-permute-start | bytes 196616 | tf_op jit(solution)/shard_map/ppermute | solution.py:428
  6.8 0.6 collective-permute-start.3
  7.4 1.6 %collective-permute-start = (bf16[2,64,1024]{2,1,0:T(8,128)(2,1)}, bf16[2,64,1024]{2,1,0:T(8,128)(2,1)S(1)}, u32[]{:S(2)}, u32[]{:S(2)}) collective-permute-start(bf16[2,64,1024]{2,1,0:T(8,128)(2,1)} %bitcast.50), channel_id=1, source_target_pairs={{0,4},{2,6},{4,0},{6,2},{1,5},{3,7},{5,1},{7,3},{8,12},{10,14},{12... | collective-permute-start | bytes 786440 | tf_op jit(solution)/shard_map/ppermute | solution.py:425
  9.1 0.7 collective-permute-done.4
  9.8 2.5 %collective-permute-done.2 = bf16[32,1024]{1,0:T(8,128)(2,1)S(1)} collective-permute-done((bf16[32,1024]{1,0:T(8,128)(2,1)S(1)}, bf16[32,1024]{1,0:T(8,128)(2,1)S(1)}, u32[]{:S(2)}, u32[]{:S(2)}) %collective-permute-start.2) | collective-permute-done | bytes 65568 | tf_op jit(solution)/shard_map/ppermute | solution.py:428
  12.3 0.4 collective-permute-done.3
  12.7 0.9 fusion.1
  13.7 1.3 collective-permute-done.5.other_half
  15.0 0.7 collective-permute-done.other_mix
  15.7 0.9 copy-done.1
  16.7 0.9 copy-done.4
  17.7 6.5 %shard_map.102 = (bf16[2,2,32,2048]{3,2,1,0:T(8,128)(2,1)S(1)}, bf16[2,2,32,2176]{3,2,1,0:T(8,128)(2,1)S(1)}, bf16[2,32,2176]{2,1,0:T(8,128)(2,1)S(1)}, bf16[2,3...) custom-call(s32[4]{0:T(128)S(1)} %pad_add_fusion.place, ...), custom_call_target="tpu_custom_call" | custom-call | tf_op jit(solution)/shard_map/pallas_call | solution.py:240
  24.2 3.3 %collective-permute-start.11 = (bf16[2,32,2048]{2,1,0:T(8,128)(2,1)S(1)}, bf16[2,32,2048]{2,1,0:T(8,128)(2,1)S(1)}, u32[]{:S(2)}, u32[]{:S(2)}) collective-permute-start(bf16[2,32,2048]{2,1,0:T(8,128)(2,1)S(1)} %get-tuple-element.48), channel_id=1, source_target_pairs={{0,8},{24,16},{1,9},{25,17},{2,10},{26,18},{3,11},{27,19},{4,12},{... | collective-permute-start | bytes 786440 | tf_op jit(solution)/shard_map/ppermute | solution.py:428
  27.5 1.3 collective-permute-start.10
  28.8 0.7 collective-permute-start.8
  29.5 0.7 collective-permute-start.9
  30.2 3.9 %collective-permute-start.7 = (bf16[2,2,32,2176]{3,2,1,0:T(8,128)(2,1)S(1)}, bf16[2,2,32,2176]{3,2,1,0:T(8,128)(2,1)S(1)}, u32[]{:S(2)}, u32[]{:S(2)}) collective-permute-start(bf16[2,2,32,2176]{3,2,1,0:T(8,128)(2,1)S(1)} %get-tuple-element.45), channel_id=1, source_target_pairs={{0,8},{8,0},{16,24},{24,16},{1,9},{9,1},{17,25},{25,17},{2,10},{10... | collective-permute-start | bytes 1671176 | tf_op jit(solution)/shard_map/ppermute | solution.py:428
  34.1 0.6 shard_map.103
  34.7 1.6 %collective-permute-start.6 = (bf16[2,2,2,16,2048]{4,3,2,1,0:T(8,128)(2,1)S(1)}, bf16[2,2,2,16,2048]{4,3,2,1,0:T(8,128)(2,1)S(1)}, u32[]{:S(2)}, u32[]{:S(2)}) collective-permute-start(bf16[2,2,2,16,2048]{4,3,2,1,0:T(8,128)(2,1)S(1)} %get-tuple-element.44), channel_id=1, source_target_pairs={{0,4},{2,6},{4,0},{6,2},{1,5},{3,7},{5,1},{7,3},{8,12},{10,14},{12... | collective-permute-start | bytes 1572872 | tf_op jit(solution)/shard_map/ppermute | solution.py:425
  36.3 3.9 %collective-permute-done.10.passed = bf16[2,32,2176]{2,1,0:T(8,128)(2,1)S(1)} collective-permute-done((bf16[2,32,2176]{2,1,0:T(8,128)(2,1)S(1)}, bf16[2,32,2176]{2,1,0:T(8,128)(2,1)S(1)}, u32[]{:S(2)}, u32[]{:S(2)}) %collective-permute-start.10) | collective-permute-done | bytes 278560 | tf_op jit(solution)/shard_map/ppermute | solution.py:428
  40.2 0.6 shard_map.104
  40.8 4.4 %collective-permute-start.12 = (bf16[2,32,2304]{2,1,0:T(8,128)(2,1)S(1)}, bf16[2,32,2304]{2,1,0:T(8,128)(2,1)S(1)}, u32[]{:S(2)}, u32[]{:S(2)}) collective-permute-start(bf16[2,32,2304]{2,1,0:T(8,128)(2,1)S(1)} %shard_map.104), channel_id=1, source_target_pairs={{0,16},{8,24},{16,0},{24,8},{1,17},{9,25},{17,1},{25,9},{2,18},{10... | collective-permute-start | bytes 884744 | tf_op jit(solution)/shard_map/ppermute | solution.py:428
  45.2 0.6 shard_map.105
  45.8 0.1 collective-permute-start.13
  45.9 1.2 collective-permute-done.6.arrived
  47.1 6.7 %collective-permute-done.7.beside.refs_16_ = bf16[2,2,32,2176]{3,2,1,0:T(8,128)(2,1)S(1)} collective-permute-done((bf16[2,2,32,2176]{3,2,1,0:T(8,128)(2,1)S(1)}, bf16[2,2,32,2176]{3,2,1,0:T(8,128)(2,1)S(1)}, u32[]{:S(2)}, u32[]{:S(2)}) %collective-permute-start.7) | collective-permute-done | bytes 557088 | tf_op jit(solution)/shard_map/ppermute | solution.py:428
  53.8 14.7 %collective-permute-done.13.refs_3_ = bf16[2,32,2048]{2,1,0:T(8,128)(2,1)S(1)} collective-permute-done((bf16[2,32,2048]{2,1,0:T(8,128)(2,1)S(1)}, bf16[2,32,2048]{2,1,0:T(8,128)(2,1)S(1)}, u32[]{:S(2)}, u32[]{:S(2)}) %collective-permute-start.13) | collective-permute-done | bytes 262176 | tf_op jit(solution)/shard_map/ppermute | solution.py:428
  68.5 0.8 shard_map.106
  69.3 1.6 %collective-permute-start.14 = (bf16[2,32,2048]{2,1,0:T(8,128)(2,1)S(1)}, bf16[2,32,2048]{2,1,0:T(8,128)(2,1)S(1)}, u32[]{:S(2)}, u32[]{:S(2)}) collective-permute-start(bf16[2,32,2048]{2,1,0:T(8,128)(2,1)S(1)} %get-tuple-element.55), channel_id=1, source_target_pairs={{0,1},{1,0},{2,3},{3,2},{4,5},{5,4},{6,7},{7,6},{8,9},{9,8},{10,11... | collective-permute-start | bytes 786440 | tf_op jit(solution)/shard_map/ppermute | solution.py:509
  70.9 4.9 %collective-permute-done.14.other = bf16[2,32,2048]{2,1,0:T(8,128)(2,1)S(1)} collective-permute-done((bf16[2,32,2048]{2,1,0:T(8,128)(2,1)S(1)}, bf16[2,32,2048]{2,1,0:T(8,128)(2,1)S(1)}, u32[]{:S(2)}, u32[]{:S(2)}) %collective-permute-start.14) | collective-permute-done | bytes 262176 | tf_op jit(solution)/shard_map/ppermute | solution.py:509
  75.7 0.9 shard_map.107
  76.6 1.6 %collective-permute-start.15 = (bf16[2,32,2048]{2,1,0:T(8,128)(2,1)S(1)}, bf16[2,32,2048]{2,1,0:T(8,128)(2,1)S(1)}, u32[]{:S(2)}, u32[]{:S(2)}) collective-permute-start(bf16[2,32,2048]{2,1,0:T(8,128)(2,1)S(1)} %get-tuple-element.57), channel_id=1, source_target_pairs={{0,1},{1,0},{2,3},{3,2},{4,5},{5,4},{6,7},{7,6},{8,9},{9,8},{10,11... | collective-permute-start | bytes 786440 | tf_op jit(solution)/shard_map/ppermute | solution.py:509
  78.2 1.5 %collective-permute-start.17 = (f32[32,128]{1,0:T(8,128)S(1)}, f32[32,128]{1,0:T(8,128)S(1)}, u32[]{:S(2)}, u32[]{:S(2)}) collective-permute-start(f32[32,128]{1,0:T(8,128)S(1)} %get-tuple-element.61.sums), channel_id=1, source_target_pairs={{0,4},{2,6},{4,0},{6,2},{1,5},{3,7},{5,1},{7,3},{8,12},{10,14},{12... | collective-permute-start | bytes 49160 | tf_op jit(solution)/shard_map/ppermute | solution.py:425
  79.7 2.3 %collective-permute-done.17.other_sums = f32[32,128]{1,0:T(8,128)S(1)} collective-permute-done((f32[32,128]{1,0:T(8,128)S(1)}, f32[32,128]{1,0:T(8,128)S(1)}, u32[]{:S(2)}, u32[]{:S(2)}) %collective-permute-start.17) | collective-permute-done | bytes 16416 | tf_op jit(solution)/shard_map/ppermute | solution.py:425
  81.9 0.8 shard_map.110.refs_0_
  82.8 1.9 %collective-permute-start.18 = (bf16[2,32,2048]{2,1,0:T(8,128)(2,1)S(1)}, bf16[2,32,2048]{2,1,0:T(8,128)(2,1)S(1)}, u32[]{:S(2)}, u32[]{:S(2)}) collective-permute-start(bf16[2,32,2048]{2,1,0:T(8,128)(2,1)S(1)} %shard_map.110.refs_0_), channel_id=1, source_target_pairs={{0,8},{8,0},{16,24},{24,16},{1,9},{9,1},{17,25},{25,17},{2,10},{10... | collective-permute-start | bytes 786440 | tf_op jit(solution)/shard_map/ppermute | solution.py:428
  84.7 1.7 %collective-permute-start.20 = (bf16[2,32,2048]{2,1,0:T(8,128)(2,1)S(1)}, bf16[2,32,2048]{2,1,0:T(8,128)(2,1)S(1)}, u32[]{:S(2)}, u32[]{:S(2)}) collective-permute-start(bf16[2,32,2048]{2,1,0:T(8,128)(2,1)S(1)} %shard_map.110.refs_0_), channel_id=1, source_target_pairs={{0,1},{1,0},{2,3},{3,2},{4,5},{5,4},{6,7},{7,6},{8,9},{9,8},{10,11... | collective-permute-start | bytes 786440 | tf_op jit(solution)/shard_map/ppermute | solution.py:509
  86.4 0.7 shard_map.108
  87.1 1.5 %collective-permute-start.16 = (bf16[2,2,16,2048]{3,2,1,0:T(8,128)(2,1)S(1)}, bf16[2,2,16,2048]{3,2,1,0:T(8,128)(2,1)S(1)}, u32[]{:S(2)}, u32[]{:S(2)}) collective-permute-start(bf16[2,2,16,2048]{3,2,1,0:T(8,128)(2,1)S(1)} %get-tuple-element.60), channel_id=1, source_target_pairs={{0,4},{2,6},{4,0},{6,2},{1,5},{3,7},{5,1},{7,3},{8,12},{10,14},{12... | collective-permute-start | bytes 786440 | tf_op jit(solution)/shard_map/ppermute | solution.py:425
  88.6 3.8 %collective-permute-done.18.refs_1_ = bf16[2,32,2048]{2,1,0:T(8,128)(2,1)S(1)} collective-permute-done((bf16[2,32,2048]{2,1,0:T(8,128)(2,1)S(1)}, bf16[2,32,2048]{2,1,0:T(8,128)(2,1)S(1)}, u32[]{:S(2)}, u32[]{:S(2)}) %collective-permute-start.18) | collective-permute-done | bytes 262176 | tf_op jit(solution)/shard_map/ppermute | solution.py:428
  92.4 1.3 collective-permute-start.22
  93.7 1.7 %collective-permute-start.23 = (bf16[2,32,2048]{2,1,0:T(8,128)(2,1)S(1)}, bf16[2,32,2048]{2,1,0:T(8,128)(2,1)S(1)}, u32[]{:S(2)}, u32[]{:S(2)}) collective-permute-start(bf16[2,32,2048]{2,1,0:T(8,128)(2,1)S(1)} %collective-permute-done.18.refs_1_), channel_id=1, source_target_pairs={{0,1},{1,0},{2,3},{3,2},{4,5},{5,4},{6,7},{7,6},{8,9},{9,8},{10,11... | collective-permute-start | bytes 786440 | tf_op jit(solution)/shard_map/ppermute | solution.py:509
  95.4 0.7 collective-permute-start.21
  96.1 0.5 collective-permute-start.24
  96.5 4.1 %collective-permute-done.22.farthest = bf16[2,32,2048]{2,1,0:T(8,128)(2,1)S(1)} collective-permute-done((bf16[2,32,2048]{2,1,0:T(8,128)(2,1)S(1)}, bf16[2,32,2048]{2,1,0:T(8,128)(2,1)S(1)}, u32[]{:S(2)}, u32[]{:S(2)}) %collective-permute-start.22) | collective-permute-done | bytes 262176 | tf_op jit(solution)/shard_map/ppermute | solution.py:428
  100.7 0.5 collective-permute-done.23.refs_5_
  101.2 0.6 shard_map.111.refs_3_
  101.7 4.0 %collective-permute-done.24.refs_6_ = bf16[2,32,2048]{2,1,0:T(8,128)(2,1)S(1)} collective-permute-done((bf16[2,32,2048]{2,1,0:T(8,128)(2,1)S(1)}, bf16[2,32,2048]{2,1,0:T(8,128)(2,1)S(1)}, u32[]{:S(2)}, u32[]{:S(2)}) %collective-permute-start.24) | collective-permute-done | bytes 262176 | tf_op jit(solution)/shard_map/ppermute | solution.py:509
  105.8 1.6 %collective-permute-start.25 = (bf16[2,32,2048]{2,1,0:T(8,128)(2,1)S(1)}, bf16[2,32,2048]{2,1,0:T(8,128)(2,1)S(1)}, u32[]{:S(2)}, u32[]{:S(2)}) collective-permute-start(bf16[2,32,2048]{2,1,0:T(8,128)(2,1)S(1)} %shard_map.111.refs_3_), channel_id=1, source_target_pairs={{0,1},{1,0},{2,3},{3,2},{4,5},{5,4},{6,7},{7,6},{8,9},{9,8},{10,11... | collective-permute-start | bytes 786440 | tf_op jit(solution)/shard_map/ppermute | solution.py:509
  107.4 4.8 %collective-permute-done.25.refs_7_ = bf16[2,32,2048]{2,1,0:T(8,128)(2,1)S(1)} collective-permute-done((bf16[2,32,2048]{2,1,0:T(8,128)(2,1)S(1)}, bf16[2,32,2048]{2,1,0:T(8,128)(2,1)S(1)}, u32[]{:S(2)}, u32[]{:S(2)}) %collective-permute-start.25) | collective-permute-done | bytes 262176 | tf_op jit(solution)/shard_map/ppermute | solution.py:509
  112.1 6.4 %shard_map.112 = (f32[2,64,1024]{2,1,0:T(8,128)S(1)}, bf16[2,64,1024]{2,1,0:T(8,128)(2,1)S(1)}, f32[192,1024]{1,0:T(8,128)S(1)}, f32[192,1024]{1,0:T(8,128)S(1)}) custom-call(s32[4]{0:T(128)S(1)} %pad_add_fusion.place, bf16[2,32,2048]{2,1,0:T(8,128)(2,1)S(1)} %shard_map.110.refs_0_, bf16[2,32,2048]{2,1,0:T(8,128)(2,1)S(1)} %collective-permute-done.18.refs_1_, ...), custom_call_target="tpu_custom_call" | custom-call | tf_op jit(solution)/shard_map/pallas_call | solution.py:351
  118.6 1.4 shard_map.109
  120.0 0.9 collective-permute-done.27
  120.9 0.1 add_convert_fusion.own_right
  121.0 1.5 %collective-permute-start.28 = (bf16[192,1024]{1,0:T(8,128)(2,1)S(1)}, bf16[192,1024]{1,0:T(8,128)(2,1)S(1)}, u32[]{:S(2)}, u32[]{:S(2)}) collective-permute-start(bf16[192,1024]{1,0:T(8,128)(2,1)S(1)} %add_convert_fusion.own_right), channel_id=1, source_target_pairs={{0,4},{2,6},{4,0},{6,2},{1,5},{3,7},{5,1},{7,3},{8,12},{10,14},{12... | collective-permute-start | bytes 1179656 | tf_op jit(solution)/shard_map/ppermute | solution.py:425
  122.5 0.6 collective-permute-start.26
  123.1 9.9 %collective-permute-done.28.other_right = bf16[192,1024]{1,0:T(8,128)(2,1)S(1)} collective-permute-done((bf16[192,1024]{1,0:T(8,128)(2,1)S(1)}, bf16[192,1024]{1,0:T(8,128)(2,1)S(1)}, u32[]{:S(2)}, u32[]{:S(2)}) %collective-permute-start.28) | collective-permute-done | bytes 393248 | tf_op jit(solution)/shard_map/ppermute | solution.py:425
  133.0 1.6 %shard_map.113 = f32[1024,128]{1,0:T(8,128)} custom-call(s32[4]{0:T(128)S(1)} %pad_add_fusion.place, bf16[192,1024]{1,0:T(8,128)(2,1)S(1)} %add_convert_fusion.own_right, bf16[192,1024]{1,0:T(8,128)(2,1)S(1)} %collective-permute-done.28.other_right), custom_call_target="tpu_custom_call" | custom-call | tf_op jit(solution)/shard_map/pallas_call | solution.py:43
  134.6 3.2 %collective-permute-done.26.arrived = bf16[2,64,1024]{2,1,0:T(8,128)(2,1)S(1)} collective-permute-done((bf16[2,64,1024]{2,1,0:T(8,128)(2,1)S(1)}, bf16[2,64,1024]{2,1,0:T(8,128)(2,1)S(1)}, u32[]{:S(2)}, u32[]{:S(2)}) %collective-permute-start.26) | collective-permute-done | bytes 262176 | tf_op jit(solution)/shard_map/ppermute | solution.py:425
  137.9 1.3 shard_map.114
  139.2 0.2 collective-permute-done.29.other_left
  139.5 1.6 %shard_map.115 = f32[128,2048]{1,0:T(8,128)} custom-call(s32[4]{0:T(128)S(1)} %pad_add_fusion.place, bf16[128,1024]{1,0:T(8,128)(2,1)S(1)} %slice_select_fusion.own_left, bf16[128,1024]{1,0:T(8,128)(2,1)S(1)} %collective-permute-done.29.other_left), custom_call_target="tpu_custom_call" | custom-call | flops 8000000000 | tf_op jit(solution)/shard_map/pallas_call | solution.py:43
  (29 shorter events, 0.5 us)
Async XLA Ops:
  0.6 15.1 %collective-permute-start.1 = (bf16[1024,2048]{1,0:T(8,128)(2,1)}, bf16[1024,2048]{1,0:T(8,128)(2,1)}, u32[]{:S(2)}, u32[]{:S(2)}) collective-permute-start(bf16[1024,2048]{1,0:T(8,128)(2,1)} %bitcast.39), channel_id=1, source_target_pairs={{0,2},{2,0},{4,6},{6,4},{1,3},{3,1},{5,7},{7,5},{8,10},{10,8},{12,... | collective-permute-start | bytes 12582920 | tf_op jit(solution)/shard_map/ppermute | solution.py:422
  2.1 7.7 %collective-permute-start.4 = (bf16[32,1024]{1,0:T(8,128)(2,1)S(1)}, bf16[32,1024]{1,0:T(8,128)(2,1)S(1)}, u32[]{:S(2)}, u32[]{:S(2)}) collective-permute-start(bf16[32,1024]{1,0:T(8,128)(2,1)S(1)} %get-tuple-element.84), channel_id=1, source_target_pairs={{0,24},{8,16},{16,8},{24,0},{1,25},{9,17},{17,9},{25,1},{2,26},{10... | collective-permute-start | bytes 196616 | tf_op jit(solution)/shard_map/ppermute | solution.py:428
  6.8 5.5 %collective-permute-start.2 = (bf16[32,1024]{1,0:T(8,128)(2,1)S(1)}, bf16[32,1024]{1,0:T(8,128)(2,1)S(1)}, u32[]{:S(2)}, u32[]{:S(2)}) collective-permute-start(bf16[32,1024]{1,0:T(8,128)(2,1)S(1)} %get-tuple-element.85), channel_id=1, source_target_pairs={{0,8},{8,0},{16,24},{24,16},{1,9},{9,1},{17,25},{25,17},{2,10},{10... | collective-permute-start | bytes 196616 | tf_op jit(solution)/shard_map/ppermute | solution.py:428
  6.8 5.9 %collective-permute-start.3 = (bf16[32,1024]{1,0:T(8,128)(2,1)S(1)}, bf16[32,1024]{1,0:T(8,128)(2,1)S(1)}, u32[]{:S(2)}, u32[]{:S(2)}) collective-permute-start(bf16[32,1024]{1,0:T(8,128)(2,1)S(1)} %get-tuple-element.86), channel_id=1, source_target_pairs={{0,16},{8,24},{16,0},{24,8},{1,17},{9,25},{17,1},{25,9},{2,18},{10... | collective-permute-start | bytes 196616 | tf_op jit(solution)/shard_map/ppermute | solution.py:428
  7.4 8.3 %collective-permute-start = (bf16[2,64,1024]{2,1,0:T(8,128)(2,1)}, bf16[2,64,1024]{2,1,0:T(8,128)(2,1)S(1)}, u32[]{:S(2)}, u32[]{:S(2)}) collective-permute-start(bf16[2,64,1024]{2,1,0:T(8,128)(2,1)} %bitcast.50), channel_id=1, source_target_pairs={{0,4},{2,6},{4,0},{6,2},{1,5},{3,7},{5,1},{7,3},{8,12},{10,14},{12... | collective-permute-start | bytes 786440 | tf_op jit(solution)/shard_map/ppermute | solution.py:425
  13.6 1.4 %collective-permute-start.5 = (bf16[2,32,1024]{2,1,0:T(8,128)(2,1)S(1)}, bf16[2,32,1024]{2,1,0:T(8,128)(2,1)S(1)}, u32[]{:S(2)}, u32[]{:S(2)}) collective-permute-start(bf16[2,32,1024]{2,1,0:T(8,128)(2,1)S(1)} %pad_maximum_fusion.own_half), channel_id=1, source_target_pairs={{0,2},{2,0},{4,6},{6,4},{1,3},{3,1},{5,7},{7,5},{8,10},{10,8},{12,... | collective-permute-start | bytes 393224 | tf_op jit(solution)/shard_map/ppermute | solution.py:422
  15.7 1.0 copy-start.1
  16.7 0.9 copy-start.4
  17.6 16.4 %copy-start.2 = (bf16[2,1,16,8192]{3,2,1,0:T(8,128)(2,1)S(1)}, bf16[2,1,16,8192]{3,2,1,0:T(8,128)(2,1)}, u32[]{:S(2)}) copy-start(bf16[2,1,16,8192]{3,2,1,0:T(8,128)(2,1)} %param.8) | copy-start | bytes 1572868
  17.7 16.4 %copy-start.3 = (bf16[2,1,16,8192]{3,2,1,0:T(8,128)(2,1)S(1)}, bf16[2,1,16,8192]{3,2,1,0:T(8,128)(2,1)}, u32[]{:S(2)}) copy-start(bf16[2,1,16,8192]{3,2,1,0:T(8,128)(2,1)} %param.9) | copy-start | bytes 1572868
  24.2 46.7 %copy-start.5 = (bf16[8192]{0:T(1024)(128)(2,1)S(1)}, bf16[8192]{0:T(1024)(128)(2,1)}, u32[]{:S(2)}) copy-start(bf16[8192]{0:T(1024)(128)(2,1)} %param.13) | copy-start | bytes 49156
  24.2 10.5 %collective-permute-start.11 = (bf16[2,32,2048]{2,1,0:T(8,128)(2,1)S(1)}, bf16[2,32,2048]{2,1,0:T(8,128)(2,1)S(1)}, u32[]{:S(2)}, u32[]{:S(2)}) collective-permute-start(bf16[2,32,2048]{2,1,0:T(8,128)(2,1)S(1)} %get-tuple-element.48), channel_id=1, source_target_pairs={{0,8},{24,16},{1,9},{25,17},{2,10},{26,18},{3,11},{27,19},{4,12},{... | collective-permute-start | bytes 786440 | tf_op jit(solution)/shard_map/ppermute | solution.py:428
  27.5 12.7 %collective-permute-start.10 = (bf16[2,32,2176]{2,1,0:T(8,128)(2,1)S(1)}, bf16[2,32,2176]{2,1,0:T(8,128)(2,1)S(1)}, u32[]{:S(2)}, u32[]{:S(2)}) collective-permute-start(bf16[2,32,2176]{2,1,0:T(8,128)(2,1)S(1)} %get-tuple-element.47), channel_id=1, source_target_pairs={{0,8},{24,16},{1,9},{25,17},{2,10},{26,18},{3,11},{27,19},{4,12},{... | collective-permute-start | bytes 835592 | tf_op jit(solution)/shard_map/ppermute | solution.py:428
  28.8 11.4 %collective-permute-start.8 = (bf16[2,32,2176]{2,1,0:T(8,128)(2,1)S(1)}, bf16[2,32,2176]{2,1,0:T(8,128)(2,1)S(1)}, u32[]{:S(2)}, u32[]{:S(2)}) collective-permute-start(bf16[2,32,2176]{2,1,0:T(8,128)(2,1)S(1)} %get-tuple-element.47), channel_id=1, source_target_pairs={{8,16},{16,8},{9,17},{17,9},{10,18},{18,10},{11,19},{19,11},{12,20... | collective-permute-start | bytes 835592 | tf_op jit(solution)/shard_map/ppermute | solution.py:428
  29.5 6.8 %collective-permute-start.9 = (bf16[2,32,2048]{2,1,0:T(8,128)(2,1)S(1)}, bf16[2,32,2048]{2,1,0:T(8,128)(2,1)S(1)}, u32[]{:S(2)}, u32[]{:S(2)}) collective-permute-start(bf16[2,32,2048]{2,1,0:T(8,128)(2,1)S(1)} %get-tuple-element.48), channel_id=1, source_target_pairs={{8,16},{16,8},{9,17},{17,9},{10,18},{18,10},{11,19},{19,11},{12,20... | collective-permute-start | bytes 786440 | tf_op jit(solution)/shard_map/ppermute | solution.py:428
  30.2 23.6 %collective-permute-start.7 = (bf16[2,2,32,2176]{3,2,1,0:T(8,128)(2,1)S(1)}, bf16[2,2,32,2176]{3,2,1,0:T(8,128)(2,1)S(1)}, u32[]{:S(2)}, u32[]{:S(2)}) collective-permute-start(bf16[2,2,32,2176]{3,2,1,0:T(8,128)(2,1)S(1)} %get-tuple-element.45), channel_id=1, source_target_pairs={{0,8},{8,0},{16,24},{24,16},{1,9},{9,1},{17,25},{25,17},{2,10},{10... | collective-permute-start | bytes 1671176 | tf_op jit(solution)/shard_map/ppermute | solution.py:428
  34.7 12.4 %collective-permute-start.6 = (bf16[2,2,2,16,2048]{4,3,2,1,0:T(8,128)(2,1)S(1)}, bf16[2,2,2,16,2048]{4,3,2,1,0:T(8,128)(2,1)S(1)}, u32[]{:S(2)}, u32[]{:S(2)}) collective-permute-start(bf16[2,2,2,16,2048]{4,3,2,1,0:T(8,128)(2,1)S(1)} %get-tuple-element.44), channel_id=1, source_target_pairs={{0,4},{2,6},{4,0},{6,2},{1,5},{3,7},{5,1},{7,3},{8,12},{10,14},{12... | collective-permute-start | bytes 1572872 | tf_op jit(solution)/shard_map/ppermute | solution.py:425
  40.8 27.7 %collective-permute-start.12 = (bf16[2,32,2304]{2,1,0:T(8,128)(2,1)S(1)}, bf16[2,32,2304]{2,1,0:T(8,128)(2,1)S(1)}, u32[]{:S(2)}, u32[]{:S(2)}) collective-permute-start(bf16[2,32,2304]{2,1,0:T(8,128)(2,1)S(1)} %shard_map.104), channel_id=1, source_target_pairs={{0,16},{8,24},{16,0},{24,8},{1,17},{9,25},{17,1},{25,9},{2,18},{10... | collective-permute-start | bytes 884744 | tf_op jit(solution)/shard_map/ppermute | solution.py:428
  45.8 22.6 %collective-permute-start.13 = (bf16[2,32,2048]{2,1,0:T(8,128)(2,1)S(1)}, bf16[2,32,2048]{2,1,0:T(8,128)(2,1)S(1)}, u32[]{:S(2)}, u32[]{:S(2)}) collective-permute-start(bf16[2,32,2048]{2,1,0:T(8,128)(2,1)S(1)} %shard_map.105), channel_id=1, source_target_pairs={{0,16},{8,24},{16,0},{24,8},{1,17},{9,25},{17,1},{25,9},{2,18},{10... | collective-permute-start | bytes 786440 | tf_op jit(solution)/shard_map/ppermute | solution.py:428
  69.3 42.8 %copy-start = (bf16[1,1024,2048]{2,1,0:T(8,128)(2,1)S(1)}, bf16[1,1024,2048]{2,1,0:T(8,128)(2,1)}, u32[]{:S(2)}) copy-start(bf16[1,1024,2048]{2,1,0:T(8,128)(2,1)} %param.10) | copy-start | bytes 12582916
  69.3 6.4 %collective-permute-start.14 = (bf16[2,32,2048]{2,1,0:T(8,128)(2,1)S(1)}, bf16[2,32,2048]{2,1,0:T(8,128)(2,1)S(1)}, u32[]{:S(2)}, u32[]{:S(2)}) collective-permute-start(bf16[2,32,2048]{2,1,0:T(8,128)(2,1)S(1)} %get-tuple-element.55), channel_id=1, source_target_pairs={{0,1},{1,0},{2,3},{3,2},{4,5},{5,4},{6,7},{7,6},{8,9},{9,8},{10,11... | collective-permute-start | bytes 786440 | tf_op jit(solution)/shard_map/ppermute | solution.py:509
  76.6 8.0 %collective-permute-start.15 = (bf16[2,32,2048]{2,1,0:T(8,128)(2,1)S(1)}, bf16[2,32,2048]{2,1,0:T(8,128)(2,1)S(1)}, u32[]{:S(2)}, u32[]{:S(2)}) collective-permute-start(bf16[2,32,2048]{2,1,0:T(8,128)(2,1)S(1)} %get-tuple-element.57), channel_id=1, source_target_pairs={{0,1},{1,0},{2,3},{3,2},{4,5},{5,4},{6,7},{7,6},{8,9},{9,8},{10,11... | collective-permute-start | bytes 786440 | tf_op jit(solution)/shard_map/ppermute | solution.py:509
  78.2 3.7 %collective-permute-start.17 = (f32[32,128]{1,0:T(8,128)S(1)}, f32[32,128]{1,0:T(8,128)S(1)}, u32[]{:S(2)}, u32[]{:S(2)}) collective-permute-start(f32[32,128]{1,0:T(8,128)S(1)} %get-tuple-element.61.sums), channel_id=1, source_target_pairs={{0,4},{2,6},{4,0},{6,2},{1,5},{3,7},{5,1},{7,3},{8,12},{10,14},{12... | collective-permute-start | bytes 49160 | tf_op jit(solution)/shard_map/ppermute | solution.py:425
  82.7 9.7 %collective-permute-start.19 = (bf16[2,32,2048]{2,1,0:T(8,128)(2,1)S(1)}, bf16[2,32,2048]{2,1,0:T(8,128)(2,1)S(1)}, u32[]{:S(2)}, u32[]{:S(2)}) collective-permute-start(bf16[2,32,2048]{2,1,0:T(8,128)(2,1)S(1)} %shard_map.110.refs_0_), channel_id=1, source_target_pairs={{0,16},{8,24},{16,0},{24,8},{1,17},{9,25},{17,1},{25,9},{2,18},{10... | collective-permute-start | bytes 786440 | tf_op jit(solution)/shard_map/ppermute | solution.py:428
  82.8 9.6 %collective-permute-start.18 = (bf16[2,32,2048]{2,1,0:T(8,128)(2,1)S(1)}, bf16[2,32,2048]{2,1,0:T(8,128)(2,1)S(1)}, u32[]{:S(2)}, u32[]{:S(2)}) collective-permute-start(bf16[2,32,2048]{2,1,0:T(8,128)(2,1)S(1)} %shard_map.110.refs_0_), channel_id=1, source_target_pairs={{0,8},{8,0},{16,24},{24,16},{1,9},{9,1},{17,25},{25,17},{2,10},{10... | collective-permute-start | bytes 786440 | tf_op jit(solution)/shard_map/ppermute | solution.py:428
  84.7 7.8 %collective-permute-start.20 = (bf16[2,32,2048]{2,1,0:T(8,128)(2,1)S(1)}, bf16[2,32,2048]{2,1,0:T(8,128)(2,1)S(1)}, u32[]{:S(2)}, u32[]{:S(2)}) collective-permute-start(bf16[2,32,2048]{2,1,0:T(8,128)(2,1)S(1)} %shard_map.110.refs_0_), channel_id=1, source_target_pairs={{0,1},{1,0},{2,3},{3,2},{4,5},{5,4},{6,7},{7,6},{8,9},{9,8},{10,11... | collective-permute-start | bytes 786440 | tf_op jit(solution)/shard_map/ppermute | solution.py:509
  87.1 6.6 %collective-permute-start.16 = (bf16[2,2,16,2048]{3,2,1,0:T(8,128)(2,1)S(1)}, bf16[2,2,16,2048]{3,2,1,0:T(8,128)(2,1)S(1)}, u32[]{:S(2)}, u32[]{:S(2)}) collective-permute-start(bf16[2,2,16,2048]{3,2,1,0:T(8,128)(2,1)S(1)} %get-tuple-element.60), channel_id=1, source_target_pairs={{0,4},{2,6},{4,0},{6,2},{1,5},{3,7},{5,1},{7,3},{8,12},{10,14},{12... | collective-permute-start | bytes 786440 | tf_op jit(solution)/shard_map/ppermute | solution.py:425
  92.4 8.3 %collective-permute-start.22 = (bf16[2,32,2048]{2,1,0:T(8,128)(2,1)S(1)}, bf16[2,32,2048]{2,1,0:T(8,128)(2,1)S(1)}, u32[]{:S(2)}, u32[]{:S(2)}) collective-permute-start(bf16[2,32,2048]{2,1,0:T(8,128)(2,1)S(1)} %collective-permute-done.19.refs_2_), channel_id=1, source_target_pairs={{8,0},{16,24},{9,1},{17,25},{10,2},{18,26},{11,3},{19,27},{12,4},{... | collective-permute-start | bytes 786440 | tf_op jit(solution)/shard_map/ppermute | solution.py:428
  93.7 7.5 %collective-permute-start.23 = (bf16[2,32,2048]{2,1,0:T(8,128)(2,1)S(1)}, bf16[2,32,2048]{2,1,0:T(8,128)(2,1)S(1)}, u32[]{:S(2)}, u32[]{:S(2)}) collective-permute-start(bf16[2,32,2048]{2,1,0:T(8,128)(2,1)S(1)} %collective-permute-done.18.refs_1_), channel_id=1, source_target_pairs={{0,1},{1,0},{2,3},{3,2},{4,5},{5,4},{6,7},{7,6},{8,9},{9,8},{10,11... | collective-permute-start | bytes 786440 | tf_op jit(solution)/shard_map/ppermute | solution.py:509
  95.4 5.8 %collective-permute-start.21 = (bf16[2,32,2048]{2,1,0:T(8,128)(2,1)S(1)}, bf16[2,32,2048]{2,1,0:T(8,128)(2,1)S(1)}, u32[]{:S(2)}, u32[]{:S(2)}) collective-permute-start(bf16[2,32,2048]{2,1,0:T(8,128)(2,1)S(1)} %shard_map.110.refs_0_), channel_id=1, source_target_pairs={{8,16},{16,8},{9,17},{17,9},{10,18},{18,10},{11,19},{19,11},{12,20... | collective-permute-start | bytes 786440 | tf_op jit(solution)/shard_map/ppermute | solution.py:428
  96.1 9.7 %collective-permute-start.24 = (bf16[2,32,2048]{2,1,0:T(8,128)(2,1)S(1)}, bf16[2,32,2048]{2,1,0:T(8,128)(2,1)S(1)}, u32[]{:S(2)}, u32[]{:S(2)}) collective-permute-start(bf16[2,32,2048]{2,1,0:T(8,128)(2,1)S(1)} %collective-permute-done.19.refs_2_), channel_id=1, source_target_pairs={{0,1},{1,0},{2,3},{3,2},{4,5},{5,4},{6,7},{7,6},{8,9},{9,8},{10,11... | collective-permute-start | bytes 786440 | tf_op jit(solution)/shard_map/ppermute | solution.py:509
  105.8 6.4 %collective-permute-start.25 = (bf16[2,32,2048]{2,1,0:T(8,128)(2,1)S(1)}, bf16[2,32,2048]{2,1,0:T(8,128)(2,1)S(1)}, u32[]{:S(2)}, u32[]{:S(2)}) collective-permute-start(bf16[2,32,2048]{2,1,0:T(8,128)(2,1)S(1)} %shard_map.111.refs_3_), channel_id=1, source_target_pairs={{0,1},{1,0},{2,3},{3,2},{4,5},{5,4},{6,7},{7,6},{8,9},{9,8},{10,11... | collective-permute-start | bytes 786440 | tf_op jit(solution)/shard_map/ppermute | solution.py:509
  118.5 2.4 %collective-permute-start.27 = (f32[192,1024]{1,0:T(8,128)S(1)}, f32[192,1024]{1,0:T(8,128)S(1)}, u32[]{:S(2)}, u32[]{:S(2)}) collective-permute-start(f32[192,1024]{1,0:T(8,128)S(1)} %get-tuple-element.74), channel_id=1, source_target_pairs={{0,2},{2,0},{4,6},{6,4},{1,3},{3,1},{5,7},{7,5},{8,10},{10,8},{12,... | collective-permute-start | bytes 2359304 | tf_op jit(solution)/shard_map/ppermute | solution.py:422
  121.0 12.0 %collective-permute-start.28 = (bf16[192,1024]{1,0:T(8,128)(2,1)S(1)}, bf16[192,1024]{1,0:T(8,128)(2,1)S(1)}, u32[]{:S(2)}, u32[]{:S(2)}) collective-permute-start(bf16[192,1024]{1,0:T(8,128)(2,1)S(1)} %add_convert_fusion.own_right), channel_id=1, source_target_pairs={{0,4},{2,6},{4,0},{6,2},{1,5},{3,7},{5,1},{7,3},{8,12},{10,14},{12... | collective-permute-start | bytes 1179656 | tf_op jit(solution)/shard_map/ppermute | solution.py:425
  122.5 15.3 %collective-permute-start.26 = (bf16[2,64,1024]{2,1,0:T(8,128)(2,1)S(1)}, bf16[2,64,1024]{2,1,0:T(8,128)(2,1)S(1)}, u32[]{:S(2)}, u32[]{:S(2)}) collective-permute-start(bf16[2,64,1024]{2,1,0:T(8,128)(2,1)S(1)} %get-tuple-element.72), channel_id=1, source_target_pairs={{0,4},{2,6},{4,0},{6,2},{1,5},{3,7},{5,1},{7,3},{8,12},{10,14},{12... | collective-permute-start | bytes 786440 | tf_op jit(solution)/shard_map/ppermute | solution.py:425
  137.8 1.6 %collective-permute-start.29 = (bf16[128,1024]{1,0:T(8,128)(2,1)S(1)}, bf16[128,1024]{1,0:T(8,128)(2,1)S(1)}, u32[]{:S(2)}, u32[]{:S(2)}) collective-permute-start(bf16[128,1024]{1,0:T(8,128)(2,1)S(1)} %slice_select_fusion.own_left), channel_id=1, source_target_pairs={{0,2},{2,0},{4,6},{6,4},{1,3},{3,1},{5,7},{7,5},{8,10},{10,8},{12,... | collective-permute-start | bytes 786440 | tf_op jit(solution)/shard_map/ppermute | solution.py:422

commit v6 on v5

--- a/solution.py
+++ b/solution.py
@@ -144,9 +144,17 @@
     last[...] = mid[...] + farthest[...]
 
 
-def project_kernel(place, own_mix, other_mix, w00, w01, w10, w11, right, own_half, other_half, *refs):
+def layout_kernel(place, mixes, right, own_rows, right_here):
+    t, section = place[0], place[3]
+    micro, _, rows, _ = own_rows.shape
+    for m in range(micro):
+        for r in range(4):
+            own_rows[m, r] = mixes[m ^ section, at_multiple(t ^ r, rows), :]
+    right_here[...] = right[...]
+
+
+def project_kernel(place, own_mix, other_mix, own_weight, other_weight, right, own_half, other_half, *refs):
     own, next_one, *sums, mix_rows, left_rows, piece, inner, turned = refs
-    cuts = ((w00, w01), (w10, w11))
     t, outer, core, section = place[0], place[1], place[2], place[3]
     micro, shards = mix_rows.shape[0], 4
     sub, half = own_half.shape[1:]
@@ -154,15 +162,15 @@
     rows = own.shape[2]
     own_rows = rows // 2
     size = shards * rows
-    depth, tile = w00.shape
+    tile = own_weight.shape[1]
 
     @pl.when(step == 0)
     def _():
         for m in range(micro):
             for r in range(shards):
-                at = pl.ds(pl.multiple_of((t ^ r) * own_rows, own_rows), own_rows)
-                for group, source in enumerate((own_mix, other_mix)):
-                    mix_rows[m, pl.ds(r * rows + group * own_rows, own_rows), :] = source[m ^ section, at, :]
+                at = at_multiple(t ^ r, own_rows)
+                mix_rows[m, pl.ds(r * rows, own_rows), :] = own_mix[m, r]
+                mix_rows[m, pl.ds(r * rows + own_rows, own_rows), :] = other_mix[m ^ section, at, :]
         product = jnp.dot(
             mix_rows[...].reshape(micro * size, -1), right[...], preferred_element_type=F32
         )
@@ -192,12 +200,10 @@
 
     at = pl.ds(pl.multiple_of(step * tile, tile), tile)
     lines = mix_rows[...].reshape(micro * size, -1)
-    for slot in range(2):
-        product = jnp.dot(inner[...], left_rows[slot, :, at], preferred_element_type=F32)
-        for i, weight in enumerate(cuts[slot]):
-            product += jnp.dot(
-                lines[:, i * depth : (i + 1) * depth], weight[...], preferred_element_type=F32
-            )
+    for slot, weight in enumerate((own_weight, other_weight)):
+        product = jnp.dot(lines, weight[...], preferred_element_type=F32) + jnp.dot(
+            inner[...], left_rows[slot, :, at], preferred_element_type=F32
+        )
         for m in range(micro):
             for r in range(shards):
                 at_row = m * size + r * rows
@@ -210,15 +216,8 @@
                     sums[(r - 2) * micro + m][slot, :, at] = value
 
 
-def doubled(weights):
-    return [weights[0], weights[0], weights[1], weights[1]]
-
-
 def weight_specs(head_cols, tile):
-    return [
-        pl.BlockSpec((head_cols // 2, tile), lambda i: (0, i)),
-        pl.BlockSpec((head_cols // 2, tile), lambda i: (1, i)),
-    ] * 2
+    return [pl.BlockSpec((head_cols, tile), lambda i: (0, i))] * 2
 
 
 def whole(*shape):
@@ -226,10 +225,10 @@
 
 
 def project(place, own_mix, other_mix, weights, right, own_half, other_half):
-    micro, tokens, head_cols = own_mix.shape
+    micro, tokens, head_cols = other_mix.shape
     width = weights[0].shape[1]
     rank = right.shape[1]
-    tile = 512
+    tile = 1024
     tiles = width // tile
     rows = tokens // 2
     size = 4 * rows
@@ -243,7 +242,7 @@
         in_specs=[
             pl.BlockSpec(memory_space=pltpu.SMEM),
             whole(*own_mix.shape),
-            whole(*own_mix.shape),
+            whole(*other_mix.shape),
             *weight_specs(head_cols, tile),
             whole(*right.shape),
             whole(*own_half.shape),
@@ -259,21 +258,22 @@
         ],
         compiler_params=pltpu.CompilerParams(vmem_limit_bytes=VMEM_ALL),
         cost_estimate=NO_COST,
-    )(place, own_mix, other_mix, *doubled(weights), right, own_half, other_half)
+    )(place, own_mix, other_mix, *weights, right, own_half, other_half)
 
 
 def back_kernel(micro, place, *refs):
     pieces, refs = refs[: 4 * micro], refs[4 * micro :]
-    cuts, refs = (refs[0:2], refs[2:4]), refs[4:]
+    (own_weight, other_weight), refs = refs[:2], refs[2:]
     left_rows, right, mix_rows = refs[:3]
     (own_piece, beside_piece, crossed_piece, relayed_piece, mid_piece), refs = refs[3:8], refs[8:]
-    mix_here, mix_sent, *factors, total, inner_grad, permuted, right_all = refs
+    mix_here, *mix_sent, kept_factors, sent_factors, total, inner_grad, permuted, right_all = refs
+    factors = (kept_factors, sent_factors)
     rank = permuted.shape[0]
     t, outer, core, section = place[0], place[1], place[2], place[3]
     step = pl.program_id(0)
     rows = pieces[0].shape[1]
     own_rows = rows // 2
-    depth, tile = cuts[0][0].shape
+    tile = own_weight.shape[1]
     half = factors[0].shape[1]
 
     @pl.when(step == 0)
@@ -294,10 +294,9 @@
             parts += [piece[slot] for piece in pieces[4 * m : 4 * m + 4]]
         grads.append(jnp.concatenate(parts, axis=0))
     over = (((1,), (1,)), ((), ()))
-    for i in range(2):
-        total[pl.ds(i * depth, depth), :] += lax.dot_general(
-            cuts[0][i][...], grads[0], over, preferred_element_type=F32
-        ) + lax.dot_general(cuts[1][i][...], grads[1], over, preferred_element_type=F32)
+    total[...] += lax.dot_general(
+        own_weight[...], grads[0], over, preferred_element_type=F32
+    ) + lax.dot_general(other_weight[...], grads[1], over, preferred_element_type=F32)
     inner_grad[...] += lax.dot_general(
         grads[0], left_rows[0], over, preferred_element_type=F32
     ) + lax.dot_general(grads[1], left_rows[1], over, preferred_element_type=F32)
@@ -323,8 +322,8 @@
             for r in range(4):
                 at = at_multiple(t ^ r, own_rows)
                 lines = everything[(4 * m + r) * rows :][:rows]
-                mix_here[m ^ section, at, :] = lines[:own_rows]
-                mix_sent[m ^ section, at, :] = lines[own_rows:].astype(BF16)
+                mix_here[m, at, :] = lines[:own_rows]
+                mix_sent[m][at, :] = lines[own_rows:].astype(BF16)
         right_all[...] = lax.dot_general(
             mine,
             mix_rows[...].reshape(mine.shape[0], -1),
@@ -340,11 +339,11 @@
     head_cols, rank = right.shape
     micro, size, _ = mix_rows.shape
     half = width // 2
-    tile = 512
+    tile = 1024
     tiles = width // tile
     shapes = [
         jax.ShapeDtypeStruct((micro, size // 2, head_cols), F32),
-        jax.ShapeDtypeStruct((micro, size // 2, head_cols), BF16),
+        *[jax.ShapeDtypeStruct((size // 2, head_cols), BF16)] * micro,
         jax.ShapeDtypeStruct((rank + rank // 2, half), F32),
         jax.ShapeDtypeStruct((rank + rank // 2, half), F32),
     ]
@@ -376,7 +375,7 @@
         ],
         compiler_params=pltpu.CompilerParams(vmem_limit_bytes=VMEM),
         cost_estimate=NO_COST,
-    )(place, *pieces, *doubled(weights), left_rows, right, mix_rows, *permuted)
+    )(place, *pieces, *weights, left_rows, right, mix_rows, *permuted)
 
 
 def gather_kernel(place, here, arrived, out):
@@ -391,8 +390,18 @@
             out[m ^ section, :, at] = arrived[m, slot]
 
 
-def add_kernel(place, here, arrived, total):
-    total[...] = (here[...] + arrived[...].astype(F32)).astype(BF16)
+def add_kernel(m, place, here, arrived, total):
+    total[...] = (here[m] + arrived[...].astype(F32)).astype(BF16)
+
+
+def place_kernel(place, first, here, arrived, total):
+    section = place[3]
+    total[section] = first[...]
+    total[1 - section] = (here[1] + arrived[...].astype(F32)).astype(BF16)
+
+
+def sum_kernel(place, kept, arrived, total):
+    total[...] = (kept[...] + arrived[...]).astype(BF16)
 
 
 def left_kernel(place, own_left, other_left, grad_left):
@@ -452,12 +461,21 @@
     cut = [
         lax.dynamic_slice(left, ((t ^ o) * sub, core * half), (sub, half)) for o in range(4)
     ]
+    laid, right_here = small(
+        layout_kernel,
+        [((micro, 4, own_rows, head_cols), BF16), (right.shape, BF16)],
+        [],
+        place,
+        mixes,
+        right,
+    )
     met = swapped(cut)
+    met[2] = after(met[2], laid, right_here)
     own_half = jnp.stack([of_block(met, 2 * outer + i) for i in range(2)])
     other_half = to_core(own_half)
 
     own, next_one, *partial, mix_rows, left_rows, own_piece = project(
-        place, mixes, other_mixes, weights, right, own_half, other_half
+        place, laid, other_mixes, weights, right_here, own_half, other_half
     )
 
     swaps = [[(i, i ^ o) for i in range(4)] for o in range(4)]
@@ -552,11 +570,13 @@
     )
     pieces = [grad, beside, relay, last]
     pieces += [own_there, beside_there, opposite_there, to_section(after(last, opposite_there))]
-    mix_here, mix_sent, kept_factors, sent_factors = back(
+    mix_here, first_sent, second_sent, kept_factors, sent_factors = back(
         place, pieces, weights, left_rows, right, mix_rows, permuted
     )
-    joined = (kept_factors + after(to_core(sent_factors), section_out)).astype(BF16)
-    other_joined = to_outer(joined)
+    (joined,) = small(
+        sum_kernel, [(kept_factors.shape, BF16)], [], place, kept_factors, to_core(sent_factors)
+    )
+    other_joined = after(to_outer(joined), section_out)
     best = jnp.where(outer == t // 2, joined[:rank], other_joined[:rank])
     (grad_right,) = small(
         right_kernel,
@@ -575,13 +595,23 @@
         after(to_core(best), grad_right),
         cost=pl.CostEstimate(flops=8 * 10**9, bytes_accessed=0, transcendentals=0),
     )
-    (grad_mix,) = small(
-        add_kernel,
-        [(mix_here.shape, BF16)],
+    (first_mix,) = small(
+        functools.partial(add_kernel, 0),
+        [(second_sent.shape, BF16)],
         [],
         place,
         mix_here,
-        after(to_outer(mix_sent), grad_right),
+        to_outer(first_sent),
+        cost=pl.CostEstimate(flops=15 * 10**9, bytes_accessed=0, transcendentals=0),
+    )
+    (grad_mix,) = small(
+        place_kernel,
+        [((micro, tokens, head_cols), BF16)],
+        [],
+        place,
+        first_mix,
+        mix_here,
+        after(to_outer(after(second_sent, joined)), grad_right),
         cost=pl.CostEstimate(flops=5 * 10**9, bytes_accessed=0, transcendentals=0),
     )
     grad_mix = grad_mix.reshape(1, micro, 1, tokens, head_cols)

time: 142 us -> 137 us (0.965)
  waiting for transfers between devices: 70.7 us -> 62.7 us
  starting transfers between devices: 41.4 us -> 43.7 us
  Pallas kernels: 24.2 us -> 25.7 us
    ppermute x6 -> x7, waiting for transfers between devices: 17.4 us -> 12.7 us  [to_outer(): return lax.ppermute(value, 'dp', [(i, i ^ 2) for i in range(4)])]
    ppermute x14, waiting for transfers between devices: 36.8 us -> 34.2 us  [along(): return lax.ppermute(value, 'tensor', pairs)]
    ppermute x6 -> x7, starting transfers between devices: 8.31 us -> 10.8 us  [to_outer(): return lax.ppermute(value, 'dp', [(i, i ^ 2) for i in range(4)])]
    pallas_call x12 -> x15, Pallas kernels: 11.3 us -> 13.4 us  [small(): pl.pallas_call(kernel, in_specs=[pl.BlockSpec(memory_space=pltpu.SMEM)] +...]
  transfers between devices with their start and end apart: 30 -> 31, of which waited for: 20 -> 18; matrix products, arithmetic and copies ran while one was open for 1% -> 1% of each run, Pallas kernels for 6% -> 7%
where the time goes in v6:
time: 137 us
  waiting for transfers between devices  62.7 us (46%)
  starting transfers between devices  43.7 us (32%)
  Pallas kernels  25.7 us (19%)
  local copies, waits for them, and re-layouts  2.85 us (2%)
    ppermute x14, waiting for transfers between devices, along(): return lax.ppermute(value, 'tensor', pairs)  34.2 us
    ppermute x14, starting transfers between devices, along(): return lax.ppermute(value, 'tensor', pairs)  23.7 us
    ppermute x6, waiting for transfers between devices, to_section(): return lax.ppermute(value, 'pipe', [(0, 1), (1, 0)])  14.1 us
    pallas_call x15, Pallas kernels, small(): pl.pallas_call(kernel, in_specs=[pl.BlockSpec(memory_space=pltpu.SMEM)] +...  13.4 us
    ppermute x7, waiting for transfers between devices, to_outer(): return lax.ppermute(value, 'dp', [(i, i ^ 2) for i in range(4)])  12.7 us
    ppermute x7, starting transfers between devices, to_outer(): return lax.ppermute(value, 'dp', [(i, i ^ 2) for i in range(4)])  10.8 us
    ppermute x6, starting transfers between devices, to_section(): return lax.ppermute(value, 'pipe', [(0, 1), (1, 0)])  8.59 us
    pallas_call x1, Pallas kernels, back(): pl.pallas_call(functools.partial(back_kernel, micro), grid=(tiles,), in_s...  6.45 us
  transfers between devices with their start and end apart: 31, of which 18 were waited for; matrix products, arithmetic and copies ran while one was open for 1% of the time, Pallas kernels for 7%

profile of v6, /device:TPU:0, one launch (start us, length us, event | category | flops | bytes accessed | tf_op | source)
XLA Modules:
  0.0 136.9 jit_solution(2604579919850151731)
XLA Ops:
  0.6 0.5 collective-permute-start.1
  1.1 0.9 dynamic-slice_bitcast_fusion
  2.1 4.7 %collective-permute-start.4 = (bf16[32,1024]{1,0:T(8,128)(2,1)S(1)}, bf16[32,1024]{1,0:T(8,128)(2,1)S(1)}, u32[]{:S(2)}, u32[]{:S(2)}) collective-permute-start(bf16[32,1024]{1,0:T(8,128)(2,1)S(1)} %get-tuple-element.94), channel_id=1, source_target_pairs={{0,24},{8,16},{16,8},{24,0},{1,25},{9,17},{17,9},{25,1},{2,26},{10... | collective-permute-start | bytes 196616 | tf_op jit(solution)/shard_map/ppermute | solution.py:437
  6.8 0.6 collective-permute-start.3
  7.4 1.6 %collective-permute-start = (bf16[2,64,1024]{2,1,0:T(8,128)(2,1)}, bf16[2,64,1024]{2,1,0:T(8,128)(2,1)S(1)}, u32[]{:S(2)}, u32[]{:S(2)}) collective-permute-start(bf16[2,64,1024]{2,1,0:T(8,128)(2,1)} %bitcast.48), channel_id=1, source_target_pairs={{0,4},{2,6},{4,0},{6,2},{1,5},{3,7},{5,1},{7,3},{8,12},{10,14},{12... | collective-permute-start | bytes 786440 | tf_op jit(solution)/shard_map/ppermute | solution.py:434
  9.2 0.9 copy-done.1
  10.1 0.9 copy-done.5
  11.1 0.6 shard_map.102
  11.6 1.0 collective-permute-done.3
  12.7 0.9 fusion.1
  13.7 1.3 collective-permute-done.5.other_half
  15.0 0.7 collective-permute-done.other_mix
  15.7 5.8 %shard_map.103 = (bf16[2,2,32,2048]{3,2,1,0:T(8,128)(2,1)S(1)}, bf16[2,2,32,2176]{3,2,1,0:T(8,128)(2,1)S(1)}, bf16[2,32,2176]{2,1,0:T(8,128)(2,1)S(1)}, bf16[2,3...) custom-call(s32[4]{0:T(128)S(1)} %pad_add_fusion.place, ...), custom_call_target="tpu_custom_call" | custom-call | tf_op jit(solution)/shard_map/pallas_call | solution.py:239
  21.6 3.3 %collective-permute-start.11 = (bf16[2,32,2048]{2,1,0:T(8,128)(2,1)S(1)}, bf16[2,32,2048]{2,1,0:T(8,128)(2,1)S(1)}, u32[]{:S(2)}, u32[]{:S(2)}) collective-permute-start(bf16[2,32,2048]{2,1,0:T(8,128)(2,1)S(1)} %get-tuple-element.56), channel_id=1, source_target_pairs={{0,8},{24,16},{1,9},{25,17},{2,10},{26,18},{3,11},{27,19},{4,12},{... | collective-permute-start | bytes 786440 | tf_op jit(solution)/shard_map/ppermute | solution.py:437
  24.9 1.3 collective-permute-start.10
  26.3 0.7 collective-permute-start.8
  26.9 0.7 collective-permute-start.9
  27.6 3.9 %collective-permute-start.7 = (bf16[2,2,32,2176]{3,2,1,0:T(8,128)(2,1)S(1)}, bf16[2,2,32,2176]{3,2,1,0:T(8,128)(2,1)S(1)}, u32[]{:S(2)}, u32[]{:S(2)}) collective-permute-start(bf16[2,2,32,2176]{3,2,1,0:T(8,128)(2,1)S(1)} %get-tuple-element.53), channel_id=1, source_target_pairs={{0,8},{8,0},{16,24},{24,16},{1,9},{9,1},{17,25},{25,17},{2,10},{10... | collective-permute-start | bytes 1671176 | tf_op jit(solution)/shard_map/ppermute | solution.py:437
  31.5 0.6 shard_map.104
  32.2 1.5 %collective-permute-start.6 = (bf16[2,2,2,16,2048]{4,3,2,1,0:T(8,128)(2,1)S(1)}, bf16[2,2,2,16,2048]{4,3,2,1,0:T(8,128)(2,1)S(1)}, u32[]{:S(2)}, u32[]{:S(2)}) collective-permute-start(bf16[2,2,2,16,2048]{4,3,2,1,0:T(8,128)(2,1)S(1)} %get-tuple-element.52), channel_id=1, source_target_pairs={{0,4},{2,6},{4,0},{6,2},{1,5},{3,7},{5,1},{7,3},{8,12},{10,14},{12... | collective-permute-start | bytes 1572872 | tf_op jit(solution)/shard_map/ppermute | solution.py:434
  33.7 3.9 %collective-permute-done.10.passed = bf16[2,32,2176]{2,1,0:T(8,128)(2,1)S(1)} collective-permute-done((bf16[2,32,2176]{2,1,0:T(8,128)(2,1)S(1)}, bf16[2,32,2176]{2,1,0:T(8,128)(2,1)S(1)}, u32[]{:S(2)}, u32[]{:S(2)}) %collective-permute-start.10) | collective-permute-done | bytes 278560 | tf_op jit(solution)/shard_map/ppermute | solution.py:437
  37.6 0.6 shard_map.105
  38.3 4.4 %collective-permute-start.12 = (bf16[2,32,2304]{2,1,0:T(8,128)(2,1)S(1)}, bf16[2,32,2304]{2,1,0:T(8,128)(2,1)S(1)}, u32[]{:S(2)}, u32[]{:S(2)}) collective-permute-start(bf16[2,32,2304]{2,1,0:T(8,128)(2,1)S(1)} %shard_map.105), channel_id=1, source_target_pairs={{0,16},{8,24},{16,0},{24,8},{1,17},{9,25},{17,1},{25,9},{2,18},{10... | collective-permute-start | bytes 884744 | tf_op jit(solution)/shard_map/ppermute | solution.py:437
  42.7 0.6 shard_map.106
  43.4 1.2 collective-permute-done.6.arrived
  44.6 6.7 %collective-permute-done.7.beside.refs_14_ = bf16[2,2,32,2176]{3,2,1,0:T(8,128)(2,1)S(1)} collective-permute-done((bf16[2,2,32,2176]{3,2,1,0:T(8,128)(2,1)S(1)}, bf16[2,2,32,2176]{3,2,1,0:T(8,128)(2,1)S(1)}, u32[]{:S(2)}, u32[]{:S(2)}) %collective-permute-start.7) | collective-permute-done | bytes 557088 | tf_op jit(solution)/shard_map/ppermute | solution.py:437
  51.3 14.7 %collective-permute-done.13.refs_3_ = bf16[2,32,2048]{2,1,0:T(8,128)(2,1)S(1)} collective-permute-done((bf16[2,32,2048]{2,1,0:T(8,128)(2,1)S(1)}, bf16[2,32,2048]{2,1,0:T(8,128)(2,1)S(1)}, u32[]{:S(2)}, u32[]{:S(2)}) %collective-permute-start.13) | collective-permute-done | bytes 262176 | tf_op jit(solution)/shard_map/ppermute | solution.py:437
  66.0 0.8 shard_map.107
  66.8 1.6 %collective-permute-start.14 = (bf16[2,32,2048]{2,1,0:T(8,128)(2,1)S(1)}, bf16[2,32,2048]{2,1,0:T(8,128)(2,1)S(1)}, u32[]{:S(2)}, u32[]{:S(2)}) collective-permute-start(bf16[2,32,2048]{2,1,0:T(8,128)(2,1)S(1)} %get-tuple-element.63), channel_id=1, source_target_pairs={{0,1},{1,0},{2,3},{3,2},{4,5},{5,4},{6,7},{7,6},{8,9},{9,8},{10,11... | collective-permute-start | bytes 786440 | tf_op jit(solution)/shard_map/ppermute | solution.py:527
  68.4 4.8 %collective-permute-done.14.other = bf16[2,32,2048]{2,1,0:T(8,128)(2,1)S(1)} collective-permute-done((bf16[2,32,2048]{2,1,0:T(8,128)(2,1)S(1)}, bf16[2,32,2048]{2,1,0:T(8,128)(2,1)S(1)}, u32[]{:S(2)}, u32[]{:S(2)}) %collective-permute-start.14) | collective-permute-done | bytes 262176 | tf_op jit(solution)/shard_map/ppermute | solution.py:527
  73.3 0.9 shard_map.108
  74.1 1.6 %collective-permute-start.15 = (bf16[2,32,2048]{2,1,0:T(8,128)(2,1)S(1)}, bf16[2,32,2048]{2,1,0:T(8,128)(2,1)S(1)}, u32[]{:S(2)}, u32[]{:S(2)}) collective-permute-start(bf16[2,32,2048]{2,1,0:T(8,128)(2,1)S(1)} %get-tuple-element.65), channel_id=1, source_target_pairs={{0,1},{1,0},{2,3},{3,2},{4,5},{5,4},{6,7},{7,6},{8,9},{9,8},{10,11... | collective-permute-start | bytes 786440 | tf_op jit(solution)/shard_map/ppermute | solution.py:527
  75.7 1.5 %collective-permute-start.17 = (f32[32,128]{1,0:T(8,128)S(1)}, f32[32,128]{1,0:T(8,128)S(1)}, u32[]{:S(2)}, u32[]{:S(2)}) collective-permute-start(f32[32,128]{1,0:T(8,128)S(1)} %get-tuple-element.69.sums), channel_id=1, source_target_pairs={{0,4},{2,6},{4,0},{6,2},{1,5},{3,7},{5,1},{7,3},{8,12},{10,14},{12... | collective-permute-start | bytes 49160 | tf_op jit(solution)/shard_map/ppermute | solution.py:434
  77.2 2.2 %collective-permute-done.17.other_sums = f32[32,128]{1,0:T(8,128)S(1)} collective-permute-done((f32[32,128]{1,0:T(8,128)S(1)}, f32[32,128]{1,0:T(8,128)S(1)}, u32[]{:S(2)}, u32[]{:S(2)}) %collective-permute-start.17) | collective-permute-done | bytes 16416 | tf_op jit(solution)/shard_map/ppermute | solution.py:434
  79.5 0.8 shard_map.111.refs_0_
  80.3 1.9 %collective-permute-start.18 = (bf16[2,32,2048]{2,1,0:T(8,128)(2,1)S(1)}, bf16[2,32,2048]{2,1,0:T(8,128)(2,1)S(1)}, u32[]{:S(2)}, u32[]{:S(2)}) collective-permute-start(bf16[2,32,2048]{2,1,0:T(8,128)(2,1)S(1)} %shard_map.111.refs_0_), channel_id=1, source_target_pairs={{0,8},{8,0},{16,24},{24,16},{1,9},{9,1},{17,25},{25,17},{2,10},{10... | collective-permute-start | bytes 786440 | tf_op jit(solution)/shard_map/ppermute | solution.py:437
  82.2 1.7 %collective-permute-start.20 = (bf16[2,32,2048]{2,1,0:T(8,128)(2,1)S(1)}, bf16[2,32,2048]{2,1,0:T(8,128)(2,1)S(1)}, u32[]{:S(2)}, u32[]{:S(2)}) collective-permute-start(bf16[2,32,2048]{2,1,0:T(8,128)(2,1)S(1)} %shard_map.111.refs_0_), channel_id=1, source_target_pairs={{0,1},{1,0},{2,3},{3,2},{4,5},{5,4},{6,7},{7,6},{8,9},{9,8},{10,11... | collective-permute-start | bytes 786440 | tf_op jit(solution)/shard_map/ppermute | solution.py:527
  83.9 0.7 shard_map.109
  84.6 1.6 %collective-permute-start.16 = (bf16[2,2,16,2048]{3,2,1,0:T(8,128)(2,1)S(1)}, bf16[2,2,16,2048]{3,2,1,0:T(8,128)(2,1)S(1)}, u32[]{:S(2)}, u32[]{:S(2)}) collective-permute-start(bf16[2,2,16,2048]{3,2,1,0:T(8,128)(2,1)S(1)} %get-tuple-element.68), channel_id=1, source_target_pairs={{0,4},{2,6},{4,0},{6,2},{1,5},{3,7},{5,1},{7,3},{8,12},{10,14},{12... | collective-permute-start | bytes 786440 | tf_op jit(solution)/shard_map/ppermute | solution.py:434
  86.1 3.7 %collective-permute-done.18.refs_1_ = bf16[2,32,2048]{2,1,0:T(8,128)(2,1)S(1)} collective-permute-done((bf16[2,32,2048]{2,1,0:T(8,128)(2,1)S(1)}, bf16[2,32,2048]{2,1,0:T(8,128)(2,1)S(1)}, u32[]{:S(2)}, u32[]{:S(2)}) %collective-permute-start.18) | collective-permute-done | bytes 262176 | tf_op jit(solution)/shard_map/ppermute | solution.py:437
  89.9 1.3 collective-permute-start.22
  91.2 1.7 %collective-permute-start.23 = (bf16[2,32,2048]{2,1,0:T(8,128)(2,1)S(1)}, bf16[2,32,2048]{2,1,0:T(8,128)(2,1)S(1)}, u32[]{:S(2)}, u32[]{:S(2)}) collective-permute-start(bf16[2,32,2048]{2,1,0:T(8,128)(2,1)S(1)} %collective-permute-done.18.refs_1_), channel_id=1, source_target_pairs={{0,1},{1,0},{2,3},{3,2},{4,5},{5,4},{6,7},{7,6},{8,9},{9,8},{10,11... | collective-permute-start | bytes 786440 | tf_op jit(solution)/shard_map/ppermute | solution.py:527
  92.8 0.7 collective-permute-start.21
  93.5 0.5 collective-permute-start.24
  94.0 4.1 %collective-permute-done.22.farthest = bf16[2,32,2048]{2,1,0:T(8,128)(2,1)S(1)} collective-permute-done((bf16[2,32,2048]{2,1,0:T(8,128)(2,1)S(1)}, bf16[2,32,2048]{2,1,0:T(8,128)(2,1)S(1)}, u32[]{:S(2)}, u32[]{:S(2)}) %collective-permute-start.22) | collective-permute-done | bytes 262176 | tf_op jit(solution)/shard_map/ppermute | solution.py:437
  98.1 0.4 collective-permute-done.23.refs_5_
  98.5 0.6 shard_map.112.refs_3_
  99.1 4.1 %collective-permute-done.24.refs_6_ = bf16[2,32,2048]{2,1,0:T(8,128)(2,1)S(1)} collective-permute-done((bf16[2,32,2048]{2,1,0:T(8,128)(2,1)S(1)}, bf16[2,32,2048]{2,1,0:T(8,128)(2,1)S(1)}, u32[]{:S(2)}, u32[]{:S(2)}) %collective-permute-start.24) | collective-permute-done | bytes 262176 | tf_op jit(solution)/shard_map/ppermute | solution.py:527
  103.2 1.6 %collective-permute-start.25 = (bf16[2,32,2048]{2,1,0:T(8,128)(2,1)S(1)}, bf16[2,32,2048]{2,1,0:T(8,128)(2,1)S(1)}, u32[]{:S(2)}, u32[]{:S(2)}) collective-permute-start(bf16[2,32,2048]{2,1,0:T(8,128)(2,1)S(1)} %shard_map.112.refs_3_), channel_id=1, source_target_pairs={{0,1},{1,0},{2,3},{3,2},{4,5},{5,4},{6,7},{7,6},{8,9},{9,8},{10,11... | collective-permute-start | bytes 786440 | tf_op jit(solution)/shard_map/ppermute | solution.py:527
  104.8 4.8 %collective-permute-done.25.refs_7_ = bf16[2,32,2048]{2,1,0:T(8,128)(2,1)S(1)} collective-permute-done((bf16[2,32,2048]{2,1,0:T(8,128)(2,1)S(1)}, bf16[2,32,2048]{2,1,0:T(8,128)(2,1)S(1)}, u32[]{:S(2)}, u32[]{:S(2)}) %collective-permute-start.25) | collective-permute-done | bytes 262176 | tf_op jit(solution)/shard_map/ppermute | solution.py:527
  109.6 6.5 %shard_map.113 = (f32[2,64,1024]{2,1,0:T(8,128)S(1)}, bf16[64,1024]{1,0:T(8,128)(2,1)}, bf16[64,1024]{1,0:T(8,128)(2,1)S(1)}, f32[192,1024]{1,0:T(8,128)S(1)}, f32[192,1024]{1,0:T(8,128)S(1)}) custom-call(s32[4]{0:T(128)S(1)} %pad_add_fusion.place, bf16[2,32,2048]{2,1,0:T(8,128)(2,1)S(1)} %shard_map.111.refs_0_, ...), custom_call_target="tpu_custom_call" | custom-call | tf_op jit(solution)/shard_map/pallas_call | solution.py:350
  116.1 1.6 %collective-permute-start.26 = (bf16[64,1024]{1,0:T(8,128)(2,1)}, bf16[64,1024]{1,0:T(8,128)(2,1)}, u32[]{:S(2)}, u32[]{:S(2)}) collective-permute-start(bf16[64,1024]{1,0:T(8,128)(2,1)} %get-tuple-element.80), channel_id=1, source_target_pairs={{0,4},{2,6},{4,0},{6,2},{1,5},{3,7},{5,1},{7,3},{8,12},{10,14},{12... | collective-permute-start | bytes 393224 | tf_op jit(solution)/shard_map/ppermute | solution.py:434
  117.6 1.4 %shard_map.110 = bf16[2,16,8192]{2,1,0:T(8,128)(2,1)} custom-call(s32[4]{0:T(128)S(1)} %pad_add_fusion.place, bf16[2,2,16,2048]{3,2,1,0:T(8,128)(2,1)S(1)} %get-tuple-element.67.here, bf16[2,2,16,2048]{3,2,1,0:T(8,128)(2,1)S(1)} %collective-permute-done.16.arrived), custom_call_target="tpu_custom_call" | custom-call | tf_op jit(solution)/shard_map/pallas_call | solution.py:43
  119.0 0.6 shard_map.115.own_right
  119.6 1.0 collective-permute-start.29
  120.6 1.7 %collective-permute-done.26.arrived = bf16[64,1024]{1,0:T(8,128)(2,1)} collective-permute-done((bf16[64,1024]{1,0:T(8,128)(2,1)}, bf16[64,1024]{1,0:T(8,128)(2,1)}, u32[]{:S(2)}, u32[]{:S(2)}) %collective-permute-start.26) | collective-permute-done | bytes 131104 | tf_op jit(solution)/shard_map/ppermute | solution.py:434
  122.3 0.9 shard_map.114.first
  123.2 2.0 %collective-permute-start.28 = (bf16[64,1024]{1,0:T(8,128)(2,1)S(1)}, bf16[64,1024]{1,0:T(8,128)(2,1)S(1)}, u32[]{:S(2)}, u32[]{:S(2)}) collective-permute-start(bf16[64,1024]{1,0:T(8,128)(2,1)S(1)} %get-tuple-element.84), channel_id=1, source_target_pairs={{0,4},{2,6},{4,0},{6,2},{1,5},{3,7},{5,1},{7,3},{8,12},{10,14},{12... | collective-permute-start | bytes 393224 | tf_op jit(solution)/shard_map/ppermute | solution.py:434
  125.2 6.4 %collective-permute-done.29.other_right = bf16[192,1024]{1,0:T(8,128)(2,1)S(1)} collective-permute-done((bf16[192,1024]{1,0:T(8,128)(2,1)S(1)}, bf16[192,1024]{1,0:T(8,128)(2,1)S(1)}, u32[]{:S(2)}, u32[]{:S(2)}) %collective-permute-start.29) | collective-permute-done | bytes 393248 | tf_op jit(solution)/shard_map/ppermute | solution.py:434
  131.6 1.6 %shard_map.116 = f32[1024,128]{1,0:T(8,128)} custom-call(s32[4]{0:T(128)S(1)} %pad_add_fusion.place, bf16[192,1024]{1,0:T(8,128)(2,1)S(1)} %shard_map.115.own_right, bf16[192,1024]{1,0:T(8,128)(2,1)S(1)} %collective-permute-done.29.other_right), custom_call_target="tpu_custom_call" | custom-call | tf_op jit(solution)/shard_map/pallas_call | solution.py:43
  133.2 0.5 collective-permute-done.28.arrived
  133.7 1.3 shard_map.117
  135.0 0.3 collective-permute-done.30.other_left
  135.3 1.6 %shard_map.118 = f32[128,2048]{1,0:T(8,128)} custom-call(s32[4]{0:T(128)S(1)} %pad_add_fusion.place, bf16[128,1024]{1,0:T(8,128)(2,1)S(1)} %slice_select_fusion.own_left, bf16[128,1024]{1,0:T(8,128)(2,1)S(1)} %collective-permute-done.30.other_left), custom_call_target="tpu_custom_call" | custom-call | flops 8000000000 | tf_op jit(solution)/shard_map/pallas_call | solution.py:43
  (35 shorter events, 0.4 us)
Async XLA Ops:
  0.6 15.1 %collective-permute-start.1 = (bf16[1024,2048]{1,0:T(8,128)(2,1)}, bf16[1024,2048]{1,0:T(8,128)(2,1)}, u32[]{:S(2)}, u32[]{:S(2)}) collective-permute-start(bf16[1024,2048]{1,0:T(8,128)(2,1)} %bitcast.39), channel_id=1, source_target_pairs={{0,2},{2,0},{4,6},{6,4},{1,3},{3,1},{5,7},{7,5},{8,10},{10,8},{12,... | collective-permute-start | bytes 12582920 | tf_op jit(solution)/shard_map/ppermute | solution.py:431
  2.1 10.6 %collective-permute-start.4 = (bf16[32,1024]{1,0:T(8,128)(2,1)S(1)}, bf16[32,1024]{1,0:T(8,128)(2,1)S(1)}, u32[]{:S(2)}, u32[]{:S(2)}) collective-permute-start(bf16[32,1024]{1,0:T(8,128)(2,1)S(1)} %get-tuple-element.94), channel_id=1, source_target_pairs={{0,24},{8,16},{16,8},{24,0},{1,25},{9,17},{17,9},{25,1},{2,26},{10... | collective-permute-start | bytes 196616 | tf_op jit(solution)/shard_map/ppermute | solution.py:437
  6.8 5.9 %collective-permute-start.2 = (bf16[32,1024]{1,0:T(8,128)(2,1)S(1)}, bf16[32,1024]{1,0:T(8,128)(2,1)S(1)}, u32[]{:S(2)}, u32[]{:S(2)}) collective-permute-start(bf16[32,1024]{1,0:T(8,128)(2,1)S(1)} %get-tuple-element.95), channel_id=1, source_target_pairs={{0,8},{8,0},{16,24},{24,16},{1,9},{9,1},{17,25},{25,17},{2,10},{10... | collective-permute-start | bytes 196616 | tf_op jit(solution)/shard_map/ppermute | solution.py:437
  6.8 5.9 %collective-permute-start.3 = (bf16[32,1024]{1,0:T(8,128)(2,1)S(1)}, bf16[32,1024]{1,0:T(8,128)(2,1)S(1)}, u32[]{:S(2)}, u32[]{:S(2)}) collective-permute-start(bf16[32,1024]{1,0:T(8,128)(2,1)S(1)} %get-tuple-element.96), channel_id=1, source_target_pairs={{0,16},{8,24},{16,0},{24,8},{1,17},{9,25},{17,1},{25,9},{2,18},{10... | collective-permute-start | bytes 196616 | tf_op jit(solution)/shard_map/ppermute | solution.py:437
  7.4 8.3 %collective-permute-start = (bf16[2,64,1024]{2,1,0:T(8,128)(2,1)}, bf16[2,64,1024]{2,1,0:T(8,128)(2,1)S(1)}, u32[]{:S(2)}, u32[]{:S(2)}) collective-permute-start(bf16[2,64,1024]{2,1,0:T(8,128)(2,1)} %bitcast.48), channel_id=1, source_target_pairs={{0,4},{2,6},{4,0},{6,2},{1,5},{3,7},{5,1},{7,3},{8,12},{10,14},{12... | collective-permute-start | bytes 786440 | tf_op jit(solution)/shard_map/ppermute | solution.py:434
  9.2 1.0 copy-start.1
  10.1 0.9 copy-start.5
  13.6 17.9 %copy-start.3 = (bf16[2,1,16,8192]{3,2,1,0:T(8,128)(2,1)S(1)}, bf16[2,1,16,8192]{3,2,1,0:T(8,128)(2,1)}, u32[]{:S(2)}) copy-start(bf16[2,1,16,8192]{3,2,1,0:T(8,128)(2,1)} %param.8) | copy-start | bytes 1572868
  13.6 17.9 %copy-start.4 = (bf16[2,1,16,8192]{3,2,1,0:T(8,128)(2,1)S(1)}, bf16[2,1,16,8192]{3,2,1,0:T(8,128)(2,1)}, u32[]{:S(2)}) copy-start(bf16[2,1,16,8192]{3,2,1,0:T(8,128)(2,1)} %param.9) | copy-start | bytes 1572868
  13.6 1.4 %collective-permute-start.5 = (bf16[2,32,1024]{2,1,0:T(8,128)(2,1)S(1)}, bf16[2,32,1024]{2,1,0:T(8,128)(2,1)S(1)}, u32[]{:S(2)}, u32[]{:S(2)}) collective-permute-start(bf16[2,32,1024]{2,1,0:T(8,128)(2,1)S(1)} %pad_maximum_fusion.own_half), channel_id=1, source_target_pairs={{0,2},{2,0},{4,6},{6,4},{1,3},{3,1},{5,7},{7,5},{8,10},{10,8},{12,... | collective-permute-start | bytes 393224 | tf_op jit(solution)/shard_map/ppermute | solution.py:431
  21.6 46.8 %copy-start.6 = (bf16[8192]{0:T(1024)(128)(2,1)S(1)}, bf16[8192]{0:T(1024)(128)(2,1)}, u32[]{:S(2)}) copy-start(bf16[8192]{0:T(1024)(128)(2,1)} %param.13) | copy-start | bytes 49156
  21.6 10.6 %collective-permute-start.11 = (bf16[2,32,2048]{2,1,0:T(8,128)(2,1)S(1)}, bf16[2,32,2048]{2,1,0:T(8,128)(2,1)S(1)}, u32[]{:S(2)}, u32[]{:S(2)}) collective-permute-start(bf16[2,32,2048]{2,1,0:T(8,128)(2,1)S(1)} %get-tuple-element.56), channel_id=1, source_target_pairs={{0,8},{24,16},{1,9},{25,17},{2,10},{26,18},{3,11},{27,19},{4,12},{... | collective-permute-start | bytes 786440 | tf_op jit(solution)/shard_map/ppermute | solution.py:437
  24.9 12.7 %collective-permute-start.10 = (bf16[2,32,2176]{2,1,0:T(8,128)(2,1)S(1)}, bf16[2,32,2176]{2,1,0:T(8,128)(2,1)S(1)}, u32[]{:S(2)}, u32[]{:S(2)}) collective-permute-start(bf16[2,32,2176]{2,1,0:T(8,128)(2,1)S(1)} %get-tuple-element.55), channel_id=1, source_target_pairs={{0,8},{24,16},{1,9},{25,17},{2,10},{26,18},{3,11},{27,19},{4,12},{... | collective-permute-start | bytes 835592 | tf_op jit(solution)/shard_map/ppermute | solution.py:437
  26.3 11.4 %collective-permute-start.8 = (bf16[2,32,2176]{2,1,0:T(8,128)(2,1)S(1)}, bf16[2,32,2176]{2,1,0:T(8,128)(2,1)S(1)}, u32[]{:S(2)}, u32[]{:S(2)}) collective-permute-start(bf16[2,32,2176]{2,1,0:T(8,128)(2,1)S(1)} %get-tuple-element.55), channel_id=1, source_target_pairs={{8,16},{16,8},{9,17},{17,9},{10,18},{18,10},{11,19},{19,11},{12,20... | collective-permute-start | bytes 835592 | tf_op jit(solution)/shard_map/ppermute | solution.py:437
  26.9 6.8 %collective-permute-start.9 = (bf16[2,32,2048]{2,1,0:T(8,128)(2,1)S(1)}, bf16[2,32,2048]{2,1,0:T(8,128)(2,1)S(1)}, u32[]{:S(2)}, u32[]{:S(2)}) collective-permute-start(bf16[2,32,2048]{2,1,0:T(8,128)(2,1)S(1)} %get-tuple-element.56), channel_id=1, source_target_pairs={{8,16},{16,8},{9,17},{17,9},{10,18},{18,10},{11,19},{19,11},{12,20... | collective-permute-start | bytes 786440 | tf_op jit(solution)/shard_map/ppermute | solution.py:437
  27.6 23.6 %collective-permute-start.7 = (bf16[2,2,32,2176]{3,2,1,0:T(8,128)(2,1)S(1)}, bf16[2,2,32,2176]{3,2,1,0:T(8,128)(2,1)S(1)}, u32[]{:S(2)}, u32[]{:S(2)}) collective-permute-start(bf16[2,2,32,2176]{3,2,1,0:T(8,128)(2,1)S(1)} %get-tuple-element.53), channel_id=1, source_target_pairs={{0,8},{8,0},{16,24},{24,16},{1,9},{9,1},{17,25},{25,17},{2,10},{10... | collective-permute-start | bytes 1671176 | tf_op jit(solution)/shard_map/ppermute | solution.py:437
  32.2 12.4 %collective-permute-start.6 = (bf16[2,2,2,16,2048]{4,3,2,1,0:T(8,128)(2,1)S(1)}, bf16[2,2,2,16,2048]{4,3,2,1,0:T(8,128)(2,1)S(1)}, u32[]{:S(2)}, u32[]{:S(2)}) collective-permute-start(bf16[2,2,2,16,2048]{4,3,2,1,0:T(8,128)(2,1)S(1)} %get-tuple-element.52), channel_id=1, source_target_pairs={{0,4},{2,6},{4,0},{6,2},{1,5},{3,7},{5,1},{7,3},{8,12},{10,14},{12... | collective-permute-start | bytes 1572872 | tf_op jit(solution)/shard_map/ppermute | solution.py:434
  38.3 27.7 %collective-permute-start.12 = (bf16[2,32,2304]{2,1,0:T(8,128)(2,1)S(1)}, bf16[2,32,2304]{2,1,0:T(8,128)(2,1)S(1)}, u32[]{:S(2)}, u32[]{:S(2)}) collective-permute-start(bf16[2,32,2304]{2,1,0:T(8,128)(2,1)S(1)} %shard_map.105), channel_id=1, source_target_pairs={{0,16},{8,24},{16,0},{24,8},{1,17},{9,25},{17,1},{25,9},{2,18},{10... | collective-permute-start | bytes 884744 | tf_op jit(solution)/shard_map/ppermute | solution.py:437
  43.3 22.7 %collective-permute-start.13 = (bf16[2,32,2048]{2,1,0:T(8,128)(2,1)S(1)}, bf16[2,32,2048]{2,1,0:T(8,128)(2,1)S(1)}, u32[]{:S(2)}, u32[]{:S(2)}) collective-permute-start(bf16[2,32,2048]{2,1,0:T(8,128)(2,1)S(1)} %shard_map.106), channel_id=1, source_target_pairs={{0,16},{8,24},{16,0},{24,8},{1,17},{9,25},{17,1},{25,9},{2,18},{10... | collective-permute-start | bytes 786440 | tf_op jit(solution)/shard_map/ppermute | solution.py:437
  66.8 42.8 %copy-start = (bf16[1,1024,2048]{2,1,0:T(8,128)(2,1)S(1)}, bf16[1,1024,2048]{2,1,0:T(8,128)(2,1)}, u32[]{:S(2)}) copy-start(bf16[1,1024,2048]{2,1,0:T(8,128)(2,1)} %param.10) | copy-start | bytes 12582916
  66.8 42.8 %copy-start.2 = (bf16[1,1,1024,128]{3,2,1,0:T(8,128)(2,1)S(1)}, bf16[1,1,1024,128]{3,2,1,0:T(8,128)(2,1)}, u32[]{:S(2)}) copy-start(bf16[1,1,1024,128]{3,2,1,0:T(8,128)(2,1)} %param.11) | copy-start | bytes 786436
  66.8 6.4 %collective-permute-start.14 = (bf16[2,32,2048]{2,1,0:T(8,128)(2,1)S(1)}, bf16[2,32,2048]{2,1,0:T(8,128)(2,1)S(1)}, u32[]{:S(2)}, u32[]{:S(2)}) collective-permute-start(bf16[2,32,2048]{2,1,0:T(8,128)(2,1)S(1)} %get-tuple-element.63), channel_id=1, source_target_pairs={{0,1},{1,0},{2,3},{3,2},{4,5},{5,4},{6,7},{7,6},{8,9},{9,8},{10,11... | collective-permute-start | bytes 786440 | tf_op jit(solution)/shard_map/ppermute | solution.py:527
  74.1 8.1 %collective-permute-start.15 = (bf16[2,32,2048]{2,1,0:T(8,128)(2,1)S(1)}, bf16[2,32,2048]{2,1,0:T(8,128)(2,1)S(1)}, u32[]{:S(2)}, u32[]{:S(2)}) collective-permute-start(bf16[2,32,2048]{2,1,0:T(8,128)(2,1)S(1)} %get-tuple-element.65), channel_id=1, source_target_pairs={{0,1},{1,0},{2,3},{3,2},{4,5},{5,4},{6,7},{7,6},{8,9},{9,8},{10,11... | collective-permute-start | bytes 786440 | tf_op jit(solution)/shard_map/ppermute | solution.py:527
  75.7 3.7 %collective-permute-start.17 = (f32[32,128]{1,0:T(8,128)S(1)}, f32[32,128]{1,0:T(8,128)S(1)}, u32[]{:S(2)}, u32[]{:S(2)}) collective-permute-start(f32[32,128]{1,0:T(8,128)S(1)} %get-tuple-element.69.sums), channel_id=1, source_target_pairs={{0,4},{2,6},{4,0},{6,2},{1,5},{3,7},{5,1},{7,3},{8,12},{10,14},{12... | collective-permute-start | bytes 49160 | tf_op jit(solution)/shard_map/ppermute | solution.py:434
  80.2 9.7 %collective-permute-start.19 = (bf16[2,32,2048]{2,1,0:T(8,128)(2,1)S(1)}, bf16[2,32,2048]{2,1,0:T(8,128)(2,1)S(1)}, u32[]{:S(2)}, u32[]{:S(2)}) collective-permute-start(bf16[2,32,2048]{2,1,0:T(8,128)(2,1)S(1)} %shard_map.111.refs_0_), channel_id=1, source_target_pairs={{0,16},{8,24},{16,0},{24,8},{1,17},{9,25},{17,1},{25,9},{2,18},{10... | collective-permute-start | bytes 786440 | tf_op jit(solution)/shard_map/ppermute | solution.py:437
  80.3 9.6 %collective-permute-start.18 = (bf16[2,32,2048]{2,1,0:T(8,128)(2,1)S(1)}, bf16[2,32,2048]{2,1,0:T(8,128)(2,1)S(1)}, u32[]{:S(2)}, u32[]{:S(2)}) collective-permute-start(bf16[2,32,2048]{2,1,0:T(8,128)(2,1)S(1)} %shard_map.111.refs_0_), channel_id=1, source_target_pairs={{0,8},{8,0},{16,24},{24,16},{1,9},{9,1},{17,25},{25,17},{2,10},{10... | collective-permute-start | bytes 786440 | tf_op jit(solution)/shard_map/ppermute | solution.py:437
  82.2 7.7 %collective-permute-start.20 = (bf16[2,32,2048]{2,1,0:T(8,128)(2,1)S(1)}, bf16[2,32,2048]{2,1,0:T(8,128)(2,1)S(1)}, u32[]{:S(2)}, u32[]{:S(2)}) collective-permute-start(bf16[2,32,2048]{2,1,0:T(8,128)(2,1)S(1)} %shard_map.111.refs_0_), channel_id=1, source_target_pairs={{0,1},{1,0},{2,3},{3,2},{4,5},{5,4},{6,7},{7,6},{8,9},{9,8},{10,11... | collective-permute-start | bytes 786440 | tf_op jit(solution)/shard_map/ppermute | solution.py:527
  84.6 6.6 %collective-permute-start.16 = (bf16[2,2,16,2048]{3,2,1,0:T(8,128)(2,1)S(1)}, bf16[2,2,16,2048]{3,2,1,0:T(8,128)(2,1)S(1)}, u32[]{:S(2)}, u32[]{:S(2)}) collective-permute-start(bf16[2,2,16,2048]{3,2,1,0:T(8,128)(2,1)S(1)} %get-tuple-element.68), channel_id=1, source_target_pairs={{0,4},{2,6},{4,0},{6,2},{1,5},{3,7},{5,1},{7,3},{8,12},{10,14},{12... | collective-permute-start | bytes 786440 | tf_op jit(solution)/shard_map/ppermute | solution.py:434
  89.9 8.3 %collective-permute-start.22 = (bf16[2,32,2048]{2,1,0:T(8,128)(2,1)S(1)}, bf16[2,32,2048]{2,1,0:T(8,128)(2,1)S(1)}, u32[]{:S(2)}, u32[]{:S(2)}) collective-permute-start(bf16[2,32,2048]{2,1,0:T(8,128)(2,1)S(1)} %collective-permute-done.19.refs_2_), channel_id=1, source_target_pairs={{8,0},{16,24},{9,1},{17,25},{10,2},{18,26},{11,3},{19,27},{12,4},{... | collective-permute-start | bytes 786440 | tf_op jit(solution)/shard_map/ppermute | solution.py:437
  91.2 7.4 %collective-permute-start.23 = (bf16[2,32,2048]{2,1,0:T(8,128)(2,1)S(1)}, bf16[2,32,2048]{2,1,0:T(8,128)(2,1)S(1)}, u32[]{:S(2)}, u32[]{:S(2)}) collective-permute-start(bf16[2,32,2048]{2,1,0:T(8,128)(2,1)S(1)} %collective-permute-done.18.refs_1_), channel_id=1, source_target_pairs={{0,1},{1,0},{2,3},{3,2},{4,5},{5,4},{6,7},{7,6},{8,9},{9,8},{10,11... | collective-permute-start | bytes 786440 | tf_op jit(solution)/shard_map/ppermute | solution.py:527
  92.8 5.7 %collective-permute-start.21 = (bf16[2,32,2048]{2,1,0:T(8,128)(2,1)S(1)}, bf16[2,32,2048]{2,1,0:T(8,128)(2,1)S(1)}, u32[]{:S(2)}, u32[]{:S(2)}) collective-permute-start(bf16[2,32,2048]{2,1,0:T(8,128)(2,1)S(1)} %shard_map.111.refs_0_), channel_id=1, source_target_pairs={{8,16},{16,8},{9,17},{17,9},{10,18},{18,10},{11,19},{19,11},{12,20... | collective-permute-start | bytes 786440 | tf_op jit(solution)/shard_map/ppermute | solution.py:437
  93.5 9.7 %collective-permute-start.24 = (bf16[2,32,2048]{2,1,0:T(8,128)(2,1)S(1)}, bf16[2,32,2048]{2,1,0:T(8,128)(2,1)S(1)}, u32[]{:S(2)}, u32[]{:S(2)}) collective-permute-start(bf16[2,32,2048]{2,1,0:T(8,128)(2,1)S(1)} %collective-permute-done.19.refs_2_), channel_id=1, source_target_pairs={{0,1},{1,0},{2,3},{3,2},{4,5},{5,4},{6,7},{7,6},{8,9},{9,8},{10,11... | collective-permute-start | bytes 786440 | tf_op jit(solution)/shard_map/ppermute | solution.py:527
  103.2 6.4 %collective-permute-start.25 = (bf16[2,32,2048]{2,1,0:T(8,128)(2,1)S(1)}, bf16[2,32,2048]{2,1,0:T(8,128)(2,1)S(1)}, u32[]{:S(2)}, u32[]{:S(2)}) collective-permute-start(bf16[2,32,2048]{2,1,0:T(8,128)(2,1)S(1)} %shard_map.112.refs_3_), channel_id=1, source_target_pairs={{0,1},{1,0},{2,3},{3,2},{4,5},{5,4},{6,7},{7,6},{8,9},{9,8},{10,11... | collective-permute-start | bytes 786440 | tf_op jit(solution)/shard_map/ppermute | solution.py:527
  116.1 2.9 %collective-permute-start.27 = (f32[192,1024]{1,0:T(8,128)S(1)}, f32[192,1024]{1,0:T(8,128)S(1)}, u32[]{:S(2)}, u32[]{:S(2)}) collective-permute-start(f32[192,1024]{1,0:T(8,128)S(1)} %get-tuple-element.83), channel_id=1, source_target_pairs={{0,2},{2,0},{4,6},{6,4},{1,3},{3,1},{5,7},{7,5},{8,10},{10,8},{12,... | collective-permute-start | bytes 2359304 | tf_op jit(solution)/shard_map/ppermute | solution.py:431
  116.1 6.2 %collective-permute-start.26 = (bf16[64,1024]{1,0:T(8,128)(2,1)}, bf16[64,1024]{1,0:T(8,128)(2,1)}, u32[]{:S(2)}, u32[]{:S(2)}) collective-permute-start(bf16[64,1024]{1,0:T(8,128)(2,1)} %get-tuple-element.80), channel_id=1, source_target_pairs={{0,4},{2,6},{4,0},{6,2},{1,5},{3,7},{5,1},{7,3},{8,12},{10,14},{12... | collective-permute-start | bytes 393224 | tf_op jit(solution)/shard_map/ppermute | solution.py:434
  119.6 12.0 %collective-permute-start.29 = (bf16[192,1024]{1,0:T(8,128)(2,1)S(1)}, bf16[192,1024]{1,0:T(8,128)(2,1)S(1)}, u32[]{:S(2)}, u32[]{:S(2)}) collective-permute-start(bf16[192,1024]{1,0:T(8,128)(2,1)S(1)} %shard_map.115.own_right), channel_id=1, source_target_pairs={{0,4},{2,6},{4,0},{6,2},{1,5},{3,7},{5,1},{7,3},{8,12},{10,14},{12... | collective-permute-start | bytes 1179656 | tf_op jit(solution)/shard_map/ppermute | solution.py:434
  123.2 10.5 %collective-permute-start.28 = (bf16[64,1024]{1,0:T(8,128)(2,1)S(1)}, bf16[64,1024]{1,0:T(8,128)(2,1)S(1)}, u32[]{:S(2)}, u32[]{:S(2)}) collective-permute-start(bf16[64,1024]{1,0:T(8,128)(2,1)S(1)} %get-tuple-element.84), channel_id=1, source_target_pairs={{0,4},{2,6},{4,0},{6,2},{1,5},{3,7},{5,1},{7,3},{8,12},{10,14},{12... | collective-permute-start | bytes 393224 | tf_op jit(solution)/shard_map/ppermute | solution.py:434
  133.7 1.5 %collective-permute-start.30 = (bf16[128,1024]{1,0:T(8,128)(2,1)S(1)}, bf16[128,1024]{1,0:T(8,128)(2,1)S(1)}, u32[]{:S(2)}, u32[]{:S(2)}) collective-permute-start(bf16[128,1024]{1,0:T(8,128)(2,1)S(1)} %slice_select_fusion.own_left), channel_id=1, source_target_pairs={{0,2},{2,0},{4,6},{6,4},{1,3},{3,1},{5,7},{7,5},{8,10},{10,8},{12,... | collective-permute-start | bytes 786440 | tf_op jit(solution)/shard_map/ppermute | solution.py:431

commit v7 on v6

--- a/solution.py
+++ b/solution.py
@@ -543,12 +543,12 @@
 
     opposite = along(grad, *swaps[2])
     beside = along(grad, *swaps[1])
-    before = to_section(after(kept, final))
-    own_there = to_section(after(grad, before))
-    relay = after(opposite, own_there, beside)
+    own_there = to_section(grad)
+    before = to_section(after(kept, grad))
+    relay = after(opposite, beside)
     mid = along(after(grad, beside), (1, 2), (2, 1))
     farthest = along(relay, (1, 0), (2, 3))
-    opposite_there = to_section(opposite)
+    opposite_there = to_section(after(opposite, own_there))
     by_group, others = small(
         later_kernel,
         [((micro, 2, own_rows, width), BF16)] * 2,
@@ -561,22 +561,29 @@
         leaving,
     )
     others = to_outer(others)
-    beside_there = to_section(after(beside, others))
+    beside_there = to_section(beside)
     (section_out,) = small(
-        gather_kernel, [((micro, own_rows, features), BF16)], [], place, by_group, others
+        gather_kernel,
+        [((micro, own_rows, features), BF16)],
+        [],
+        place,
+        by_group,
+        others,
+        cost=pl.CostEstimate(flops=3 * 10**9, bytes_accessed=0, transcendentals=0),
     )
     (last,) = small(
-        join_kernel, [(shape, BF16)], [], place, mid, after(farthest, beside_there)
+        join_kernel, [(shape, BF16)], [], place, mid, after(farthest, beside_there, opposite_there),
+        cost=pl.CostEstimate(flops=5 * 10**9, bytes_accessed=0, transcendentals=0),
     )
     pieces = [grad, beside, relay, last]
-    pieces += [own_there, beside_there, opposite_there, to_section(after(last, opposite_there))]
+    pieces += [own_there, beside_there, opposite_there, to_section(after(last, section_out))]
     mix_here, first_sent, second_sent, kept_factors, sent_factors = back(
         place, pieces, weights, left_rows, right, mix_rows, permuted
     )
     (joined,) = small(
         sum_kernel, [(kept_factors.shape, BF16)], [], place, kept_factors, to_core(sent_factors)
     )
-    other_joined = after(to_outer(joined), section_out)
+    other_joined = to_outer(joined)
     best = jnp.where(outer == t // 2, joined[:rank], other_joined[:rank])
     (grad_right,) = small(
         right_kernel,

time: 137 us -> 137 us (level); the launches traced: 137 us -> 134 us
  starting transfers between devices: 43.7 us -> 41.2 us
    ppermute x14, waiting for transfers between devices: 34.2 us -> 31.1 us  [along(): return lax.ppermute(value, 'tensor', pairs)]
    ppermute x6, waiting for transfers between devices: 14.1 us -> 16.2 us  [to_section(): return lax.ppermute(value, 'pipe', [(0, 1), (1, 0)])]
    ppermute x6, starting transfers between devices: 8.59 us -> 6.88 us  [to_section(): return lax.ppermute(value, 'pipe', [(0, 1), (1, 0)])]
    ppermute x7, waiting for transfers between devices: 12.7 us -> 14.2 us  [to_outer(): return lax.ppermute(value, 'dp', [(i, i ^ 2) for i in range(4)])]
  transfers between devices with their start and end apart: 31 -> 31, of which waited for: 18 -> 21; matrix products, arithmetic and copies ran while one was open for 1% -> 1% of each run, Pallas kernels for 7% -> 6%
where the time goes in v7:
time: 137 us; the launch traced here: 134 us
  waiting for transfers between devices  63.8 us (47%)
  starting transfers between devices  41.2 us (30%)
  Pallas kernels  24.7 us (18%)
  local copies, waits for them, and re-layouts  2.84 us (2%)
    ppermute x14, waiting for transfers between devices, along(): return lax.ppermute(value, 'tensor', pairs)  31.1 us
    ppermute x14, starting transfers between devices, along(): return lax.ppermute(value, 'tensor', pairs)  23.7 us
    ppermute x6, waiting for transfers between devices, to_section(): return lax.ppermute(value, 'pipe', [(0, 1), (1, 0)])  16.2 us
    ppermute x7, waiting for transfers between devices, to_outer(): return lax.ppermute(value, 'dp', [(i, i ^ 2) for i in range(4)])  14.2 us
    pallas_call x15, Pallas kernels, small(): pl.pallas_call(kernel, in_specs=[pl.BlockSpec(memory_space=pltpu.SMEM)] +...  13 us
    ppermute x7, starting transfers between devices, to_outer(): return lax.ppermute(value, 'dp', [(i, i ^ 2) for i in range(4)])  9.94 us
    ppermute x6, starting transfers between devices, to_section(): return lax.ppermute(value, 'pipe', [(0, 1), (1, 0)])  6.88 us
    pallas_call x1, Pallas kernels, project(): pl.pallas_call(project_kernel, grid=(tiles,), in_specs=[pl.BlockSpec(memo...  5.85 us
  transfers between devices with their start and end apart: 31, of which 21 were waited for; matrix products, arithmetic and copies ran while one was open for 1% of the time, Pallas kernels for 6%

profile of v7, /device:TPU:0, one launch (start us, length us, event | category | flops | bytes accessed | tf_op | source)
XLA Modules:
  0.0 134.5 jit_solution(2432264970347777622)
XLA Ops:
  0.6 0.5 collective-permute-start.1
  1.1 0.9 dynamic-slice_bitcast_fusion
  2.1 4.7 %collective-permute-start.4 = (bf16[32,1024]{1,0:T(8,128)(2,1)S(1)}, bf16[32,1024]{1,0:T(8,128)(2,1)S(1)}, u32[]{:S(2)}, u32[]{:S(2)}) collective-permute-start(bf16[32,1024]{1,0:T(8,128)(2,1)S(1)} %get-tuple-element.90), channel_id=1, source_target_pairs={{0,24},{8,16},{16,8},{24,0},{1,25},{9,17},{17,9},{25,1},{2,26},{10... | collective-permute-start | bytes 196616 | tf_op jit(solution)/shard_map/ppermute | solution.py:437
  6.8 0.6 collective-permute-start.3
  7.4 1.6 %collective-permute-start = (bf16[2,64,1024]{2,1,0:T(8,128)(2,1)}, bf16[2,64,1024]{2,1,0:T(8,128)(2,1)S(1)}, u32[]{:S(2)}, u32[]{:S(2)}) collective-permute-start(bf16[2,64,1024]{2,1,0:T(8,128)(2,1)} %bitcast.48), channel_id=1, source_target_pairs={{0,4},{2,6},{4,0},{6,2},{1,5},{3,7},{5,1},{7,3},{8,12},{10,14},{12... | collective-permute-start | bytes 786440 | tf_op jit(solution)/shard_map/ppermute | solution.py:434
  9.2 0.9 copy-done.1
  10.1 0.9 copy-done.5
  11.1 0.6 shard_map.102
  11.6 1.0 collective-permute-done.3
  12.7 0.9 fusion.1
  13.7 1.3 collective-permute-done.5.other_half
  15.0 0.7 collective-permute-done.other_mix
  15.7 5.8 %shard_map.103 = (bf16[2,2,32,2048]{3,2,1,0:T(8,128)(2,1)S(1)}, bf16[2,2,32,2176]{3,2,1,0:T(8,128)(2,1)S(1)}, bf16[2,32,2176]{2,1,0:T(8,128)(2,1)S(1)}, bf16[2,3...) custom-call(s32[4]{0:T(128)S(1)} %pad_add_fusion.place, ...), custom_call_target="tpu_custom_call" | custom-call | tf_op jit(solution)/shard_map/pallas_call | solution.py:239
  21.6 3.3 %collective-permute-start.11 = (bf16[2,32,2048]{2,1,0:T(8,128)(2,1)S(1)}, bf16[2,32,2048]{2,1,0:T(8,128)(2,1)S(1)}, u32[]{:S(2)}, u32[]{:S(2)}) collective-permute-start(bf16[2,32,2048]{2,1,0:T(8,128)(2,1)S(1)} %get-tuple-element.54), channel_id=1, source_target_pairs={{0,8},{24,16},{1,9},{25,17},{2,10},{26,18},{3,11},{27,19},{4,12},{... | collective-permute-start | bytes 786440 | tf_op jit(solution)/shard_map/ppermute | solution.py:437
  24.9 1.3 collective-permute-start.10
  26.3 0.7 collective-permute-start.8
  26.9 0.7 collective-permute-start.9
  27.6 3.9 %collective-permute-start.7 = (bf16[2,2,32,2176]{3,2,1,0:T(8,128)(2,1)S(1)}, bf16[2,2,32,2176]{3,2,1,0:T(8,128)(2,1)S(1)}, u32[]{:S(2)}, u32[]{:S(2)}) collective-permute-start(bf16[2,2,32,2176]{3,2,1,0:T(8,128)(2,1)S(1)} %get-tuple-element.51), channel_id=1, source_target_pairs={{0,8},{8,0},{16,24},{24,16},{1,9},{9,1},{17,25},{25,17},{2,10},{10... | collective-permute-start | bytes 1671176 | tf_op jit(solution)/shard_map/ppermute | solution.py:437
  31.5 0.6 shard_map.104
  32.2 1.5 %collective-permute-start.6 = (bf16[2,2,2,16,2048]{4,3,2,1,0:T(8,128)(2,1)S(1)}, bf16[2,2,2,16,2048]{4,3,2,1,0:T(8,128)(2,1)S(1)}, u32[]{:S(2)}, u32[]{:S(2)}) collective-permute-start(bf16[2,2,2,16,2048]{4,3,2,1,0:T(8,128)(2,1)S(1)} %get-tuple-element.50), channel_id=1, source_target_pairs={{0,4},{2,6},{4,0},{6,2},{1,5},{3,7},{5,1},{7,3},{8,12},{10,14},{12... | collective-permute-start | bytes 1572872 | tf_op jit(solution)/shard_map/ppermute | solution.py:434
  33.7 3.9 %collective-permute-done.10.passed = bf16[2,32,2176]{2,1,0:T(8,128)(2,1)S(1)} collective-permute-done((bf16[2,32,2176]{2,1,0:T(8,128)(2,1)S(1)}, bf16[2,32,2176]{2,1,0:T(8,128)(2,1)S(1)}, u32[]{:S(2)}, u32[]{:S(2)}) %collective-permute-start.10) | collective-permute-done | bytes 278560 | tf_op jit(solution)/shard_map/ppermute | solution.py:437
  37.6 0.6 shard_map.105
  38.3 4.4 %collective-permute-start.12 = (bf16[2,32,2304]{2,1,0:T(8,128)(2,1)S(1)}, bf16[2,32,2304]{2,1,0:T(8,128)(2,1)S(1)}, u32[]{:S(2)}, u32[]{:S(2)}) collective-permute-start(bf16[2,32,2304]{2,1,0:T(8,128)(2,1)S(1)} %shard_map.105), channel_id=1, source_target_pairs={{0,16},{8,24},{16,0},{24,8},{1,17},{9,25},{17,1},{25,9},{2,18},{10... | collective-permute-start | bytes 884744 | tf_op jit(solution)/shard_map/ppermute | solution.py:437
  42.7 0.6 shard_map.106
  43.4 1.2 collective-permute-done.6.arrived
  44.6 6.7 %collective-permute-done.7.beside.refs_14_ = bf16[2,2,32,2176]{3,2,1,0:T(8,128)(2,1)S(1)} collective-permute-done((bf16[2,2,32,2176]{3,2,1,0:T(8,128)(2,1)S(1)}, bf16[2,2,32,2176]{3,2,1,0:T(8,128)(2,1)S(1)}, u32[]{:S(2)}, u32[]{:S(2)}) %collective-permute-start.7) | collective-permute-done | bytes 557088 | tf_op jit(solution)/shard_map/ppermute | solution.py:437
  51.3 14.7 %collective-permute-done.13.refs_3_ = bf16[2,32,2048]{2,1,0:T(8,128)(2,1)S(1)} collective-permute-done((bf16[2,32,2048]{2,1,0:T(8,128)(2,1)S(1)}, bf16[2,32,2048]{2,1,0:T(8,128)(2,1)S(1)}, u32[]{:S(2)}, u32[]{:S(2)}) %collective-permute-start.13) | collective-permute-done | bytes 262176 | tf_op jit(solution)/shard_map/ppermute | solution.py:437
  66.0 0.8 shard_map.107
  66.8 1.6 %collective-permute-start.14 = (bf16[2,32,2048]{2,1,0:T(8,128)(2,1)S(1)}, bf16[2,32,2048]{2,1,0:T(8,128)(2,1)S(1)}, u32[]{:S(2)}, u32[]{:S(2)}) collective-permute-start(bf16[2,32,2048]{2,1,0:T(8,128)(2,1)S(1)} %get-tuple-element.61), channel_id=1, source_target_pairs={{0,1},{1,0},{2,3},{3,2},{4,5},{5,4},{6,7},{7,6},{8,9},{9,8},{10,11... | collective-permute-start | bytes 786440 | tf_op jit(solution)/shard_map/ppermute | solution.py:527
  68.4 4.8 %collective-permute-done.14.other = bf16[2,32,2048]{2,1,0:T(8,128)(2,1)S(1)} collective-permute-done((bf16[2,32,2048]{2,1,0:T(8,128)(2,1)S(1)}, bf16[2,32,2048]{2,1,0:T(8,128)(2,1)S(1)}, u32[]{:S(2)}, u32[]{:S(2)}) %collective-permute-start.14) | collective-permute-done | bytes 262176 | tf_op jit(solution)/shard_map/ppermute | solution.py:527
  73.2 0.9 shard_map.108
  74.1 1.6 %collective-permute-start.15 = (f32[32,128]{1,0:T(8,128)S(1)}, f32[32,128]{1,0:T(8,128)S(1)}, u32[]{:S(2)}, u32[]{:S(2)}) collective-permute-start(f32[32,128]{1,0:T(8,128)S(1)} %get-tuple-element.63.sums), channel_id=1, source_target_pairs={{0,4},{2,6},{4,0},{6,2},{1,5},{3,7},{5,1},{7,3},{8,12},{10,14},{12... | collective-permute-start | bytes 49160 | tf_op jit(solution)/shard_map/ppermute | solution.py:434
  75.7 2.2 %collective-permute-done.15.other_sums = f32[32,128]{1,0:T(8,128)S(1)} collective-permute-done((f32[32,128]{1,0:T(8,128)S(1)}, f32[32,128]{1,0:T(8,128)S(1)}, u32[]{:S(2)}, u32[]{:S(2)}) %collective-permute-start.15) | collective-permute-done | bytes 16416 | tf_op jit(solution)/shard_map/ppermute | solution.py:434
  77.9 0.8 shard_map.109.refs_0_
  78.7 1.6 %collective-permute-start.23 = (bf16[2,32,2048]{2,1,0:T(8,128)(2,1)S(1)}, bf16[2,32,2048]{2,1,0:T(8,128)(2,1)S(1)}, u32[]{:S(2)}, u32[]{:S(2)}) collective-permute-start(bf16[2,32,2048]{2,1,0:T(8,128)(2,1)S(1)} %shard_map.109.refs_0_), channel_id=1, source_target_pairs={{0,1},{1,0},{2,3},{3,2},{4,5},{5,4},{6,7},{7,6},{8,9},{9,8},{10,11... | collective-permute-start | bytes 786440 | tf_op jit(solution)/shard_map/ppermute | solution.py:527
  80.3 1.9 %collective-permute-start.18 = (bf16[2,32,2048]{2,1,0:T(8,128)(2,1)S(1)}, bf16[2,32,2048]{2,1,0:T(8,128)(2,1)S(1)}, u32[]{:S(2)}, u32[]{:S(2)}) collective-permute-start(bf16[2,32,2048]{2,1,0:T(8,128)(2,1)S(1)} %shard_map.109.refs_0_), channel_id=1, source_target_pairs={{0,8},{8,0},{16,24},{24,16},{1,9},{9,1},{17,25},{25,17},{2,10},{10... | collective-permute-start | bytes 786440 | tf_op jit(solution)/shard_map/ppermute | solution.py:437
  82.2 0.5 collective-permute-start.16
  82.7 2.7 %collective-permute-done.23.refs_4_ = bf16[2,32,2048]{2,1,0:T(8,128)(2,1)S(1)} collective-permute-done((bf16[2,32,2048]{2,1,0:T(8,128)(2,1)S(1)}, bf16[2,32,2048]{2,1,0:T(8,128)(2,1)S(1)}, u32[]{:S(2)}, u32[]{:S(2)}) %collective-permute-start.23) | collective-permute-done | bytes 262176 | tf_op jit(solution)/shard_map/ppermute | solution.py:527
  85.4 3.8 %collective-permute-done.19.refs_2_ = bf16[2,32,2048]{2,1,0:T(8,128)(2,1)S(1)} collective-permute-done((bf16[2,32,2048]{2,1,0:T(8,128)(2,1)S(1)}, bf16[2,32,2048]{2,1,0:T(8,128)(2,1)S(1)}, u32[]{:S(2)}, u32[]{:S(2)}) %collective-permute-start.19) | collective-permute-done | bytes 262176 | tf_op jit(solution)/shard_map/ppermute | solution.py:437
  89.7 1.3 collective-permute-start.21
  91.0 1.5 %collective-permute-start.22 = (bf16[2,32,2048]{2,1,0:T(8,128)(2,1)S(1)}, bf16[2,32,2048]{2,1,0:T(8,128)(2,1)S(1)}, u32[]{:S(2)}, u32[]{:S(2)}) collective-permute-start(bf16[2,32,2048]{2,1,0:T(8,128)(2,1)S(1)} %collective-permute-done.18.refs_1_), channel_id=1, source_target_pairs={{0,1},{1,0},{2,3},{3,2},{4,5},{5,4},{6,7},{7,6},{8,9},{9,8},{10,11... | collective-permute-start | bytes 786440 | tf_op jit(solution)/shard_map/ppermute | solution.py:527
  92.5 0.7 shard_map.110
  93.2 1.6 %collective-permute-start.17 = (bf16[2,2,16,2048]{3,2,1,0:T(8,128)(2,1)S(1)}, bf16[2,2,16,2048]{3,2,1,0:T(8,128)(2,1)S(1)}, u32[]{:S(2)}, u32[]{:S(2)}) collective-permute-start(bf16[2,2,16,2048]{3,2,1,0:T(8,128)(2,1)S(1)} %get-tuple-element.67), channel_id=1, source_target_pairs={{0,4},{2,6},{4,0},{6,2},{1,5},{3,7},{5,1},{7,3},{8,12},{10,14},{12... | collective-permute-start | bytes 786440 | tf_op jit(solution)/shard_map/ppermute | solution.py:434
  94.8 0.7 collective-permute-start.20
  95.4 1.6 %collective-permute-done.24.refs_6_ = bf16[2,32,2048]{2,1,0:T(8,128)(2,1)S(1)} collective-permute-done((bf16[2,32,2048]{2,1,0:T(8,128)(2,1)S(1)}, bf16[2,32,2048]{2,1,0:T(8,128)(2,1)S(1)}, u32[]{:S(2)}, u32[]{:S(2)}) %collective-permute-start.24) | collective-permute-done | bytes 262176 | tf_op jit(solution)/shard_map/ppermute | solution.py:527
  97.0 1.0 collective-permute-done.21.farthest
  98.0 1.8 %collective-permute-done.22.refs_5_ = bf16[2,32,2048]{2,1,0:T(8,128)(2,1)S(1)} collective-permute-done((bf16[2,32,2048]{2,1,0:T(8,128)(2,1)S(1)}, bf16[2,32,2048]{2,1,0:T(8,128)(2,1)S(1)}, u32[]{:S(2)}, u32[]{:S(2)}) %collective-permute-start.22) | collective-permute-done | bytes 262176 | tf_op jit(solution)/shard_map/ppermute | solution.py:527
  99.8 1.4 %shard_map.111 = bf16[2,16,8192]{2,1,0:T(8,128)(2,1)} custom-call(s32[4]{0:T(128)S(1)} %pad_add_fusion.place, bf16[2,2,16,2048]{3,2,1,0:T(8,128)(2,1)S(1)} %get-tuple-element.66.here, bf16[2,2,16,2048]{3,2,1,0:T(8,128)(2,1)S(1)} %collective-permute-done.17.arrived), custom_call_target="tpu_custom_call" | custom-call | flops 3000000000 | tf_op jit(solution)/shard_map/pallas_call | solution.py:43
  101.2 0.6 shard_map.112.refs_3_
  101.8 1.2 collective-permute-start.25
  103.0 5.2 %collective-permute-done.25.refs_7_ = bf16[2,32,2048]{2,1,0:T(8,128)(2,1)S(1)} collective-permute-done((bf16[2,32,2048]{2,1,0:T(8,128)(2,1)S(1)}, bf16[2,32,2048]{2,1,0:T(8,128)(2,1)S(1)}, u32[]{:S(2)}, u32[]{:S(2)}) %collective-permute-start.25) | collective-permute-done | bytes 262176 | tf_op jit(solution)/shard_map/ppermute | solution.py:527
  108.2 5.8 %shard_map.113 = (f32[2,64,1024]{2,1,0:T(8,128)S(1)}, bf16[64,1024]{1,0:T(8,128)(2,1)S(1)}, bf16[64,1024]{1,0:T(8,128)(2,1)S(1)}, f32[192,1024]{1,0:T(8,128)S(1)}, f32[192,1024]{1,0:T(8,128)S(1)}) custom-call(s32[4]{0:T(128)S(1)} %pad_add_fusion.place, bf16[2,32,2048]{2,1,0:T(8,128)(2,1)S(1)} %shard_map.109.refs_0_, ...), custom_call_target="tpu_custom_call" | custom-call | tf_op jit(solution)/shard_map/pallas_call | solution.py:350
  114.1 1.6 %collective-permute-start.26 = (bf16[64,1024]{1,0:T(8,128)(2,1)S(1)}, bf16[64,1024]{1,0:T(8,128)(2,1)S(1)}, u32[]{:S(2)}, u32[]{:S(2)}) collective-permute-start(bf16[64,1024]{1,0:T(8,128)(2,1)S(1)} %get-tuple-element.77), channel_id=1, source_target_pairs={{0,4},{2,6},{4,0},{6,2},{1,5},{3,7},{5,1},{7,3},{8,12},{10,14},{12... | collective-permute-start | bytes 393224 | tf_op jit(solution)/shard_map/ppermute | solution.py:434
  115.6 0.7 collective-permute-done.27.arrived
  116.4 0.6 shard_map.115.own_right
  117.0 1.6 %collective-permute-start.29 = (bf16[192,1024]{1,0:T(8,128)(2,1)S(1)}, bf16[192,1024]{1,0:T(8,128)(2,1)S(1)}, u32[]{:S(2)}, u32[]{:S(2)}) collective-permute-start(bf16[192,1024]{1,0:T(8,128)(2,1)S(1)} %shard_map.115.own_right), channel_id=1, source_target_pairs={{0,4},{2,6},{4,0},{6,2},{1,5},{3,7},{5,1},{7,3},{8,12},{10,14},{12... | collective-permute-start | bytes 1179656 | tf_op jit(solution)/shard_map/ppermute | solution.py:434
  118.5 0.5 collective-permute-start.28
  119.1 1.1 collective-permute-done.26.arrived
  120.2 0.6 shard_map.114.first
  120.7 8.3 %collective-permute-done.29.other_right = bf16[192,1024]{1,0:T(8,128)(2,1)S(1)} collective-permute-done((bf16[192,1024]{1,0:T(8,128)(2,1)S(1)}, bf16[192,1024]{1,0:T(8,128)(2,1)S(1)}, u32[]{:S(2)}, u32[]{:S(2)}) %collective-permute-start.29) | collective-permute-done | bytes 393248 | tf_op jit(solution)/shard_map/ppermute | solution.py:434
  129.0 1.6 %shard_map.116 = f32[1024,128]{1,0:T(8,128)} custom-call(s32[4]{0:T(128)S(1)} %pad_add_fusion.place, bf16[192,1024]{1,0:T(8,128)(2,1)S(1)} %shard_map.115.own_right, bf16[192,1024]{1,0:T(8,128)(2,1)S(1)} %collective-permute-done.29.other_right), custom_call_target="tpu_custom_call" | custom-call | tf_op jit(solution)/shard_map/pallas_call | solution.py:43
  130.6 0.7 collective-permute-done.28.arrived
  131.4 1.3 shard_map.117
  132.9 1.6 %shard_map.118 = f32[128,2048]{1,0:T(8,128)} custom-call(s32[4]{0:T(128)S(1)} %pad_add_fusion.place, bf16[128,1024]{1,0:T(8,128)(2,1)S(1)} %slice_select_fusion.own_left, bf16[128,1024]{1,0:T(8,128)(2,1)S(1)} %collective-permute-done.30.other_left), custom_call_target="tpu_custom_call" | custom-call | flops 8000000000 | tf_op jit(solution)/shard_map/pallas_call | solution.py:43
  (35 shorter events, 1.3 us)
Async XLA Ops:
  0.6 15.1 %collective-permute-start.1 = (bf16[1024,2048]{1,0:T(8,128)(2,1)}, bf16[1024,2048]{1,0:T(8,128)(2,1)}, u32[]{:S(2)}, u32[]{:S(2)}) collective-permute-start(bf16[1024,2048]{1,0:T(8,128)(2,1)} %bitcast.39), channel_id=1, source_target_pairs={{0,2},{2,0},{4,6},{6,4},{1,3},{3,1},{5,7},{7,5},{8,10},{10,8},{12,... | collective-permute-start | bytes 12582920 | tf_op jit(solution)/shard_map/ppermute | solution.py:431
  2.1 10.6 %collective-permute-start.4 = (bf16[32,1024]{1,0:T(8,128)(2,1)S(1)}, bf16[32,1024]{1,0:T(8,128)(2,1)S(1)}, u32[]{:S(2)}, u32[]{:S(2)}) collective-permute-start(bf16[32,1024]{1,0:T(8,128)(2,1)S(1)} %get-tuple-element.90), channel_id=1, source_target_pairs={{0,24},{8,16},{16,8},{24,0},{1,25},{9,17},{17,9},{25,1},{2,26},{10... | collective-permute-start | bytes 196616 | tf_op jit(solution)/shard_map/ppermute | solution.py:437
  6.8 5.9 %collective-permute-start.2 = (bf16[32,1024]{1,0:T(8,128)(2,1)S(1)}, bf16[32,1024]{1,0:T(8,128)(2,1)S(1)}, u32[]{:S(2)}, u32[]{:S(2)}) collective-permute-start(bf16[32,1024]{1,0:T(8,128)(2,1)S(1)} %get-tuple-element.91), channel_id=1, source_target_pairs={{0,8},{8,0},{16,24},{24,16},{1,9},{9,1},{17,25},{25,17},{2,10},{10... | collective-permute-start | bytes 196616 | tf_op jit(solution)/shard_map/ppermute | solution.py:437
  6.8 5.9 %collective-permute-start.3 = (bf16[32,1024]{1,0:T(8,128)(2,1)S(1)}, bf16[32,1024]{1,0:T(8,128)(2,1)S(1)}, u32[]{:S(2)}, u32[]{:S(2)}) collective-permute-start(bf16[32,1024]{1,0:T(8,128)(2,1)S(1)} %get-tuple-element.92), channel_id=1, source_target_pairs={{0,16},{8,24},{16,0},{24,8},{1,17},{9,25},{17,1},{25,9},{2,18},{10... | collective-permute-start | bytes 196616 | tf_op jit(solution)/shard_map/ppermute | solution.py:437
  7.4 8.3 %collective-permute-start = (bf16[2,64,1024]{2,1,0:T(8,128)(2,1)}, bf16[2,64,1024]{2,1,0:T(8,128)(2,1)S(1)}, u32[]{:S(2)}, u32[]{:S(2)}) collective-permute-start(bf16[2,64,1024]{2,1,0:T(8,128)(2,1)} %bitcast.48), channel_id=1, source_target_pairs={{0,4},{2,6},{4,0},{6,2},{1,5},{3,7},{5,1},{7,3},{8,12},{10,14},{12... | collective-permute-start | bytes 786440 | tf_op jit(solution)/shard_map/ppermute | solution.py:434
  9.2 1.0 copy-start.1
  10.1 0.9 copy-start.5
  13.6 17.9 %copy-start.3 = (bf16[2,1,16,8192]{3,2,1,0:T(8,128)(2,1)S(1)}, bf16[2,1,16,8192]{3,2,1,0:T(8,128)(2,1)}, u32[]{:S(2)}) copy-start(bf16[2,1,16,8192]{3,2,1,0:T(8,128)(2,1)} %param.8) | copy-start | bytes 1572868
  13.6 17.9 %copy-start.4 = (bf16[2,1,16,8192]{3,2,1,0:T(8,128)(2,1)S(1)}, bf16[2,1,16,8192]{3,2,1,0:T(8,128)(2,1)}, u32[]{:S(2)}) copy-start(bf16[2,1,16,8192]{3,2,1,0:T(8,128)(2,1)} %param.9) | copy-start | bytes 1572868
  13.6 1.4 %collective-permute-start.5 = (bf16[2,32,1024]{2,1,0:T(8,128)(2,1)S(1)}, bf16[2,32,1024]{2,1,0:T(8,128)(2,1)S(1)}, u32[]{:S(2)}, u32[]{:S(2)}) collective-permute-start(bf16[2,32,1024]{2,1,0:T(8,128)(2,1)S(1)} %pad_maximum_fusion.own_half), channel_id=1, source_target_pairs={{0,2},{2,0},{4,6},{6,4},{1,3},{3,1},{5,7},{7,5},{8,10},{10,8},{12,... | collective-permute-start | bytes 393224 | tf_op jit(solution)/shard_map/ppermute | solution.py:431
  21.6 46.8 %copy-start.6 = (bf16[8192]{0:T(1024)(128)(2,1)S(1)}, bf16[8192]{0:T(1024)(128)(2,1)}, u32[]{:S(2)}) copy-start(bf16[8192]{0:T(1024)(128)(2,1)} %param.13) | copy-start | bytes 49156
  21.6 10.6 %collective-permute-start.11 = (bf16[2,32,2048]{2,1,0:T(8,128)(2,1)S(1)}, bf16[2,32,2048]{2,1,0:T(8,128)(2,1)S(1)}, u32[]{:S(2)}, u32[]{:S(2)}) collective-permute-start(bf16[2,32,2048]{2,1,0:T(8,128)(2,1)S(1)} %get-tuple-element.54), channel_id=1, source_target_pairs={{0,8},{24,16},{1,9},{25,17},{2,10},{26,18},{3,11},{27,19},{4,12},{... | collective-permute-start | bytes 786440 | tf_op jit(solution)/shard_map/ppermute | solution.py:437
  24.9 12.7 %collective-permute-start.10 = (bf16[2,32,2176]{2,1,0:T(8,128)(2,1)S(1)}, bf16[2,32,2176]{2,1,0:T(8,128)(2,1)S(1)}, u32[]{:S(2)}, u32[]{:S(2)}) collective-permute-start(bf16[2,32,2176]{2,1,0:T(8,128)(2,1)S(1)} %get-tuple-element.53), channel_id=1, source_target_pairs={{0,8},{24,16},{1,9},{25,17},{2,10},{26,18},{3,11},{27,19},{4,12},{... | collective-permute-start | bytes 835592 | tf_op jit(solution)/shard_map/ppermute | solution.py:437
  26.3 11.4 %collective-permute-start.8 = (bf16[2,32,2176]{2,1,0:T(8,128)(2,1)S(1)}, bf16[2,32,2176]{2,1,0:T(8,128)(2,1)S(1)}, u32[]{:S(2)}, u32[]{:S(2)}) collective-permute-start(bf16[2,32,2176]{2,1,0:T(8,128)(2,1)S(1)} %get-tuple-element.53), channel_id=1, source_target_pairs={{8,16},{16,8},{9,17},{17,9},{10,18},{18,10},{11,19},{19,11},{12,20... | collective-permute-start | bytes 835592 | tf_op jit(solution)/shard_map/ppermute | solution.py:437
  26.9 6.8 %collective-permute-start.9 = (bf16[2,32,2048]{2,1,0:T(8,128)(2,1)S(1)}, bf16[2,32,2048]{2,1,0:T(8,128)(2,1)S(1)}, u32[]{:S(2)}, u32[]{:S(2)}) collective-permute-start(bf16[2,32,2048]{2,1,0:T(8,128)(2,1)S(1)} %get-tuple-element.54), channel_id=1, source_target_pairs={{8,16},{16,8},{9,17},{17,9},{10,18},{18,10},{11,19},{19,11},{12,20... | collective-permute-start | bytes 786440 | tf_op jit(solution)/shard_map/ppermute | solution.py:437
  27.6 23.6 %collective-permute-start.7 = (bf16[2,2,32,2176]{3,2,1,0:T(8,128)(2,1)S(1)}, bf16[2,2,32,2176]{3,2,1,0:T(8,128)(2,1)S(1)}, u32[]{:S(2)}, u32[]{:S(2)}) collective-permute-start(bf16[2,2,32,2176]{3,2,1,0:T(8,128)(2,1)S(1)} %get-tuple-element.51), channel_id=1, source_target_pairs={{0,8},{8,0},{16,24},{24,16},{1,9},{9,1},{17,25},{25,17},{2,10},{10... | collective-permute-start | bytes 1671176 | tf_op jit(solution)/shard_map/ppermute | solution.py:437
  32.2 12.4 %collective-permute-start.6 = (bf16[2,2,2,16,2048]{4,3,2,1,0:T(8,128)(2,1)S(1)}, bf16[2,2,2,16,2048]{4,3,2,1,0:T(8,128)(2,1)S(1)}, u32[]{:S(2)}, u32[]{:S(2)}) collective-permute-start(bf16[2,2,2,16,2048]{4,3,2,1,0:T(8,128)(2,1)S(1)} %get-tuple-element.50), channel_id=1, source_target_pairs={{0,4},{2,6},{4,0},{6,2},{1,5},{3,7},{5,1},{7,3},{8,12},{10,14},{12... | collective-permute-start | bytes 1572872 | tf_op jit(solution)/shard_map/ppermute | solution.py:434
  38.3 27.7 %collective-permute-start.12 = (bf16[2,32,2304]{2,1,0:T(8,128)(2,1)S(1)}, bf16[2,32,2304]{2,1,0:T(8,128)(2,1)S(1)}, u32[]{:S(2)}, u32[]{:S(2)}) collective-permute-start(bf16[2,32,2304]{2,1,0:T(8,128)(2,1)S(1)} %shard_map.105), channel_id=1, source_target_pairs={{0,16},{8,24},{16,0},{24,8},{1,17},{9,25},{17,1},{25,9},{2,18},{10... | collective-permute-start | bytes 884744 | tf_op jit(solution)/shard_map/ppermute | solution.py:437
  43.3 22.7 %collective-permute-start.13 = (bf16[2,32,2048]{2,1,0:T(8,128)(2,1)S(1)}, bf16[2,32,2048]{2,1,0:T(8,128)(2,1)S(1)}, u32[]{:S(2)}, u32[]{:S(2)}) collective-permute-start(bf16[2,32,2048]{2,1,0:T(8,128)(2,1)S(1)} %shard_map.106), channel_id=1, source_target_pairs={{0,16},{8,24},{16,0},{24,8},{1,17},{9,25},{17,1},{25,9},{2,18},{10... | collective-permute-start | bytes 786440 | tf_op jit(solution)/shard_map/ppermute | solution.py:437
  66.8 6.4 %collective-permute-start.14 = (bf16[2,32,2048]{2,1,0:T(8,128)(2,1)S(1)}, bf16[2,32,2048]{2,1,0:T(8,128)(2,1)S(1)}, u32[]{:S(2)}, u32[]{:S(2)}) collective-permute-start(bf16[2,32,2048]{2,1,0:T(8,128)(2,1)S(1)} %get-tuple-element.61), channel_id=1, source_target_pairs={{0,1},{1,0},{2,3},{3,2},{4,5},{5,4},{6,7},{7,6},{8,9},{9,8},{10,11... | collective-permute-start | bytes 786440 | tf_op jit(solution)/shard_map/ppermute | solution.py:527
  74.1 3.8 %collective-permute-start.15 = (f32[32,128]{1,0:T(8,128)S(1)}, f32[32,128]{1,0:T(8,128)S(1)}, u32[]{:S(2)}, u32[]{:S(2)}) collective-permute-start(f32[32,128]{1,0:T(8,128)S(1)} %get-tuple-element.63.sums), channel_id=1, source_target_pairs={{0,4},{2,6},{4,0},{6,2},{1,5},{3,7},{5,1},{7,3},{8,12},{10,14},{12... | collective-permute-start | bytes 49160 | tf_op jit(solution)/shard_map/ppermute | solution.py:434
  78.7 6.7 %collective-permute-start.23 = (bf16[2,32,2048]{2,1,0:T(8,128)(2,1)S(1)}, bf16[2,32,2048]{2,1,0:T(8,128)(2,1)S(1)}, u32[]{:S(2)}, u32[]{:S(2)}) collective-permute-start(bf16[2,32,2048]{2,1,0:T(8,128)(2,1)S(1)} %shard_map.109.refs_0_), channel_id=1, source_target_pairs={{0,1},{1,0},{2,3},{3,2},{4,5},{5,4},{6,7},{7,6},{8,9},{9,8},{10,11... | collective-permute-start | bytes 786440 | tf_op jit(solution)/shard_map/ppermute | solution.py:527
  80.3 8.9 %collective-permute-start.19 = (bf16[2,32,2048]{2,1,0:T(8,128)(2,1)S(1)}, bf16[2,32,2048]{2,1,0:T(8,128)(2,1)S(1)}, u32[]{:S(2)}, u32[]{:S(2)}) collective-permute-start(bf16[2,32,2048]{2,1,0:T(8,128)(2,1)S(1)} %shard_map.109.refs_0_), channel_id=1, source_target_pairs={{0,16},{8,24},{16,0},{24,8},{1,17},{9,25},{17,1},{25,9},{2,18},{10... | collective-permute-start | bytes 786440 | tf_op jit(solution)/shard_map/ppermute | solution.py:437
  80.3 9.4 %collective-permute-start.18 = (bf16[2,32,2048]{2,1,0:T(8,128)(2,1)S(1)}, bf16[2,32,2048]{2,1,0:T(8,128)(2,1)S(1)}, u32[]{:S(2)}, u32[]{:S(2)}) collective-permute-start(bf16[2,32,2048]{2,1,0:T(8,128)(2,1)S(1)} %shard_map.109.refs_0_), channel_id=1, source_target_pairs={{0,8},{8,0},{16,24},{24,16},{1,9},{9,1},{17,25},{25,17},{2,10},{10... | collective-permute-start | bytes 786440 | tf_op jit(solution)/shard_map/ppermute | solution.py:437
  82.2 10.3 %collective-permute-start.16 = (bf16[2,32,2048]{2,1,0:T(8,128)(2,1)S(1)}, bf16[2,32,2048]{2,1,0:T(8,128)(2,1)S(1)}, u32[]{:S(2)}, u32[]{:S(2)}) collective-permute-start(bf16[2,32,2048]{2,1,0:T(8,128)(2,1)S(1)} %get-tuple-element.64), channel_id=1, source_target_pairs={{0,1},{1,0},{2,3},{3,2},{4,5},{5,4},{6,7},{7,6},{8,9},{9,8},{10,11... | collective-permute-start | bytes 786440 | tf_op jit(solution)/shard_map/ppermute | solution.py:527
  89.1 7.8 %collective-permute-start.24 = (bf16[2,32,2048]{2,1,0:T(8,128)(2,1)S(1)}, bf16[2,32,2048]{2,1,0:T(8,128)(2,1)S(1)}, u32[]{:S(2)}, u32[]{:S(2)}) collective-permute-start(bf16[2,32,2048]{2,1,0:T(8,128)(2,1)S(1)} %collective-permute-done.19.refs_2_), channel_id=1, source_target_pairs={{0,1},{1,0},{2,3},{3,2},{4,5},{5,4},{6,7},{7,6},{8,9},{9,8},{10,11... | collective-permute-start | bytes 786440 | tf_op jit(solution)/shard_map/ppermute | solution.py:527
  89.7 8.3 %collective-permute-start.21 = (bf16[2,32,2048]{2,1,0:T(8,128)(2,1)S(1)}, bf16[2,32,2048]{2,1,0:T(8,128)(2,1)S(1)}, u32[]{:S(2)}, u32[]{:S(2)}) collective-permute-start(bf16[2,32,2048]{2,1,0:T(8,128)(2,1)S(1)} %collective-permute-done.19.refs_2_), channel_id=1, source_target_pairs={{8,0},{16,24},{9,1},{17,25},{10,2},{18,26},{11,3},{19,27},{12,4},{... | collective-permute-start | bytes 786440 | tf_op jit(solution)/shard_map/ppermute | solution.py:437
  91.0 8.8 %collective-permute-start.22 = (bf16[2,32,2048]{2,1,0:T(8,128)(2,1)S(1)}, bf16[2,32,2048]{2,1,0:T(8,128)(2,1)S(1)}, u32[]{:S(2)}, u32[]{:S(2)}) collective-permute-start(bf16[2,32,2048]{2,1,0:T(8,128)(2,1)S(1)} %collective-permute-done.18.refs_1_), channel_id=1, source_target_pairs={{0,1},{1,0},{2,3},{3,2},{4,5},{5,4},{6,7},{7,6},{8,9},{9,8},{10,11... | collective-permute-start | bytes 786440 | tf_op jit(solution)/shard_map/ppermute | solution.py:527
  93.2 6.6 %collective-permute-start.17 = (bf16[2,2,16,2048]{3,2,1,0:T(8,128)(2,1)S(1)}, bf16[2,2,16,2048]{3,2,1,0:T(8,128)(2,1)S(1)}, u32[]{:S(2)}, u32[]{:S(2)}) collective-permute-start(bf16[2,2,16,2048]{3,2,1,0:T(8,128)(2,1)S(1)} %get-tuple-element.67), channel_id=1, source_target_pairs={{0,4},{2,6},{4,0},{6,2},{1,5},{3,7},{5,1},{7,3},{8,12},{10,14},{12... | collective-permute-start | bytes 786440 | tf_op jit(solution)/shard_map/ppermute | solution.py:434
  94.8 6.4 %collective-permute-start.20 = (bf16[2,32,2048]{2,1,0:T(8,128)(2,1)S(1)}, bf16[2,32,2048]{2,1,0:T(8,128)(2,1)S(1)}, u32[]{:S(2)}, u32[]{:S(2)}) collective-permute-start(bf16[2,32,2048]{2,1,0:T(8,128)(2,1)S(1)} %shard_map.109.refs_0_), channel_id=1, source_target_pairs={{8,16},{16,8},{9,17},{17,9},{10,18},{18,10},{11,19},{19,11},{12,20... | collective-permute-start | bytes 786440 | tf_op jit(solution)/shard_map/ppermute | solution.py:437
  101.2 7.0 %copy-start = (bf16[1,1024,2048]{2,1,0:T(8,128)(2,1)S(1)}, bf16[1,1024,2048]{2,1,0:T(8,128)(2,1)}, u32[]{:S(2)}) copy-start(bf16[1,1024,2048]{2,1,0:T(8,128)(2,1)} %param.10) | copy-start | bytes 12582916
  101.2 7.0 %copy-start.2 = (bf16[1,1,1024,128]{3,2,1,0:T(8,128)(2,1)S(1)}, bf16[1,1,1024,128]{3,2,1,0:T(8,128)(2,1)}, u32[]{:S(2)}) copy-start(bf16[1,1,1024,128]{3,2,1,0:T(8,128)(2,1)} %param.11) | copy-start | bytes 786436
  101.8 6.4 %collective-permute-start.25 = (bf16[2,32,2048]{2,1,0:T(8,128)(2,1)S(1)}, bf16[2,32,2048]{2,1,0:T(8,128)(2,1)S(1)}, u32[]{:S(2)}, u32[]{:S(2)}) collective-permute-start(bf16[2,32,2048]{2,1,0:T(8,128)(2,1)S(1)} %shard_map.112.refs_3_), channel_id=1, source_target_pairs={{0,1},{1,0},{2,3},{3,2},{4,5},{5,4},{6,7},{7,6},{8,9},{9,8},{10,11... | collective-permute-start | bytes 786440 | tf_op jit(solution)/shard_map/ppermute | solution.py:527
  114.0 2.4 %collective-permute-start.27 = (f32[192,1024]{1,0:T(8,128)S(1)}, f32[192,1024]{1,0:T(8,128)S(1)}, u32[]{:S(2)}, u32[]{:S(2)}) collective-permute-start(f32[192,1024]{1,0:T(8,128)S(1)} %get-tuple-element.80), channel_id=1, source_target_pairs={{0,2},{2,0},{4,6},{6,4},{1,3},{3,1},{5,7},{7,5},{8,10},{10,8},{12,... | collective-permute-start | bytes 2359304 | tf_op jit(solution)/shard_map/ppermute | solution.py:431
  114.1 6.1 %collective-permute-start.26 = (bf16[64,1024]{1,0:T(8,128)(2,1)S(1)}, bf16[64,1024]{1,0:T(8,128)(2,1)S(1)}, u32[]{:S(2)}, u32[]{:S(2)}) collective-permute-start(bf16[64,1024]{1,0:T(8,128)(2,1)S(1)} %get-tuple-element.77), channel_id=1, source_target_pairs={{0,4},{2,6},{4,0},{6,2},{1,5},{3,7},{5,1},{7,3},{8,12},{10,14},{12... | collective-permute-start | bytes 393224 | tf_op jit(solution)/shard_map/ppermute | solution.py:434
  117.0 12.0 %collective-permute-start.29 = (bf16[192,1024]{1,0:T(8,128)(2,1)S(1)}, bf16[192,1024]{1,0:T(8,128)(2,1)S(1)}, u32[]{:S(2)}, u32[]{:S(2)}) collective-permute-start(bf16[192,1024]{1,0:T(8,128)(2,1)S(1)} %shard_map.115.own_right), channel_id=1, source_target_pairs={{0,4},{2,6},{4,0},{6,2},{1,5},{3,7},{5,1},{7,3},{8,12},{10,14},{12... | collective-permute-start | bytes 1179656 | tf_op jit(solution)/shard_map/ppermute | solution.py:434
  118.5 12.7 %collective-permute-start.28 = (bf16[64,1024]{1,0:T(8,128)(2,1)S(1)}, bf16[64,1024]{1,0:T(8,128)(2,1)S(1)}, u32[]{:S(2)}, u32[]{:S(2)}) collective-permute-start(bf16[64,1024]{1,0:T(8,128)(2,1)S(1)} %get-tuple-element.81), channel_id=1, source_target_pairs={{0,4},{2,6},{4,0},{6,2},{1,5},{3,7},{5,1},{7,3},{8,12},{10,14},{12... | collective-permute-start | bytes 393224 | tf_op jit(solution)/shard_map/ppermute | solution.py:434
  131.3 1.6 %collective-permute-start.30 = (bf16[128,1024]{1,0:T(8,128)(2,1)S(1)}, bf16[128,1024]{1,0:T(8,128)(2,1)S(1)}, u32[]{:S(2)}, u32[]{:S(2)}) collective-permute-start(bf16[128,1024]{1,0:T(8,128)(2,1)S(1)} %slice_select_fusion.own_left), channel_id=1, source_target_pairs={{0,2},{2,0},{4,6},{6,4},{1,3},{3,1},{5,7},{7,5},{8,10},{10,8},{12,... | collective-permute-start | bytes 786440 | tf_op jit(solution)/shard_map/ppermute | solution.py:431

commit v8 on v7

--- a/solution.py
+++ b/solution.py
@@ -404,13 +404,6 @@
     total[...] = (kept[...] + arrived[...]).astype(BF16)
 
 
-def left_kernel(place, own_left, other_left, grad_left):
-    core = place[2]
-    half = own_left.shape[1]
-    grad_left[:, pl.ds(pl.multiple_of(core * half, half), half)] = own_left[...].astype(F32)
-    grad_left[:, pl.ds(pl.multiple_of((1 - core) * half, half), half)] = other_left[...].astype(F32)
-
-
 def right_kernel(place, own_right, other_right, grad_right, wide):
     outer = place[1]
     rank = wide.shape[0]
@@ -593,15 +586,12 @@
         joined,
         other_joined,
     )
-    (grad_left,) = small(
-        left_kernel,
-        [((rank, width), F32)],
-        [],
-        place,
-        best,
-        after(to_core(best), grad_right),
-        cost=pl.CostEstimate(flops=8 * 10**9, bytes_accessed=0, transcendentals=0),
-    )
+    there = after(to_core(best), grad_right)
+    grad_left = jnp.where(
+        core == 0,
+        jnp.concatenate([best, there], axis=1),
+        jnp.concatenate([there, best], axis=1),
+    ).astype(F32)
     (first_mix,) = small(
         functools.partial(add_kernel, 0),
         [(second_sent.shape, BF16)],

time: 137 us -> 136 us (level)
  Pallas kernels: 24.7 us -> 23.1 us
    pallas_call x15 -> x14, Pallas kernels: 13 us -> 11.5 us  [small(): pl.pallas_call(kernel, in_specs=[pl.BlockSpec(memory_space=pltpu.SMEM)] +...]
where the time goes in v8:
time: 136 us; the launch traced here: 134 us
  waiting for transfers between devices  63.8 us (47%)
  starting transfers between devices  41.2 us (30%)
  Pallas kernels  23.1 us (17%)
  local copies, waits for them, and re-layouts  2.84 us (2%)
  other arithmetic  2.12 us (2%)
    ppermute x14, waiting for transfers between devices, along(): return lax.ppermute(value, 'tensor', pairs)  31.1 us
    ppermute x14, starting transfers between devices, along(): return lax.ppermute(value, 'tensor', pairs)  23.7 us
    ppermute x6, waiting for transfers between devices, to_section(): return lax.ppermute(value, 'pipe', [(0, 1), (1, 0)])  16.2 us
    ppermute x7, waiting for transfers between devices, to_outer(): return lax.ppermute(value, 'dp', [(i, i ^ 2) for i in range(4)])  14.2 us
    pallas_call x14, Pallas kernels, small(): pl.pallas_call(kernel, in_specs=[pl.BlockSpec(memory_space=pltpu.SMEM)] +...  11.5 us
    ppermute x7, starting transfers between devices, to_outer(): return lax.ppermute(value, 'dp', [(i, i ^ 2) for i in range(4)])  9.94 us
    ppermute x6, starting transfers between devices, to_section(): return lax.ppermute(value, 'pipe', [(0, 1), (1, 0)])  6.88 us
    pallas_call x1, Pallas kernels, project(): pl.pallas_call(project_kernel, grid=(tiles,), in_specs=[pl.BlockSpec(memo...  5.85 us
  transfers between devices with their start and end apart: 31, of which 21 were waited for; matrix products, arithmetic and copies ran while one was open for 1% of the time, Pallas kernels for 6%

profile of v8, /device:TPU:0, one launch (start us, length us, event | category | flops | bytes accessed | tf_op | source)
XLA Modules:
  0.0 134.0 jit_solution(676942090843022511)
XLA Ops:
  0.6 0.5 collective-permute-start.1
  1.1 0.9 dynamic-slice_bitcast_fusion
  2.1 4.7 %collective-permute-start.4 = (bf16[32,1024]{1,0:T(8,128)(2,1)S(1)}, bf16[32,1024]{1,0:T(8,128)(2,1)S(1)}, u32[]{:S(2)}, u32[]{:S(2)}) collective-permute-start(bf16[32,1024]{1,0:T(8,128)(2,1)S(1)} %get-tuple-element.90), channel_id=1, source_target_pairs={{0,24},{8,16},{16,8},{24,0},{1,25},{9,17},{17,9},{25,1},{2,26},{10... | collective-permute-start | bytes 196616 | tf_op jit(solution)/shard_map/ppermute | solution.py:430
  6.8 0.6 collective-permute-start.3
  7.4 1.6 %collective-permute-start = (bf16[2,64,1024]{2,1,0:T(8,128)(2,1)}, bf16[2,64,1024]{2,1,0:T(8,128)(2,1)S(1)}, u32[]{:S(2)}, u32[]{:S(2)}) collective-permute-start(bf16[2,64,1024]{2,1,0:T(8,128)(2,1)} %bitcast.49), channel_id=1, source_target_pairs={{0,4},{2,6},{4,0},{6,2},{1,5},{3,7},{5,1},{7,3},{8,12},{10,14},{12... | collective-permute-start | bytes 786440 | tf_op jit(solution)/shard_map/ppermute | solution.py:427
  9.2 0.9 copy-done.1
  10.1 0.9 copy-done.5
  11.1 0.6 shard_map.102
  11.6 1.0 collective-permute-done.3
  12.7 0.9 fusion.2
  13.7 1.3 collective-permute-done.5.other_half
  15.0 0.7 collective-permute-done.other_mix
  15.7 5.8 %shard_map.103 = (bf16[2,2,32,2048]{3,2,1,0:T(8,128)(2,1)S(1)}, bf16[2,2,32,2176]{3,2,1,0:T(8,128)(2,1)S(1)}, bf16[2,32,2176]{2,1,0:T(8,128)(2,1)S(1)}, bf16[2,3...) custom-call(s32[4]{0:T(128)S(1)} %pad_add_fusion.place, ...), custom_call_target="tpu_custom_call" | custom-call | tf_op jit(solution)/shard_map/pallas_call | solution.py:239
  21.6 3.3 %collective-permute-start.11 = (bf16[2,32,2048]{2,1,0:T(8,128)(2,1)S(1)}, bf16[2,32,2048]{2,1,0:T(8,128)(2,1)S(1)}, u32[]{:S(2)}, u32[]{:S(2)}) collective-permute-start(bf16[2,32,2048]{2,1,0:T(8,128)(2,1)S(1)} %get-tuple-element.54), channel_id=1, source_target_pairs={{0,8},{24,16},{1,9},{25,17},{2,10},{26,18},{3,11},{27,19},{4,12},{... | collective-permute-start | bytes 786440 | tf_op jit(solution)/shard_map/ppermute | solution.py:430
  24.9 1.3 collective-permute-start.10
  26.3 0.7 collective-permute-start.8
  26.9 0.7 collective-permute-start.9
  27.6 3.9 %collective-permute-start.7 = (bf16[2,2,32,2176]{3,2,1,0:T(8,128)(2,1)S(1)}, bf16[2,2,32,2176]{3,2,1,0:T(8,128)(2,1)S(1)}, u32[]{:S(2)}, u32[]{:S(2)}) collective-permute-start(bf16[2,2,32,2176]{3,2,1,0:T(8,128)(2,1)S(1)} %get-tuple-element.51), channel_id=1, source_target_pairs={{0,8},{8,0},{16,24},{24,16},{1,9},{9,1},{17,25},{25,17},{2,10},{10... | collective-permute-start | bytes 1671176 | tf_op jit(solution)/shard_map/ppermute | solution.py:430
  31.5 0.6 shard_map.104
  32.2 1.5 %collective-permute-start.6 = (bf16[2,2,2,16,2048]{4,3,2,1,0:T(8,128)(2,1)S(1)}, bf16[2,2,2,16,2048]{4,3,2,1,0:T(8,128)(2,1)S(1)}, u32[]{:S(2)}, u32[]{:S(2)}) collective-permute-start(bf16[2,2,2,16,2048]{4,3,2,1,0:T(8,128)(2,1)S(1)} %get-tuple-element.50), channel_id=1, source_target_pairs={{0,4},{2,6},{4,0},{6,2},{1,5},{3,7},{5,1},{7,3},{8,12},{10,14},{12... | collective-permute-start | bytes 1572872 | tf_op jit(solution)/shard_map/ppermute | solution.py:427
  33.7 3.9 %collective-permute-done.10.passed = bf16[2,32,2176]{2,1,0:T(8,128)(2,1)S(1)} collective-permute-done((bf16[2,32,2176]{2,1,0:T(8,128)(2,1)S(1)}, bf16[2,32,2176]{2,1,0:T(8,128)(2,1)S(1)}, u32[]{:S(2)}, u32[]{:S(2)}) %collective-permute-start.10) | collective-permute-done | bytes 278560 | tf_op jit(solution)/shard_map/ppermute | solution.py:430
  37.6 0.6 shard_map.105
  38.3 4.4 %collective-permute-start.12 = (bf16[2,32,2304]{2,1,0:T(8,128)(2,1)S(1)}, bf16[2,32,2304]{2,1,0:T(8,128)(2,1)S(1)}, u32[]{:S(2)}, u32[]{:S(2)}) collective-permute-start(bf16[2,32,2304]{2,1,0:T(8,128)(2,1)S(1)} %shard_map.105), channel_id=1, source_target_pairs={{0,16},{8,24},{16,0},{24,8},{1,17},{9,25},{17,1},{25,9},{2,18},{10... | collective-permute-start | bytes 884744 | tf_op jit(solution)/shard_map/ppermute | solution.py:430
  42.7 0.6 shard_map.106
  43.4 1.2 collective-permute-done.6.arrived
  44.6 6.7 %collective-permute-done.7.beside.refs_14_ = bf16[2,2,32,2176]{3,2,1,0:T(8,128)(2,1)S(1)} collective-permute-done((bf16[2,2,32,2176]{3,2,1,0:T(8,128)(2,1)S(1)}, bf16[2,2,32,2176]{3,2,1,0:T(8,128)(2,1)S(1)}, u32[]{:S(2)}, u32[]{:S(2)}) %collective-permute-start.7) | collective-permute-done | bytes 557088 | tf_op jit(solution)/shard_map/ppermute | solution.py:430
  51.3 14.7 %collective-permute-done.13.refs_3_ = bf16[2,32,2048]{2,1,0:T(8,128)(2,1)S(1)} collective-permute-done((bf16[2,32,2048]{2,1,0:T(8,128)(2,1)S(1)}, bf16[2,32,2048]{2,1,0:T(8,128)(2,1)S(1)}, u32[]{:S(2)}, u32[]{:S(2)}) %collective-permute-start.13) | collective-permute-done | bytes 262176 | tf_op jit(solution)/shard_map/ppermute | solution.py:430
  66.0 0.8 shard_map.107
  66.8 1.6 %collective-permute-start.14 = (bf16[2,32,2048]{2,1,0:T(8,128)(2,1)S(1)}, bf16[2,32,2048]{2,1,0:T(8,128)(2,1)S(1)}, u32[]{:S(2)}, u32[]{:S(2)}) collective-permute-start(bf16[2,32,2048]{2,1,0:T(8,128)(2,1)S(1)} %get-tuple-element.61), channel_id=1, source_target_pairs={{0,1},{1,0},{2,3},{3,2},{4,5},{5,4},{6,7},{7,6},{8,9},{9,8},{10,11... | collective-permute-start | bytes 786440 | tf_op jit(solution)/shard_map/ppermute | solution.py:520
  68.4 4.8 %collective-permute-done.14.other = bf16[2,32,2048]{2,1,0:T(8,128)(2,1)S(1)} collective-permute-done((bf16[2,32,2048]{2,1,0:T(8,128)(2,1)S(1)}, bf16[2,32,2048]{2,1,0:T(8,128)(2,1)S(1)}, u32[]{:S(2)}, u32[]{:S(2)}) %collective-permute-start.14) | collective-permute-done | bytes 262176 | tf_op jit(solution)/shard_map/ppermute | solution.py:520
  73.2 0.9 shard_map.108
  74.1 1.6 %collective-permute-start.15 = (f32[32,128]{1,0:T(8,128)S(1)}, f32[32,128]{1,0:T(8,128)S(1)}, u32[]{:S(2)}, u32[]{:S(2)}) collective-permute-start(f32[32,128]{1,0:T(8,128)S(1)} %get-tuple-element.63.sums), channel_id=1, source_target_pairs={{0,4},{2,6},{4,0},{6,2},{1,5},{3,7},{5,1},{7,3},{8,12},{10,14},{12... | collective-permute-start | bytes 49160 | tf_op jit(solution)/shard_map/ppermute | solution.py:427
  75.7 2.2 %collective-permute-done.15.other_sums = f32[32,128]{1,0:T(8,128)S(1)} collective-permute-done((f32[32,128]{1,0:T(8,128)S(1)}, f32[32,128]{1,0:T(8,128)S(1)}, u32[]{:S(2)}, u32[]{:S(2)}) %collective-permute-start.15) | collective-permute-done | bytes 16416 | tf_op jit(solution)/shard_map/ppermute | solution.py:427
  77.9 0.8 shard_map.109.refs_0_
  78.7 1.6 %collective-permute-start.23 = (bf16[2,32,2048]{2,1,0:T(8,128)(2,1)S(1)}, bf16[2,32,2048]{2,1,0:T(8,128)(2,1)S(1)}, u32[]{:S(2)}, u32[]{:S(2)}) collective-permute-start(bf16[2,32,2048]{2,1,0:T(8,128)(2,1)S(1)} %shard_map.109.refs_0_), channel_id=1, source_target_pairs={{0,1},{1,0},{2,3},{3,2},{4,5},{5,4},{6,7},{7,6},{8,9},{9,8},{10,11... | collective-permute-start | bytes 786440 | tf_op jit(solution)/shard_map/ppermute | solution.py:520
  80.3 1.9 %collective-permute-start.18 = (bf16[2,32,2048]{2,1,0:T(8,128)(2,1)S(1)}, bf16[2,32,2048]{2,1,0:T(8,128)(2,1)S(1)}, u32[]{:S(2)}, u32[]{:S(2)}) collective-permute-start(bf16[2,32,2048]{2,1,0:T(8,128)(2,1)S(1)} %shard_map.109.refs_0_), channel_id=1, source_target_pairs={{0,8},{8,0},{16,24},{24,16},{1,9},{9,1},{17,25},{25,17},{2,10},{10... | collective-permute-start | bytes 786440 | tf_op jit(solution)/shard_map/ppermute | solution.py:430
  82.2 0.5 collective-permute-start.16
  82.7 2.7 %collective-permute-done.23.refs_4_ = bf16[2,32,2048]{2,1,0:T(8,128)(2,1)S(1)} collective-permute-done((bf16[2,32,2048]{2,1,0:T(8,128)(2,1)S(1)}, bf16[2,32,2048]{2,1,0:T(8,128)(2,1)S(1)}, u32[]{:S(2)}, u32[]{:S(2)}) %collective-permute-start.23) | collective-permute-done | bytes 262176 | tf_op jit(solution)/shard_map/ppermute | solution.py:520
  85.4 3.8 %collective-permute-done.19.refs_2_ = bf16[2,32,2048]{2,1,0:T(8,128)(2,1)S(1)} collective-permute-done((bf16[2,32,2048]{2,1,0:T(8,128)(2,1)S(1)}, bf16[2,32,2048]{2,1,0:T(8,128)(2,1)S(1)}, u32[]{:S(2)}, u32[]{:S(2)}) %collective-permute-start.19) | collective-permute-done | bytes 262176 | tf_op jit(solution)/shard_map/ppermute | solution.py:430
  89.7 1.3 collective-permute-start.21
  91.0 1.5 %collective-permute-start.22 = (bf16[2,32,2048]{2,1,0:T(8,128)(2,1)S(1)}, bf16[2,32,2048]{2,1,0:T(8,128)(2,1)S(1)}, u32[]{:S(2)}, u32[]{:S(2)}) collective-permute-start(bf16[2,32,2048]{2,1,0:T(8,128)(2,1)S(1)} %collective-permute-done.18.refs_1_), channel_id=1, source_target_pairs={{0,1},{1,0},{2,3},{3,2},{4,5},{5,4},{6,7},{7,6},{8,9},{9,8},{10,11... | collective-permute-start | bytes 786440 | tf_op jit(solution)/shard_map/ppermute | solution.py:520
  92.5 0.7 shard_map.110
  93.2 1.6 %collective-permute-start.17 = (bf16[2,2,16,2048]{3,2,1,0:T(8,128)(2,1)S(1)}, bf16[2,2,16,2048]{3,2,1,0:T(8,128)(2,1)S(1)}, u32[]{:S(2)}, u32[]{:S(2)}) collective-permute-start(bf16[2,2,16,2048]{3,2,1,0:T(8,128)(2,1)S(1)} %get-tuple-element.67), channel_id=1, source_target_pairs={{0,4},{2,6},{4,0},{6,2},{1,5},{3,7},{5,1},{7,3},{8,12},{10,14},{12... | collective-permute-start | bytes 786440 | tf_op jit(solution)/shard_map/ppermute | solution.py:427
  94.8 0.7 collective-permute-start.20
  95.4 1.6 %collective-permute-done.24.refs_6_ = bf16[2,32,2048]{2,1,0:T(8,128)(2,1)S(1)} collective-permute-done((bf16[2,32,2048]{2,1,0:T(8,128)(2,1)S(1)}, bf16[2,32,2048]{2,1,0:T(8,128)(2,1)S(1)}, u32[]{:S(2)}, u32[]{:S(2)}) %collective-permute-start.24) | collective-permute-done | bytes 262176 | tf_op jit(solution)/shard_map/ppermute | solution.py:520
  97.0 1.0 collective-permute-done.21.farthest
  98.0 1.8 %collective-permute-done.22.refs_5_ = bf16[2,32,2048]{2,1,0:T(8,128)(2,1)S(1)} collective-permute-done((bf16[2,32,2048]{2,1,0:T(8,128)(2,1)S(1)}, bf16[2,32,2048]{2,1,0:T(8,128)(2,1)S(1)}, u32[]{:S(2)}, u32[]{:S(2)}) %collective-permute-start.22) | collective-permute-done | bytes 262176 | tf_op jit(solution)/shard_map/ppermute | solution.py:520
  99.8 1.4 %shard_map.111 = bf16[2,16,8192]{2,1,0:T(8,128)(2,1)} custom-call(s32[4]{0:T(128)S(1)} %pad_add_fusion.place, bf16[2,2,16,2048]{3,2,1,0:T(8,128)(2,1)S(1)} %get-tuple-element.66.here, bf16[2,2,16,2048]{3,2,1,0:T(8,128)(2,1)S(1)} %collective-permute-done.17.arrived), custom_call_target="tpu_custom_call" | custom-call | flops 3000000000 | tf_op jit(solution)/shard_map/pallas_call | solution.py:43
  101.2 0.6 shard_map.112.refs_3_
  101.8 1.2 collective-permute-start.25
  103.0 5.2 %collective-permute-done.25.refs_7_ = bf16[2,32,2048]{2,1,0:T(8,128)(2,1)S(1)} collective-permute-done((bf16[2,32,2048]{2,1,0:T(8,128)(2,1)S(1)}, bf16[2,32,2048]{2,1,0:T(8,128)(2,1)S(1)}, u32[]{:S(2)}, u32[]{:S(2)}) %collective-permute-start.25) | collective-permute-done | bytes 262176 | tf_op jit(solution)/shard_map/ppermute | solution.py:520
  108.2 5.8 %shard_map.113 = (f32[2,64,1024]{2,1,0:T(8,128)S(1)}, bf16[64,1024]{1,0:T(8,128)(2,1)S(1)}, bf16[64,1024]{1,0:T(8,128)(2,1)S(1)}, f32[192,1024]{1,0:T(8,128)S(1)}, f32[192,1024]{1,0:T(8,128)S(1)}) custom-call(s32[4]{0:T(128)S(1)} %pad_add_fusion.place, bf16[2,32,2048]{2,1,0:T(8,128)(2,1)S(1)} %shard_map.109.refs_0_, ...), custom_call_target="tpu_custom_call" | custom-call | tf_op jit(solution)/shard_map/pallas_call | solution.py:350
  114.1 1.6 %collective-permute-start.26 = (bf16[64,1024]{1,0:T(8,128)(2,1)S(1)}, bf16[64,1024]{1,0:T(8,128)(2,1)S(1)}, u32[]{:S(2)}, u32[]{:S(2)}) collective-permute-start(bf16[64,1024]{1,0:T(8,128)(2,1)S(1)} %get-tuple-element.77), channel_id=1, source_target_pairs={{0,4},{2,6},{4,0},{6,2},{1,5},{3,7},{5,1},{7,3},{8,12},{10,14},{12... | collective-permute-start | bytes 393224 | tf_op jit(solution)/shard_map/ppermute | solution.py:427
  115.6 0.7 collective-permute-done.27.arrived
  116.4 0.6 shard_map.115.own_right
  117.0 1.6 %collective-permute-start.29 = (bf16[192,1024]{1,0:T(8,128)(2,1)S(1)}, bf16[192,1024]{1,0:T(8,128)(2,1)S(1)}, u32[]{:S(2)}, u32[]{:S(2)}) collective-permute-start(bf16[192,1024]{1,0:T(8,128)(2,1)S(1)} %shard_map.115.own_right), channel_id=1, source_target_pairs={{0,4},{2,6},{4,0},{6,2},{1,5},{3,7},{5,1},{7,3},{8,12},{10,14},{12... | collective-permute-start | bytes 1179656 | tf_op jit(solution)/shard_map/ppermute | solution.py:427
  118.5 0.5 collective-permute-start.28
  119.1 1.1 collective-permute-done.26.arrived
  120.2 0.6 shard_map.114.first
  120.7 8.3 %collective-permute-done.29.other_right = bf16[192,1024]{1,0:T(8,128)(2,1)S(1)} collective-permute-done((bf16[192,1024]{1,0:T(8,128)(2,1)S(1)}, bf16[192,1024]{1,0:T(8,128)(2,1)S(1)}, u32[]{:S(2)}, u32[]{:S(2)}) %collective-permute-start.29) | collective-permute-done | bytes 393248 | tf_op jit(solution)/shard_map/ppermute | solution.py:427
  129.0 1.6 %shard_map.116 = f32[1024,128]{1,0:T(8,128)} custom-call(s32[4]{0:T(128)S(1)} %pad_add_fusion.place, bf16[192,1024]{1,0:T(8,128)(2,1)S(1)} %shard_map.115.own_right, bf16[192,1024]{1,0:T(8,128)(2,1)S(1)} %collective-permute-done.29.other_right), custom_call_target="tpu_custom_call" | custom-call | tf_op jit(solution)/shard_map/pallas_call | solution.py:43
  130.6 0.7 collective-permute-done.28.arrived
  131.4 1.3 shard_map.117
  132.9 1.1 fusion
  (35 shorter events, 1.3 us)
Async XLA Ops:
  0.6 15.1 %collective-permute-start.1 = (bf16[1024,2048]{1,0:T(8,128)(2,1)}, bf16[1024,2048]{1,0:T(8,128)(2,1)}, u32[]{:S(2)}, u32[]{:S(2)}) collective-permute-start(bf16[1024,2048]{1,0:T(8,128)(2,1)} %bitcast.40), channel_id=1, source_target_pairs={{0,2},{2,0},{4,6},{6,4},{1,3},{3,1},{5,7},{7,5},{8,10},{10,8},{12,... | collective-permute-start | bytes 12582920 | tf_op jit(solution)/shard_map/ppermute | solution.py:424
  2.1 10.6 %collective-permute-start.4 = (bf16[32,1024]{1,0:T(8,128)(2,1)S(1)}, bf16[32,1024]{1,0:T(8,128)(2,1)S(1)}, u32[]{:S(2)}, u32[]{:S(2)}) collective-permute-start(bf16[32,1024]{1,0:T(8,128)(2,1)S(1)} %get-tuple-element.90), channel_id=1, source_target_pairs={{0,24},{8,16},{16,8},{24,0},{1,25},{9,17},{17,9},{25,1},{2,26},{10... | collective-permute-start | bytes 196616 | tf_op jit(solution)/shard_map/ppermute | solution.py:430
  6.8 5.9 %collective-permute-start.2 = (bf16[32,1024]{1,0:T(8,128)(2,1)S(1)}, bf16[32,1024]{1,0:T(8,128)(2,1)S(1)}, u32[]{:S(2)}, u32[]{:S(2)}) collective-permute-start(bf16[32,1024]{1,0:T(8,128)(2,1)S(1)} %get-tuple-element.91), channel_id=1, source_target_pairs={{0,8},{8,0},{16,24},{24,16},{1,9},{9,1},{17,25},{25,17},{2,10},{10... | collective-permute-start | bytes 196616 | tf_op jit(solution)/shard_map/ppermute | solution.py:430
  6.8 5.9 %collective-permute-start.3 = (bf16[32,1024]{1,0:T(8,128)(2,1)S(1)}, bf16[32,1024]{1,0:T(8,128)(2,1)S(1)}, u32[]{:S(2)}, u32[]{:S(2)}) collective-permute-start(bf16[32,1024]{1,0:T(8,128)(2,1)S(1)} %get-tuple-element.92), channel_id=1, source_target_pairs={{0,16},{8,24},{16,0},{24,8},{1,17},{9,25},{17,1},{25,9},{2,18},{10... | collective-permute-start | bytes 196616 | tf_op jit(solution)/shard_map/ppermute | solution.py:430
  7.4 8.3 %collective-permute-start = (bf16[2,64,1024]{2,1,0:T(8,128)(2,1)}, bf16[2,64,1024]{2,1,0:T(8,128)(2,1)S(1)}, u32[]{:S(2)}, u32[]{:S(2)}) collective-permute-start(bf16[2,64,1024]{2,1,0:T(8,128)(2,1)} %bitcast.49), channel_id=1, source_target_pairs={{0,4},{2,6},{4,0},{6,2},{1,5},{3,7},{5,1},{7,3},{8,12},{10,14},{12... | collective-permute-start | bytes 786440 | tf_op jit(solution)/shard_map/ppermute | solution.py:427
  9.2 1.0 copy-start.1
  10.1 0.9 copy-start.5
  13.6 17.9 %copy-start.3 = (bf16[2,1,16,8192]{3,2,1,0:T(8,128)(2,1)S(1)}, bf16[2,1,16,8192]{3,2,1,0:T(8,128)(2,1)}, u32[]{:S(2)}) copy-start(bf16[2,1,16,8192]{3,2,1,0:T(8,128)(2,1)} %param.8) | copy-start | bytes 1572868
  13.6 17.9 %copy-start.4 = (bf16[2,1,16,8192]{3,2,1,0:T(8,128)(2,1)S(1)}, bf16[2,1,16,8192]{3,2,1,0:T(8,128)(2,1)}, u32[]{:S(2)}) copy-start(bf16[2,1,16,8192]{3,2,1,0:T(8,128)(2,1)} %param.9) | copy-start | bytes 1572868
  13.6 1.4 %collective-permute-start.5 = (bf16[2,32,1024]{2,1,0:T(8,128)(2,1)S(1)}, bf16[2,32,1024]{2,1,0:T(8,128)(2,1)S(1)}, u32[]{:S(2)}, u32[]{:S(2)}) collective-permute-start(bf16[2,32,1024]{2,1,0:T(8,128)(2,1)S(1)} %pad_maximum_fusion.own_half), channel_id=1, source_target_pairs={{0,2},{2,0},{4,6},{6,4},{1,3},{3,1},{5,7},{7,5},{8,10},{10,8},{12,... | collective-permute-start | bytes 393224 | tf_op jit(solution)/shard_map/ppermute | solution.py:424
  21.6 46.8 %copy-start.6 = (bf16[8192]{0:T(1024)(128)(2,1)S(1)}, bf16[8192]{0:T(1024)(128)(2,1)}, u32[]{:S(2)}) copy-start(bf16[8192]{0:T(1024)(128)(2,1)} %param.13) | copy-start | bytes 49156
  21.6 10.6 %collective-permute-start.11 = (bf16[2,32,2048]{2,1,0:T(8,128)(2,1)S(1)}, bf16[2,32,2048]{2,1,0:T(8,128)(2,1)S(1)}, u32[]{:S(2)}, u32[]{:S(2)}) collective-permute-start(bf16[2,32,2048]{2,1,0:T(8,128)(2,1)S(1)} %get-tuple-element.54), channel_id=1, source_target_pairs={{0,8},{24,16},{1,9},{25,17},{2,10},{26,18},{3,11},{27,19},{4,12},{... | collective-permute-start | bytes 786440 | tf_op jit(solution)/shard_map/ppermute | solution.py:430
  24.9 12.7 %collective-permute-start.10 = (bf16[2,32,2176]{2,1,0:T(8,128)(2,1)S(1)}, bf16[2,32,2176]{2,1,0:T(8,128)(2,1)S(1)}, u32[]{:S(2)}, u32[]{:S(2)}) collective-permute-start(bf16[2,32,2176]{2,1,0:T(8,128)(2,1)S(1)} %get-tuple-element.53), channel_id=1, source_target_pairs={{0,8},{24,16},{1,9},{25,17},{2,10},{26,18},{3,11},{27,19},{4,12},{... | collective-permute-start | bytes 835592 | tf_op jit(solution)/shard_map/ppermute | solution.py:430
  26.3 11.4 %collective-permute-start.8 = (bf16[2,32,2176]{2,1,0:T(8,128)(2,1)S(1)}, bf16[2,32,2176]{2,1,0:T(8,128)(2,1)S(1)}, u32[]{:S(2)}, u32[]{:S(2)}) collective-permute-start(bf16[2,32,2176]{2,1,0:T(8,128)(2,1)S(1)} %get-tuple-element.53), channel_id=1, source_target_pairs={{8,16},{16,8},{9,17},{17,9},{10,18},{18,10},{11,19},{19,11},{12,20... | collective-permute-start | bytes 835592 | tf_op jit(solution)/shard_map/ppermute | solution.py:430
  26.9 6.8 %collective-permute-start.9 = (bf16[2,32,2048]{2,1,0:T(8,128)(2,1)S(1)}, bf16[2,32,2048]{2,1,0:T(8,128)(2,1)S(1)}, u32[]{:S(2)}, u32[]{:S(2)}) collective-permute-start(bf16[2,32,2048]{2,1,0:T(8,128)(2,1)S(1)} %get-tuple-element.54), channel_id=1, source_target_pairs={{8,16},{16,8},{9,17},{17,9},{10,18},{18,10},{11,19},{19,11},{12,20... | collective-permute-start | bytes 786440 | tf_op jit(solution)/shard_map/ppermute | solution.py:430
  27.6 23.6 %collective-permute-start.7 = (bf16[2,2,32,2176]{3,2,1,0:T(8,128)(2,1)S(1)}, bf16[2,2,32,2176]{3,2,1,0:T(8,128)(2,1)S(1)}, u32[]{:S(2)}, u32[]{:S(2)}) collective-permute-start(bf16[2,2,32,2176]{3,2,1,0:T(8,128)(2,1)S(1)} %get-tuple-element.51), channel_id=1, source_target_pairs={{0,8},{8,0},{16,24},{24,16},{1,9},{9,1},{17,25},{25,17},{2,10},{10... | collective-permute-start | bytes 1671176 | tf_op jit(solution)/shard_map/ppermute | solution.py:430
  32.2 12.4 %collective-permute-start.6 = (bf16[2,2,2,16,2048]{4,3,2,1,0:T(8,128)(2,1)S(1)}, bf16[2,2,2,16,2048]{4,3,2,1,0:T(8,128)(2,1)S(1)}, u32[]{:S(2)}, u32[]{:S(2)}) collective-permute-start(bf16[2,2,2,16,2048]{4,3,2,1,0:T(8,128)(2,1)S(1)} %get-tuple-element.50), channel_id=1, source_target_pairs={{0,4},{2,6},{4,0},{6,2},{1,5},{3,7},{5,1},{7,3},{8,12},{10,14},{12... | collective-permute-start | bytes 1572872 | tf_op jit(solution)/shard_map/ppermute | solution.py:427
  38.3 27.7 %collective-permute-start.12 = (bf16[2,32,2304]{2,1,0:T(8,128)(2,1)S(1)}, bf16[2,32,2304]{2,1,0:T(8,128)(2,1)S(1)}, u32[]{:S(2)}, u32[]{:S(2)}) collective-permute-start(bf16[2,32,2304]{2,1,0:T(8,128)(2,1)S(1)} %shard_map.105), channel_id=1, source_target_pairs={{0,16},{8,24},{16,0},{24,8},{1,17},{9,25},{17,1},{25,9},{2,18},{10... | collective-permute-start | bytes 884744 | tf_op jit(solution)/shard_map/ppermute | solution.py:430
  43.3 22.7 %collective-permute-start.13 = (bf16[2,32,2048]{2,1,0:T(8,128)(2,1)S(1)}, bf16[2,32,2048]{2,1,0:T(8,128)(2,1)S(1)}, u32[]{:S(2)}, u32[]{:S(2)}) collective-permute-start(bf16[2,32,2048]{2,1,0:T(8,128)(2,1)S(1)} %shard_map.106), channel_id=1, source_target_pairs={{0,16},{8,24},{16,0},{24,8},{1,17},{9,25},{17,1},{25,9},{2,18},{10... | collective-permute-start | bytes 786440 | tf_op jit(solution)/shard_map/ppermute | solution.py:430
  66.8 6.4 %collective-permute-start.14 = (bf16[2,32,2048]{2,1,0:T(8,128)(2,1)S(1)}, bf16[2,32,2048]{2,1,0:T(8,128)(2,1)S(1)}, u32[]{:S(2)}, u32[]{:S(2)}) collective-permute-start(bf16[2,32,2048]{2,1,0:T(8,128)(2,1)S(1)} %get-tuple-element.61), channel_id=1, source_target_pairs={{0,1},{1,0},{2,3},{3,2},{4,5},{5,4},{6,7},{7,6},{8,9},{9,8},{10,11... | collective-permute-start | bytes 786440 | tf_op jit(solution)/shard_map/ppermute | solution.py:520
  74.1 3.8 %collective-permute-start.15 = (f32[32,128]{1,0:T(8,128)S(1)}, f32[32,128]{1,0:T(8,128)S(1)}, u32[]{:S(2)}, u32[]{:S(2)}) collective-permute-start(f32[32,128]{1,0:T(8,128)S(1)} %get-tuple-element.63.sums), channel_id=1, source_target_pairs={{0,4},{2,6},{4,0},{6,2},{1,5},{3,7},{5,1},{7,3},{8,12},{10,14},{12... | collective-permute-start | bytes 49160 | tf_op jit(solution)/shard_map/ppermute | solution.py:427
  78.7 6.7 %collective-permute-start.23 = (bf16[2,32,2048]{2,1,0:T(8,128)(2,1)S(1)}, bf16[2,32,2048]{2,1,0:T(8,128)(2,1)S(1)}, u32[]{:S(2)}, u32[]{:S(2)}) collective-permute-start(bf16[2,32,2048]{2,1,0:T(8,128)(2,1)S(1)} %shard_map.109.refs_0_), channel_id=1, source_target_pairs={{0,1},{1,0},{2,3},{3,2},{4,5},{5,4},{6,7},{7,6},{8,9},{9,8},{10,11... | collective-permute-start | bytes 786440 | tf_op jit(solution)/shard_map/ppermute | solution.py:520
  80.3 8.9 %collective-permute-start.19 = (bf16[2,32,2048]{2,1,0:T(8,128)(2,1)S(1)}, bf16[2,32,2048]{2,1,0:T(8,128)(2,1)S(1)}, u32[]{:S(2)}, u32[]{:S(2)}) collective-permute-start(bf16[2,32,2048]{2,1,0:T(8,128)(2,1)S(1)} %shard_map.109.refs_0_), channel_id=1, source_target_pairs={{0,16},{8,24},{16,0},{24,8},{1,17},{9,25},{17,1},{25,9},{2,18},{10... | collective-permute-start | bytes 786440 | tf_op jit(solution)/shard_map/ppermute | solution.py:430
  80.3 9.4 %collective-permute-start.18 = (bf16[2,32,2048]{2,1,0:T(8,128)(2,1)S(1)}, bf16[2,32,2048]{2,1,0:T(8,128)(2,1)S(1)}, u32[]{:S(2)}, u32[]{:S(2)}) collective-permute-start(bf16[2,32,2048]{2,1,0:T(8,128)(2,1)S(1)} %shard_map.109.refs_0_), channel_id=1, source_target_pairs={{0,8},{8,0},{16,24},{24,16},{1,9},{9,1},{17,25},{25,17},{2,10},{10... | collective-permute-start | bytes 786440 | tf_op jit(solution)/shard_map/ppermute | solution.py:430
  82.2 10.3 %collective-permute-start.16 = (bf16[2,32,2048]{2,1,0:T(8,128)(2,1)S(1)}, bf16[2,32,2048]{2,1,0:T(8,128)(2,1)S(1)}, u32[]{:S(2)}, u32[]{:S(2)}) collective-permute-start(bf16[2,32,2048]{2,1,0:T(8,128)(2,1)S(1)} %get-tuple-element.64), channel_id=1, source_target_pairs={{0,1},{1,0},{2,3},{3,2},{4,5},{5,4},{6,7},{7,6},{8,9},{9,8},{10,11... | collective-permute-start | bytes 786440 | tf_op jit(solution)/shard_map/ppermute | solution.py:520
  89.1 7.8 %collective-permute-start.24 = (bf16[2,32,2048]{2,1,0:T(8,128)(2,1)S(1)}, bf16[2,32,2048]{2,1,0:T(8,128)(2,1)S(1)}, u32[]{:S(2)}, u32[]{:S(2)}) collective-permute-start(bf16[2,32,2048]{2,1,0:T(8,128)(2,1)S(1)} %collective-permute-done.19.refs_2_), channel_id=1, source_target_pairs={{0,1},{1,0},{2,3},{3,2},{4,5},{5,4},{6,7},{7,6},{8,9},{9,8},{10,11... | collective-permute-start | bytes 786440 | tf_op jit(solution)/shard_map/ppermute | solution.py:520
  89.7 8.3 %collective-permute-start.21 = (bf16[2,32,2048]{2,1,0:T(8,128)(2,1)S(1)}, bf16[2,32,2048]{2,1,0:T(8,128)(2,1)S(1)}, u32[]{:S(2)}, u32[]{:S(2)}) collective-permute-start(bf16[2,32,2048]{2,1,0:T(8,128)(2,1)S(1)} %collective-permute-done.19.refs_2_), channel_id=1, source_target_pairs={{8,0},{16,24},{9,1},{17,25},{10,2},{18,26},{11,3},{19,27},{12,4},{... | collective-permute-start | bytes 786440 | tf_op jit(solution)/shard_map/ppermute | solution.py:430
  91.0 8.8 %collective-permute-start.22 = (bf16[2,32,2048]{2,1,0:T(8,128)(2,1)S(1)}, bf16[2,32,2048]{2,1,0:T(8,128)(2,1)S(1)}, u32[]{:S(2)}, u32[]{:S(2)}) collective-permute-start(bf16[2,32,2048]{2,1,0:T(8,128)(2,1)S(1)} %collective-permute-done.18.refs_1_), channel_id=1, source_target_pairs={{0,1},{1,0},{2,3},{3,2},{4,5},{5,4},{6,7},{7,6},{8,9},{9,8},{10,11... | collective-permute-start | bytes 786440 | tf_op jit(solution)/shard_map/ppermute | solution.py:520
  93.2 6.6 %collective-permute-start.17 = (bf16[2,2,16,2048]{3,2,1,0:T(8,128)(2,1)S(1)}, bf16[2,2,16,2048]{3,2,1,0:T(8,128)(2,1)S(1)}, u32[]{:S(2)}, u32[]{:S(2)}) collective-permute-start(bf16[2,2,16,2048]{3,2,1,0:T(8,128)(2,1)S(1)} %get-tuple-element.67), channel_id=1, source_target_pairs={{0,4},{2,6},{4,0},{6,2},{1,5},{3,7},{5,1},{7,3},{8,12},{10,14},{12... | collective-permute-start | bytes 786440 | tf_op jit(solution)/shard_map/ppermute | solution.py:427
  94.8 6.4 %collective-permute-start.20 = (bf16[2,32,2048]{2,1,0:T(8,128)(2,1)S(1)}, bf16[2,32,2048]{2,1,0:T(8,128)(2,1)S(1)}, u32[]{:S(2)}, u32[]{:S(2)}) collective-permute-start(bf16[2,32,2048]{2,1,0:T(8,128)(2,1)S(1)} %shard_map.109.refs_0_), channel_id=1, source_target_pairs={{8,16},{16,8},{9,17},{17,9},{10,18},{18,10},{11,19},{19,11},{12,20... | collective-permute-start | bytes 786440 | tf_op jit(solution)/shard_map/ppermute | solution.py:430
  101.2 7.0 %copy-start = (bf16[1,1024,2048]{2,1,0:T(8,128)(2,1)S(1)}, bf16[1,1024,2048]{2,1,0:T(8,128)(2,1)}, u32[]{:S(2)}) copy-start(bf16[1,1024,2048]{2,1,0:T(8,128)(2,1)} %param.10) | copy-start | bytes 12582916
  101.2 7.0 %copy-start.2 = (bf16[1,1,1024,128]{3,2,1,0:T(8,128)(2,1)S(1)}, bf16[1,1,1024,128]{3,2,1,0:T(8,128)(2,1)}, u32[]{:S(2)}) copy-start(bf16[1,1,1024,128]{3,2,1,0:T(8,128)(2,1)} %param.11) | copy-start | bytes 786436
  101.8 6.4 %collective-permute-start.25 = (bf16[2,32,2048]{2,1,0:T(8,128)(2,1)S(1)}, bf16[2,32,2048]{2,1,0:T(8,128)(2,1)S(1)}, u32[]{:S(2)}, u32[]{:S(2)}) collective-permute-start(bf16[2,32,2048]{2,1,0:T(8,128)(2,1)S(1)} %shard_map.112.refs_3_), channel_id=1, source_target_pairs={{0,1},{1,0},{2,3},{3,2},{4,5},{5,4},{6,7},{7,6},{8,9},{9,8},{10,11... | collective-permute-start | bytes 786440 | tf_op jit(solution)/shard_map/ppermute | solution.py:520
  114.0 2.4 %collective-permute-start.27 = (f32[192,1024]{1,0:T(8,128)S(1)}, f32[192,1024]{1,0:T(8,128)S(1)}, u32[]{:S(2)}, u32[]{:S(2)}) collective-permute-start(f32[192,1024]{1,0:T(8,128)S(1)} %get-tuple-element.80), channel_id=1, source_target_pairs={{0,2},{2,0},{4,6},{6,4},{1,3},{3,1},{5,7},{7,5},{8,10},{10,8},{12,... | collective-permute-start | bytes 2359304 | tf_op jit(solution)/shard_map/ppermute | solution.py:424
  114.1 6.1 %collective-permute-start.26 = (bf16[64,1024]{1,0:T(8,128)(2,1)S(1)}, bf16[64,1024]{1,0:T(8,128)(2,1)S(1)}, u32[]{:S(2)}, u32[]{:S(2)}) collective-permute-start(bf16[64,1024]{1,0:T(8,128)(2,1)S(1)} %get-tuple-element.77), channel_id=1, source_target_pairs={{0,4},{2,6},{4,0},{6,2},{1,5},{3,7},{5,1},{7,3},{8,12},{10,14},{12... | collective-permute-start | bytes 393224 | tf_op jit(solution)/shard_map/ppermute | solution.py:427
  117.0 12.0 %collective-permute-start.29 = (bf16[192,1024]{1,0:T(8,128)(2,1)S(1)}, bf16[192,1024]{1,0:T(8,128)(2,1)S(1)}, u32[]{:S(2)}, u32[]{:S(2)}) collective-permute-start(bf16[192,1024]{1,0:T(8,128)(2,1)S(1)} %shard_map.115.own_right), channel_id=1, source_target_pairs={{0,4},{2,6},{4,0},{6,2},{1,5},{3,7},{5,1},{7,3},{8,12},{10,14},{12... | collective-permute-start | bytes 1179656 | tf_op jit(solution)/shard_map/ppermute | solution.py:427
  118.5 12.7 %collective-permute-start.28 = (bf16[64,1024]{1,0:T(8,128)(2,1)S(1)}, bf16[64,1024]{1,0:T(8,128)(2,1)S(1)}, u32[]{:S(2)}, u32[]{:S(2)}) collective-permute-start(bf16[64,1024]{1,0:T(8,128)(2,1)S(1)} %get-tuple-element.81), channel_id=1, source_target_pairs={{0,4},{2,6},{4,0},{6,2},{1,5},{3,7},{5,1},{7,3},{8,12},{10,14},{12... | collective-permute-start | bytes 393224 | tf_op jit(solution)/shard_map/ppermute | solution.py:427
  131.3 1.6 %collective-permute-start.30 = (bf16[128,1024]{1,0:T(8,128)(2,1)S(1)}, bf16[128,1024]{1,0:T(8,128)(2,1)S(1)}, u32[]{:S(2)}, u32[]{:S(2)}) collective-permute-start(bf16[128,1024]{1,0:T(8,128)(2,1)S(1)} %slice_select_fusion), channel_id=1, source_target_pairs={{0,2},{2,0},{4,6},{6,4},{1,3},{3,1},{5,7},{7,5},{8,10},{10,8},{12,... | collective-permute-start | bytes 786440 | tf_op jit(solution)/shard_map/ppermute | solution.py:424
